TPU v7x, 32 devices: a whole 2x2x4 slice. The times are simulated.
32 devices in a mesh: az: 8 (over z, x), ax: 4 (over y, core).
Axes of the slice: x: 2, y: 2, z: 4, core: 2. Of those that a mesh axis runs over, the one named last changes fastest.
Arguments:
- fields: float32 [5, 64, 128, 512], P(None, 'ax', 'az'), may hold values from -6.5 to 6.5, as said below
Outputs:
- advanced: float32 [5, 64, 128, 512], P(None, 'ax', 'az')
Inputs may be any that keep to these rules, and one draw needn't show every extreme that they name: `fields`: each field is a rough part plus, on every axial plane and cycle, a constant and a first azimuthal harmonic.
All inputs are finite; a program needn't handle non-finite values.
Results may differ from a plain program's by a relative error of at most 0.0003.
Values sent between devices are 32-bit elements; how exact they have to be, the bound alone decides.
No kernel may reach another device: no remote copies, remote signals or barrier semaphores. Data moves between devices by JAX's collectives and lax.ppermute only.
A program may use at most 128 MiB of HBM per device.

v0:
```python
import jax
import jax.numpy as jnp
from jax import lax
from jax.sharding import PartitionSpec as P

NEAR = 40


viscosity = 0.2
time_step = 0.1
buoyancy = 1.0


def swapped(block, axis, distance):
    count = lax.axis_size(axis)
    route = []
    for low in range(count):
        high = low | 1 << distance
        if high != low and high < count:
            route += [(low, high), (high, low)]
    return lax.ppermute(block, axis, route)


def with_halo(block, sides, width, periodic):
    for axis, dim in sides:
        count = lax.axis_size(axis)
        forward = [(i, i + 1) for i in range(count - 1)]
        if periodic:
            forward.append((count - 1, 0))
        backward = [(target, source) for source, target in forward]
        low = lax.ppermute(
            lax.slice_in_dim(block, block.shape[dim] - width, None, axis=dim), axis, forward
        )
        high = lax.ppermute(lax.slice_in_dim(block, 0, width, axis=dim), axis, backward)
        block = jnp.concatenate([low, block, high], axis=dim)
    return block


def mode_tables(theta_index, total_theta, modes):
    column = jnp.arange(modes, dtype=jnp.int32)
    product = theta_index[:, None] * column[None, :] % total_theta
    angle = product.astype(jnp.float32) * (2.0 * jnp.pi / total_theta)
    cosine = jnp.cos(angle)
    sine = jnp.sin(angle)
    weight = jnp.where(column == 0, 1.0, 2.0).astype(jnp.float32) / total_theta
    forward = jnp.concatenate([cosine * weight[None, :], sine * (2.0 / total_theta)], axis=1)
    inverse = jnp.concatenate([cosine, sine], axis=1)
    return (forward, inverse)


def cycle_mask(cycles, modes):
    cycle_index = jnp.arange(cycles, dtype=jnp.int32)
    cutoff = jnp.minimum(355 * (2 * cycle_index + 1) // 226, modes - 1)
    column = jnp.arange(modes, dtype=jnp.int32)
    keep = (column[None, :] <= cutoff[:, None]).astype(jnp.float32)
    return jnp.concatenate([keep, keep], axis=1)


def operators(
    center, radial_plus, radial_minus, theta_plus, theta_minus, axial_plus, axial_minus, total_theta
):
    radius = jnp.arange(center.shape[-1], dtype=jnp.float32) + 0.5
    step_angle = 2.0 * jnp.pi / total_theta
    d_radial = (radial_plus - radial_minus) * 0.5
    d_theta = (theta_plus - theta_minus) / (2.0 * step_angle)
    d_axial = (axial_plus - axial_minus) * 0.5
    laplace = (
        radial_plus - 2.0 * center + radial_minus + (radial_plus - radial_minus) / (2.0 * radius)
    )
    laplace = laplace + (theta_plus - 2.0 * center + theta_minus) / (
        radius * radius * step_angle * step_angle
    )
    laplace = laplace + axial_plus - 2.0 * center + axial_minus
    return (d_radial, d_theta, d_axial, laplace)


def on_device(fields):
    count_fields, planes, theta_dev, radial = fields.shape
    sectors = lax.axis_size("az")
    total_theta = theta_dev * sectors
    modes = min(128, total_theta // 2)
    sector = lax.axis_index("az")
    own_index = sector * theta_dev + jnp.arange(theta_dev, dtype=jnp.int32)
    own_forward, own_inverse = mode_tables(own_index, total_theta, modes)
    inner_cycles = fields[:, :, :, :NEAR]
    kept = None
    piece = lax.all_gather(inner_cycles, "az", axis=2, tiled=True)
    piece_index = jnp.arange(piece.shape[2], dtype=jnp.int32)
    piece_forward, unused_inverse = mode_tables(piece_index, total_theta, modes)
    spectra = jnp.einsum("fztj,tc->fzjc", piece, piece_forward, precision=lax.Precision.HIGHEST)
    kept = spectra * cycle_mask(NEAR, modes)[None, None]
    smoothed = jnp.einsum("fzjc,tc->fztj", kept, own_inverse, precision=lax.Precision.HIGHEST)
    state = jnp.concatenate([smoothed, fields[:, :, :, NEAR:]], axis=3)
    flip = jnp.array([-1.0, -1.0, 1.0, 1.0, 1.0], dtype=jnp.float32)[:, None, None]
    top_bit = sectors.bit_length() - 1
    opposite = swapped(state[:, :, :, 0], "az", top_bit - 1)
    opposite = opposite * flip
    theta_padded = with_halo(state, (("az", 2),), 1, True)
    axial_padded = with_halo(state, (("ax", 1),), 1, False)
    radial_plus = jnp.concatenate([state[:, :, :, 1:], jnp.zeros_like(state[:, :, :, :1])], axis=3)
    radial_minus = jnp.concatenate([opposite[:, :, :, None], state[:, :, :, :-1]], axis=3)
    d_radial, d_theta, d_axial, laplace = operators(
        state,
        radial_plus,
        radial_minus,
        theta_padded[:, :, 2:, :],
        theta_padded[:, :, :-2, :],
        axial_padded[:, 2:, :, :],
        axial_padded[:, :-2, :, :],
        total_theta,
    )
    radius = jnp.arange(radial, dtype=jnp.float32) + 0.5
    radial_u = state[0]
    theta_u = state[1]
    axial_u = state[2]
    change = (
        -(radial_u[None] * d_radial + (theta_u / radius)[None] * d_theta + axial_u[None] * d_axial)
        + viscosity * laplace
    )
    inverse_square = 1.0 / (radius * radius)
    first = (
        change[0]
        + theta_u * theta_u / radius
        - viscosity * (radial_u * inverse_square + 2.0 * inverse_square * d_theta[1])
    )
    second = (
        change[1]
        - radial_u * theta_u / radius
        - viscosity * (theta_u * inverse_square - 2.0 * inverse_square * d_theta[0])
    )
    third = change[2] + buoyancy * state[3]
    change = jnp.concatenate([first[None], second[None], third[None], change[3:]], axis=0)
    return state + time_step * change


def solution(mesh):
    placed = (P(None, "ax", "az", None),)
    return jax.shard_map(
        on_device, mesh=mesh, in_specs=placed, out_specs=P(None, "ax", "az", None), check_vma=False
    )
```

profile of v0, /device:TPU:0, one launch (start us, length us, event | category | flops | bytes accessed | tf_op | source)
XLA Modules:
  0.0 157.3 jit_solution(12849067688981512183)
XLA Ops:
  6.5 0.0 all-gather.2.cloned.1.call-start
  6.5 2.0 %slice.73 = f32[5,16,16,40]{3,2,1,0:T(8,128)} slice(f32[5,16,16,512]{3,2,1,0:T(8,128)} %param.2), slice={[0:5], [0:16], [0:16], [0:40]} | slice | bytes 409600 | tf_op jit(solution)/shard_map/slice | solution.py:85
  8.6 0.0 all-gather.2.cloned.1.call-update
  8.6 4.0 %slice.74 = f32[5,16,16,472]{3,2,1,0:T(8,128)} slice(f32[5,16,16,512]{3,2,1,0:T(8,128)} %param.2), slice={[0:5], [0:16], [0:16], [40:512]} | slice | bytes 4833280 | tf_op jit(solution)/shard_map/slice | solution.py:93
  12.6 3.2 %copy.19 = f32[5,16,16,472]{3,1,2,0:T(8,128)S(1)} copy(f32[5,16,16,472]{3,2,1,0:T(8,128)} %slice.74) | data formatting | bytes 4833280
  15.9 0.1 iota_compare_fusion
  16.0 0.1 add_convert_fusion
  16.1 0.1 fusion.43
  16.2 0.3 sine_multiply_fusion
  16.5 82.9 %all-gather.2.cloned.1.call-done = f32[5,16,128,40]{3,2,1,0:T(8,128)} async-done(((f32[5,16,16,40]{3,2,1,0:T(8,128)}), f32[5,16,128,40]{3,2,1,0:T(8,128)}) %all-gather.2.cloned.1.call-update) | async-done | bytes 1638416 | tf_op jit(solution)/shard_map/all_gather | solution.py:87
  99.3 10.3 %fusion.28 = f32[128,5,16,40]{0,3,2,1:T(8,128)S(1)} fusion(f32[5,16,128,40]{3,2,1,0:T(8,128)} %all-gather.2.cloned.1.call-done, f32[128,64]{1,0:T(8,128)S(1)} %get-tuple-element.19, f32[128,64]{1,0:T(8,128)S(1)} %get-tuple-element.20), kind=kOutput, calls=%fused_computation.70 | convolution fusion | flops 629161984 | bytes 3342336 | tf_op jit(solution)/shard_map/fztj,tc->fzjc/dot_general | solution.py:90
  109.7 5.5 %fusion.6 = f32[5,16,16,40]{3,2,1,0:T(8,128)S(1)} fusion(f32[128,5,16,40]{0,3,2,1:T(8,128)S(1)} %fusion.28, f32[40,128]{1,0:T(8,128)S(1)} %add_convert_fusion, f32[16,64]{1,0:T(8,128)S(1)} %get-tuple-element.18, f32[16,64]{1,0:T(8,128)S(1)} %get-tuple-element.17), kind=kOutput, calls=%fused_computation.37 | convolution fusion | flops 79054848 | bytes 1871872 | tf_op jit(solution)/shard_map/fzjc,tc->fztj/dot_general | solution.py:92
  115.1 0.2 copy.10
  115.3 0.9 fusion.24
  116.2 3.9 %fusion = (f32[5,16,16,511]{3,1,2,0:T(8,128)}, f32[5,16,16,511]{3,1,2,0:T(8,128)}) fusion(f32[5,16,16,40]{3,1,2,0:T(8,128)S(1)} %copy.10, f32[5,16,16,472]{3,1,2,0:T(8,128)S(1)} %copy.19), kind=kLoop, calls=%fused_computation.11 | loop fusion | flops 1308160 | bytes 7854080 | tf_op jit(solution)/shard_map/concatenate | solution.py:93
  120.1 0.2 slice_reduce_fusion
  120.4 1.6 %multiply_bitcast_fusion.1 = (f32[16,16,512]{2,0,1:T(8,128)}, f32[16,16,512]{2,0,1:T(8,128)}, f32[16,16,512]{2,0,1:T(8,128)}) fusion(f32[5,16,16,472]{3,1,2,0:T(8,128)S(1)} %copy.19, f32[5,16,16,40]{3,1,2,0:T(8,128)S(1)} %copy.10, f32[512]{0:T(512)S(1)} %get-tuple-element.23), kind=kLoop, calls=%fused_computation.58 | loop fusion | flops 917504 | bytes 4196352 | tf_op jit(solution)/shard_map/mul | solution.py:117
  122.0 0.0 copy-start
  122.0 1.5 collective-permute-start
  123.5 0.7 fusion.22
  124.3 0.5 collective-permute-start.1
  124.7 1.6 %collective-permute-start.2 = (f32[5,16,1,512]{3,1,2,0:T(8,128)}, f32[5,16,1,512]{3,1,2,0:T(8,128)}, u32[]{:S(2)}, u32[]{:S(2)}) collective-permute-start(f32[5,16,1,512]{3,1,2,0:T(8,128)} %get-tuple-element.11), channel_id=1, source_target_pairs={{0,4},{4,8},{8,12},{12,16},{16,20},{20,24},{24,28},{28,0},{1,5},{5... | collective-permute-start | bytes 491528 | tf_op jit(solution)/shard_map/ppermute | solution.py:31
  126.3 0.7 copy.12
  127.0 1.3 collective-permute-start.3
  128.3 0.7 copy.14
  129.0 3.7 %collective-permute-start.4 = (f32[5,1,16,512]{3,2,1,0:T(8,128)}, f32[5,1,16,512]{3,2,1,0:T(8,128)}, u32[]{:S(2)}, u32[]{:S(2)}) collective-permute-start(f32[5,1,16,512]{3,2,1,0:T(8,128)} %copy.14), channel_id=1, source_target_pairs={{0,1},{1,2},{2,3},{4,5},{5,6},{6,7},{8,9},{9,10},{10,11},{12,13},{... | collective-permute-start | bytes 491528 | tf_op jit(solution)/shard_map/ppermute | solution.py:31
  132.7 0.0 collective-permute-done
  132.7 0.0 copy-done
  132.7 0.1 multiply_bitcast_fusion.2
  132.8 1.4 copy.11
  134.2 0.0 collective-permute-done.3
  134.2 1.1 copy.13
  135.2 0.0 collective-permute-done.4
  135.3 1.1 copy.15
  136.3 0.0 collective-permute-done.1
  136.4 0.0 collective-permute-done.2
  136.4 7.1 %multiply_add_fusion = f32[5,16,16,512]{3,1,2,0:T(8,128)S(1)} fusion(f32[5,1,16,512]{3,1,2,0:T(1,128)S(1)} %copy.13, f32[5,16,16,472]{3,1,2,0:T(8,128)S(1)} %copy.19, f32[5,16,16,40]{3,1,2,0:T(8,128)S(1)} %copy.10, f32[5,1,16,512]{3,1,2,0:T(1,128)S(1)} %copy.15, f32[5,16,16,511]{3,1,2,0:T(8,128)} %get-tuple-element.14, f32[5,16,16,1]{3,1,2,0:T(8,128)} %copy.11, ...), kind=kLoop, calls=%fused_computation.24 | loop fusion | flops 21626880 | bytes 12712960 | tf_op jit(solution)/shard_map/add | solution.py:117
  143.5 0.1 slice.122
  143.6 2.3 %fusion.5 = f32[5,16,16,512]{3,1,2,0:T(8,128)S(1)} fusion(f32[5,16,1,512]{3,1,2,0:T(8,128)S(1)} %collective-permute-done.1, f32[5,16,16,472]{3,1,2,0:T(8,128)S(1)} %copy.19, f32[5,16,16,40]{3,1,2,0:T(8,128)S(1)} %copy.10, f32[5,16,1,512]{3,1,2,0:T(8,128)} %collective-permute-done.2), kind=kLoop, calls=%fused_computation.36 | loop fusion | flops 3932160 | bytes 5570560 | tf_op jit(solution)/shard_map/div | solution.py:65
  145.9 0.8 fusion.20
  146.7 0.8 fusion.2
  147.5 3.0 %copy.16 = f32[5,16,16,512]{3,2,1,0:T(8,128)} copy(f32[5,16,16,512]{3,1,2,0:T(8,128)S(1)} %fusion.2) | data formatting | bytes 5242880 | tf_op jit(solution)/shard_map/add | solution.py:133
  (6 shorter events, 0.1 us)
Async XLA Ops:
  6.5 92.8 %all-gather.2.cloned.1.call-start = ((), (), s32[]{:S(2)}) async-start(), calls=%async_computation | async-start | bytes 5898240 | tf_op jit(solution)/shard_map/all_gather | solution.py:87
  122.0 10.7 %copy-start = (f32[5]{0:T(128)S(1)}, f32[5]{0:T(128)}, u32[]{:S(2)}) copy-start(f32[5]{0:T(128)} %constant.82.clone) | copy-start | bytes 64
  122.0 10.7 %collective-permute-start = (f32[5,16,16]{2,1,0:T(8,128)S(1)}, f32[5,16,16]{2,1,0:T(8,128)S(1)}, u32[]{:S(2)}, u32[]{:S(2)}) collective-permute-start(f32[5,16,16]{2,1,0:T(8,128)S(1)} %slice_reduce_fusion), channel_id=1, source_target_pairs={{0,16},{16,0},{4,20},{20,4},{8,24},{24,8},{12,28},{28,12},{1,17},{... | collective-permute-start | bytes 15368 | tf_op jit(solution)/shard_map/ppermute | solution.py:21
  124.3 12.1 %collective-permute-start.1 = (f32[5,16,1,512]{3,1,2,0:T(8,128)}, f32[5,16,1,512]{3,1,2,0:T(8,128)S(1)}, u32[]{:S(2)}, u32[]{:S(2)}) collective-permute-start(f32[5,16,1,512]{3,1,2,0:T(8,128)} %get-tuple-element.12), channel_id=1, source_target_pairs={{4,0},{8,4},{12,8},{16,12},{20,16},{24,20},{28,24},{0,28},{5,1},{9... | collective-permute-start | bytes 491528 | tf_op jit(solution)/shard_map/ppermute | solution.py:34
  124.7 11.6 %collective-permute-start.2 = (f32[5,16,1,512]{3,1,2,0:T(8,128)}, f32[5,16,1,512]{3,1,2,0:T(8,128)}, u32[]{:S(2)}, u32[]{:S(2)}) collective-permute-start(f32[5,16,1,512]{3,1,2,0:T(8,128)} %get-tuple-element.11), channel_id=1, source_target_pairs={{0,4},{4,8},{8,12},{12,16},{16,20},{20,24},{24,28},{28,0},{1,5},{5... | collective-permute-start | bytes 491528 | tf_op jit(solution)/shard_map/ppermute | solution.py:31
  127.0 7.1 %collective-permute-start.3 = (f32[5,1,16,512]{3,2,1,0:T(8,128)}, f32[5,1,16,512]{3,2,1,0:T(8,128)}, u32[]{:S(2)}, u32[]{:S(2)}) collective-permute-start(f32[5,1,16,512]{3,2,1,0:T(8,128)} %copy.12), channel_id=1, source_target_pairs={{1,0},{2,1},{3,2},{5,4},{6,5},{7,6},{9,8},{10,9},{11,10},{13,12},{... | collective-permute-start | bytes 491528 | tf_op jit(solution)/shard_map/ppermute | solution.py:34
  129.0 6.3 %collective-permute-start.4 = (f32[5,1,16,512]{3,2,1,0:T(8,128)}, f32[5,1,16,512]{3,2,1,0:T(8,128)}, u32[]{:S(2)}, u32[]{:S(2)}) collective-permute-start(f32[5,1,16,512]{3,2,1,0:T(8,128)} %copy.14), channel_id=1, source_target_pairs={{0,1},{1,2},{2,3},{4,5},{5,6},{6,7},{8,9},{9,10},{10,11},{12,13},{... | collective-permute-start | bytes 491528 | tf_op jit(solution)/shard_map/ppermute | solution.py:31
Sparse Core Ops, SparseCore 0:
  9.4 89.8 all-gather.1
where the time goes:
time: 158 us; the launch traced here: 157 us
  waiting for transfers between devices  82.9 us (52%)
  other arithmetic  18.9 us (12%)
  local copies, waits for them, and re-layouts  17.7 us (11%)
  matrix products  15.8 us (10%)
  between operations  13.5 us (9%)
  starting transfers between devices  8.57 us (5%)
    all_gather x1, waiting for transfers between devices, on_device(): piece = lax.all_gather(inner_cycles, 'az', axis=2, tiled=True)  82.9 us
    dot_general x1, matrix products, on_device(): jnp.einsum('fztj,tc->fzjc', piece, piece_forward, precision=lax.Precision...  10.3 us
    add x1, other arithmetic, on_device(): -(radial_u[None] * d_radial + (theta_u / radius)[None] * d_theta + axial_...  7.15 us
    concatenate x3, other arithmetic, on_device(): state = jnp.concatenate([smoothed, fields[:, :, :, NEAR:]], axis=3)  5.55 us
    dot_general x1, matrix products, on_device(): jnp.einsum('fzjc,tc->fztj', kept, own_inverse, precision=lax.Precision.HI...  5.46 us
    ppermute x2, starting transfers between devices, with_halo(): lax.ppermute(lax.slice_in_dim(block, block.shape[dim] - width, None, axis...  5.32 us
    slice x1, local copies, waits for them, and re-layouts, on_device(): state = jnp.concatenate([smoothed, fields[:, :, :, NEAR:]], axis=3)  3.98 us
    unnamed x3, local copies, waits for them, and re-layouts  3.25 us
  transfers between devices with their start and end apart: 6, of which 1 were waited for; matrix products, arithmetic and copies ran while one was open for 9% of the time, Pallas kernels for 0%

commit v1 on v0

--- a/solution.py
+++ b/solution.py
@@ -1,6 +1,11 @@
+import functools
+
 import jax
 import jax.numpy as jnp
+import numpy as np
 from jax import lax
+from jax.experimental import pallas as pl
+from jax.experimental.pallas import tpu as pltpu
 from jax.sharding import PartitionSpec as P
 
 NEAR = 40
@@ -9,6 +14,9 @@
 viscosity = 0.2
 time_step = 0.1
 buoyancy = 1.0
+
+LANES = 128
+VMEM_LIMIT = 48 * 1024 * 1024
 
 
 def swapped(block, axis, distance):
@@ -74,7 +82,7 @@
     return (d_radial, d_theta, d_axial, laplace)
 
 
-def on_device(fields):
+def general_on_device(fields):
     count_fields, planes, theta_dev, radial = fields.shape
     sectors = lax.axis_size("az")
     total_theta = theta_dev * sectors
@@ -133,6 +141,543 @@
     return state + time_step * change
 
 
+class Plan:
+    def __init__(self, shape, sectors):
+        self.fields, self.planes, self.theta, self.radial = shape
+        self.sectors = sectors
+        self.total = self.theta * sectors
+        self.modes = min(128, self.total // 2)
+        cycle = np.arange(NEAR)
+        self.cut = np.minimum(355 * (2 * cycle + 1) // 226, self.modes - 1)
+        self.full = int(np.sum(self.cut < self.modes - 1))
+        self.seg = LANES // self.fields
+        self.extra = self.seg - self.full
+        self.rows = -(-(NEAR - self.full) // max(self.extra, 1))
+
+    @staticmethod
+    def fits(shape, sectors, total):
+        if sectors & (sectors - 1) or total // 2 > 128 or total != LANES or shape[2] % 16:
+            return False
+        plan = Plan(shape, sectors)
+        return (
+            plan.extra > 0
+            and plan.rows <= 8
+            and plan.fields == 5
+            and plan.planes % 8 == 0
+            and plan.radial % LANES == 0
+            and plan.radial > 2 * LANES
+        )
+
+    def split(self, table):
+        high = table.astype(jnp.bfloat16)
+        low = (table - high.astype(np.float32)).astype(jnp.bfloat16)
+        return np.concatenate([high, high, low], axis=-1)
+
+    def forward(self):
+        theta = np.arange(self.total)
+        mode = np.arange(self.modes)
+        angle = (np.outer(mode, theta) % self.total) * (2.0 * np.pi / self.total)
+        weight = np.where(mode == 0, 1.0, 2.0)[:, None] / self.total
+        table = np.concatenate([np.cos(angle) * weight, np.sin(angle) * 2.0 / self.total], axis=0)
+        return self.split(table.astype(np.float32))
+
+    def inverse(self):
+        mode = np.arange(self.modes)
+        blocks = []
+        for sector in range(self.sectors):
+            own = sector * self.theta + np.arange(self.theta)
+            index = np.concatenate([own, own + self.total // 2, own[:1] - 1, own[-1:] + 1])
+            angle = (np.outer(index, mode) % self.total) * (2.0 * np.pi / self.total)
+            table = np.concatenate([np.cos(angle), np.sin(angle)], axis=1)
+            pad = np.zeros((16 - 2, table.shape[1]))
+            blocks.append(np.concatenate([table, pad], axis=0))
+        return self.split(np.stack(blocks).astype(np.float32))
+
+    def mask(self):
+        mode = np.arange(self.modes)
+        keep = np.zeros((self.modes, LANES), np.float32)
+        for field in range(self.fields):
+            keep[:, field * self.seg : field * self.seg + self.full] = (
+                mode[:, None] <= self.cut[None, : self.full]
+            )
+        return np.concatenate([keep, keep], axis=0)
+
+    def coefficients(self):
+        radius = np.arange(self.radial) + 0.5
+        step = 2.0 * np.pi / self.total
+        nu_dt = viscosity * time_step
+        square = 1.0 / (radius * radius * step * step)
+        rows = [
+            1.0 - nu_dt * (4.0 + 2.0 * square),
+            nu_dt * square,
+            nu_dt / (2.0 * radius),
+            time_step / (2.0 * step * radius),
+            time_step / radius,
+            nu_dt / (radius * radius),
+            nu_dt / (step * radius * radius),
+        ]
+        rows.append(np.zeros(self.radial))
+        return np.stack(rows).astype(np.float32)
+
+
+def pack_kernel(plan, x_ref, out_ref):
+    shape = (plan.theta, LANES)
+    lane = lax.broadcasted_iota(jnp.int32, shape, 1)
+    row = lax.broadcasted_iota(jnp.int32, shape, 0)
+    sign = (1 - 2 * (row & 1)).astype(jnp.float32)
+    for k in range(out_ref.shape[0]):
+        packed = jnp.zeros(shape, jnp.float32)
+        for f in range(plan.fields):
+            x = x_ref[f, k]
+            alternating = jnp.sum(x * sign, axis=0, keepdims=True)
+            part = jnp.where(lane < plan.full, x, 0.0)
+            for r in range(plan.rows):
+                piece = pltpu.roll(
+                    jnp.broadcast_to(alternating, shape), (LANES - plan.extra * r) % LANES, 1
+                )
+                part = jnp.where(
+                    (row == r) & (lane >= plan.full) & (lane < plan.seg), piece, part
+                )
+            part = part if f == 0 else pltpu.roll(part, plan.seg * f, 1)
+            packed = packed + part
+        out_ref[k] = packed
+
+
+def pack(plan, fields):
+    chunk = 4
+    return pl.pallas_call(
+        functools.partial(pack_kernel, plan),
+        grid=(plan.planes // chunk,),
+        in_specs=[pl.BlockSpec((plan.fields, chunk, plan.theta, LANES), lambda i: (0, i, 0, 0))],
+        out_specs=pl.BlockSpec((chunk, plan.theta, LANES), lambda i: (i, 0, 0)),
+        out_shape=jax.ShapeDtypeStruct((plan.planes, plan.theta, LANES), jnp.float32),
+        name="pack",
+        cost_estimate=pl.CostEstimate(flops=1000000, bytes_accessed=800000, transcendentals=0),
+    )(fields)
+
+
+def edges_kernel(plan, place_ref, x_ref, az_a, az_b, ax_a, ax_b, sems):
+    odd_theta = place_ref[1]
+    odd_plane = place_ref[2]
+    first = odd_theta * (1 - plan.theta) + plan.theta - 1
+    plane = odd_plane * (1 - plan.planes) + plan.planes - 1
+    copies = [
+        pltpu.make_async_copy(x_ref.at[:, :, first], az_a, sems.at[0]),
+        pltpu.make_async_copy(x_ref.at[:, :, plan.theta - 1 - first], az_b, sems.at[1]),
+        pltpu.make_async_copy(x_ref.at[:, plane], ax_a, sems.at[2]),
+        pltpu.make_async_copy(x_ref.at[:, plan.planes - 1 - plane], ax_b, sems.at[3]),
+    ]
+    for copy in copies:
+        copy.start()
+    for copy in copies:
+        copy.wait()
+
+
+def edges(plan, place, fields):
+    column = jax.ShapeDtypeStruct((plan.fields, plan.planes, plan.radial), jnp.float32)
+    plane = jax.ShapeDtypeStruct((plan.fields, plan.theta, plan.radial), jnp.float32)
+    anywhere = pl.BlockSpec(memory_space=pl.ANY)
+    return pl.pallas_call(
+        functools.partial(edges_kernel, plan),
+        in_specs=[pl.BlockSpec(memory_space=pltpu.SMEM), anywhere],
+        out_specs=[anywhere] * 4,
+        out_shape=[column, column, plane, plane],
+        scratch_shapes=[pltpu.SemaphoreType.DMA((4,))],
+        name="edges",
+        cost_estimate=pl.CostEstimate(flops=0, bytes_accessed=1300000, transcendentals=0),
+    )(place, fields)
+
+
+def advance(coef, q, jp, jm, tp, tm, kp, km):
+    c0, c2, half, angular, over, square, cross = coef
+    ur, ut, uz, temp = q[:4]
+    radial = half - (0.5 * time_step) * ur
+    azimuthal = angular * ut
+    axial = (0.5 * time_step) * uz
+    nu_dt = viscosity * time_step
+    out = []
+    d_theta = []
+    for f in range(5):
+        dt = tp[f] - tm[f]
+        if f < 2:
+            d_theta.append(dt)
+        value = c0 * q[f] + nu_dt * ((jp[f] + jm[f]) + (kp[f] + km[f]))
+        value = value + c2 * (tp[f] + tm[f])
+        value = value + (jp[f] - jm[f]) * radial
+        value = value - dt * azimuthal
+        value = value - (kp[f] - km[f]) * axial
+        out.append(value)
+    swirl = over * ut
+    out[0] = out[0] + swirl * ut - square * ur - cross * d_theta[1]
+    out[1] = out[1] - swirl * ur - square * ut + cross * d_theta[0]
+    out[2] = out[2] + (time_step * buoyancy) * temp
+    return out
+
+
+def turned(x, row, before, after):
+    last = x.shape[0] - 1
+    up = jnp.where(row == last, after, pltpu.roll(x, last, 0))
+    down = jnp.where(row == 0, before, pltpu.roll(x, 1, 0))
+    return up, down
+
+
+def load_halos(plan, place_ref, copies, az_a, az_b, ax_a, ax_b, width, buf, side, sems):
+    odd_theta = place_ref[1]
+    odd_plane = place_ref[2]
+    high = plan.planes + 1
+    slot_a = (1 - odd_plane) * high
+    lanes = pl.ds(0, width)
+    copies += [
+        pltpu.make_async_copy(az_a.at[:, :, lanes], side.at[1 - odd_theta], sems.at[0]),
+        pltpu.make_async_copy(az_b.at[:, :, lanes], side.at[odd_theta], sems.at[1]),
+        pltpu.make_async_copy(ax_a.at[:, :, lanes], buf.at[slot_a], sems.at[2]),
+        pltpu.make_async_copy(ax_b.at[:, :, lanes], buf.at[high - slot_a], sems.at[3]),
+    ]
+
+
+def outer_kernel(
+    plan, place_ref, coef_ref, x_ref, az_a, az_b, ax_a, ax_b, out_ref, buf, side, done, sems, ins, outs
+):
+    planes = plan.planes
+    halos = []
+    load_halos(plan, place_ref, halos, az_a, az_b, ax_a, ax_b, plan.radial, buf, side, sems)
+    for copy in halos:
+        copy.start()
+
+    def fetch(k):
+        return pltpu.make_async_copy(x_ref.at[:, k], buf.at[k + 1], ins.at[k])
+
+    def store(k):
+        return pltpu.make_async_copy(
+            done.at[k], out_ref.at[:, k, :, pl.ds(LANES, plan.radial - LANES)], outs.at[k]
+        )
+
+    for k in range(planes):
+        fetch(k).start()
+    for copy in halos:
+        copy.wait()
+    fetch(0).wait()
+    shape = (plan.theta, LANES)
+    lane = lax.broadcasted_iota(jnp.int32, shape, 1)
+    row = lax.broadcasted_iota(jnp.int32, shape, 0)
+    tiles = plan.radial // LANES
+
+    def step(group, carry):
+        start = pl.multiple_of(group * 8, 8)
+        for i in range(8):
+            k = start + i
+            if i < 7:
+                fetch(k + 1).wait()
+            else:
+                pl.when(k < planes - 1)(lambda: fetch(k + 1).wait())
+            for tile in range(1, tiles):
+                here = pl.ds(tile * LANES, LANES)
+                coef = [coef_ref[j : j + 1, here] for j in range(7)]
+                q, jp, jm, tp, tm, kp, km = ([] for _ in range(7))
+                for f in range(plan.fields):
+                    x = buf[k + 1, f, :, here]
+                    low = buf[k + 1, f, :, pl.ds((tile - 1) * LANES, LANES)]
+                    q.append(x)
+                    high = 0.0
+                    if tile + 1 < tiles:
+                        high = buf[k + 1, f, :, pl.ds((tile + 1) * LANES, LANES)]
+                        high = pltpu.roll(high, LANES - 1, 1)
+                    jp.append(jnp.where(lane == LANES - 1, high, pltpu.roll(x, LANES - 1, 1)))
+                    jm.append(jnp.where(lane == 0, pltpu.roll(low, 1, 1), pltpu.roll(x, 1, 1)))
+                    before = side[0, f, pl.ds(start, 8), here][i : i + 1]
+                    after = side[1, f, pl.ds(start, 8), here][i : i + 1]
+                    up, down = turned(x, row, before, after)
+                    tp.append(up)
+                    tm.append(down)
+                    kp.append(buf[k + 2, f, :, here])
+                    km.append(buf[k, f, :, here])
+                result = advance(coef, q, jp, jm, tp, tm, kp, km)
+                for f in range(plan.fields):
+                    done[k, f, :, pl.ds((tile - 1) * LANES, LANES)] = result[f]
+            store(k).start()
+        return carry
+
+    lax.fori_loop(0, planes // 8, step, 0)
+    for k in range(planes):
+        store(k).wait()
+
+
+def outer(plan, place, coef, fields, halos):
+    anywhere = pl.BlockSpec(memory_space=pl.ANY)
+    f32 = jnp.float32
+    return pl.pallas_call(
+        functools.partial(outer_kernel, plan),
+        in_specs=[pl.BlockSpec(memory_space=pltpu.SMEM), pl.BlockSpec(memory_space=pltpu.VMEM)]
+        + [anywhere] * 5,
+        out_specs=anywhere,
+        out_shape=jax.ShapeDtypeStruct(fields.shape, f32),
+        scratch_shapes=[
+            pltpu.VMEM((plan.planes + 2, plan.fields, plan.theta, plan.radial), f32),
+            pltpu.VMEM((2, plan.fields, plan.planes, plan.radial), f32),
+            pltpu.VMEM((plan.planes, plan.fields, plan.theta, plan.radial - LANES), f32),
+            pltpu.SemaphoreType.DMA((4,)),
+            pltpu.SemaphoreType.DMA((plan.planes,)),
+            pltpu.SemaphoreType.DMA((plan.planes,)),
+        ],
+        compiler_params=pltpu.CompilerParams(vmem_limit_bytes=VMEM_LIMIT),
+        name="outer",
+        cost_estimate=pl.CostEstimate(flops=16000000, bytes_accessed=5000000, transcendentals=0),
+    )(place, coef, fields, *halos)
+
+
+def halves(x):
+    high = x.astype(jnp.bfloat16)
+    low = (x - high.astype(jnp.float32)).astype(jnp.bfloat16)
+    return jnp.concatenate([high, low, high], axis=0)
+
+
+def filter_kernel(
+    plan, place_ref, forward_ref, inverse_ref, mask_ref, *refs
+):
+    pieces = refs[: plan.sectors]
+    own_ref, across_ref, edge_ref, nyquist_ref, message_a, message_b = refs[plan.sectors : plan.sectors + 6]
+    data, table, totals, sems = refs[plan.sectors + 6 :]
+    sector = place_ref[0]
+    odd_plane = place_ref[2]
+    theta = plan.theta
+    copies = [pltpu.make_async_copy(inverse_ref.at[sector], table, sems.at[plan.sectors])]
+    for p in range(plan.sectors):
+        copies.append(
+            pltpu.make_async_copy(pieces[p], data.at[:, sector ^ p], sems.at[p])
+        )
+    for copy in copies:
+        copy.start()
+    for copy in copies:
+        copy.wait()
+    mask = mask_ref[...]
+    mask = jnp.concatenate([mask, mask], axis=1)
+
+    for k in range(0, plan.planes, 2):
+        both = jnp.concatenate(
+            [data[k].reshape(plan.total, LANES), data[k + 1].reshape(plan.total, LANES)], axis=1
+        )
+        spectra = jnp.dot(forward_ref[...], halves(both), preferred_element_type=jnp.float32)
+        kept = halves(spectra * mask)
+        state = jnp.dot(table[...], kept, preferred_element_type=jnp.float32)
+        for i in range(2):
+            lanes = slice(i * LANES, (i + 1) * LANES)
+            own_ref[k + i] = state[:theta, lanes]
+            across_ref[k + i] = state[theta : 2 * theta, lanes]
+            edge_ref[k + i] = state[2 * theta : 2 * theta + 8, lanes]
+            top = data[k + i, 0, :8]
+            for p in range(1, plan.sectors):
+                top = top + data[k + i, p, :8]
+            for r in range(plan.rows):
+                totals[r, k + i : k + i + 1, :] = top[r : r + 1]
+
+    lane = lax.broadcasted_iota(jnp.int32, (plan.planes, LANES), 1)
+    for f in range(plan.fields):
+        total = jnp.zeros((plan.planes, LANES), jnp.float32)
+        for r in range(plan.rows):
+            first = plan.full + plan.extra * r
+            shift = (plan.extra * r - plan.seg * f) % LANES
+            value = totals[r] if shift == 0 else pltpu.roll(totals[r], shift, 1)
+            last = min(first + plan.extra, NEAR)
+            total = jnp.where((lane >= first) & (lane < last), value, total)
+        nyquist_ref[f] = total * (1.0 / plan.total)
+
+    def message(ref, plane):
+        ref[pl.ds(0, theta)] = own_ref[plane]
+        for f in range(plan.fields):
+            ref[pl.ds(theta + f, 1)] = nyquist_ref[f, pl.ds(plane, 1)]
+        ref[pl.ds(theta + 5, 3)] = jnp.zeros((3, LANES), jnp.float32)
+
+    plane = odd_plane * (1 - plan.planes) + plan.planes - 1
+    message(message_a, plane)
+    message(message_b, plan.planes - 1 - plane)
+
+
+def filtered(plan, place, pieces):
+    anywhere = pl.BlockSpec(memory_space=pl.ANY)
+    inside = pl.BlockSpec(memory_space=pltpu.VMEM)
+    f32 = jnp.float32
+    cube = jax.ShapeDtypeStruct((plan.planes, plan.theta, LANES), f32)
+    return pl.pallas_call(
+        functools.partial(filter_kernel, plan),
+        in_specs=[pl.BlockSpec(memory_space=pltpu.SMEM), inside, anywhere, inside]
+        + [anywhere] * plan.sectors,
+        out_specs=[inside] * 6,
+        out_shape=[
+            cube,
+            cube,
+            jax.ShapeDtypeStruct((plan.planes, 8, LANES), f32),
+            jax.ShapeDtypeStruct((plan.fields, plan.planes, LANES), f32),
+            jax.ShapeDtypeStruct((plan.theta + 8, LANES), f32),
+            jax.ShapeDtypeStruct((plan.theta + 8, LANES), f32),
+        ],
+        scratch_shapes=[
+            pltpu.VMEM((plan.planes, plan.sectors, plan.theta, LANES), f32),
+            pltpu.VMEM((2 * plan.theta + 16, 6 * plan.modes), jnp.bfloat16),
+            pltpu.VMEM((plan.rows, plan.planes, LANES), f32),
+            pltpu.SemaphoreType.DMA((plan.sectors + 1,)),
+        ],
+        compiler_params=pltpu.CompilerParams(vmem_limit_bytes=VMEM_LIMIT),
+        name="filter",
+        cost_estimate=pl.CostEstimate(flops=200000000, bytes_accessed=1500000, transcendentals=0),
+    )(
+        place,
+        jnp.asarray(plan.forward()),
+        jnp.asarray(plan.inverse()),
+        jnp.asarray(plan.mask()),
+        *pieces,
+    )
+
+
+def inner_kernel(
+    plan, place_ref, coef_ref, own_ref, across_ref, edge_ref, nyquist_ref, message_a, message_b,
+    x_ref, az_a, az_b, ax_a, ax_b, other_ref, out_ref, buf, side, state, done, sems, ins, outs
+):
+    planes = plan.planes
+    theta = plan.theta
+    halos = []
+    load_halos(plan, place_ref, halos, az_a, az_b, ax_a, ax_b, 2 * LANES, buf, side, sems)
+    fetch = [
+        pltpu.make_async_copy(x_ref.at[:, k, :, pl.ds(0, 2 * LANES)], buf.at[k + 1], ins.at[k])
+        for k in range(planes)
+    ]
+    store = [
+        pltpu.make_async_copy(done.at[k], out_ref.at[:, k, :, pl.ds(0, LANES)], outs.at[k])
+        for k in range(planes)
+    ]
+    for copy in halos + fetch:
+        copy.start()
+    shape = (theta, LANES)
+    lane = lax.broadcasted_iota(jnp.int32, shape, 1)
+    row = lax.broadcasted_iota(jnp.int32, shape, 0)
+    sign = (1 - 2 * (row & 1)).astype(jnp.float32)
+    lane1 = lax.broadcasted_iota(jnp.int32, (1, LANES), 1)
+    first = pl.ds(0, LANES)
+    coef = [coef_ref[i : i + 1, :LANES] for i in range(7)]
+    flips = (-1.0, -1.0, 1.0, 1.0, 1.0)
+
+    def aligned(x, f):
+        return x if f == 0 else pltpu.roll(x, LANES - plan.seg * f, 1)
+
+    def smooth(raw, packed, total, f):
+        return jnp.where(lane < plan.full, aligned(packed, f), raw - sign * total)
+
+    for copy in halos + fetch:
+        copy.wait()
+    for k in range(planes):
+        for f in range(plan.fields):
+            state[k + 1, f] = smooth(
+                buf[k + 1, f, :, first], own_ref[k], nyquist_ref[f, k : k + 1], f
+            )
+    odd_plane = place_ref[2]
+    high = planes + 1
+    slot_a = (1 - odd_plane) * high
+    for message, slot in ((message_a, slot_a), (message_b, high - slot_a)):
+        for f in range(plan.fields):
+            state[slot, f] = smooth(
+                buf[slot, f, :, first], message[:theta], message[theta + f : theta + f + 1], f
+            )
+
+    for k in range(planes):
+        q, jp, jm, tp, tm, kp, km = ([] for _ in range(7))
+        for f in range(plan.fields):
+            x = state[k + 1, f]
+            q.append(x)
+            high_part = pltpu.roll(buf[k + 1, f, :, pl.ds(LANES, LANES)], LANES - 1, 1)
+            jp.append(jnp.where(lane == LANES - 1, high_part, pltpu.roll(x, LANES - 1, 1)))
+            opposite = flips[f] * aligned(across_ref[k], f)
+            jm.append(jnp.where(lane == 0, opposite, pltpu.roll(x, 1, 1)))
+            total = nyquist_ref[f, k : k + 1]
+            before = jnp.where(
+                lane1 < plan.full, aligned(edge_ref[k, 0:1], f), side[0, f, k : k + 1, first] + total
+            )
+            after = jnp.where(
+                lane1 < plan.full, aligned(edge_ref[k, 1:2], f), side[1, f, k : k + 1, first] - total
+            )
+            up, down = turned(x, row, before, after)
+            tp.append(up)
+            tm.append(down)
+            kp.append(state[k + 2, f])
+            km.append(state[k, f])
+        result = advance(coef, q, jp, jm, tp, tm, kp, km)
+        for f in range(plan.fields):
+            done[k, f] = result[f]
+        store[k].start()
+    for copy in store:
+        copy.wait()
+
+
+def inner(plan, place, coef, parts, messages, fields, halos, partial):
+    anywhere = pl.BlockSpec(memory_space=pl.ANY)
+    inside = pl.BlockSpec(memory_space=pltpu.VMEM)
+    f32 = jnp.float32
+    operands = (place, coef, *parts, *messages, fields, *halos, partial)
+    return pl.pallas_call(
+        functools.partial(inner_kernel, plan),
+        in_specs=[pl.BlockSpec(memory_space=pltpu.SMEM)] + [inside] * 7 + [anywhere] * 6,
+        out_specs=anywhere,
+        out_shape=jax.ShapeDtypeStruct(fields.shape, f32),
+        input_output_aliases={len(operands) - 1: 0},
+        scratch_shapes=[
+            pltpu.VMEM((plan.planes + 2, plan.fields, plan.theta, 2 * LANES), f32),
+            pltpu.VMEM((2, plan.fields, plan.planes, 2 * LANES), f32),
+            pltpu.VMEM((plan.planes + 2, plan.fields, plan.theta, LANES), f32),
+            pltpu.VMEM((plan.planes, plan.fields, plan.theta, LANES), f32),
+            pltpu.SemaphoreType.DMA((4,)),
+            pltpu.SemaphoreType.DMA((plan.planes,)),
+            pltpu.SemaphoreType.DMA((plan.planes,)),
+        ],
+        compiler_params=pltpu.CompilerParams(vmem_limit_bytes=VMEM_LIMIT),
+        name="inner",
+        cost_estimate=pl.CostEstimate(flops=6000000, bytes_accessed=2500000, transcendentals=0),
+    )(*operands)
+
+
+def pairs(count, start, periodic):
+    route = []
+    for low in range(start, count, 2):
+        high = low + 1
+        if high == count and not periodic:
+            continue
+        route += [(low, high % count), (high % count, low)]
+    return route
+
+
+def fast_on_device(fields):
+    sectors = lax.axis_size("az")
+    slabs = lax.axis_size("ax")
+    plan = Plan(fields.shape, sectors)
+    sector = lax.axis_index("az")
+    place = jnp.stack([sector, sector % 2, lax.axis_index("ax") % 2]).astype(jnp.int32)
+    coef = jnp.asarray(plan.coefficients())
+
+    packed = pack(plan, fields)
+    pieces = [packed]
+    for p in range(1, sectors):
+        pieces.append(lax.ppermute(packed, "az", [(i, i ^ p) for i in range(sectors)]))
+
+    az_a, az_b, ax_a, ax_b = edges(plan, place, fields)
+    halos = (
+        lax.ppermute(az_a, "az", pairs(sectors, 0, True)),
+        lax.ppermute(az_b, "az", pairs(sectors, 1, True)),
+        lax.ppermute(ax_a, "ax", pairs(slabs, 0, False)),
+        lax.ppermute(ax_b, "ax", pairs(slabs, 1, False)),
+    )
+    partial = outer(plan, place, coef, fields, halos)
+    *parts, message_a, message_b = filtered(plan, place, pieces)
+    messages = (
+        lax.ppermute(message_a, "ax", pairs(slabs, 0, False)),
+        lax.ppermute(message_b, "ax", pairs(slabs, 1, False)),
+    )
+    return inner(plan, place, coef, parts, messages, fields, halos, partial)
+
+
+def on_device(fields):
+    total_theta = fields.shape[2] * lax.axis_size("az")
+    if Plan.fits(fields.shape, lax.axis_size("az"), total_theta):
+        return fast_on_device(fields)
+    return general_on_device(fields)
+
+
 def solution(mesh):
     placed = (P(None, "ax", "az", None),)
     return jax.shard_map(

time: 158 us -> 80.1 us (0.51)
  the two profiles are of different devices: /device:TPU:0 before, /device:TPU:1 now
where the time goes in v1:
time: 80.1 us; the launch traced here: 79.8 us
  Pallas kernels  39.2 us (49%)
  starting transfers between devices  32.7 us (41%)
  waiting for transfers between devices  4.81 us (6%)
  local copies, waits for them, and re-layouts  2.35 us (3%)
    pallas_call x1, Pallas kernels, edges(): pl.pallas_call(functools.partial(edges_kernel, plan), in_specs=[pl.BlockS...  21.7 us
    ppermute x7, starting transfers between devices, fast_on_device(): lax.ppermute(packed, 'az', [(i, i ^ p) for i in range(sectors)])  18.1 us
    ppermute x1, starting transfers between devices, fast_on_device(): lax.ppermute(ax_a, 'ax', pairs(slabs, 0, False))  6.31 us
    pallas_call x1, Pallas kernels, outer(): pl.pallas_call(functools.partial(outer_kernel, plan), in_specs=[pl.BlockS...  6.16 us
    ppermute x7, waiting for transfers between devices, fast_on_device(): lax.ppermute(packed, 'az', [(i, i ^ p) for i in range(sectors)])  4.79 us
    pallas_call x1, Pallas kernels, inner(): pl.pallas_call(functools.partial(inner_kernel, plan), in_specs=[pl.BlockS...  4.01 us
    pallas_call x1, Pallas kernels, filtered(): pl.pallas_call(functools.partial(filter_kernel, plan), in_specs=[pl.Block...  3.82 us
    ppermute x1, starting transfers between devices, fast_on_device(): lax.ppermute(message_b, 'ax', pairs(slabs, 1, False))  3.72 us
  transfers between devices with their start and end apart: 13, of which 1 were waited for; matrix products, arithmetic and copies ran while one was open for 1% of the time, Pallas kernels for 40%

profile of v1, /device:TPU:1, one launch (start us, length us, event | category | flops | bytes accessed | tf_op | source)
XLA Modules:
  0.0 79.8 jit_solution(12216223412433618893)
XLA Ops:
  0.0 0.0 copy-start.2
  0.0 0.0 copy-start.3
  0.0 3.5 %pack.1.refs_0_ = f32[16,16,128]{2,1,0:T(8,128)} custom-call(f32[5,16,16,512]{3,2,1,0:T(8,128)} %x_ref.7), custom_call_target="tpu_custom_call" | custom-call | flops 1000000 | bytes 800000 | tf_op jit(solution)/shard_map/pack/pallas_call | solution.py:248
  3.6 0.0 copy-start
  3.6 0.0 copy-start.4
  3.6 5.1 %collective-permute-start.6 = (f32[16,16,128]{2,1,0:T(8,128)}, f32[16,16,128]{2,1,0:T(8,128)S(1)}, u32[]{:S(2)}, u32[]{:S(2)}) collective-permute-start(f32[16,16,128]{2,1,0:T(8,128)} %pack.1.refs_0_), channel_id=1, source_target_pairs={{0,28},{4,24},{8,20},{12,16},{16,12},{20,8},{24,4},{28,0},{1,29},{... | collective-permute-start | bytes 393224 | tf_op jit(solution)/shard_map/ppermute | solution.py:656
  8.6 0.0 collective-permute-start.5
  8.6 0.4 collective-permute-start.4
  9.1 2.0 %collective-permute-start.3 = (f32[16,16,128]{2,1,0:T(8,128)}, f32[16,16,128]{2,1,0:T(8,128)S(1)}, u32[]{:S(2)}, u32[]{:S(2)}) collective-permute-start(f32[16,16,128]{2,1,0:T(8,128)} %pack.1.refs_0_), channel_id=1, source_target_pairs={{0,16},{4,20},{8,24},{12,28},{16,0},{20,4},{24,8},{28,12},{1,17},{... | collective-permute-start | bytes 393224 | tf_op jit(solution)/shard_map/ppermute | solution.py:656
  11.1 2.0 %collective-permute-start.2 = (f32[16,16,128]{2,1,0:T(8,128)}, f32[16,16,128]{2,1,0:T(8,128)}, u32[]{:S(2)}, u32[]{:S(2)}) collective-permute-start(f32[16,16,128]{2,1,0:T(8,128)} %pack.1.refs_0_), channel_id=1, source_target_pairs={{0,12},{4,8},{8,4},{12,0},{16,28},{20,24},{24,20},{28,16},{1,13},{... | collective-permute-start | bytes 393224 | tf_op jit(solution)/shard_map/ppermute | solution.py:656
  13.1 0.0 collective-permute-done.6.refs_7_
  13.1 8.5 %collective-permute-start.1 = (f32[16,16,128]{2,1,0:T(8,128)}, f32[16,16,128]{2,1,0:T(8,128)}, u32[]{:S(2)}, u32[]{:S(2)}) collective-permute-start(f32[16,16,128]{2,1,0:T(8,128)} %pack.1.refs_0_), channel_id=1, source_target_pairs={{0,8},{4,12},{8,0},{12,4},{16,24},{20,28},{24,16},{28,20},{1,9},{5... | collective-permute-start | bytes 393224 | tf_op jit(solution)/shard_map/ppermute | solution.py:656
  21.6 0.6 pad_add_fusion.place_ref
  22.2 21.7 %edges.1 = (f32[5,16,512]{2,1,0:T(8,128)}, f32[5,16,512]{2,1,0:T(8,128)}, f32[5,16,512]{2,1,0:T(8,128)}, f32[5,16,512]{2,1,0:T(8,128)}) custom-call(s32[3]{0:T(128)} %pad_add_fusion.place_ref, f32[5,16,16,512]{3,2,1,0:T(8,128)} %x_ref.7), custom_call_target="tpu_custom_call" | custom-call | bytes 1300000 | tf_op jit(solution)/shard_map/edges/pallas_call | solution.py:280
  43.8 0.0 collective-permute-done.5.refs_6_
  43.9 1.5 %collective-permute-start.9 = (f32[5,16,512]{2,1,0:T(8,128)}, f32[5,16,512]{2,1,0:T(8,128)S(1)}, u32[]{:S(2)}, u32[]{:S(2)}) collective-permute-start(f32[5,16,512]{2,1,0:T(8,128)} %get-tuple-element.21), channel_id=1, source_target_pairs={{0,4},{4,0},{8,12},{12,8},{16,20},{20,16},{24,28},{28,24},{1,5},{5... | collective-permute-start | bytes 491528 | tf_op jit(solution)/shard_map/ppermute | solution.py:660
  45.3 0.0 collective-permute-done.4.refs_5_
  45.3 0.0 collective-permute-start.10
  45.3 0.0 collective-permute-done.3.refs_4_
  45.3 6.3 %collective-permute-start.11 = (f32[5,16,512]{2,1,0:T(8,128)}, f32[5,16,512]{2,1,0:T(8,128)S(1)}, u32[]{:S(2)}, u32[]{:S(2)}) collective-permute-start(f32[5,16,512]{2,1,0:T(8,128)} %get-tuple-element.23), channel_id=1, source_target_pairs={{0,1},{1,0},{2,3},{3,2},{4,5},{5,4},{6,7},{7,6},{8,9},{9,8},{10,11... | collective-permute-start | bytes 491528 | tf_op jit(solution)/shard_map/ppermute | solution.py:662
  51.6 0.0 collective-permute-done.2.refs_3_
  51.6 3.0 %collective-permute-start.12 = (f32[5,16,512]{2,1,0:T(8,128)}, f32[5,16,512]{2,1,0:T(8,128)S(1)}, u32[]{:S(2)}, u32[]{:S(2)}) collective-permute-start(f32[5,16,512]{2,1,0:T(8,128)} %get-tuple-element.24), channel_id=1, source_target_pairs={{1,2},{2,1},{5,6},{6,5},{9,10},{10,9},{13,14},{14,13},{17,18},{18,... | collective-permute-start | bytes 491528 | tf_op jit(solution)/shard_map/ppermute | solution.py:663
  54.7 0.0 collective-permute-done.1.refs_2_
  54.7 0.1 collective-permute-start
  54.8 4.8 %collective-permute-done.refs_1_ = f32[16,16,128]{2,1,0:T(8,128)S(1)} collective-permute-done((f32[16,16,128]{2,1,0:T(8,128)}, f32[16,16,128]{2,1,0:T(8,128)S(1)}, u32[]{:S(2)}, u32[]{:S(2)}) %collective-permute-start) | collective-permute-done | bytes 131104 | tf_op jit(solution)/shard_map/ppermute | solution.py:656
  59.5 0.0 copy-done.2
  59.6 0.0 copy-done.3
  59.6 0.0 copy-start.1
  59.6 0.9 %copy-done.1 = f32[16,16,128]{2,1,0:T(8,128)S(1)} copy-done((f32[16,16,128]{2,1,0:T(8,128)S(1)}, f32[16,16,128]{2,1,0:T(8,128)}, u32[]{:S(2)}) %copy-start.1) | copy-done | bytes 131096
  60.5 0.0 copy-start.5
  60.5 0.8 %copy-done.5 = f32[128,128]{1,0:T(8,128)S(1)} copy-done((f32[128,128]{1,0:T(8,128)S(1)}, f32[128,128]{1,0:T(8,128)}, u32[]{:S(2)}) %copy-start.5) | copy-done | bytes 65560
  61.3 0.0 copy-start.6
  61.3 0.6 copy-done.6
  61.9 3.8 %filter.1 = (f32[16,16,128]{2,1,0:T(8,128)S(1)}, f32[16,16,128]{2,1,0:T(8,128)S(1)}, f32[16,8,128]{2,1,0:T(8,128)S(1)}, f32[5,16,128]{2,1,0:T(8,128)S(1)}, f32[24,128]{1,0:T(8,128)S(1)}, /*index=5*/f32[24,128]{1,0:T(8,128)S(1)}) custom-call(s32[3]{0:T(128)S(1)} %copy-done.6, bf16[128,384]{1,0:T(8,128)(2,1)S(1)} %copy-done.3, ...), custom_call_target="tpu_custom_call" | custom-call | flops 200000000 | bytes 1500000 | tf_op jit(solution)/shard_map/filter/pallas_call | solution.py:500
  65.7 0.1 collective-permute-start.7
  65.8 0.0 collective-permute-done.9.az_a
  65.8 3.7 %collective-permute-start.8 = (f32[24,128]{1,0:T(8,128)S(1)}, f32[24,128]{1,0:T(8,128)S(1)}, u32[]{:S(2)}, u32[]{:S(2)}) collective-permute-start(f32[24,128]{1,0:T(8,128)S(1)} %get-tuple-element.20), channel_id=1, source_target_pairs={{1,2},{2,1},{5,6},{6,5},{9,10},{10,9},{13,14},{14,13},{17,18},{18,... | collective-permute-start | bytes 36872 | tf_op jit(solution)/shard_map/ppermute | solution.py:669
  69.5 0.0 collective-permute-done.10.az_b
  69.5 0.0 collective-permute-done.11.ax_a
  69.6 0.0 collective-permute-done.12.ax_b
  69.6 0.0 copy-done
  69.6 0.0 copy-done.4
  69.6 6.2 %outer.1.other_ref = f32[5,16,16,512]{3,2,1,0:T(8,128)} custom-call(s32[3]{0:T(128)S(1)} %copy-done.6, f32[8,512]{1,0:T(8,128)S(1)} %copy-done.4, f32[5,16,16,512]{3,2,1,0:T(8,128)S(1)} %copy-done, f32[5,16,512]{2,1,0:T(8,128)S(1)} %collective-permute-done.9.az_a, f32[5,16,512]{2,1,0:T(8,128)S(1)} %collective-permute-done.10.az_b, ...), custom_call_target="tpu_custom_call" | custom-call | flops 16000000 | bytes 5000000 | tf_op jit(solution)/shard_map/outer/pallas_call | solution.py:408
  75.8 0.0 collective-permute-done.7.message_a
  75.8 0.0 collective-permute-done.8.message_b
  75.8 4.0 %inner.1 = f32[5,16,16,512]{3,2,1,0:T(8,128)} custom-call(s32[3]{0:T(128)S(1)} %copy-done.6, f32[8,512]{1,0:T(8,128)S(1)} %copy-done.4, f32[16,16,128]{2,1,0:T(8,128)S(1)} %get-tuple-element.15.own_ref, f32[16,16,128]{2,1,0:T(8,128)S(1)} %get-tuple-element.16.across_ref, ...), custom_call_target="tpu_custom_call", output_to_operand_aliasing={{}: (13, {})} | custom-call | flops 6000000 | bytes 2500000 | tf_op jit(solution)/shard_map/inner/pallas_call | solution.py:614
Async XLA Ops:
  0.0 59.5 %copy-start.2 = (bf16[8,48,384]{2,1,0:T(8,128)(2,1)S(1)}, bf16[8,48,384]{2,1,0:T(8,128)(2,1)}, u32[]{:S(2)}) copy-start(bf16[8,48,384]{2,1,0:T(8,128)(2,1)} %constant.36.clone.inverse_ref) | copy-start | bytes 884740
  0.0 59.5 %copy-start.3 = (bf16[128,384]{1,0:T(8,128)(2,1)S(1)}, bf16[128,384]{1,0:T(8,128)(2,1)}, u32[]{:S(2)}) copy-start(bf16[128,384]{1,0:T(8,128)(2,1)} %constant.35.clone.forward_ref) | copy-start | bytes 294916
  3.6 66.0 %copy-start = (f32[5,16,16,512]{3,2,1,0:T(8,128)S(1)}, f32[5,16,16,512]{3,2,1,0:T(8,128)}, u32[]{:S(2)}) copy-start(f32[5,16,16,512]{3,2,1,0:T(8,128)} %x_ref.7) | copy-start | bytes 7864324
  3.6 66.0 %copy-start.4 = (f32[8,512]{1,0:T(8,128)S(1)}, f32[8,512]{1,0:T(8,128)}, u32[]{:S(2)}) copy-start(f32[8,512]{1,0:T(8,128)} %constant.34.clone.coef_ref) | copy-start | bytes 49156
  3.6 9.5 %collective-permute-start.6 = (f32[16,16,128]{2,1,0:T(8,128)}, f32[16,16,128]{2,1,0:T(8,128)S(1)}, u32[]{:S(2)}, u32[]{:S(2)}) collective-permute-start(f32[16,16,128]{2,1,0:T(8,128)} %pack.1.refs_0_), channel_id=1, source_target_pairs={{0,28},{4,24},{8,20},{12,16},{16,12},{20,8},{24,4},{28,0},{1,29},{... | collective-permute-start | bytes 393224 | tf_op jit(solution)/shard_map/ppermute | solution.py:656
  8.6 35.2 %collective-permute-start.5 = (f32[16,16,128]{2,1,0:T(8,128)}, f32[16,16,128]{2,1,0:T(8,128)S(1)}, u32[]{:S(2)}, u32[]{:S(2)}) collective-permute-start(f32[16,16,128]{2,1,0:T(8,128)} %pack.1.refs_0_), channel_id=1, source_target_pairs={{0,24},{4,28},{8,16},{12,20},{16,8},{20,12},{24,0},{28,4},{1,25},{... | collective-permute-start | bytes 393224 | tf_op jit(solution)/shard_map/ppermute | solution.py:656
  8.6 36.7 %collective-permute-start.4 = (f32[16,16,128]{2,1,0:T(8,128)}, f32[16,16,128]{2,1,0:T(8,128)S(1)}, u32[]{:S(2)}, u32[]{:S(2)}) collective-permute-start(f32[16,16,128]{2,1,0:T(8,128)} %pack.1.refs_0_), channel_id=1, source_target_pairs={{0,20},{4,16},{8,28},{12,24},{16,4},{20,0},{24,12},{28,8},{1,21},{... | collective-permute-start | bytes 393224 | tf_op jit(solution)/shard_map/ppermute | solution.py:656
  9.1 36.3 %collective-permute-start.3 = (f32[16,16,128]{2,1,0:T(8,128)}, f32[16,16,128]{2,1,0:T(8,128)S(1)}, u32[]{:S(2)}, u32[]{:S(2)}) collective-permute-start(f32[16,16,128]{2,1,0:T(8,128)} %pack.1.refs_0_), channel_id=1, source_target_pairs={{0,16},{4,20},{8,24},{12,28},{16,0},{20,4},{24,8},{28,12},{1,17},{... | collective-permute-start | bytes 393224 | tf_op jit(solution)/shard_map/ppermute | solution.py:656
  11.1 40.6 %collective-permute-start.2 = (f32[16,16,128]{2,1,0:T(8,128)}, f32[16,16,128]{2,1,0:T(8,128)}, u32[]{:S(2)}, u32[]{:S(2)}) collective-permute-start(f32[16,16,128]{2,1,0:T(8,128)} %pack.1.refs_0_), channel_id=1, source_target_pairs={{0,12},{4,8},{8,4},{12,0},{16,28},{20,24},{24,20},{28,16},{1,13},{... | collective-permute-start | bytes 393224 | tf_op jit(solution)/shard_map/ppermute | solution.py:656
  13.1 41.6 %collective-permute-start.1 = (f32[16,16,128]{2,1,0:T(8,128)}, f32[16,16,128]{2,1,0:T(8,128)}, u32[]{:S(2)}, u32[]{:S(2)}) collective-permute-start(f32[16,16,128]{2,1,0:T(8,128)} %pack.1.refs_0_), channel_id=1, source_target_pairs={{0,8},{4,12},{8,0},{12,4},{16,24},{20,28},{24,16},{28,20},{1,9},{5... | collective-permute-start | bytes 393224 | tf_op jit(solution)/shard_map/ppermute | solution.py:656
  43.9 21.9 %collective-permute-start.9 = (f32[5,16,512]{2,1,0:T(8,128)}, f32[5,16,512]{2,1,0:T(8,128)S(1)}, u32[]{:S(2)}, u32[]{:S(2)}) collective-permute-start(f32[5,16,512]{2,1,0:T(8,128)} %get-tuple-element.21), channel_id=1, source_target_pairs={{0,4},{4,0},{8,12},{12,8},{16,20},{20,16},{24,28},{28,24},{1,5},{5... | collective-permute-start | bytes 491528 | tf_op jit(solution)/shard_map/ppermute | solution.py:660
  45.3 24.2 %collective-permute-start.10 = (f32[5,16,512]{2,1,0:T(8,128)}, f32[5,16,512]{2,1,0:T(8,128)S(1)}, u32[]{:S(2)}, u32[]{:S(2)}) collective-permute-start(f32[5,16,512]{2,1,0:T(8,128)} %get-tuple-element.22), channel_id=1, source_target_pairs={{4,8},{8,4},{12,16},{16,12},{20,24},{24,20},{28,0},{0,28},{5,9},{9... | collective-permute-start | bytes 491528 | tf_op jit(solution)/shard_map/ppermute | solution.py:661
  45.3 24.2 %collective-permute-start.11 = (f32[5,16,512]{2,1,0:T(8,128)}, f32[5,16,512]{2,1,0:T(8,128)S(1)}, u32[]{:S(2)}, u32[]{:S(2)}) collective-permute-start(f32[5,16,512]{2,1,0:T(8,128)} %get-tuple-element.23), channel_id=1, source_target_pairs={{0,1},{1,0},{2,3},{3,2},{4,5},{5,4},{6,7},{7,6},{8,9},{9,8},{10,11... | collective-permute-start | bytes 491528 | tf_op jit(solution)/shard_map/ppermute | solution.py:662
  51.6 17.9 %collective-permute-start.12 = (f32[5,16,512]{2,1,0:T(8,128)}, f32[5,16,512]{2,1,0:T(8,128)S(1)}, u32[]{:S(2)}, u32[]{:S(2)}) collective-permute-start(f32[5,16,512]{2,1,0:T(8,128)} %get-tuple-element.24), channel_id=1, source_target_pairs={{1,2},{2,1},{5,6},{6,5},{9,10},{10,9},{13,14},{14,13},{17,18},{18,... | collective-permute-start | bytes 491528 | tf_op jit(solution)/shard_map/ppermute | solution.py:663
  54.7 4.9 %collective-permute-start = (f32[16,16,128]{2,1,0:T(8,128)}, f32[16,16,128]{2,1,0:T(8,128)S(1)}, u32[]{:S(2)}, u32[]{:S(2)}) collective-permute-start(f32[16,16,128]{2,1,0:T(8,128)} %pack.1.refs_0_), channel_id=1, source_target_pairs={{0,4},{4,0},{8,12},{12,8},{16,20},{20,16},{24,28},{28,24},{1,5},{5... | collective-permute-start | bytes 393224 | tf_op jit(solution)/shard_map/ppermute | solution.py:656
  59.6 0.9 %copy-start.1 = (f32[16,16,128]{2,1,0:T(8,128)S(1)}, f32[16,16,128]{2,1,0:T(8,128)}, u32[]{:S(2)}) copy-start(f32[16,16,128]{2,1,0:T(8,128)} %pack.1.refs_0_) | copy-start | bytes 393220
  60.5 0.8 %copy-start.5 = (f32[128,128]{1,0:T(8,128)S(1)}, f32[128,128]{1,0:T(8,128)}, u32[]{:S(2)}) copy-start(f32[128,128]{1,0:T(8,128)} %constant.37.clone.mask_ref) | copy-start | bytes 196612
  61.3 0.6 copy-start.6
  65.7 10.0 %collective-permute-start.7 = (f32[24,128]{1,0:T(8,128)S(1)}, f32[24,128]{1,0:T(8,128)S(1)}, u32[]{:S(2)}, u32[]{:S(2)}) collective-permute-start(f32[24,128]{1,0:T(8,128)S(1)} %get-tuple-element.19), channel_id=1, source_target_pairs={{0,1},{1,0},{2,3},{3,2},{4,5},{5,4},{6,7},{7,6},{8,9},{9,8},{10,11... | collective-permute-start | bytes 36872 | tf_op jit(solution)/shard_map/ppermute | solution.py:668
  65.8 10.0 %collective-permute-start.8 = (f32[24,128]{1,0:T(8,128)S(1)}, f32[24,128]{1,0:T(8,128)S(1)}, u32[]{:S(2)}, u32[]{:S(2)}) collective-permute-start(f32[24,128]{1,0:T(8,128)S(1)} %get-tuple-element.20), channel_id=1, source_target_pairs={{1,2},{2,1},{5,6},{6,5},{9,10},{10,9},{13,14},{14,13},{17,18},{18,... | collective-permute-start | bytes 36872 | tf_op jit(solution)/shard_map/ppermute | solution.py:669

commit v2 on v1

--- a/solution.py
+++ b/solution.py
@@ -150,20 +150,25 @@
         cycle = np.arange(NEAR)
         self.cut = np.minimum(355 * (2 * cycle + 1) // 226, self.modes - 1)
         self.full = int(np.sum(self.cut < self.modes - 1))
-        self.seg = LANES // self.fields
-        self.extra = self.seg - self.full
-        self.rows = -(-(NEAR - self.full) // max(self.extra, 1))
+        self.rest = NEAR - self.full
+        self.beside = LANES // max(self.full, 1)
+        self.groups = -(-self.fields * self.planes // self.beside)
+
+    def place(self, f, k):
+        index = k * self.fields + f
+        return index // self.beside, index % self.beside * self.full
 
     @staticmethod
     def fits(shape, sectors, total):
-        if sectors & (sectors - 1) or total // 2 > 128 or total != LANES or shape[2] % 16:
+        if sectors & (sectors - 1) or total // 2 > 128 or total != LANES or shape[2] != 16:
             return False
         plan = Plan(shape, sectors)
         return (
-            plan.extra > 0
-            and plan.rows <= 8
+            plan.full > 0
             and plan.fields == 5
-            and plan.planes % 8 == 0
+            and plan.planes == plan.theta
+            and plan.rest * plan.fields <= LANES
+            and plan.groups % 2 == 0
             and plan.radial % LANES == 0
             and plan.radial > 2 * LANES
         )
@@ -196,8 +201,8 @@
     def mask(self):
         mode = np.arange(self.modes)
         keep = np.zeros((self.modes, LANES), np.float32)
-        for field in range(self.fields):
-            keep[:, field * self.seg : field * self.seg + self.full] = (
+        for i in range(self.beside):
+            keep[:, i * self.full : (i + 1) * self.full] = (
                 mode[:, None] <= self.cut[None, : self.full]
             )
         return np.concatenate([keep, keep], axis=0)
@@ -220,72 +225,98 @@
         return np.stack(rows).astype(np.float32)
 
 
+def moved(x, lanes):
+    return x if lanes % LANES == 0 else pltpu.roll(x, lanes % LANES, 1)
+
+
 def pack_kernel(plan, x_ref, out_ref):
     shape = (plan.theta, LANES)
     lane = lax.broadcasted_iota(jnp.int32, shape, 1)
     row = lax.broadcasted_iota(jnp.int32, shape, 0)
     sign = (1 - 2 * (row & 1)).astype(jnp.float32)
-    for k in range(out_ref.shape[0]):
-        packed = jnp.zeros(shape, jnp.float32)
+    group = jnp.zeros(shape, jnp.float32)
+    sums = [jnp.zeros(shape, jnp.float32) for _ in range(plan.fields)]
+    for k in range(plan.planes):
         for f in range(plan.fields):
             x = x_ref[f, k]
+            number, first = plan.place(f, k)
+            part = moved(x, first)
+            if first:
+                part = jnp.where((lane >= first) & (lane < first + plan.full), part, group)
+            group = part
+            if first // plan.full == plan.beside - 1 or (f, k) == (plan.fields - 1, plan.planes - 1):
+                out_ref[number] = group
             alternating = jnp.sum(x * sign, axis=0, keepdims=True)
-            part = jnp.where(lane < plan.full, x, 0.0)
-            for r in range(plan.rows):
-                piece = pltpu.roll(
-                    jnp.broadcast_to(alternating, shape), (LANES - plan.extra * r) % LANES, 1
-                )
-                part = jnp.where(
-                    (row == r) & (lane >= plan.full) & (lane < plan.seg), piece, part
-                )
-            part = part if f == 0 else pltpu.roll(part, plan.seg * f, 1)
-            packed = packed + part
-        out_ref[k] = packed
+            sums[f] = jnp.where(row == k, alternating, sums[f])
+    last = sums[0]
+    for f in range(plan.fields):
+        start = f * plan.rest
+        last = jnp.where(lane >= start, moved(sums[f], start - plan.full), last)
+    out_ref[plan.groups] = last
 
 
 def pack(plan, fields):
-    chunk = 4
     return pl.pallas_call(
         functools.partial(pack_kernel, plan),
-        grid=(plan.planes // chunk,),
-        in_specs=[pl.BlockSpec((plan.fields, chunk, plan.theta, LANES), lambda i: (0, i, 0, 0))],
-        out_specs=pl.BlockSpec((chunk, plan.theta, LANES), lambda i: (i, 0, 0)),
-        out_shape=jax.ShapeDtypeStruct((plan.planes, plan.theta, LANES), jnp.float32),
+        grid=(1,),
+        in_specs=[
+            pl.BlockSpec((plan.fields, plan.planes, plan.theta, LANES), lambda i: (0, 0, 0, 0))
+        ],
+        out_specs=pl.BlockSpec((plan.groups + 1, plan.theta, LANES), lambda i: (0, 0, 0)),
+        out_shape=jax.ShapeDtypeStruct((plan.groups + 1, plan.theta, LANES), jnp.float32),
         name="pack",
         cost_estimate=pl.CostEstimate(flops=1000000, bytes_accessed=800000, transcendentals=0),
     )(fields)
 
 
-def edges_kernel(plan, place_ref, x_ref, az_a, az_b, ax_a, ax_b, sems):
-    odd_theta = place_ref[1]
-    odd_plane = place_ref[2]
-    first = odd_theta * (1 - plan.theta) + plan.theta - 1
-    plane = odd_plane * (1 - plan.planes) + plan.planes - 1
-    copies = [
-        pltpu.make_async_copy(x_ref.at[:, :, first], az_a, sems.at[0]),
-        pltpu.make_async_copy(x_ref.at[:, :, plan.theta - 1 - first], az_b, sems.at[1]),
-        pltpu.make_async_copy(x_ref.at[:, plane], ax_a, sems.at[2]),
-        pltpu.make_async_copy(x_ref.at[:, plan.planes - 1 - plane], ax_b, sems.at[3]),
-    ]
-    for copy in copies:
-        copy.start()
-    for copy in copies:
-        copy.wait()
-
-
-def edges(plan, place, fields):
+def edges_kernel(plan, x_ref, az_a, az_b, ax_a, ax_b):
+    step = pl.program_id(0)
+    even_theta = lax.axis_index("az") % 2 == 0
+    even_plane = lax.axis_index("ax") % 2 == 0
+    rows = x_ref.shape[1]
+    for f in range(plan.fields):
+        for k in range(rows):
+            low = x_ref[f, k, 0:1, :]
+            high = x_ref[f, k, plan.theta - 1 : plan.theta, :]
+            az_a[f, k : k + 1, :] = jnp.where(even_theta, high, low)
+            az_b[f, k : k + 1, :] = jnp.where(even_theta, low, high)
+    first = step == 0
+    last = step == pl.num_programs(0) - 1
+
+    @pl.when(first & even_plane)
+    def _():
+        ax_b[...] = x_ref[:, 0]
+
+    @pl.when(first & jnp.logical_not(even_plane))
+    def _():
+        ax_a[...] = x_ref[:, 0]
+
+    @pl.when(last & even_plane)
+    def _():
+        ax_a[...] = x_ref[:, rows - 1]
+
+    @pl.when(last & jnp.logical_not(even_plane))
+    def _():
+        ax_b[...] = x_ref[:, rows - 1]
+
+
+def edges(plan, fields):
     column = jax.ShapeDtypeStruct((plan.fields, plan.planes, plan.radial), jnp.float32)
     plane = jax.ShapeDtypeStruct((plan.fields, plan.theta, plan.radial), jnp.float32)
-    anywhere = pl.BlockSpec(memory_space=pl.ANY)
+    part = pl.BlockSpec((plan.fields, 8, plan.radial), lambda i: (0, i, 0))
+    whole = pl.BlockSpec((plan.fields, plan.theta, plan.radial), lambda i: (0, 0, 0))
     return pl.pallas_call(
         functools.partial(edges_kernel, plan),
-        in_specs=[pl.BlockSpec(memory_space=pltpu.SMEM), anywhere],
-        out_specs=[anywhere] * 4,
+        grid=(plan.planes // 8,),
+        in_specs=[
+            pl.BlockSpec((plan.fields, 8, plan.theta, plan.radial), lambda i: (0, i, 0, 0))
+        ],
+        out_specs=[part, part, whole, whole],
         out_shape=[column, column, plane, plane],
-        scratch_shapes=[pltpu.SemaphoreType.DMA((4,))],
+        compiler_params=pltpu.CompilerParams(vmem_limit_bytes=VMEM_LIMIT),
         name="edges",
-        cost_estimate=pl.CostEstimate(flops=0, bytes_accessed=1300000, transcendentals=0),
-    )(place, fields)
+        cost_estimate=pl.CostEstimate(flops=0, bytes_accessed=4000000, transcendentals=0),
+    )(fields)
 
 
 def advance(coef, q, jp, jm, tp, tm, kp, km):
@@ -321,9 +352,9 @@
     return up, down
 
 
-def load_halos(plan, place_ref, copies, az_a, az_b, ax_a, ax_b, width, buf, side, sems):
-    odd_theta = place_ref[1]
-    odd_plane = place_ref[2]
+def load_halos(plan, copies, az_a, az_b, ax_a, ax_b, width, buf, side, sems):
+    odd_theta = lax.axis_index("az") % 2
+    odd_plane = lax.axis_index("ax") % 2
     high = plan.planes + 1
     slot_a = (1 - odd_plane) * high
     lanes = pl.ds(0, width)
@@ -336,11 +367,11 @@
 
 
 def outer_kernel(
-    plan, place_ref, coef_ref, x_ref, az_a, az_b, ax_a, ax_b, out_ref, buf, side, done, sems, ins, outs
+    plan, coef_ref, x_ref, az_a, az_b, ax_a, ax_b, out_ref, buf, side, done, sems, ins, outs
 ):
     planes = plan.planes
     halos = []
-    load_halos(plan, place_ref, halos, az_a, az_b, ax_a, ax_b, plan.radial, buf, side, sems)
+    load_halos(plan, halos, az_a, az_b, ax_a, ax_b, plan.radial, buf, side, sems)
     for copy in halos:
         copy.start()
 
@@ -402,13 +433,12 @@
         store(k).wait()
 
 
-def outer(plan, place, coef, fields, halos):
+def outer(plan, coef, fields, halos):
     anywhere = pl.BlockSpec(memory_space=pl.ANY)
     f32 = jnp.float32
     return pl.pallas_call(
         functools.partial(outer_kernel, plan),
-        in_specs=[pl.BlockSpec(memory_space=pltpu.SMEM), pl.BlockSpec(memory_space=pltpu.VMEM)]
-        + [anywhere] * 5,
+        in_specs=[pl.BlockSpec(memory_space=pltpu.VMEM)] + [anywhere] * 5,
         out_specs=anywhere,
         out_shape=jax.ShapeDtypeStruct(fields.shape, f32),
         scratch_shapes=[
@@ -422,7 +452,7 @@
         compiler_params=pltpu.CompilerParams(vmem_limit_bytes=VMEM_LIMIT),
         name="outer",
         cost_estimate=pl.CostEstimate(flops=16000000, bytes_accessed=5000000, transcendentals=0),
-    )(place, coef, fields, *halos)
+    )(coef, fields, *halos)
 
 
 def halves(x):
@@ -431,20 +461,17 @@
     return jnp.concatenate([high, low, high], axis=0)
 
 
-def filter_kernel(
-    plan, place_ref, forward_ref, inverse_ref, mask_ref, *refs
-):
+def filter_kernel(plan, forward_ref, inverse_ref, mask_ref, after_ref, *refs):
+    del after_ref
     pieces = refs[: plan.sectors]
-    own_ref, across_ref, edge_ref, nyquist_ref, message_a, message_b = refs[plan.sectors : plan.sectors + 6]
-    data, table, totals, sems = refs[plan.sectors + 6 :]
-    sector = place_ref[0]
-    odd_plane = place_ref[2]
+    own_ref, across_ref, edge_ref, sums_ref, message_a, message_b = refs[plan.sectors : plan.sectors + 6]
+    data, table, sems = refs[plan.sectors + 6 :]
+    sector = lax.axis_index("az")
+    odd_plane = lax.axis_index("ax") % 2
     theta = plan.theta
     copies = [pltpu.make_async_copy(inverse_ref.at[sector], table, sems.at[plan.sectors])]
     for p in range(plan.sectors):
-        copies.append(
-            pltpu.make_async_copy(pieces[p], data.at[:, sector ^ p], sems.at[p])
-        )
+        copies.append(pltpu.make_async_copy(pieces[p], data.at[:, sector ^ p], sems.at[p]))
     for copy in copies:
         copy.start()
     for copy in copies:
@@ -452,90 +479,87 @@
     mask = mask_ref[...]
     mask = jnp.concatenate([mask, mask], axis=1)
 
-    for k in range(0, plan.planes, 2):
+    for g in range(0, plan.groups, 2):
         both = jnp.concatenate(
-            [data[k].reshape(plan.total, LANES), data[k + 1].reshape(plan.total, LANES)], axis=1
+            [data[g].reshape(plan.total, LANES), data[g + 1].reshape(plan.total, LANES)], axis=1
         )
         spectra = jnp.dot(forward_ref[...], halves(both), preferred_element_type=jnp.float32)
         kept = halves(spectra * mask)
         state = jnp.dot(table[...], kept, preferred_element_type=jnp.float32)
         for i in range(2):
             lanes = slice(i * LANES, (i + 1) * LANES)
-            own_ref[k + i] = state[:theta, lanes]
-            across_ref[k + i] = state[theta : 2 * theta, lanes]
-            edge_ref[k + i] = state[2 * theta : 2 * theta + 8, lanes]
-            top = data[k + i, 0, :8]
-            for p in range(1, plan.sectors):
-                top = top + data[k + i, p, :8]
-            for r in range(plan.rows):
-                totals[r, k + i : k + i + 1, :] = top[r : r + 1]
-
+            own_ref[g + i] = state[:theta, lanes]
+            across_ref[g + i] = state[theta : 2 * theta, lanes]
+            edge_ref[g + i] = state[2 * theta : 2 * theta + 8, lanes]
+
+    total = data[plan.groups, 0]
+    for p in range(1, plan.sectors):
+        total = total + data[plan.groups, p]
+    total = total * (1.0 / plan.total)
     lane = lax.broadcasted_iota(jnp.int32, (plan.planes, LANES), 1)
     for f in range(plan.fields):
-        total = jnp.zeros((plan.planes, LANES), jnp.float32)
-        for r in range(plan.rows):
-            first = plan.full + plan.extra * r
-            shift = (plan.extra * r - plan.seg * f) % LANES
-            value = totals[r] if shift == 0 else pltpu.roll(totals[r], shift, 1)
-            last = min(first + plan.extra, NEAR)
-            total = jnp.where((lane >= first) & (lane < last), value, total)
-        nyquist_ref[f] = total * (1.0 / plan.total)
-
-    def message(ref, plane):
-        ref[pl.ds(0, theta)] = own_ref[plane]
+        value = moved(total, plan.full - f * plan.rest)
+        sums_ref[f] = jnp.where((lane >= plan.full) & (lane < NEAR), value, 0.0)
+
+    def message(ref, k):
         for f in range(plan.fields):
-            ref[pl.ds(theta + f, 1)] = nyquist_ref[f, pl.ds(plane, 1)]
-        ref[pl.ds(theta + 5, 3)] = jnp.zeros((3, LANES), jnp.float32)
-
-    plane = odd_plane * (1 - plan.planes) + plan.planes - 1
-    message(message_a, plane)
-    message(message_b, plan.planes - 1 - plane)
-
-
-def filtered(plan, place, pieces):
+            number, first = plan.place(f, k)
+            own = own_ref[number]
+            value = jnp.where(lane < plan.full, moved(own, -first), sums_ref[f, k : k + 1])
+            ref[f] = value
+
+    def both_messages(ref_low, ref_high):
+        message(ref_low, 0)
+        message(ref_high, plan.planes - 1)
+
+    pl.when(odd_plane == 1)(lambda: both_messages(message_a, message_b))
+    pl.when(odd_plane == 0)(lambda: both_messages(message_b, message_a))
+
+
+def filtered(plan, pieces, after):
     anywhere = pl.BlockSpec(memory_space=pl.ANY)
     inside = pl.BlockSpec(memory_space=pltpu.VMEM)
     f32 = jnp.float32
-    cube = jax.ShapeDtypeStruct((plan.planes, plan.theta, LANES), f32)
+    cube = jax.ShapeDtypeStruct((plan.groups, plan.theta, LANES), f32)
+    plane = jax.ShapeDtypeStruct((plan.fields, plan.theta, LANES), f32)
     return pl.pallas_call(
         functools.partial(filter_kernel, plan),
-        in_specs=[pl.BlockSpec(memory_space=pltpu.SMEM), inside, anywhere, inside]
-        + [anywhere] * plan.sectors,
+        in_specs=[inside, anywhere, inside, anywhere] + [anywhere] * plan.sectors,
         out_specs=[inside] * 6,
         out_shape=[
             cube,
             cube,
-            jax.ShapeDtypeStruct((plan.planes, 8, LANES), f32),
+            jax.ShapeDtypeStruct((plan.groups, 8, LANES), f32),
             jax.ShapeDtypeStruct((plan.fields, plan.planes, LANES), f32),
-            jax.ShapeDtypeStruct((plan.theta + 8, LANES), f32),
-            jax.ShapeDtypeStruct((plan.theta + 8, LANES), f32),
+            plane,
+            plane,
         ],
         scratch_shapes=[
-            pltpu.VMEM((plan.planes, plan.sectors, plan.theta, LANES), f32),
+            pltpu.VMEM((plan.groups + 1, plan.sectors, plan.theta, LANES), f32),
             pltpu.VMEM((2 * plan.theta + 16, 6 * plan.modes), jnp.bfloat16),
-            pltpu.VMEM((plan.rows, plan.planes, LANES), f32),
             pltpu.SemaphoreType.DMA((plan.sectors + 1,)),
         ],
         compiler_params=pltpu.CompilerParams(vmem_limit_bytes=VMEM_LIMIT),
         name="filter",
         cost_estimate=pl.CostEstimate(flops=200000000, bytes_accessed=1500000, transcendentals=0),
     )(
-        place,
         jnp.asarray(plan.forward()),
         jnp.asarray(plan.inverse()),
         jnp.asarray(plan.mask()),
+        after,
         *pieces,
     )
 
 
 def inner_kernel(
-    plan, place_ref, coef_ref, own_ref, across_ref, edge_ref, nyquist_ref, message_a, message_b,
+    plan, coef_ref, own_ref, across_ref, edge_ref, sums_ref, message_a, message_b,
     x_ref, az_a, az_b, ax_a, ax_b, other_ref, out_ref, buf, side, state, done, sems, ins, outs
 ):
+    del other_ref
     planes = plan.planes
     theta = plan.theta
     halos = []
-    load_halos(plan, place_ref, halos, az_a, az_b, ax_a, ax_b, 2 * LANES, buf, side, sems)
+    load_halos(plan, halos, az_a, az_b, ax_a, ax_b, 2 * LANES, buf, side, sems)
     fetch = [
         pltpu.make_async_copy(x_ref.at[:, k, :, pl.ds(0, 2 * LANES)], buf.at[k + 1], ins.at[k])
         for k in range(planes)
@@ -555,44 +579,38 @@
     coef = [coef_ref[i : i + 1, :LANES] for i in range(7)]
     flips = (-1.0, -1.0, 1.0, 1.0, 1.0)
 
-    def aligned(x, f):
-        return x if f == 0 else pltpu.roll(x, LANES - plan.seg * f, 1)
-
-    def smooth(raw, packed, total, f):
-        return jnp.where(lane < plan.full, aligned(packed, f), raw - sign * total)
-
     for copy in halos + fetch:
         copy.wait()
     for k in range(planes):
         for f in range(plan.fields):
-            state[k + 1, f] = smooth(
-                buf[k + 1, f, :, first], own_ref[k], nyquist_ref[f, k : k + 1], f
+            number, start = plan.place(f, k)
+            state[k + 1, f] = jnp.where(
+                lane < plan.full,
+                moved(own_ref[number], -start),
+                buf[k + 1, f, :, first] - sign * sums_ref[f, k : k + 1],
             )
-    odd_plane = place_ref[2]
+    odd_plane = lax.axis_index("ax") % 2
     high = planes + 1
     slot_a = (1 - odd_plane) * high
     for message, slot in ((message_a, slot_a), (message_b, high - slot_a)):
         for f in range(plan.fields):
-            state[slot, f] = smooth(
-                buf[slot, f, :, first], message[:theta], message[theta + f : theta + f + 1], f
-            )
+            raw = buf[slot, f, :, first]
+            state[slot, f] = jnp.where(lane < plan.full, message[f], raw - sign * message[f])
 
     for k in range(planes):
         q, jp, jm, tp, tm, kp, km = ([] for _ in range(7))
         for f in range(plan.fields):
+            number, start = plan.place(f, k)
             x = state[k + 1, f]
             q.append(x)
             high_part = pltpu.roll(buf[k + 1, f, :, pl.ds(LANES, LANES)], LANES - 1, 1)
             jp.append(jnp.where(lane == LANES - 1, high_part, pltpu.roll(x, LANES - 1, 1)))
-            opposite = flips[f] * aligned(across_ref[k], f)
+            opposite = flips[f] * moved(across_ref[number], -start)
             jm.append(jnp.where(lane == 0, opposite, pltpu.roll(x, 1, 1)))
-            total = nyquist_ref[f, k : k + 1]
-            before = jnp.where(
-                lane1 < plan.full, aligned(edge_ref[k, 0:1], f), side[0, f, k : k + 1, first] + total
-            )
-            after = jnp.where(
-                lane1 < plan.full, aligned(edge_ref[k, 1:2], f), side[1, f, k : k + 1, first] - total
-            )
+            total = sums_ref[f, k : k + 1]
+            sides = moved(edge_ref[number], -start)
+            before = jnp.where(lane1 < plan.full, sides[0:1], side[0, f, k : k + 1, first] + total)
+            after = jnp.where(lane1 < plan.full, sides[1:2], side[1, f, k : k + 1, first] - total)
             up, down = turned(x, row, before, after)
             tp.append(up)
             tm.append(down)
@@ -606,14 +624,14 @@
         copy.wait()
 
 
-def inner(plan, place, coef, parts, messages, fields, halos, partial):
+def inner(plan, coef, parts, messages, fields, halos, partial):
     anywhere = pl.BlockSpec(memory_space=pl.ANY)
     inside = pl.BlockSpec(memory_space=pltpu.VMEM)
     f32 = jnp.float32
-    operands = (place, coef, *parts, *messages, fields, *halos, partial)
+    operands = (coef, *parts, *messages, fields, *halos, partial)
     return pl.pallas_call(
         functools.partial(inner_kernel, plan),
-        in_specs=[pl.BlockSpec(memory_space=pltpu.SMEM)] + [inside] * 7 + [anywhere] * 6,
+        in_specs=[inside] * 7 + [anywhere] * 6,
         out_specs=anywhere,
         out_shape=jax.ShapeDtypeStruct(fields.shape, f32),
         input_output_aliases={len(operands) - 1: 0},
@@ -646,8 +664,6 @@
     sectors = lax.axis_size("az")
     slabs = lax.axis_size("ax")
     plan = Plan(fields.shape, sectors)
-    sector = lax.axis_index("az")
-    place = jnp.stack([sector, sector % 2, lax.axis_index("ax") % 2]).astype(jnp.int32)
     coef = jnp.asarray(plan.coefficients())
 
     packed = pack(plan, fields)
@@ -655,20 +671,20 @@
     for p in range(1, sectors):
         pieces.append(lax.ppermute(packed, "az", [(i, i ^ p) for i in range(sectors)]))
 
-    az_a, az_b, ax_a, ax_b = edges(plan, place, fields)
+    az_a, az_b, ax_a, ax_b = edges(plan, fields)
     halos = (
         lax.ppermute(az_a, "az", pairs(sectors, 0, True)),
         lax.ppermute(az_b, "az", pairs(sectors, 1, True)),
         lax.ppermute(ax_a, "ax", pairs(slabs, 0, False)),
         lax.ppermute(ax_b, "ax", pairs(slabs, 1, False)),
     )
-    partial = outer(plan, place, coef, fields, halos)
-    *parts, message_a, message_b = filtered(plan, place, pieces)
+    partial = outer(plan, coef, fields, halos)
+    *parts, message_a, message_b = filtered(plan, pieces, partial)
     messages = (
         lax.ppermute(message_a, "ax", pairs(slabs, 0, False)),
         lax.ppermute(message_b, "ax", pairs(slabs, 1, False)),
     )
-    return inner(plan, place, coef, parts, messages, fields, halos, partial)
+    return inner(plan, coef, parts, messages, fields, halos, partial)
 
 
 def on_device(fields):

time: 80.1 us -> 48.7 us (0.61)
  Pallas kernels: 39.2 us -> 13.6 us
  starting transfers between devices: 32.7 us -> 23.8 us
  waiting for transfers between devices: 4.81 us -> 9.23 us
    pallas_call x4, Pallas kernels: 33 us -> 8.02 us  [the longest x1 3.37 us: inner(): pl.pallas_call(functools.partial(inner_kernel, plan), in_specs=[inside] *...]
    ppermute x7, starting transfers between devices: 18.1 us -> 12.8 us  [fast_on_device(): lax.ppermute(packed, 'az', [(i, i ^ p) for i in range(sectors)])]
    ppermute x1, starting transfers between devices: 6.31 us -> 1.52 us  [fast_on_device(): lax.ppermute(ax_a, 'ax', pairs(slabs, 0, False))]
    ppermute x7, waiting for transfers between devices: 4.79 us -> 7.23 us  [fast_on_device(): lax.ppermute(packed, 'az', [(i, i ^ p) for i in range(sectors)])]
    ppermute x1, waiting for transfers between devices: 0.01 us -> 1.99 us  [fast_on_device(): lax.ppermute(message_b, 'ax', pairs(slabs, 1, False))]
    ppermute x1, starting transfers between devices: 0.07 us -> 1.79 us  [fast_on_device(): lax.ppermute(message_a, 'ax', pairs(slabs, 0, False))]
    ppermute x1, starting transfers between devices: 1.45 us -> 0.32 us  [fast_on_device(): lax.ppermute(az_a, 'az', pairs(sectors, 0, True))]
    ppermute x1, starting transfers between devices: 0.01 us -> 0.87 us  [fast_on_device(): lax.ppermute(az_b, 'az', pairs(sectors, 1, True))]
  transfers between devices with their start and end apart: 13 -> 13, of which waited for: 1 -> 3; matrix products, arithmetic and copies ran while one was open for 1% -> 0% of each run, Pallas kernels for 40% -> 12%
where the time goes in v2:
time: 48.7 us; the launch traced here: 48.5 us
  starting transfers between devices  23.8 us (49%)
  Pallas kernels  13.6 us (28%)
  waiting for transfers between devices  9.23 us (19%)
  local copies, waits for them, and re-layouts  1.76 us (4%)
    ppermute x7, starting transfers between devices, fast_on_device(): lax.ppermute(packed, 'az', [(i, i ^ p) for i in range(sectors)])  12.8 us
    ppermute x7, waiting for transfers between devices, fast_on_device(): lax.ppermute(packed, 'az', [(i, i ^ p) for i in range(sectors)])  7.23 us
    pallas_call x1, Pallas kernels, outer(): pl.pallas_call(functools.partial(outer_kernel, plan), in_specs=[pl.BlockS...  5.59 us
    pallas_call x1, Pallas kernels, inner(): pl.pallas_call(functools.partial(inner_kernel, plan), in_specs=[inside] *...  3.37 us
    ppermute x1, starting transfers between devices, fast_on_device(): lax.ppermute(message_b, 'ax', pairs(slabs, 1, False))  3.3 us
    ppermute x1, starting transfers between devices, fast_on_device(): lax.ppermute(ax_b, 'ax', pairs(slabs, 1, False))  3.17 us
    pallas_call x1, Pallas kernels, filtered(): pl.pallas_call(functools.partial(filter_kernel, plan), in_specs=[inside,...  2.15 us
    pallas_call x1, Pallas kernels, pack(): pl.pallas_call(functools.partial(pack_kernel, plan), grid=(1,), in_specs=...  2.1 us
  transfers between devices with their start and end apart: 13, of which 3 were waited for; matrix products, arithmetic and copies ran while one was open for 0% of the time, Pallas kernels for 12%

profile of v2, /device:TPU:1, one launch (start us, length us, event | category | flops | bytes accessed | tf_op | source)
XLA Modules:
  0.0 48.5 jit_solution(8075687995669803307)
XLA Ops:
  0.0 0.0 copy-start.6
  0.0 0.0 copy-start
  0.0 2.1 %pack.1.refs_0_ = f32[15,16,128]{2,1,0:T(8,128)} custom-call(f32[5,16,16,512]{3,2,1,0:T(8,128)} %x_ref.7), custom_call_target="tpu_custom_call" | custom-call | flops 1000000 | bytes 800000 | tf_op jit(solution)/shard_map/pack/pallas_call | solution.py:259
  2.1 0.0 copy-start.2
  2.1 5.1 %collective-permute-start.10 = (f32[15,16,128]{2,1,0:T(8,128)}, f32[15,16,128]{2,1,0:T(8,128)S(1)}, u32[]{:S(2)}, u32[]{:S(2)}) collective-permute-start(f32[15,16,128]{2,1,0:T(8,128)} %pack.1.refs_0_), channel_id=1, source_target_pairs={{0,28},{4,24},{8,20},{12,16},{16,12},{20,8},{24,4},{28,0},{1,29},{... | collective-permute-start | bytes 368648 | tf_op jit(solution)/shard_map/ppermute | solution.py:672
  7.2 0.0 copy-done
  7.2 0.4 edges.1
  7.6 0.3 collective-permute-start
  7.9 0.9 %collective-permute-start.1 = (f32[5,16,512]{2,1,0:T(8,128)S(1)}, f32[5,16,512]{2,1,0:T(8,128)S(1)}, u32[]{:S(2)}, u32[]{:S(2)}) collective-permute-start(f32[5,16,512]{2,1,0:T(8,128)S(1)} %get-tuple-element.16), channel_id=1, source_target_pairs={{4,8},{8,4},{12,16},{16,12},{20,24},{24,20},{28,0},{0,28},{5,9},{9... | collective-permute-start | bytes 491528 | tf_op jit(solution)/shard_map/ppermute | solution.py:677
  8.8 1.5 %collective-permute-start.2 = (f32[5,16,512]{2,1,0:T(8,128)S(1)}, f32[5,16,512]{2,1,0:T(8,128)S(1)}, u32[]{:S(2)}, u32[]{:S(2)}) collective-permute-start(f32[5,16,512]{2,1,0:T(8,128)S(1)} %get-tuple-element.17), channel_id=1, source_target_pairs={{0,1},{1,0},{2,3},{3,2},{4,5},{5,4},{6,7},{7,6},{8,9},{9,8},{10,11... | collective-permute-start | bytes 491528 | tf_op jit(solution)/shard_map/ppermute | solution.py:678
  10.3 0.0 copy-start.3
  10.3 0.0 copy-start.4
  10.3 0.0 copy-start.5
  10.3 3.2 %collective-permute-start.3 = (f32[5,16,512]{2,1,0:T(8,128)S(1)}, f32[5,16,512]{2,1,0:T(8,128)S(1)}, u32[]{:S(2)}, u32[]{:S(2)}) collective-permute-start(f32[5,16,512]{2,1,0:T(8,128)S(1)} %get-tuple-element.18), channel_id=1, source_target_pairs={{1,2},{2,1},{5,6},{6,5},{9,10},{10,9},{13,14},{14,13},{17,18},{18,... | collective-permute-start | bytes 491528 | tf_op jit(solution)/shard_map/ppermute | solution.py:679
  13.5 0.0 collective-permute-done.10.refs_7_
  13.5 0.0 copy-done.2
  13.5 0.5 collective-permute-start.9
  14.0 6.0 %collective-permute-done.9.refs_6_ = f32[15,16,128]{2,1,0:T(8,128)S(1)} collective-permute-done((f32[15,16,128]{2,1,0:T(8,128)S(1)}, f32[15,16,128]{2,1,0:T(8,128)S(1)}, u32[]{:S(2)}, u32[]{:S(2)}) %collective-permute-start.9) | collective-permute-done | bytes 122912 | tf_op jit(solution)/shard_map/ppermute | solution.py:672
  20.0 0.0 collective-permute-start.8
  20.0 0.0 collective-permute-done.az_a
  20.0 2.9 %collective-permute-start.7 = (f32[15,16,128]{2,1,0:T(8,128)S(1)}, f32[15,16,128]{2,1,0:T(8,128)S(1)}, u32[]{:S(2)}, u32[]{:S(2)}) collective-permute-start(f32[15,16,128]{2,1,0:T(8,128)S(1)} %copy-done.2), channel_id=1, source_target_pairs={{0,16},{4,20},{8,24},{12,28},{16,0},{20,4},{24,8},{28,12},{1,17},{... | collective-permute-start | bytes 368648 | tf_op jit(solution)/shard_map/ppermute | solution.py:672
  22.8 0.0 collective-permute-done.1.az_b
  22.9 4.1 %collective-permute-start.6 = (f32[15,16,128]{2,1,0:T(8,128)S(1)}, f32[15,16,128]{2,1,0:T(8,128)S(1)}, u32[]{:S(2)}, u32[]{:S(2)}) collective-permute-start(f32[15,16,128]{2,1,0:T(8,128)S(1)} %copy-done.2), channel_id=1, source_target_pairs={{0,12},{4,8},{8,4},{12,0},{16,28},{20,24},{24,20},{28,16},{1,13},{... | collective-permute-start | bytes 368648 | tf_op jit(solution)/shard_map/ppermute | solution.py:672
  26.9 0.0 collective-permute-done.2.ax_a
  26.9 0.0 collective-permute-start.5
  26.9 0.0 collective-permute-done.3.ax_b
  26.9 0.3 collective-permute-start.4
  27.3 0.0 copy-done.6
  27.3 5.6 %outer.1.after_ref.other_ref = f32[5,16,16,512]{3,2,1,0:T(8,128)} custom-call(f32[8,512]{1,0:T(8,128)S(1)} %copy-done.6, f32[5,16,16,512]{3,2,1,0:T(8,128)S(1)} %copy-done, f32[5,16,512]{2,1,0:T(8,128)S(1)} %collective-permute-done.az_a, f32[5,16,512]{2,1,0:T(8,128)S(1)} %collective-permute-done.1.az_b, f32[5,16,512]{2,1,0:T(8,128)S(1)} %collective-permute-done.2.ax_a, ...), custom_call_target="tpu_custom_call" | custom-call | flops 16000000 | bytes 5000000 | tf_op jit(solution)/shard_map/outer/pallas_call | solution.py:439
  32.9 0.0 collective-permute-done.8.refs_5_
  32.9 0.0 collective-permute-done.7.refs_4_
  32.9 0.0 collective-permute-done.6.refs_3_
  32.9 1.2 %collective-permute-done.5.refs_2_ = f32[15,16,128]{2,1,0:T(8,128)S(1)} collective-permute-done((f32[15,16,128]{2,1,0:T(8,128)S(1)}, f32[15,16,128]{2,1,0:T(8,128)S(1)}, u32[]{:S(2)}, u32[]{:S(2)}) %collective-permute-start.5) | collective-permute-done | bytes 122912 | tf_op jit(solution)/shard_map/ppermute | solution.py:672
  34.1 0.0 collective-permute-done.4.refs_1_
  34.1 0.0 copy-done.3
  34.1 0.0 copy-done.4
  34.1 0.0 copy-done.5
  34.1 0.0 copy-start.1
  34.2 1.7 %copy-done.1 = f32[5,16,16,512]{3,2,1,0:T(8,128)S(1)} copy-done((f32[5,16,16,512]{3,2,1,0:T(8,128)S(1)}, f32[5,16,16,512]{3,2,1,0:T(8,128)}, u32[]{:S(2)}) %copy-start.1) | copy-done | bytes 2621464
  35.9 2.1 %filter.1 = (f32[14,16,128]{2,1,0:T(8,128)S(1)}, f32[14,16,128]{2,1,0:T(8,128)S(1)}, f32[14,8,128]{2,1,0:T(8,128)S(1)}, f32[5,16,128]{2,1,0:T(8,128)S(1)}, f32[5...) custom-call(bf16[128,384]{1,0:T(8,128)(2,1)S(1)} %copy-done.4, bf16[8,48,384]{2,1,0:T(8,128)(2,1)S(1)} %copy-done.3, ...), custom_call_target="tpu_custom_call" | custom-call | flops 200000000 | bytes 1500000 | tf_op jit(solution)/shard_map/filter/pallas_call | solution.py:525
  38.0 1.8 %collective-permute-start.11 = (f32[5,16,128]{2,1,0:T(8,128)S(1)}, f32[5,16,128]{2,1,0:T(8,128)S(1)}, u32[]{:S(2)}, u32[]{:S(2)}) collective-permute-start(f32[5,16,128]{2,1,0:T(8,128)S(1)} %get-tuple-element.23), channel_id=1, source_target_pairs={{0,1},{1,0},{2,3},{3,2},{4,5},{5,4},{6,7},{7,6},{8,9},{9,8},{10,11... | collective-permute-start | bytes 122888 | tf_op jit(solution)/shard_map/ppermute | solution.py:684
  39.8 3.3 %collective-permute-start.12 = (f32[5,16,128]{2,1,0:T(8,128)S(1)}, f32[5,16,128]{2,1,0:T(8,128)S(1)}, u32[]{:S(2)}, u32[]{:S(2)}) collective-permute-start(f32[5,16,128]{2,1,0:T(8,128)S(1)} %get-tuple-element.24), channel_id=1, source_target_pairs={{1,2},{2,1},{5,6},{6,5},{9,10},{10,9},{13,14},{14,13},{17,18},{18,... | collective-permute-start | bytes 122888 | tf_op jit(solution)/shard_map/ppermute | solution.py:685
  43.1 0.0 collective-permute-done.11.message_a
  43.2 2.0 %collective-permute-done.12.message_b = f32[5,16,128]{2,1,0:T(8,128)S(1)} collective-permute-done((f32[5,16,128]{2,1,0:T(8,128)S(1)}, f32[5,16,128]{2,1,0:T(8,128)S(1)}, u32[]{:S(2)}, u32[]{:S(2)}) %collective-permute-start.12) | collective-permute-done | bytes 40992 | tf_op jit(solution)/shard_map/ppermute | solution.py:685
  45.1 3.4 %inner.1 = f32[5,16,16,512]{3,2,1,0:T(8,128)} custom-call(f32[8,512]{1,0:T(8,128)S(1)} %copy-done.6, f32[14,16,128]{2,1,0:T(8,128)S(1)} %get-tuple-element.19.own_ref, f32[14,16,128]{2,1,0:T(8,128)S(1)} %get-tuple-element.20.across_ref, f32[14,8,128]{2,1,0:T(8,128)S(1)} %get-tuple-element.21.edge_ref, ...), custom_call_target="tpu_custom_call", output_to_operand_aliasing={{}: (12, {})} | custom-call | flops 6000000 | bytes 2500000 | tf_op jit(solution)/shard_map/inner/pallas_call | solution.py:632
Async XLA Ops:
  0.0 27.3 %copy-start.6 = (f32[8,512]{1,0:T(8,128)S(1)}, f32[8,512]{1,0:T(8,128)}, u32[]{:S(2)}) copy-start(f32[8,512]{1,0:T(8,128)} %constant.8.clone.coef_ref) | copy-start | bytes 49156
  0.0 7.2 %copy-start = (f32[5,16,16,512]{3,2,1,0:T(8,128)S(1)}, f32[5,16,16,512]{3,2,1,0:T(8,128)}, u32[]{:S(2)}) copy-start(f32[5,16,16,512]{3,2,1,0:T(8,128)} %x_ref.7) | copy-start | bytes 7864324
  2.1 11.4 %copy-start.2 = (f32[15,16,128]{2,1,0:T(8,128)S(1)}, f32[15,16,128]{2,1,0:T(8,128)}, u32[]{:S(2)}) copy-start(f32[15,16,128]{2,1,0:T(8,128)} %pack.1.refs_0_) | copy-start | bytes 368644
  2.1 11.4 %collective-permute-start.10 = (f32[15,16,128]{2,1,0:T(8,128)}, f32[15,16,128]{2,1,0:T(8,128)S(1)}, u32[]{:S(2)}, u32[]{:S(2)}) collective-permute-start(f32[15,16,128]{2,1,0:T(8,128)} %pack.1.refs_0_), channel_id=1, source_target_pairs={{0,28},{4,24},{8,20},{12,16},{16,12},{20,8},{24,4},{28,0},{1,29},{... | collective-permute-start | bytes 368648 | tf_op jit(solution)/shard_map/ppermute | solution.py:672
  7.6 12.4 %collective-permute-start = (f32[5,16,512]{2,1,0:T(8,128)S(1)}, f32[5,16,512]{2,1,0:T(8,128)S(1)}, u32[]{:S(2)}, u32[]{:S(2)}) collective-permute-start(f32[5,16,512]{2,1,0:T(8,128)S(1)} %get-tuple-element.15), channel_id=1, source_target_pairs={{0,4},{4,0},{8,12},{12,8},{16,20},{20,16},{24,28},{28,24},{1,5},{5... | collective-permute-start | bytes 491528 | tf_op jit(solution)/shard_map/ppermute | solution.py:676
  7.9 14.9 %collective-permute-start.1 = (f32[5,16,512]{2,1,0:T(8,128)S(1)}, f32[5,16,512]{2,1,0:T(8,128)S(1)}, u32[]{:S(2)}, u32[]{:S(2)}) collective-permute-start(f32[5,16,512]{2,1,0:T(8,128)S(1)} %get-tuple-element.16), channel_id=1, source_target_pairs={{4,8},{8,4},{12,16},{16,12},{20,24},{24,20},{28,0},{0,28},{5,9},{9... | collective-permute-start | bytes 491528 | tf_op jit(solution)/shard_map/ppermute | solution.py:677
  8.8 18.1 %collective-permute-start.2 = (f32[5,16,512]{2,1,0:T(8,128)S(1)}, f32[5,16,512]{2,1,0:T(8,128)S(1)}, u32[]{:S(2)}, u32[]{:S(2)}) collective-permute-start(f32[5,16,512]{2,1,0:T(8,128)S(1)} %get-tuple-element.17), channel_id=1, source_target_pairs={{0,1},{1,0},{2,3},{3,2},{4,5},{5,4},{6,7},{7,6},{8,9},{9,8},{10,11... | collective-permute-start | bytes 491528 | tf_op jit(solution)/shard_map/ppermute | solution.py:678
  10.3 23.8 %copy-start.3 = (bf16[8,48,384]{2,1,0:T(8,128)(2,1)S(1)}, bf16[8,48,384]{2,1,0:T(8,128)(2,1)}, u32[]{:S(2)}) copy-start(bf16[8,48,384]{2,1,0:T(8,128)(2,1)} %constant.10.clone.inverse_ref) | copy-start | bytes 884740
  10.3 23.8 %copy-start.4 = (bf16[128,384]{1,0:T(8,128)(2,1)S(1)}, bf16[128,384]{1,0:T(8,128)(2,1)}, u32[]{:S(2)}) copy-start(bf16[128,384]{1,0:T(8,128)(2,1)} %constant.9.clone.forward_ref) | copy-start | bytes 294916
  10.3 23.8 %copy-start.5 = (f32[128,128]{1,0:T(8,128)S(1)}, f32[128,128]{1,0:T(8,128)}, u32[]{:S(2)}) copy-start(f32[128,128]{1,0:T(8,128)} %constant.11.clone.mask_ref) | copy-start | bytes 196612
  10.3 16.6 %collective-permute-start.3 = (f32[5,16,512]{2,1,0:T(8,128)S(1)}, f32[5,16,512]{2,1,0:T(8,128)S(1)}, u32[]{:S(2)}, u32[]{:S(2)}) collective-permute-start(f32[5,16,512]{2,1,0:T(8,128)S(1)} %get-tuple-element.18), channel_id=1, source_target_pairs={{1,2},{2,1},{5,6},{6,5},{9,10},{10,9},{13,14},{14,13},{17,18},{18,... | collective-permute-start | bytes 491528 | tf_op jit(solution)/shard_map/ppermute | solution.py:679
  13.5 6.5 %collective-permute-start.9 = (f32[15,16,128]{2,1,0:T(8,128)S(1)}, f32[15,16,128]{2,1,0:T(8,128)S(1)}, u32[]{:S(2)}, u32[]{:S(2)}) collective-permute-start(f32[15,16,128]{2,1,0:T(8,128)S(1)} %copy-done.2), channel_id=1, source_target_pairs={{0,24},{4,28},{8,16},{12,20},{16,8},{20,12},{24,0},{28,4},{1,25},{... | collective-permute-start | bytes 368648 | tf_op jit(solution)/shard_map/ppermute | solution.py:672
  20.0 12.9 %collective-permute-start.8 = (f32[15,16,128]{2,1,0:T(8,128)S(1)}, f32[15,16,128]{2,1,0:T(8,128)S(1)}, u32[]{:S(2)}, u32[]{:S(2)}) collective-permute-start(f32[15,16,128]{2,1,0:T(8,128)S(1)} %copy-done.2), channel_id=1, source_target_pairs={{0,20},{4,16},{8,28},{12,24},{16,4},{20,0},{24,12},{28,8},{1,21},{... | collective-permute-start | bytes 368648 | tf_op jit(solution)/shard_map/ppermute | solution.py:672
  20.0 12.9 %collective-permute-start.7 = (f32[15,16,128]{2,1,0:T(8,128)S(1)}, f32[15,16,128]{2,1,0:T(8,128)S(1)}, u32[]{:S(2)}, u32[]{:S(2)}) collective-permute-start(f32[15,16,128]{2,1,0:T(8,128)S(1)} %copy-done.2), channel_id=1, source_target_pairs={{0,16},{4,20},{8,24},{12,28},{16,0},{20,4},{24,8},{28,12},{1,17},{... | collective-permute-start | bytes 368648 | tf_op jit(solution)/shard_map/ppermute | solution.py:672
  22.9 10.1 %collective-permute-start.6 = (f32[15,16,128]{2,1,0:T(8,128)S(1)}, f32[15,16,128]{2,1,0:T(8,128)S(1)}, u32[]{:S(2)}, u32[]{:S(2)}) collective-permute-start(f32[15,16,128]{2,1,0:T(8,128)S(1)} %copy-done.2), channel_id=1, source_target_pairs={{0,12},{4,8},{8,4},{12,0},{16,28},{20,24},{24,20},{28,16},{1,13},{... | collective-permute-start | bytes 368648 | tf_op jit(solution)/shard_map/ppermute | solution.py:672
  26.9 7.2 %collective-permute-start.5 = (f32[15,16,128]{2,1,0:T(8,128)S(1)}, f32[15,16,128]{2,1,0:T(8,128)S(1)}, u32[]{:S(2)}, u32[]{:S(2)}) collective-permute-start(f32[15,16,128]{2,1,0:T(8,128)S(1)} %copy-done.2), channel_id=1, source_target_pairs={{0,8},{4,12},{8,0},{12,4},{16,24},{20,28},{24,16},{28,20},{1,9},{5... | collective-permute-start | bytes 368648 | tf_op jit(solution)/shard_map/ppermute | solution.py:672
  26.9 7.2 %collective-permute-start.4 = (f32[15,16,128]{2,1,0:T(8,128)S(1)}, f32[15,16,128]{2,1,0:T(8,128)S(1)}, u32[]{:S(2)}, u32[]{:S(2)}) collective-permute-start(f32[15,16,128]{2,1,0:T(8,128)S(1)} %copy-done.2), channel_id=1, source_target_pairs={{0,4},{4,0},{8,12},{12,8},{16,20},{20,16},{24,28},{28,24},{1,5},{5... | collective-permute-start | bytes 368648 | tf_op jit(solution)/shard_map/ppermute | solution.py:672
  34.1 1.7 %copy-start.1 = (f32[5,16,16,512]{3,2,1,0:T(8,128)S(1)}, f32[5,16,16,512]{3,2,1,0:T(8,128)}, u32[]{:S(2)}) copy-start(f32[5,16,16,512]{3,2,1,0:T(8,128)} %outer.1.after_ref.other_ref) | copy-start | bytes 7864324
  38.0 5.1 %collective-permute-start.11 = (f32[5,16,128]{2,1,0:T(8,128)S(1)}, f32[5,16,128]{2,1,0:T(8,128)S(1)}, u32[]{:S(2)}, u32[]{:S(2)}) collective-permute-start(f32[5,16,128]{2,1,0:T(8,128)S(1)} %get-tuple-element.23), channel_id=1, source_target_pairs={{0,1},{1,0},{2,3},{3,2},{4,5},{5,4},{6,7},{7,6},{8,9},{9,8},{10,11... | collective-permute-start | bytes 122888 | tf_op jit(solution)/shard_map/ppermute | solution.py:684
  39.8 5.3 %collective-permute-start.12 = (f32[5,16,128]{2,1,0:T(8,128)S(1)}, f32[5,16,128]{2,1,0:T(8,128)S(1)}, u32[]{:S(2)}, u32[]{:S(2)}) collective-permute-start(f32[5,16,128]{2,1,0:T(8,128)S(1)} %get-tuple-element.24), channel_id=1, source_target_pairs={{1,2},{2,1},{5,6},{6,5},{9,10},{10,9},{13,14},{14,13},{17,18},{18,... | collective-permute-start | bytes 122888 | tf_op jit(solution)/shard_map/ppermute | solution.py:685

commit v3 on v2

--- a/solution.py
+++ b/solution.py
@@ -16,7 +16,7 @@
 buoyancy = 1.0
 
 LANES = 128
-VMEM_LIMIT = 48 * 1024 * 1024
+VMEM_LIMIT = 24 * 1024 * 1024
 
 
 def swapped(block, axis, distance):
@@ -153,6 +153,9 @@
         self.rest = NEAR - self.full
         self.beside = LANES // max(self.full, 1)
         self.groups = -(-self.fields * self.planes // self.beside)
+        self.early = tuple(range(sectors // 2 + 1))
+        self.late = tuple(range(sectors // 2 + 1, sectors))
+        self.depth = 256
 
     def place(self, f, k):
         index = k * self.fields + f
@@ -169,6 +172,7 @@
             and plan.planes == plan.theta
             and plan.rest * plan.fields <= LANES
             and plan.groups % 2 == 0
+            and 3 * len(plan.early) * plan.theta <= plan.depth
             and plan.radial % LANES == 0
             and plan.radial > 2 * LANES
         )
@@ -178,13 +182,20 @@
         low = (table - high.astype(np.float32)).astype(jnp.bfloat16)
         return np.concatenate([high, high, low], axis=-1)
 
-    def forward(self):
+    def forward(self, pieces):
         theta = np.arange(self.total)
         mode = np.arange(self.modes)
         angle = (np.outer(mode, theta) % self.total) * (2.0 * np.pi / self.total)
         weight = np.where(mode == 0, 1.0, 2.0)[:, None] / self.total
         table = np.concatenate([np.cos(angle) * weight, np.sin(angle) * 2.0 / self.total], axis=0)
-        return self.split(table.astype(np.float32))
+        table = table.astype(np.float32).reshape(2 * self.modes, self.sectors, self.theta)
+        blocks = []
+        for sector in range(self.sectors):
+            chosen = np.concatenate([table[:, sector ^ p] for p in pieces], axis=1)
+            chosen = self.split(chosen)
+            pad = np.zeros((chosen.shape[0], self.depth - chosen.shape[1]), chosen.dtype)
+            blocks.append(np.concatenate([chosen, pad], axis=1))
+        return np.stack(blocks)
 
     def inverse(self):
         mode = np.arange(self.modes)
@@ -229,16 +240,27 @@
     return x if lanes % LANES == 0 else pltpu.roll(x, lanes % LANES, 1)
 
 
-def pack_kernel(plan, x_ref, out_ref):
+def pack_kernel(plan, x_ref, out_ref, buf, sems):
     shape = (plan.theta, LANES)
     lane = lax.broadcasted_iota(jnp.int32, shape, 1)
     row = lax.broadcasted_iota(jnp.int32, shape, 0)
     sign = (1 - 2 * (row & 1)).astype(jnp.float32)
+    chunk = 4
+    copies = [
+        pltpu.make_async_copy(
+            x_ref.at[:, pl.ds(i * chunk, chunk), :, pl.ds(0, LANES)], buf.at[i], sems.at[i]
+        )
+        for i in range(plan.planes // chunk)
+    ]
+    for copy in copies:
+        copy.start()
     group = jnp.zeros(shape, jnp.float32)
     sums = [jnp.zeros(shape, jnp.float32) for _ in range(plan.fields)]
     for k in range(plan.planes):
+        if k % chunk == 0:
+            copies[k // chunk].wait()
         for f in range(plan.fields):
-            x = x_ref[f, k]
+            x = buf[k // chunk, f, k % chunk]
             number, first = plan.place(f, k)
             part = moved(x, first)
             if first:
@@ -256,67 +278,90 @@
 
 
 def pack(plan, fields):
+    f32 = jnp.float32
+    chunks = plan.planes // 4
     return pl.pallas_call(
         functools.partial(pack_kernel, plan),
-        grid=(1,),
-        in_specs=[
-            pl.BlockSpec((plan.fields, plan.planes, plan.theta, LANES), lambda i: (0, 0, 0, 0))
+        in_specs=[pl.BlockSpec(memory_space=pl.ANY)],
+        out_specs=pl.BlockSpec(memory_space=pltpu.VMEM),
+        out_shape=jax.ShapeDtypeStruct((plan.groups + 1, plan.theta, LANES), f32),
+        scratch_shapes=[
+            pltpu.VMEM((chunks, plan.fields, 4, plan.theta, LANES), f32),
+            pltpu.SemaphoreType.DMA((chunks,)),
         ],
-        out_specs=pl.BlockSpec((plan.groups + 1, plan.theta, LANES), lambda i: (0, 0, 0)),
-        out_shape=jax.ShapeDtypeStruct((plan.groups + 1, plan.theta, LANES), jnp.float32),
         name="pack",
         cost_estimate=pl.CostEstimate(flops=1000000, bytes_accessed=800000, transcendentals=0),
     )(fields)
 
 
-def edges_kernel(plan, x_ref, az_a, az_b, ax_a, ax_b):
-    step = pl.program_id(0)
+def pick_columns(plan, x_ref, keep_high, ref, base):
+    last = plan.theta - 1
+    tiles = plan.radial // LANES
+    for f in range(plan.fields):
+        for k in range(plan.planes):
+            for tile in range(tiles):
+                here = slice(tile * LANES, (tile + 1) * LANES)
+                low = x_ref[f, k, 0:1, here]
+                high = x_ref[f, k, last : last + 1, here]
+                ref[base + f * tiles + tile, k : k + 1, :] = jnp.where(keep_high, high, low)
+
+
+def beside_kernel(plan, x_ref, packed_ref, again, beside):
+    again[...] = packed_ref[...]
+    beside[pl.ds(0, plan.groups + 1)] = packed_ref[...]
+    even_theta = lax.axis_index("az") % 2 == 0
+    pick_columns(plan, x_ref, even_theta, beside, plan.groups + 1)
+
+
+def edges_kernel(plan, x_ref, after_ref, az_b, ax_a, ax_b):
+    del after_ref
     even_theta = lax.axis_index("az") % 2 == 0
     even_plane = lax.axis_index("ax") % 2 == 0
-    rows = x_ref.shape[1]
-    for f in range(plan.fields):
-        for k in range(rows):
-            low = x_ref[f, k, 0:1, :]
-            high = x_ref[f, k, plan.theta - 1 : plan.theta, :]
-            az_a[f, k : k + 1, :] = jnp.where(even_theta, high, low)
-            az_b[f, k : k + 1, :] = jnp.where(even_theta, low, high)
-    first = step == 0
-    last = step == pl.num_programs(0) - 1
-
-    @pl.when(first & even_plane)
+    pick_columns(plan, x_ref, jnp.logical_not(even_theta), az_b, 0)
+
+    @pl.when(even_plane)
     def _():
+        ax_a[...] = x_ref[:, plan.planes - 1]
         ax_b[...] = x_ref[:, 0]
 
-    @pl.when(first & jnp.logical_not(even_plane))
+    @pl.when(jnp.logical_not(even_plane))
     def _():
         ax_a[...] = x_ref[:, 0]
-
-    @pl.when(last & even_plane)
-    def _():
-        ax_a[...] = x_ref[:, rows - 1]
-
-    @pl.when(last & jnp.logical_not(even_plane))
-    def _():
-        ax_b[...] = x_ref[:, rows - 1]
-
-
-def edges(plan, fields):
-    column = jax.ShapeDtypeStruct((plan.fields, plan.planes, plan.radial), jnp.float32)
-    plane = jax.ShapeDtypeStruct((plan.fields, plan.theta, plan.radial), jnp.float32)
-    part = pl.BlockSpec((plan.fields, 8, plan.radial), lambda i: (0, i, 0))
-    whole = pl.BlockSpec((plan.fields, plan.theta, plan.radial), lambda i: (0, 0, 0))
+        ax_b[...] = x_ref[:, plan.planes - 1]
+
+
+def beside(plan, fields, packed):
+    f32 = jnp.float32
+    columns = plan.fields * plan.radial // LANES
+    inside = pl.BlockSpec(memory_space=pltpu.VMEM)
+    return pl.pallas_call(
+        functools.partial(beside_kernel, plan),
+        in_specs=[inside] * 2,
+        out_specs=[inside] * 2,
+        out_shape=[
+            jax.ShapeDtypeStruct(packed.shape, f32),
+            jax.ShapeDtypeStruct((plan.groups + 1 + columns, plan.theta, LANES), f32),
+        ],
+        compiler_params=pltpu.CompilerParams(vmem_limit_bytes=VMEM_LIMIT),
+        name="beside",
+        cost_estimate=pl.CostEstimate(flops=0, bytes_accessed=1000000, transcendentals=0),
+    )(fields, packed)
+
+
+def edges(plan, fields, after):
+    f32 = jnp.float32
+    columns = plan.fields * plan.radial // LANES
+    plane = jax.ShapeDtypeStruct((plan.fields, plan.theta, plan.radial), f32)
+    inside = pl.BlockSpec(memory_space=pltpu.VMEM)
     return pl.pallas_call(
         functools.partial(edges_kernel, plan),
-        grid=(plan.planes // 8,),
-        in_specs=[
-            pl.BlockSpec((plan.fields, 8, plan.theta, plan.radial), lambda i: (0, i, 0, 0))
-        ],
-        out_specs=[part, part, whole, whole],
-        out_shape=[column, column, plane, plane],
+        in_specs=[inside, inside],
+        out_specs=[inside] * 3,
+        out_shape=[jax.ShapeDtypeStruct((columns, plan.theta, LANES), f32), plane, plane],
         compiler_params=pltpu.CompilerParams(vmem_limit_bytes=VMEM_LIMIT),
         name="edges",
-        cost_estimate=pl.CostEstimate(flops=0, bytes_accessed=4000000, transcendentals=0),
-    )(fields)
+        cost_estimate=pl.CostEstimate(flops=0, bytes_accessed=1000000, transcendentals=0),
+    )(fields, after)
 
 
 def advance(coef, q, jp, jm, tp, tm, kp, km):
@@ -352,149 +397,247 @@
     return up, down
 
 
-def load_halos(plan, copies, az_a, az_b, ax_a, ax_b, width, buf, side, sems):
-    odd_theta = lax.axis_index("az") % 2
-    odd_plane = lax.axis_index("ax") % 2
-    high = plan.planes + 1
-    slot_a = (1 - odd_plane) * high
-    lanes = pl.ds(0, width)
-    copies += [
-        pltpu.make_async_copy(az_a.at[:, :, lanes], side.at[1 - odd_theta], sems.at[0]),
-        pltpu.make_async_copy(az_b.at[:, :, lanes], side.at[odd_theta], sems.at[1]),
-        pltpu.make_async_copy(ax_a.at[:, :, lanes], buf.at[slot_a], sems.at[2]),
-        pltpu.make_async_copy(ax_b.at[:, :, lanes], buf.at[high - slot_a], sems.at[3]),
-    ]
-
-
-def outer_kernel(
-    plan, coef_ref, x_ref, az_a, az_b, ax_a, ax_b, out_ref, buf, side, done, sems, ins, outs
-):
+def choose_halos(plan, tiles, az_a, az_b, ax_a, ax_b, side, ends):
+    even_theta = lax.axis_index("az") % 2 == 0
+    even_plane = lax.axis_index("ax") % 2 == 0
+    all_tiles = plan.radial // LANES
+    for f in range(plan.fields):
+        for tile in tiles:
+            here = slice(tile * LANES, (tile + 1) * LANES)
+            number = f * all_tiles + tile
+            a = az_a[plan.groups + 1 + number]
+            b = az_b[number]
+            side[0, number] = jnp.where(even_theta, b, a)
+            side[1, number] = jnp.where(even_theta, a, b)
+            a = ax_a[f, :, here]
+            b = ax_b[f, :, here]
+            ends[0, f, :, here] = jnp.where(even_plane, b, a)
+            ends[1, f, :, here] = jnp.where(even_plane, a, b)
+
+
+def outer_kernel(plan, coef_ref, x_ref, done, token):
     planes = plan.planes
-    halos = []
-    load_halos(plan, halos, az_a, az_b, ax_a, ax_b, plan.radial, buf, side, sems)
-    for copy in halos:
-        copy.start()
-
-    def fetch(k):
-        return pltpu.make_async_copy(x_ref.at[:, k], buf.at[k + 1], ins.at[k])
-
-    def store(k):
-        return pltpu.make_async_copy(
-            done.at[k], out_ref.at[:, k, :, pl.ds(LANES, plan.radial - LANES)], outs.at[k]
-        )
-
-    for k in range(planes):
-        fetch(k).start()
-    for copy in halos:
-        copy.wait()
-    fetch(0).wait()
+    tiles = plan.radial // LANES
+    token[...] = jnp.zeros_like(token)
     shape = (plan.theta, LANES)
     lane = lax.broadcasted_iota(jnp.int32, shape, 1)
     row = lax.broadcasted_iota(jnp.int32, shape, 0)
-    tiles = plan.radial // LANES
 
     def step(group, carry):
-        start = pl.multiple_of(group * 8, 8)
-        for i in range(8):
+        start = pl.multiple_of(group * 4, 4)
+        for i in range(4):
             k = start + i
-            if i < 7:
-                fetch(k + 1).wait()
-            else:
-                pl.when(k < planes - 1)(lambda: fetch(k + 1).wait())
             for tile in range(1, tiles):
                 here = pl.ds(tile * LANES, LANES)
                 coef = [coef_ref[j : j + 1, here] for j in range(7)]
                 q, jp, jm, tp, tm, kp, km = ([] for _ in range(7))
                 for f in range(plan.fields):
-                    x = buf[k + 1, f, :, here]
-                    low = buf[k + 1, f, :, pl.ds((tile - 1) * LANES, LANES)]
+                    x = x_ref[f, k, :, here]
+                    low = x_ref[f, k, :, pl.ds((tile - 1) * LANES, LANES)]
                     q.append(x)
                     high = 0.0
                     if tile + 1 < tiles:
-                        high = buf[k + 1, f, :, pl.ds((tile + 1) * LANES, LANES)]
+                        high = x_ref[f, k, :, pl.ds((tile + 1) * LANES, LANES)]
                         high = pltpu.roll(high, LANES - 1, 1)
                     jp.append(jnp.where(lane == LANES - 1, high, pltpu.roll(x, LANES - 1, 1)))
                     jm.append(jnp.where(lane == 0, pltpu.roll(low, 1, 1), pltpu.roll(x, 1, 1)))
-                    before = side[0, f, pl.ds(start, 8), here][i : i + 1]
-                    after = side[1, f, pl.ds(start, 8), here][i : i + 1]
-                    up, down = turned(x, row, before, after)
+                    up, down = turned(x, row, 0.0, 0.0)
                     tp.append(up)
                     tm.append(down)
-                    kp.append(buf[k + 2, f, :, here])
-                    km.append(buf[k, f, :, here])
+                    if i < 3:
+                        above = x_ref[f, k + 1, :, here]
+                    else:
+                        above = x_ref[f, jnp.minimum(k + 1, planes - 1), :, here]
+                        above = jnp.where(k == planes - 1, 0.0, above)
+                    if i > 0:
+                        below = x_ref[f, k - 1, :, here]
+                    else:
+                        below = x_ref[f, jnp.maximum(k - 1, 0), :, here]
+                        below = jnp.where(k == 0, 0.0, below)
+                    kp.append(above)
+                    km.append(below)
                 result = advance(coef, q, jp, jm, tp, tm, kp, km)
                 for f in range(plan.fields):
                     done[k, f, :, pl.ds((tile - 1) * LANES, LANES)] = result[f]
-            store(k).start()
         return carry
 
-    lax.fori_loop(0, planes // 8, step, 0)
-    for k in range(planes):
-        store(k).wait()
-
-
-def outer(plan, coef, fields, halos):
-    anywhere = pl.BlockSpec(memory_space=pl.ANY)
+    lax.fori_loop(0, planes // 4, step, 0)
+
+
+def outer(plan, coef, fields):
+    inside = pl.BlockSpec(memory_space=pltpu.VMEM)
     f32 = jnp.float32
     return pl.pallas_call(
         functools.partial(outer_kernel, plan),
-        in_specs=[pl.BlockSpec(memory_space=pltpu.VMEM)] + [anywhere] * 5,
-        out_specs=anywhere,
-        out_shape=jax.ShapeDtypeStruct(fields.shape, f32),
-        scratch_shapes=[
-            pltpu.VMEM((plan.planes + 2, plan.fields, plan.theta, plan.radial), f32),
-            pltpu.VMEM((2, plan.fields, plan.planes, plan.radial), f32),
-            pltpu.VMEM((plan.planes, plan.fields, plan.theta, plan.radial - LANES), f32),
-            pltpu.SemaphoreType.DMA((4,)),
-            pltpu.SemaphoreType.DMA((plan.planes,)),
-            pltpu.SemaphoreType.DMA((plan.planes,)),
+        in_specs=[inside] * 2,
+        out_specs=[inside] * 2,
+        out_shape=[
+            jax.ShapeDtypeStruct((plan.planes, plan.fields, plan.theta, plan.radial - LANES), f32),
+            jax.ShapeDtypeStruct((8, LANES), f32),
         ],
         compiler_params=pltpu.CompilerParams(vmem_limit_bytes=VMEM_LIMIT),
         name="outer",
         cost_estimate=pl.CostEstimate(flops=16000000, bytes_accessed=5000000, transcendentals=0),
-    )(coef, fields, *halos)
-
-
-def halves(x):
+    )(coef, fields)
+
+
+def seams_kernel(
+    plan, coef_ref, x_ref, own_a, own_b, az_a, az_b, ax_a, ax_b, part_ref, out_ref, done, outs
+):
+    del part_ref
+    planes = plan.planes
+    tiles = plan.radial // LANES
+    even_theta = lax.axis_index("az") % 2 == 0
+    even_plane = lax.axis_index("ax") % 2 == 0
+    base = plan.groups + 1
+    nu_dt = viscosity * time_step
+    last = plan.theta - 1
+
+    def store(k):
+        return pltpu.make_async_copy(
+            done.at[k], out_ref.at[:, k, :, pl.ds(LANES, plan.radial - LANES)], outs.at[k]
+        )
+
+    for tile in range(1, tiles):
+        here = slice(tile * LANES, (tile + 1) * LANES)
+        there = slice((tile - 1) * LANES, tile * LANES)
+        c2 = coef_ref[1:2, here]
+        angular = coef_ref[3:4, here]
+        cross = coef_ref[6:7, here]
+        number = tiles + tile
+        mine_a = own_a[base + number]
+        mine_b = own_b[number]
+        turn_low = angular * jnp.where(even_theta, mine_b, mine_a)
+        turn_high = angular * jnp.where(even_theta, mine_a, mine_b)
+        before = []
+        after = []
+        for f in range(plan.fields):
+            a = az_a[base + f * tiles + tile]
+            b = az_b[f * tiles + tile]
+            before.append(jnp.where(even_theta, b, a))
+            after.append(jnp.where(even_theta, a, b))
+        for f in range(plan.fields):
+            low = (c2 + turn_low) * before[f]
+            high = (c2 - turn_high) * after[f]
+            if f == 0:
+                low = low + cross * before[1]
+                high = high - cross * after[1]
+            if f == 1:
+                low = low - cross * before[0]
+                high = high + cross * after[0]
+            for k in range(planes):
+                done[k, f, 0:1, there] += low[k : k + 1]
+                done[k, f, last : last + 1, there] += high[k : k + 1]
+            a = ax_a[f, :, here]
+            b = ax_b[f, :, here]
+            axial = (0.5 * time_step) * x_ref[2, 0, :, here]
+            done[0, f, :, there] += (nu_dt + axial) * jnp.where(even_plane, b, a)
+            axial = (0.5 * time_step) * x_ref[2, planes - 1, :, here]
+            done[planes - 1, f, :, there] += (nu_dt - axial) * jnp.where(even_plane, a, b)
+    for k in range(planes):
+        store(k).start()
+    for k in range(planes):
+        store(k).wait()
+
+
+def seams(plan, coef, fields, own, halos, part):
+    inside = pl.BlockSpec(memory_space=pltpu.VMEM)
+    return pl.pallas_call(
+        functools.partial(seams_kernel, plan),
+        in_specs=[inside] * 9,
+        out_specs=[pl.BlockSpec(memory_space=pl.ANY), inside],
+        out_shape=[
+            jax.ShapeDtypeStruct(fields.shape, jnp.float32),
+            jax.ShapeDtypeStruct(part.shape, jnp.float32),
+        ],
+        input_output_aliases={8: 1},
+        scratch_shapes=[pltpu.SemaphoreType.DMA((plan.planes,))],
+        compiler_params=pltpu.CompilerParams(vmem_limit_bytes=VMEM_LIMIT),
+        name="seams",
+        cost_estimate=pl.CostEstimate(flops=1000000, bytes_accessed=4000000, transcendentals=0),
+    )(coef, fields, *own, *halos, part)[0]
+
+
+def halo_scratch(plan):
+    columns = plan.fields * plan.radial // LANES
+    return [
+        pltpu.VMEM((2, columns, plan.planes, LANES), jnp.float32),
+        pltpu.VMEM((2, plan.fields, plan.theta, plan.radial), jnp.float32),
+    ]
+
+
+def halves(x, depth=None):
     high = x.astype(jnp.bfloat16)
     low = (x - high.astype(jnp.float32)).astype(jnp.bfloat16)
-    return jnp.concatenate([high, low, high], axis=0)
-
-
-def filter_kernel(plan, forward_ref, inverse_ref, mask_ref, after_ref, *refs):
-    del after_ref
-    pieces = refs[: plan.sectors]
-    own_ref, across_ref, edge_ref, sums_ref, message_a, message_b = refs[plan.sectors : plan.sectors + 6]
-    data, table, sems = refs[plan.sectors + 6 :]
-    sector = lax.axis_index("az")
+    parts = [high, low, high]
+    if depth is not None:
+        parts.append(jnp.zeros((depth - 3 * x.shape[0], x.shape[1]), jnp.bfloat16))
+    return jnp.concatenate(parts, axis=0)
+
+
+def two_groups(pieces, g):
+    return jnp.concatenate(
+        [jnp.concatenate([piece[g + i] for piece in pieces], axis=0) for i in range(2)], axis=1
+    )
+
+
+def early_kernel(plan, forward_ref, token_ref, *refs):
+    del token_ref
+    pieces = refs[: len(plan.early)]
+    spectra_ref, total_ref = refs[len(plan.early) :]
+    table = forward_ref[lax.axis_index("az")]
+    for g in range(0, plan.groups, 2):
+        both = halves(two_groups(pieces, g), plan.depth)
+        spectra_ref[g // 2] = jnp.dot(table, both, preferred_element_type=jnp.float32)
+    total = pieces[0][plan.groups]
+    for piece in pieces[1:]:
+        total = total + piece[plan.groups]
+    total_ref[...] = total
+
+
+def early_spectra(plan, pieces, token):
+    inside = pl.BlockSpec(memory_space=pltpu.VMEM)
+    f32 = jnp.float32
+    return pl.pallas_call(
+        functools.partial(early_kernel, plan),
+        in_specs=[inside] * (2 + len(pieces)),
+        out_specs=[inside] * 2,
+        out_shape=[
+            jax.ShapeDtypeStruct((plan.groups // 2, 2 * plan.modes, 2 * LANES), f32),
+            jax.ShapeDtypeStruct((plan.theta, LANES), f32),
+        ],
+        compiler_params=pltpu.CompilerParams(vmem_limit_bytes=VMEM_LIMIT),
+        name="early",
+        cost_estimate=pl.CostEstimate(flops=200000000, bytes_accessed=1500000, transcendentals=0),
+    )(jnp.asarray(plan.forward(plan.early)), token, *pieces)
+
+
+def filter_kernel(plan, forward_ref, inverse_ref, mask_ref, early_ref, early_total, *refs):
+    count = len(plan.late)
+    pieces = refs[:count]
+    own_ref, across_ref, edge_ref, sums_ref, message_a, message_b = refs[count:]
     odd_plane = lax.axis_index("ax") % 2
     theta = plan.theta
-    copies = [pltpu.make_async_copy(inverse_ref.at[sector], table, sems.at[plan.sectors])]
-    for p in range(plan.sectors):
-        copies.append(pltpu.make_async_copy(pieces[p], data.at[:, sector ^ p], sems.at[p]))
-    for copy in copies:
-        copy.start()
-    for copy in copies:
-        copy.wait()
+    sector = lax.axis_index("az")
+    forward = forward_ref[sector]
+    table = inverse_ref[sector]
     mask = mask_ref[...]
     mask = jnp.concatenate([mask, mask], axis=1)
 
     for g in range(0, plan.groups, 2):
-        both = jnp.concatenate(
-            [data[g].reshape(plan.total, LANES), data[g + 1].reshape(plan.total, LANES)], axis=1
-        )
-        spectra = jnp.dot(forward_ref[...], halves(both), preferred_element_type=jnp.float32)
+        both = halves(two_groups(pieces, g), plan.depth)
+        spectra = early_ref[g // 2] + jnp.dot(forward, both, preferred_element_type=jnp.float32)
         kept = halves(spectra * mask)
-        state = jnp.dot(table[...], kept, preferred_element_type=jnp.float32)
+        state = jnp.dot(table, kept, preferred_element_type=jnp.float32)
         for i in range(2):
             lanes = slice(i * LANES, (i + 1) * LANES)
             own_ref[g + i] = state[:theta, lanes]
             across_ref[g + i] = state[theta : 2 * theta, lanes]
             edge_ref[g + i] = state[2 * theta : 2 * theta + 8, lanes]
 
-    total = data[plan.groups, 0]
-    for p in range(1, plan.sectors):
-        total = total + data[plan.groups, p]
+    total = early_total[...]
+    for piece in pieces:
+        total = total + piece[plan.groups]
     total = total * (1.0 / plan.total)
     lane = lax.broadcasted_iota(jnp.int32, (plan.planes, LANES), 1)
     for f in range(plan.fields):
@@ -516,15 +659,14 @@
     pl.when(odd_plane == 0)(lambda: both_messages(message_b, message_a))
 
 
-def filtered(plan, pieces, after):
-    anywhere = pl.BlockSpec(memory_space=pl.ANY)
+def filtered(plan, pieces, early):
     inside = pl.BlockSpec(memory_space=pltpu.VMEM)
     f32 = jnp.float32
     cube = jax.ShapeDtypeStruct((plan.groups, plan.theta, LANES), f32)
     plane = jax.ShapeDtypeStruct((plan.fields, plan.theta, LANES), f32)
     return pl.pallas_call(
         functools.partial(filter_kernel, plan),
-        in_specs=[inside, anywhere, inside, anywhere] + [anywhere] * plan.sectors,
+        in_specs=[inside] * (5 + len(pieces)),
         out_specs=[inside] * 6,
         out_shape=[
             cube,
@@ -534,68 +676,55 @@
             plane,
             plane,
         ],
-        scratch_shapes=[
-            pltpu.VMEM((plan.groups + 1, plan.sectors, plan.theta, LANES), f32),
-            pltpu.VMEM((2 * plan.theta + 16, 6 * plan.modes), jnp.bfloat16),
-            pltpu.SemaphoreType.DMA((plan.sectors + 1,)),
-        ],
         compiler_params=pltpu.CompilerParams(vmem_limit_bytes=VMEM_LIMIT),
         name="filter",
         cost_estimate=pl.CostEstimate(flops=200000000, bytes_accessed=1500000, transcendentals=0),
     )(
-        jnp.asarray(plan.forward()),
+        jnp.asarray(plan.forward(plan.late)),
         jnp.asarray(plan.inverse()),
         jnp.asarray(plan.mask()),
-        after,
+        *early,
         *pieces,
     )
 
 
 def inner_kernel(
     plan, coef_ref, own_ref, across_ref, edge_ref, sums_ref, message_a, message_b,
-    x_ref, az_a, az_b, ax_a, ax_b, other_ref, out_ref, buf, side, state, done, sems, ins, outs
+    x_ref, az_a, az_b, ax_a, ax_b, other_ref, out_ref, side, ends, state, done, outs
 ):
     del other_ref
     planes = plan.planes
     theta = plan.theta
-    halos = []
-    load_halos(plan, halos, az_a, az_b, ax_a, ax_b, 2 * LANES, buf, side, sems)
-    fetch = [
-        pltpu.make_async_copy(x_ref.at[:, k, :, pl.ds(0, 2 * LANES)], buf.at[k + 1], ins.at[k])
-        for k in range(planes)
-    ]
+    tiles = plan.radial // LANES
     store = [
         pltpu.make_async_copy(done.at[k], out_ref.at[:, k, :, pl.ds(0, LANES)], outs.at[k])
         for k in range(planes)
     ]
-    for copy in halos + fetch:
-        copy.start()
     shape = (theta, LANES)
     lane = lax.broadcasted_iota(jnp.int32, shape, 1)
     row = lax.broadcasted_iota(jnp.int32, shape, 0)
     sign = (1 - 2 * (row & 1)).astype(jnp.float32)
     lane1 = lax.broadcasted_iota(jnp.int32, (1, LANES), 1)
-    first = pl.ds(0, LANES)
-    coef = [coef_ref[i : i + 1, :LANES] for i in range(7)]
+    first = slice(0, LANES)
+    coef = [coef_ref[i : i + 1, first] for i in range(7)]
     flips = (-1.0, -1.0, 1.0, 1.0, 1.0)
-
-    for copy in halos + fetch:
-        copy.wait()
+    choose_halos(plan, range(1), az_a, az_b, ax_a, ax_b, side, ends)
+
     for k in range(planes):
         for f in range(plan.fields):
             number, start = plan.place(f, k)
             state[k + 1, f] = jnp.where(
                 lane < plan.full,
                 moved(own_ref[number], -start),
-                buf[k + 1, f, :, first] - sign * sums_ref[f, k : k + 1],
+                x_ref[f, k, :, first] - sign * sums_ref[f, k : k + 1],
             )
-    odd_plane = lax.axis_index("ax") % 2
-    high = planes + 1
-    slot_a = (1 - odd_plane) * high
-    for message, slot in ((message_a, slot_a), (message_b, high - slot_a)):
-        for f in range(plan.fields):
-            raw = buf[slot, f, :, first]
-            state[slot, f] = jnp.where(lane < plan.full, message[f], raw - sign * message[f])
+    even_plane = lax.axis_index("ax") % 2 == 0
+    for f in range(plan.fields):
+        a = message_a[f]
+        b = message_b[f]
+        for end, slot, message in ((0, 0, jnp.where(even_plane, b, a)), (1, planes + 1, jnp.where(even_plane, a, b))):
+            raw = ends[end, f, :, first]
+            state[slot, f] = jnp.where(lane < plan.full, message, raw - sign * message)
 
     for k in range(planes):
         q, jp, jm, tp, tm, kp, km = ([] for _ in range(7))
@@ -603,14 +732,15 @@
             number, start = plan.place(f, k)
             x = state[k + 1, f]
             q.append(x)
-            high_part = pltpu.roll(buf[k + 1, f, :, pl.ds(LANES, LANES)], LANES - 1, 1)
+            high_part = pltpu.roll(x_ref[f, k, :, LANES : 2 * LANES], LANES - 1, 1)
             jp.append(jnp.where(lane == LANES - 1, high_part, pltpu.roll(x, LANES - 1, 1)))
             opposite = flips[f] * moved(across_ref[number], -start)
             jm.append(jnp.where(lane == 0, opposite, pltpu.roll(x, 1, 1)))
             total = sums_ref[f, k : k + 1]
             sides = moved(edge_ref[number], -start)
-            before = jnp.where(lane1 < plan.full, sides[0:1], side[0, f, k : k + 1, first] + total)
-            after = jnp.where(lane1 < plan.full, sides[1:2], side[1, f, k : k + 1, first] - total)
+            column = f * tiles
+            before = jnp.where(lane1 < plan.full, sides[0:1], side[0, column, k : k + 1] + total)
+            after = jnp.where(lane1 < plan.full, sides[1:2], side[1, column, k : k + 1] - total)
             up, down = turned(x, row, before, after)
             tp.append(up)
             tm.append(down)
@@ -631,17 +761,14 @@
     operands = (coef, *parts, *messages, fields, *halos, partial)
     return pl.pallas_call(
         functools.partial(inner_kernel, plan),
-        in_specs=[inside] * 7 + [anywhere] * 6,
+        in_specs=[inside] * 12 + [anywhere],
         out_specs=anywhere,
         out_shape=jax.ShapeDtypeStruct(fields.shape, f32),
         input_output_aliases={len(operands) - 1: 0},
-        scratch_shapes=[
-            pltpu.VMEM((plan.planes + 2, plan.fields, plan.theta, 2 * LANES), f32),
-            pltpu.VMEM((2, plan.fields, plan.planes, 2 * LANES), f32),
+        scratch_shapes=halo_scratch(plan)
+        + [
             pltpu.VMEM((plan.planes + 2, plan.fields, plan.theta, LANES), f32),
             pltpu.VMEM((plan.planes, plan.fields, plan.theta, LANES), f32),
-            pltpu.SemaphoreType.DMA((4,)),
-            pltpu.SemaphoreType.DMA((plan.planes,)),
             pltpu.SemaphoreType.DMA((plan.planes,)),
         ],
         compiler_params=pltpu.CompilerParams(vmem_limit_bytes=VMEM_LIMIT),
@@ -666,24 +793,35 @@
     plan = Plan(fields.shape, sectors)
     coef = jnp.asarray(plan.coefficients())
 
+    def send(x, distance):
+        return lax.ppermute(x, "az", [(i, i ^ distance) for i in range(sectors)])
+
     packed = pack(plan, fields)
-    pieces = [packed]
-    for p in range(1, sectors):
-        pieces.append(lax.ppermute(packed, "az", [(i, i ^ p) for i in range(sectors)]))
-
-    az_a, az_b, ax_a, ax_b = edges(plan, fields)
+    half = sectors // 2
+    far = send(packed, half)
+    again, wide = beside(plan, fields, packed)
+    pieces = [None] * sectors
+    pieces[0] = packed
+    pieces[half] = far
+    for p in range(half - 1, 0, -1):
+        pieces[p] = send(wide if p == 1 else again, p)
+    for p in range(half - 1, 0, -1):
+        pieces[half + p] = send(far, p)
+    part, token = outer(plan, coef, fields)
+    early = early_spectra(plan, pieces[: half + 1], token)
+    az_b, ax_a, ax_b = edges(plan, fields, early[1])
     halos = (
-        lax.ppermute(az_a, "az", pairs(sectors, 0, True)),
+        pieces[1],
         lax.ppermute(az_b, "az", pairs(sectors, 1, True)),
         lax.ppermute(ax_a, "ax", pairs(slabs, 0, False)),
         lax.ppermute(ax_b, "ax", pairs(slabs, 1, False)),
     )
-    partial = outer(plan, coef, fields, halos)
-    *parts, message_a, message_b = filtered(plan, pieces, partial)
+    *parts, message_a, message_b = filtered(plan, pieces[half + 1 :], early)
     messages = (
         lax.ppermute(message_a, "ax", pairs(slabs, 0, False)),
         lax.ppermute(message_b, "ax", pairs(slabs, 1, False)),
     )
+    partial = seams(plan, coef, fields, (wide, az_b), halos, part)
     return inner(plan, coef, parts, messages, fields, halos, partial)
 
 

time: 48.7 us -> 36.5 us (0.75)
  waiting for transfers between devices: 9.23 us -> 3.77 us
  Pallas kernels: 13.6 us -> 10.3 us
  starting transfers between devices: 23.8 us -> 21.2 us
  local copies, waits for them, and re-layouts: 1.76 us -> 0.93 us
    ppermute x8 -> x7, waiting for transfers between devices: 7.23 us -> 2.95 us  [send(): return lax.ppermute(x, 'az', [(i, i ^ distance) for i in range(sectors)])]
    ppermute x8 -> x7, starting transfers between devices: 13.1 us -> 9.57 us  [send(): return lax.ppermute(x, 'az', [(i, i ^ distance) for i in range(sectors)])]
    pallas_call x4 -> x7, Pallas kernels: 10.3 us -> 7.71 us  [the longest x1 2.25 us: outer(): pl.pallas_call(functools.partial(outer_kernel, plan), in_specs=[inside] *...]
    ppermute x1, starting transfers between devices: 0.87 us -> 3.24 us  [fast_on_device(): lax.ppermute(az_b, 'az', pairs(sectors, 1, True))]
    ppermute x1, starting transfers between devices: 1.79 us -> 0.07 us  [fast_on_device(): lax.ppermute(message_a, 'ax', pairs(slabs, 0, False))]
    ppermute x1, waiting for transfers between devices: 1.99 us -> 0.8 us  [fast_on_device(): lax.ppermute(message_b, 'ax', pairs(slabs, 1, False))]
    ppermute x1, starting transfers between devices: 1.52 us -> 2.47 us  [fast_on_device(): lax.ppermute(ax_a, 'ax', pairs(slabs, 0, False))]
    unnamed x14 -> x16, local copies, waits for them, and re-layouts: 1.76 us -> 0.93 us
  transfers between devices with their start and end apart: 13 -> 12, of which waited for: 3 -> 2; matrix products, arithmetic and copies ran while one was open for 0% -> 0% of each run, Pallas kernels for 12% -> 15%
where the time goes in v3:
time: 36.5 us; the launch traced here: 36.4 us
  starting transfers between devices  21.2 us (58%)
  Pallas kernels  10.3 us (28%)
  waiting for transfers between devices  3.77 us (10%)
  local copies, waits for them, and re-layouts  0.93 us (3%)
    ppermute x7, starting transfers between devices, send(): return lax.ppermute(x, 'az', [(i, i ^ distance) for i in range(sectors)])  9.57 us
    ppermute x1, starting transfers between devices, fast_on_device(): lax.ppermute(az_b, 'az', pairs(sectors, 1, True))  3.24 us
    ppermute x1, starting transfers between devices, fast_on_device(): lax.ppermute(ax_b, 'ax', pairs(slabs, 1, False))  3.04 us
    ppermute x7, waiting for transfers between devices, send(): return lax.ppermute(x, 'az', [(i, i ^ distance) for i in range(sectors)])  2.95 us
    ppermute x1, starting transfers between devices, fast_on_device(): lax.ppermute(message_b, 'ax', pairs(slabs, 1, False))  2.78 us
    pallas_call x1, Pallas kernels, inner(): pl.pallas_call(functools.partial(inner_kernel, plan), in_specs=[inside] *...  2.57 us
    ppermute x1, starting transfers between devices, fast_on_device(): lax.ppermute(ax_a, 'ax', pairs(slabs, 0, False))  2.47 us
    pallas_call x1, Pallas kernels, outer(): pl.pallas_call(functools.partial(outer_kernel, plan), in_specs=[inside] *...  2.25 us
  transfers between devices with their start and end apart: 12, of which 2 were waited for; matrix products, arithmetic and copies ran while one was open for 0% of the time, Pallas kernels for 15%

profile of v3, /device:TPU:1, one launch (start us, length us, event | category | flops | bytes accessed | tf_op | source)
XLA Modules:
  0.0 36.4 jit_solution(16408528214621799719)
XLA Ops:
  0.0 0.0 copy-start.6
  0.0 0.0 copy-start
  0.0 2.2 %pack.1.packed_ref.refs_0_ = f32[15,16,128]{2,1,0:T(8,128)} custom-call(f32[5,16,16,512]{3,2,1,0:T(8,128)} %x_ref.11), custom_call_target="tpu_custom_call" | custom-call | flops 1000000 | bytes 800000 | tf_op jit(solution)/shard_map/pack/pallas_call | solution.py:283
  2.2 0.0 copy-done
  2.2 0.0 copy-start.1
  2.2 0.9 %copy-done.1 = f32[15,16,128]{2,1,0:T(8,128)S(1)} copy-done((f32[15,16,128]{2,1,0:T(8,128)S(1)}, f32[15,16,128]{2,1,0:T(8,128)}, u32[]{:S(2)}) %copy-start.1) | copy-done | bytes 122904
  3.1 0.0 copy-start.2
  3.1 0.0 copy-start.3
  3.1 0.2 beside.1
  3.3 2.1 %collective-permute-start = (f32[35,16,128]{2,1,0:T(8,128)S(1)}, f32[35,16,128]{2,1,0:T(8,128)S(1)}, u32[]{:S(2)}, u32[]{:S(2)}) collective-permute-start(f32[35,16,128]{2,1,0:T(8,128)S(1)} %get-tuple-element.22.own_a), channel_id=1, source_target_pairs={{0,4},{4,0},{8,12},{12,8},{16,20},{20,16},{24,28},{28,24},{1,5},{5... | collective-permute-start | bytes 860168 | tf_op jit(solution)/shard_map/ppermute | solution.py:797
  5.4 2.3 %collective-permute-start.3 = (f32[15,16,128]{2,1,0:T(8,128)S(1)}, f32[15,16,128]{2,1,0:T(8,128)S(1)}, u32[]{:S(2)}, u32[]{:S(2)}) collective-permute-start(f32[15,16,128]{2,1,0:T(8,128)S(1)} %copy-done.1), channel_id=1, source_target_pairs={{0,16},{4,20},{8,24},{12,28},{16,0},{20,4},{24,8},{28,12},{1,17},{... | collective-permute-start | bytes 368648 | tf_op jit(solution)/shard_map/ppermute | solution.py:797
  7.7 1.3 %collective-permute-start.2 = (f32[15,16,128]{2,1,0:T(8,128)S(1)}, f32[15,16,128]{2,1,0:T(8,128)S(1)}, u32[]{:S(2)}, u32[]{:S(2)}) collective-permute-start(f32[15,16,128]{2,1,0:T(8,128)S(1)} %get-tuple-element.23), channel_id=1, source_target_pairs={{0,12},{4,8},{8,4},{12,0},{16,28},{20,24},{24,20},{28,16},{1,13},{... | collective-permute-start | bytes 368648 | tf_op jit(solution)/shard_map/ppermute | solution.py:797
  9.0 0.2 collective-permute-start.1
  9.1 2.9 %collective-permute-done.3.refs_4_ = f32[15,16,128]{2,1,0:T(8,128)S(1)} collective-permute-done((f32[15,16,128]{2,1,0:T(8,128)S(1)}, f32[15,16,128]{2,1,0:T(8,128)S(1)}, u32[]{:S(2)}, u32[]{:S(2)}) %collective-permute-start.3) | collective-permute-done | bytes 122912 | tf_op jit(solution)/shard_map/ppermute | solution.py:797
  12.1 2.5 %collective-permute-start.6 = (f32[15,16,128]{2,1,0:T(8,128)S(1)}, f32[15,16,128]{2,1,0:T(8,128)S(1)}, u32[]{:S(2)}, u32[]{:S(2)}) collective-permute-start(f32[15,16,128]{2,1,0:T(8,128)S(1)} %collective-permute-done.3.refs_4_), channel_id=1, source_target_pairs={{0,12},{4,8},{8,4},{12,0},{16,28},{20,24},{24,20},{28,16},{1,13},{... | collective-permute-start | bytes 368648 | tf_op jit(solution)/shard_map/ppermute | solution.py:797
  14.5 0.0 copy-done.6
  14.5 2.3 %outer.1 = (f32[16,5,16,384]{3,2,1,0:T(8,128)S(1)}, f32[8,128]{1,0:T(8,128)S(1)}) custom-call(f32[8,512]{1,0:T(8,128)S(1)} %copy-done.6, f32[5,16,16,512]{3,2,1,0:T(8,128)S(1)} %copy-done), custom_call_target="tpu_custom_call" | custom-call | flops 16000000 | bytes 5000000 | tf_op jit(solution)/shard_map/outer/pallas_call | solution.py:470
  16.8 0.0 copy-start.4
  16.8 0.0 copy-start.5
  16.8 0.0 copy-start.7
  16.8 0.1 collective-permute-start.5
  16.9 0.0 collective-permute-done.2.refs_3_
  16.9 1.2 %collective-permute-start.4 = (f32[15,16,128]{2,1,0:T(8,128)S(1)}, f32[15,16,128]{2,1,0:T(8,128)S(1)}, u32[]{:S(2)}, u32[]{:S(2)}) collective-permute-start(f32[15,16,128]{2,1,0:T(8,128)S(1)} %collective-permute-done.3.refs_4_), channel_id=1, source_target_pairs={{0,4},{4,0},{8,12},{12,8},{16,20},{20,16},{24,28},{28,24},{1,5},{5... | collective-permute-start | bytes 368648 | tf_op jit(solution)/shard_map/ppermute | solution.py:797
  18.1 0.0 collective-permute-done.1.refs_2_
  18.1 0.0 collective-permute-done.refs_1_.az_a
  18.1 0.0 copy-done.2
  18.1 0.0 copy-done.3
  18.1 0.3 early.1
  18.5 0.2 edges.1
  18.7 2.5 %collective-permute-start.10 = (f32[5,16,512]{2,1,0:T(8,128)S(1)}, f32[5,16,512]{2,1,0:T(8,128)S(1)}, u32[]{:S(2)}, u32[]{:S(2)}) collective-permute-start(f32[5,16,512]{2,1,0:T(8,128)S(1)} %get-tuple-element.33), channel_id=1, source_target_pairs={{0,1},{1,0},{2,3},{3,2},{4,5},{5,4},{6,7},{7,6},{8,9},{9,8},{10,11... | collective-permute-start | bytes 491528 | tf_op jit(solution)/shard_map/ppermute | solution.py:816
  21.1 3.0 %collective-permute-start.11 = (f32[5,16,512]{2,1,0:T(8,128)S(1)}, f32[5,16,512]{2,1,0:T(8,128)S(1)}, u32[]{:S(2)}, u32[]{:S(2)}) collective-permute-start(f32[5,16,512]{2,1,0:T(8,128)S(1)} %get-tuple-element.34), channel_id=1, source_target_pairs={{1,2},{2,1},{5,6},{6,5},{9,10},{10,9},{13,14},{14,13},{17,18},{18,... | collective-permute-start | bytes 491528 | tf_op jit(solution)/shard_map/ppermute | solution.py:817
  24.2 0.0 collective-permute-done.6.refs_2_
  24.2 3.2 %collective-permute-start.9 = (f32[20,16,128]{2,1,0:T(8,128)S(1)}, f32[20,16,128]{2,1,0:T(8,128)S(1)}, u32[]{:S(2)}, u32[]{:S(2)}) collective-permute-start(f32[20,16,128]{2,1,0:T(8,128)S(1)} %get-tuple-element.32.own_b), channel_id=1, source_target_pairs={{4,8},{8,4},{12,16},{16,12},{20,24},{24,20},{28,0},{0,28},{5,9},{9... | collective-permute-start | bytes 491528 | tf_op jit(solution)/shard_map/ppermute | solution.py:815
  27.4 0.0 collective-permute-done.5.refs_1_
  27.5 0.0 collective-permute-done.4.refs_0_
  27.5 0.0 copy-done.4
  27.5 0.0 copy-done.5
  27.5 0.0 copy-done.7
  27.5 0.9 %filter.1 = (f32[14,16,128]{2,1,0:T(8,128)S(1)}, f32[14,16,128]{2,1,0:T(8,128)S(1)}, f32[14,8,128]{2,1,0:T(8,128)S(1)}, f32[5,16,128]{2,1,0:T(8,128)S(1)}, f32[5...) custom-call(bf16[8,128,256]{2,1,0:T(8,128)(2,1)S(1)} %copy-done.4, bf16[8,48,384]{2,1,0:T(8,128)(2,1)S(1)} %copy-done.5, ...), custom_call_target="tpu_custom_call" | custom-call | flops 200000000 | bytes 1500000 | tf_op jit(solution)/shard_map/filter/pallas_call | solution.py:667
  28.4 0.1 collective-permute-start.7
  28.5 2.8 %collective-permute-start.8 = (f32[5,16,128]{2,1,0:T(8,128)S(1)}, f32[5,16,128]{2,1,0:T(8,128)S(1)}, u32[]{:S(2)}, u32[]{:S(2)}) collective-permute-start(f32[5,16,128]{2,1,0:T(8,128)S(1)} %get-tuple-element.31), channel_id=1, source_target_pairs={{1,2},{2,1},{5,6},{6,5},{9,10},{10,9},{13,14},{14,13},{17,18},{18,... | collective-permute-start | bytes 122888 | tf_op jit(solution)/shard_map/ppermute | solution.py:822
  31.3 0.0 collective-permute-done.10.ax_a
  31.3 0.0 collective-permute-done.11.ax_b
  31.3 0.0 collective-permute-done.9.az_b
  31.3 1.7 %seams.1 = (f32[5,16,16,512]{3,2,1,0:T(8,128)}, f32[16,5,16,384]{3,2,1,0:T(8,128)S(1)}) custom-call(f32[8,512]{1,0:T(8,128)S(1)} %copy-done.6, f32[5,16,16,512]{3,2,1,0:T(8,128)S(1)} %copy-done, f32[35,16,128]{2,1,0:T(8,128)S(1)} %get-tuple-element.22.own_a, f32[20,16,128]{2,1,0:T(8,128)S(1)} %get-tuple-element.32.own_b, ...), custom_call_target="tpu_custom_call", output_to_operand_aliasing={{1}: (8, {})} | custom-call | flops 1000000 | bytes 4000000 | tf_op jit(solution)/shard_map/seams/pallas_call | solution.py:545
  33.0 0.0 collective-permute-done.7.message_a
  33.0 0.8 %collective-permute-done.8.message_b = f32[5,16,128]{2,1,0:T(8,128)S(1)} collective-permute-done((f32[5,16,128]{2,1,0:T(8,128)S(1)}, f32[5,16,128]{2,1,0:T(8,128)S(1)}, u32[]{:S(2)}, u32[]{:S(2)}) %collective-permute-start.8) | collective-permute-done | bytes 40992 | tf_op jit(solution)/shard_map/ppermute | solution.py:822
  33.8 2.6 %inner.1 = f32[5,16,16,512]{3,2,1,0:T(8,128)} custom-call(f32[8,512]{1,0:T(8,128)S(1)} %copy-done.6, f32[14,16,128]{2,1,0:T(8,128)S(1)} %get-tuple-element.26.own_ref, f32[14,16,128]{2,1,0:T(8,128)S(1)} %get-tuple-element.27.across_ref, f32[14,8,128]{2,1,0:T(8,128)S(1)} %get-tuple-element.28.edge_ref, ...), custom_call_target="tpu_custom_call", output_to_operand_aliasing={{}: (12, {})} | custom-call | flops 6000000 | bytes 2500000 | tf_op jit(solution)/shard_map/inner/pallas_call | solution.py:762
Async XLA Ops:
  0.0 14.5 %copy-start.6 = (f32[8,512]{1,0:T(8,128)S(1)}, f32[8,512]{1,0:T(8,128)}, u32[]{:S(2)}) copy-start(f32[8,512]{1,0:T(8,128)} %constant.10.clone.coef_ref) | copy-start | bytes 49156
  0.0 2.2 %copy-start = (f32[5,16,16,512]{3,2,1,0:T(8,128)S(1)}, f32[5,16,16,512]{3,2,1,0:T(8,128)}, u32[]{:S(2)}) copy-start(f32[5,16,16,512]{3,2,1,0:T(8,128)} %x_ref.11) | copy-start | bytes 7864324
  2.2 0.9 %copy-start.1 = (f32[15,16,128]{2,1,0:T(8,128)S(1)}, f32[15,16,128]{2,1,0:T(8,128)}, u32[]{:S(2)}) copy-start(f32[15,16,128]{2,1,0:T(8,128)} %pack.1.packed_ref.refs_0_) | copy-start | bytes 368644
  3.1 15.0 %copy-start.2 = (f32[15,16,128]{2,1,0:T(8,128)S(1)}, f32[15,16,128]{2,1,0:T(8,128)}, u32[]{:S(2)}) copy-start(f32[15,16,128]{2,1,0:T(8,128)} %pack.1.packed_ref.refs_0_) | copy-start | bytes 368644
  3.1 15.0 %copy-start.3 = (bf16[8,128,256]{2,1,0:T(8,128)(2,1)S(1)}, bf16[8,128,256]{2,1,0:T(8,128)(2,1)}, u32[]{:S(2)}) copy-start(bf16[8,128,256]{2,1,0:T(8,128)(2,1)} %constant.11.clone.forward_ref) | copy-start | bytes 1572868
  3.3 14.8 %collective-permute-start = (f32[35,16,128]{2,1,0:T(8,128)S(1)}, f32[35,16,128]{2,1,0:T(8,128)S(1)}, u32[]{:S(2)}, u32[]{:S(2)}) collective-permute-start(f32[35,16,128]{2,1,0:T(8,128)S(1)} %get-tuple-element.22.own_a), channel_id=1, source_target_pairs={{0,4},{4,0},{8,12},{12,8},{16,20},{20,16},{24,28},{28,24},{1,5},{5... | collective-permute-start | bytes 860168 | tf_op jit(solution)/shard_map/ppermute | solution.py:797
  5.4 6.7 %collective-permute-start.3 = (f32[15,16,128]{2,1,0:T(8,128)S(1)}, f32[15,16,128]{2,1,0:T(8,128)S(1)}, u32[]{:S(2)}, u32[]{:S(2)}) collective-permute-start(f32[15,16,128]{2,1,0:T(8,128)S(1)} %copy-done.1), channel_id=1, source_target_pairs={{0,16},{4,20},{8,24},{12,28},{16,0},{20,4},{24,8},{28,12},{1,17},{... | collective-permute-start | bytes 368648 | tf_op jit(solution)/shard_map/ppermute | solution.py:797
  7.7 9.2 %collective-permute-start.2 = (f32[15,16,128]{2,1,0:T(8,128)S(1)}, f32[15,16,128]{2,1,0:T(8,128)S(1)}, u32[]{:S(2)}, u32[]{:S(2)}) collective-permute-start(f32[15,16,128]{2,1,0:T(8,128)S(1)} %get-tuple-element.23), channel_id=1, source_target_pairs={{0,12},{4,8},{8,4},{12,0},{16,28},{20,24},{24,20},{28,16},{1,13},{... | collective-permute-start | bytes 368648 | tf_op jit(solution)/shard_map/ppermute | solution.py:797
  9.0 9.1 %collective-permute-start.1 = (f32[15,16,128]{2,1,0:T(8,128)S(1)}, f32[15,16,128]{2,1,0:T(8,128)S(1)}, u32[]{:S(2)}, u32[]{:S(2)}) collective-permute-start(f32[15,16,128]{2,1,0:T(8,128)S(1)} %get-tuple-element.23), channel_id=1, source_target_pairs={{0,8},{4,12},{8,0},{12,4},{16,24},{20,28},{24,16},{28,20},{1,9},{5... | collective-permute-start | bytes 368648 | tf_op jit(solution)/shard_map/ppermute | solution.py:797
  12.1 12.1 %collective-permute-start.6 = (f32[15,16,128]{2,1,0:T(8,128)S(1)}, f32[15,16,128]{2,1,0:T(8,128)S(1)}, u32[]{:S(2)}, u32[]{:S(2)}) collective-permute-start(f32[15,16,128]{2,1,0:T(8,128)S(1)} %collective-permute-done.3.refs_4_), channel_id=1, source_target_pairs={{0,12},{4,8},{8,4},{12,0},{16,28},{20,24},{24,20},{28,16},{1,13},{... | collective-permute-start | bytes 368648 | tf_op jit(solution)/shard_map/ppermute | solution.py:797
  16.8 10.7 %copy-start.4 = (bf16[8,128,256]{2,1,0:T(8,128)(2,1)S(1)}, bf16[8,128,256]{2,1,0:T(8,128)(2,1)}, u32[]{:S(2)}) copy-start(bf16[8,128,256]{2,1,0:T(8,128)(2,1)} %constant.12.clone.forward_ref) | copy-start | bytes 1572868
  16.8 10.6 %copy-start.5 = (bf16[8,48,384]{2,1,0:T(8,128)(2,1)S(1)}, bf16[8,48,384]{2,1,0:T(8,128)(2,1)}, u32[]{:S(2)}) copy-start(bf16[8,48,384]{2,1,0:T(8,128)(2,1)} %constant.13.clone.inverse_ref) | copy-start | bytes 884740
  16.8 10.6 %copy-start.7 = (f32[128,128]{1,0:T(8,128)S(1)}, f32[128,128]{1,0:T(8,128)}, u32[]{:S(2)}) copy-start(f32[128,128]{1,0:T(8,128)} %constant.14.clone.mask_ref) | copy-start | bytes 196612
  16.8 10.6 %collective-permute-start.5 = (f32[15,16,128]{2,1,0:T(8,128)S(1)}, f32[15,16,128]{2,1,0:T(8,128)S(1)}, u32[]{:S(2)}, u32[]{:S(2)}) collective-permute-start(f32[15,16,128]{2,1,0:T(8,128)S(1)} %collective-permute-done.3.refs_4_), channel_id=1, source_target_pairs={{0,8},{4,12},{8,0},{12,4},{16,24},{20,28},{24,16},{28,20},{1,9},{5... | collective-permute-start | bytes 368648 | tf_op jit(solution)/shard_map/ppermute | solution.py:797
  16.9 10.5 %collective-permute-start.4 = (f32[15,16,128]{2,1,0:T(8,128)S(1)}, f32[15,16,128]{2,1,0:T(8,128)S(1)}, u32[]{:S(2)}, u32[]{:S(2)}) collective-permute-start(f32[15,16,128]{2,1,0:T(8,128)S(1)} %collective-permute-done.3.refs_4_), channel_id=1, source_target_pairs={{0,4},{4,0},{8,12},{12,8},{16,20},{20,16},{24,28},{28,24},{1,5},{5... | collective-permute-start | bytes 368648 | tf_op jit(solution)/shard_map/ppermute | solution.py:797
  18.7 12.6 %collective-permute-start.10 = (f32[5,16,512]{2,1,0:T(8,128)S(1)}, f32[5,16,512]{2,1,0:T(8,128)S(1)}, u32[]{:S(2)}, u32[]{:S(2)}) collective-permute-start(f32[5,16,512]{2,1,0:T(8,128)S(1)} %get-tuple-element.33), channel_id=1, source_target_pairs={{0,1},{1,0},{2,3},{3,2},{4,5},{5,4},{6,7},{7,6},{8,9},{9,8},{10,11... | collective-permute-start | bytes 491528 | tf_op jit(solution)/shard_map/ppermute | solution.py:816
  21.1 10.1 %collective-permute-start.11 = (f32[5,16,512]{2,1,0:T(8,128)S(1)}, f32[5,16,512]{2,1,0:T(8,128)S(1)}, u32[]{:S(2)}, u32[]{:S(2)}) collective-permute-start(f32[5,16,512]{2,1,0:T(8,128)S(1)} %get-tuple-element.34), channel_id=1, source_target_pairs={{1,2},{2,1},{5,6},{6,5},{9,10},{10,9},{13,14},{14,13},{17,18},{18,... | collective-permute-start | bytes 491528 | tf_op jit(solution)/shard_map/ppermute | solution.py:817
  24.2 7.1 %collective-permute-start.9 = (f32[20,16,128]{2,1,0:T(8,128)S(1)}, f32[20,16,128]{2,1,0:T(8,128)S(1)}, u32[]{:S(2)}, u32[]{:S(2)}) collective-permute-start(f32[20,16,128]{2,1,0:T(8,128)S(1)} %get-tuple-element.32.own_b), channel_id=1, source_target_pairs={{4,8},{8,4},{12,16},{16,12},{20,24},{24,20},{28,0},{0,28},{5,9},{9... | collective-permute-start | bytes 491528 | tf_op jit(solution)/shard_map/ppermute | solution.py:815
  28.4 4.6 %collective-permute-start.7 = (f32[5,16,128]{2,1,0:T(8,128)S(1)}, f32[5,16,128]{2,1,0:T(8,128)S(1)}, u32[]{:S(2)}, u32[]{:S(2)}) collective-permute-start(f32[5,16,128]{2,1,0:T(8,128)S(1)} %get-tuple-element.30), channel_id=1, source_target_pairs={{0,1},{1,0},{2,3},{3,2},{4,5},{5,4},{6,7},{7,6},{8,9},{9,8},{10,11... | collective-permute-start | bytes 122888 | tf_op jit(solution)/shard_map/ppermute | solution.py:821
  28.5 5.3 %collective-permute-start.8 = (f32[5,16,128]{2,1,0:T(8,128)S(1)}, f32[5,16,128]{2,1,0:T(8,128)S(1)}, u32[]{:S(2)}, u32[]{:S(2)}) collective-permute-start(f32[5,16,128]{2,1,0:T(8,128)S(1)} %get-tuple-element.31), channel_id=1, source_target_pairs={{1,2},{2,1},{5,6},{6,5},{9,10},{10,9},{13,14},{14,13},{17,18},{18,... | collective-permute-start | bytes 122888 | tf_op jit(solution)/shard_map/ppermute | solution.py:822

commit v4 on v3

--- a/solution.py
+++ b/solution.py
@@ -306,58 +306,22 @@
                 ref[base + f * tiles + tile, k : k + 1, :] = jnp.where(keep_high, high, low)
 
 
-def beside_kernel(plan, x_ref, packed_ref, again, beside):
-    again[...] = packed_ref[...]
-    beside[pl.ds(0, plan.groups + 1)] = packed_ref[...]
-    even_theta = lax.axis_index("az") % 2 == 0
-    pick_columns(plan, x_ref, even_theta, beside, plan.groups + 1)
-
-
-def edges_kernel(plan, x_ref, after_ref, az_b, ax_a, ax_b):
+def edges_kernel(plan, x_ref, after_ref, az_a, az_b):
     del after_ref
     even_theta = lax.axis_index("az") % 2 == 0
-    even_plane = lax.axis_index("ax") % 2 == 0
+    pick_columns(plan, x_ref, even_theta, az_a, 0)
     pick_columns(plan, x_ref, jnp.logical_not(even_theta), az_b, 0)
 
-    @pl.when(even_plane)
-    def _():
-        ax_a[...] = x_ref[:, plan.planes - 1]
-        ax_b[...] = x_ref[:, 0]
-
-    @pl.when(jnp.logical_not(even_plane))
-    def _():
-        ax_a[...] = x_ref[:, 0]
-        ax_b[...] = x_ref[:, plan.planes - 1]
-
-
-def beside(plan, fields, packed):
+
+def edges(plan, fields, after):
     f32 = jnp.float32
     columns = plan.fields * plan.radial // LANES
     inside = pl.BlockSpec(memory_space=pltpu.VMEM)
     return pl.pallas_call(
-        functools.partial(beside_kernel, plan),
+        functools.partial(edges_kernel, plan),
         in_specs=[inside] * 2,
         out_specs=[inside] * 2,
-        out_shape=[
-            jax.ShapeDtypeStruct(packed.shape, f32),
-            jax.ShapeDtypeStruct((plan.groups + 1 + columns, plan.theta, LANES), f32),
-        ],
-        compiler_params=pltpu.CompilerParams(vmem_limit_bytes=VMEM_LIMIT),
-        name="beside",
-        cost_estimate=pl.CostEstimate(flops=0, bytes_accessed=1000000, transcendentals=0),
-    )(fields, packed)
-
-
-def edges(plan, fields, after):
-    f32 = jnp.float32
-    columns = plan.fields * plan.radial // LANES
-    plane = jax.ShapeDtypeStruct((plan.fields, plan.theta, plan.radial), f32)
-    inside = pl.BlockSpec(memory_space=pltpu.VMEM)
-    return pl.pallas_call(
-        functools.partial(edges_kernel, plan),
-        in_specs=[inside, inside],
-        out_specs=[inside] * 3,
-        out_shape=[jax.ShapeDtypeStruct((columns, plan.theta, LANES), f32), plane, plane],
+        out_shape=[jax.ShapeDtypeStruct((columns, plan.theta, LANES), f32)] * 2,
         compiler_params=pltpu.CompilerParams(vmem_limit_bytes=VMEM_LIMIT),
         name="edges",
         cost_estimate=pl.CostEstimate(flops=0, bytes_accessed=1000000, transcendentals=0),
@@ -481,16 +445,11 @@
     )(coef, fields)
 
 
-def seams_kernel(
-    plan, coef_ref, x_ref, own_a, own_b, az_a, az_b, ax_a, ax_b, part_ref, out_ref, done, outs
-):
+def seams_kernel(plan, coef_ref, own_a, own_b, az_a, az_b, part_ref, out_ref, done, outs):
     del part_ref
     planes = plan.planes
     tiles = plan.radial // LANES
     even_theta = lax.axis_index("az") % 2 == 0
-    even_plane = lax.axis_index("ax") % 2 == 0
-    base = plan.groups + 1
-    nu_dt = viscosity * time_step
     last = plan.theta - 1
 
     def store(k):
@@ -505,14 +464,14 @@
         angular = coef_ref[3:4, here]
         cross = coef_ref[6:7, here]
         number = tiles + tile
-        mine_a = own_a[base + number]
+        mine_a = own_a[number]
         mine_b = own_b[number]
         turn_low = angular * jnp.where(even_theta, mine_b, mine_a)
         turn_high = angular * jnp.where(even_theta, mine_a, mine_b)
         before = []
         after = []
         for f in range(plan.fields):
-            a = az_a[base + f * tiles + tile]
+            a = az_a[f * tiles + tile]
             b = az_b[f * tiles + tile]
             before.append(jnp.where(even_theta, b, a))
             after.append(jnp.where(even_theta, a, b))
@@ -528,42 +487,28 @@
             for k in range(planes):
                 done[k, f, 0:1, there] += low[k : k + 1]
                 done[k, f, last : last + 1, there] += high[k : k + 1]
-            a = ax_a[f, :, here]
-            b = ax_b[f, :, here]
-            axial = (0.5 * time_step) * x_ref[2, 0, :, here]
-            done[0, f, :, there] += (nu_dt + axial) * jnp.where(even_plane, b, a)
-            axial = (0.5 * time_step) * x_ref[2, planes - 1, :, here]
-            done[planes - 1, f, :, there] += (nu_dt - axial) * jnp.where(even_plane, a, b)
-    for k in range(planes):
+    for k in range(1, planes - 1):
         store(k).start()
-    for k in range(planes):
+    for k in range(1, planes - 1):
         store(k).wait()
 
 
-def seams(plan, coef, fields, own, halos, part):
+def seams(plan, coef, fields, own, sides, part):
     inside = pl.BlockSpec(memory_space=pltpu.VMEM)
     return pl.pallas_call(
         functools.partial(seams_kernel, plan),
-        in_specs=[inside] * 9,
+        in_specs=[inside] * 6,
         out_specs=[pl.BlockSpec(memory_space=pl.ANY), inside],
         out_shape=[
             jax.ShapeDtypeStruct(fields.shape, jnp.float32),
             jax.ShapeDtypeStruct(part.shape, jnp.float32),
         ],
-        input_output_aliases={8: 1},
+        input_output_aliases={5: 1},
         scratch_shapes=[pltpu.SemaphoreType.DMA((plan.planes,))],
         compiler_params=pltpu.CompilerParams(vmem_limit_bytes=VMEM_LIMIT),
         name="seams",
         cost_estimate=pl.CostEstimate(flops=1000000, bytes_accessed=4000000, transcendentals=0),
-    )(coef, fields, *own, *halos, part)[0]
-
-
-def halo_scratch(plan):
-    columns = plan.fields * plan.radial // LANES
-    return [
-        pltpu.VMEM((2, columns, plan.planes, LANES), jnp.float32),
-        pltpu.VMEM((2, plan.fields, plan.theta, plan.radial), jnp.float32),
-    ]
+    )(coef, *own, *sides, part)
 
 
 def halves(x, depth=None):
@@ -581,8 +526,7 @@
     )
 
 
-def early_kernel(plan, forward_ref, token_ref, *refs):
-    del token_ref
+def early_kernel(plan, forward_ref, *refs):
     pieces = refs[: len(plan.early)]
     spectra_ref, total_ref = refs[len(plan.early) :]
     table = forward_ref[lax.axis_index("az")]
@@ -595,12 +539,12 @@
     total_ref[...] = total
 
 
-def early_spectra(plan, pieces, token):
+def early_spectra(plan, pieces):
     inside = pl.BlockSpec(memory_space=pltpu.VMEM)
     f32 = jnp.float32
     return pl.pallas_call(
         functools.partial(early_kernel, plan),
-        in_specs=[inside] * (2 + len(pieces)),
+        in_specs=[inside] * (1 + len(pieces)),
         out_specs=[inside] * 2,
         out_shape=[
             jax.ShapeDtypeStruct((plan.groups // 2, 2 * plan.modes, 2 * LANES), f32),
@@ -609,10 +553,11 @@
         compiler_params=pltpu.CompilerParams(vmem_limit_bytes=VMEM_LIMIT),
         name="early",
         cost_estimate=pl.CostEstimate(flops=200000000, bytes_accessed=1500000, transcendentals=0),
-    )(jnp.asarray(plan.forward(plan.early)), token, *pieces)
-
-
-def filter_kernel(plan, forward_ref, inverse_ref, mask_ref, early_ref, early_total, *refs):
+    )(jnp.asarray(plan.forward(plan.early)), *pieces)
+
+
+def filter_kernel(plan, token_ref, x_ref, forward_ref, inverse_ref, mask_ref, early_ref, early_total, *refs):
+    del token_ref
     count = len(plan.late)
     pieces = refs[:count]
     own_ref, across_ref, edge_ref, sums_ref, message_a, message_b = refs[count:]
@@ -644,12 +589,15 @@
         value = moved(total, plan.full - f * plan.rest)
         sums_ref[f] = jnp.where((lane >= plan.full) & (lane < NEAR), value, 0.0)
 
+    row = lax.broadcasted_iota(jnp.int32, (theta, LANES), 0)
+    sign = (1 - 2 * (row & 1)).astype(jnp.float32)
+
     def message(ref, k):
         for f in range(plan.fields):
             number, first = plan.place(f, k)
-            own = own_ref[number]
-            value = jnp.where(lane < plan.full, moved(own, -first), sums_ref[f, k : k + 1])
-            ref[f] = value
+            raw = x_ref[f, k, :, :LANES] - sign * sums_ref[f, k : k + 1]
+            ref[f, :, :LANES] = jnp.where(lane < plan.full, moved(own_ref[number], -first), raw)
+            ref[f, :, LANES:] = x_ref[f, k, :, LANES:]
 
     def both_messages(ref_low, ref_high):
         message(ref_low, 0)
@@ -659,14 +607,14 @@
     pl.when(odd_plane == 0)(lambda: both_messages(message_b, message_a))
 
 
-def filtered(plan, pieces, early):
+def filtered(plan, token, fields, pieces, early):
     inside = pl.BlockSpec(memory_space=pltpu.VMEM)
     f32 = jnp.float32
     cube = jax.ShapeDtypeStruct((plan.groups, plan.theta, LANES), f32)
-    plane = jax.ShapeDtypeStruct((plan.fields, plan.theta, LANES), f32)
+    plane = jax.ShapeDtypeStruct((plan.fields, plan.theta, plan.radial), f32)
     return pl.pallas_call(
         functools.partial(filter_kernel, plan),
-        in_specs=[inside] * (5 + len(pieces)),
+        in_specs=[inside] * (7 + len(pieces)),
         out_specs=[inside] * 6,
         out_shape=[
             cube,
@@ -680,6 +628,8 @@
         name="filter",
         cost_estimate=pl.CostEstimate(flops=200000000, bytes_accessed=1500000, transcendentals=0),
     )(
+        token,
+        fields,
         jnp.asarray(plan.forward(plan.late)),
         jnp.asarray(plan.inverse()),
         jnp.asarray(plan.mask()),
@@ -689,17 +639,11 @@
 
 
 def inner_kernel(
-    plan, coef_ref, own_ref, across_ref, edge_ref, sums_ref, message_a, message_b,
-    x_ref, az_a, az_b, ax_a, ax_b, other_ref, out_ref, side, ends, state, done, outs
+    plan, coef_ref, own_ref, across_ref, edge_ref, sums_ref, x_ref, az_a, az_b, done, state
 ):
-    del other_ref
     planes = plan.planes
     theta = plan.theta
     tiles = plan.radial // LANES
-    store = [
-        pltpu.make_async_copy(done.at[k], out_ref.at[:, k, :, pl.ds(0, LANES)], outs.at[k])
-        for k in range(planes)
-    ]
     shape = (theta, LANES)
     lane = lax.broadcasted_iota(jnp.int32, shape, 1)
     row = lax.broadcasted_iota(jnp.int32, shape, 0)
@@ -708,73 +652,118 @@
     first = slice(0, LANES)
     coef = [coef_ref[i : i + 1, first] for i in range(7)]
     flips = (-1.0, -1.0, 1.0, 1.0, 1.0)
-    choose_halos(plan, range(1), az_a, az_b, ax_a, ax_b, side, ends)
+    even_theta = lax.axis_index("az") % 2 == 0
 
     for k in range(planes):
         for f in range(plan.fields):
             number, start = plan.place(f, k)
-            state[k + 1, f] = jnp.where(
+            state[k, f] = jnp.where(
                 lane < plan.full,
                 moved(own_ref[number], -start),
                 x_ref[f, k, :, first] - sign * sums_ref[f, k : k + 1],
             )
-    even_plane = lax.axis_index("ax") % 2 == 0
+
+    befores = []
+    afters = []
     for f in range(plan.fields):
-        a = message_a[f]
-        b = message_b[f]
-        for end, slot, message in ((0, 0, jnp.where(even_plane, b, a)), (1, planes + 1, jnp.where(even_plane, a, b))):
-            raw = ends[end, f, :, first]
-            state[slot, f] = jnp.where(lane < plan.full, message, raw - sign * message)
-
+        a = az_a[f * tiles]
+        b = az_b[f * tiles]
+        befores.append(jnp.where(even_theta, b, a) + sums_ref[f])
+        afters.append(jnp.where(even_theta, a, b) - sums_ref[f])
+
+    zero = jnp.zeros(shape, jnp.float32)
     for k in range(planes):
         q, jp, jm, tp, tm, kp, km = ([] for _ in range(7))
         for f in range(plan.fields):
             number, start = plan.place(f, k)
-            x = state[k + 1, f]
+            x = state[k, f]
             q.append(x)
             high_part = pltpu.roll(x_ref[f, k, :, LANES : 2 * LANES], LANES - 1, 1)
             jp.append(jnp.where(lane == LANES - 1, high_part, pltpu.roll(x, LANES - 1, 1)))
             opposite = flips[f] * moved(across_ref[number], -start)
             jm.append(jnp.where(lane == 0, opposite, pltpu.roll(x, 1, 1)))
-            total = sums_ref[f, k : k + 1]
             sides = moved(edge_ref[number], -start)
-            column = f * tiles
-            before = jnp.where(lane1 < plan.full, sides[0:1], side[0, column, k : k + 1] + total)
-            after = jnp.where(lane1 < plan.full, sides[1:2], side[1, column, k : k + 1] - total)
+            before = jnp.where(lane1 < plan.full, sides[0:1], befores[f][k : k + 1])
+            after = jnp.where(lane1 < plan.full, sides[1:2], afters[f][k : k + 1])
             up, down = turned(x, row, before, after)
             tp.append(up)
             tm.append(down)
-            kp.append(state[k + 2, f])
-            km.append(state[k, f])
+            kp.append(state[k + 1, f] if k + 1 < planes else zero)
+            km.append(state[k - 1, f] if k > 0 else zero)
         result = advance(coef, q, jp, jm, tp, tm, kp, km)
         for f in range(plan.fields):
             done[k, f] = result[f]
-        store[k].start()
-    for copy in store:
+
+
+def inner(plan, coef, parts, fields, sides):
+    inside = pl.BlockSpec(memory_space=pltpu.VMEM)
+    f32 = jnp.float32
+    return pl.pallas_call(
+        functools.partial(inner_kernel, plan),
+        in_specs=[inside] * 8,
+        out_specs=inside,
+        out_shape=jax.ShapeDtypeStruct((plan.planes, plan.fields, plan.theta, LANES), f32),
+        scratch_shapes=[pltpu.VMEM((plan.planes, plan.fields, plan.theta, LANES), f32)],
+        compiler_params=pltpu.CompilerParams(vmem_limit_bytes=VMEM_LIMIT),
+        name="inner",
+        cost_estimate=pl.CostEstimate(flops=6000000, bytes_accessed=2500000, transcendentals=0),
+    )(coef, *parts, fields, *sides)
+
+
+def finish_kernel(plan, near_ref, part_ref, own_a, own_b, ax_a, ax_b, other_ref, out_ref, ends, sems):
+    del other_ref
+    planes = plan.planes
+    copies = [
+        pltpu.make_async_copy(near_ref.at[k], out_ref.at[:, k, :, pl.ds(0, LANES)], sems.at[k])
+        for k in range(1, planes - 1)
+    ]
+    for copy in copies:
+        copy.start()
+    even_plane = lax.axis_index("ax") % 2 == 0
+    nu_dt = viscosity * time_step
+    half = 0.5 * time_step
+    tiles = plan.radial // LANES
+    for end, k in ((0, 0), (1, planes - 1)):
+        for tile in range(tiles):
+            here = slice(tile * LANES, (tile + 1) * LANES)
+            sent_a = own_a[2, :, here]
+            sent_b = own_b[2, :, here]
+            if end == 0:
+                factor = nu_dt + half * jnp.where(even_plane, sent_b, sent_a)
+            else:
+                factor = nu_dt - half * jnp.where(even_plane, sent_a, sent_b)
+            for f in range(plan.fields):
+                a = ax_a[f, :, here]
+                b = ax_b[f, :, here]
+                value = jnp.where(even_plane, b, a) if end == 0 else jnp.where(even_plane, a, b)
+                if tile == 0:
+                    start = near_ref[k, f]
+                else:
+                    start = part_ref[k, f, :, (tile - 1) * LANES : tile * LANES]
+                ends[end, f, :, here] = start + factor * value
+        copies.append(pltpu.make_async_copy(ends.at[end], out_ref.at[:, k], sems.at[k]))
+        copies[-1].start()
+    for copy in copies:
         copy.wait()
 
 
-def inner(plan, coef, parts, messages, fields, halos, partial):
+def finish(plan, near, part, sent, messages, partial):
     anywhere = pl.BlockSpec(memory_space=pl.ANY)
     inside = pl.BlockSpec(memory_space=pltpu.VMEM)
-    f32 = jnp.float32
-    operands = (coef, *parts, *messages, fields, *halos, partial)
     return pl.pallas_call(
-        functools.partial(inner_kernel, plan),
-        in_specs=[inside] * 12 + [anywhere],
+        functools.partial(finish_kernel, plan),
+        in_specs=[inside] * 6 + [anywhere],
         out_specs=anywhere,
-        out_shape=jax.ShapeDtypeStruct(fields.shape, f32),
-        input_output_aliases={len(operands) - 1: 0},
-        scratch_shapes=halo_scratch(plan)
-        + [
-            pltpu.VMEM((plan.planes + 2, plan.fields, plan.theta, LANES), f32),
-            pltpu.VMEM((plan.planes, plan.fields, plan.theta, LANES), f32),
+        out_shape=jax.ShapeDtypeStruct(partial.shape, jnp.float32),
+        input_output_aliases={6: 0},
+        scratch_shapes=[
+            pltpu.VMEM((2, plan.fields, plan.theta, plan.radial), jnp.float32),
             pltpu.SemaphoreType.DMA((plan.planes,)),
         ],
         compiler_params=pltpu.CompilerParams(vmem_limit_bytes=VMEM_LIMIT),
-        name="inner",
-        cost_estimate=pl.CostEstimate(flops=6000000, bytes_accessed=2500000, transcendentals=0),
-    )(*operands)
+        name="finish",
+        cost_estimate=pl.CostEstimate(flops=100000, bytes_accessed=1500000, transcendentals=0),
+    )(near, part, *sent, *messages, partial)
 
 
 def pairs(count, start, periodic):
@@ -798,31 +787,29 @@
 
     packed = pack(plan, fields)
     half = sectors // 2
-    far = send(packed, half)
-    again, wide = beside(plan, fields, packed)
     pieces = [None] * sectors
     pieces[0] = packed
+    far = send(packed, half)
     pieces[half] = far
     for p in range(half - 1, 0, -1):
-        pieces[p] = send(wide if p == 1 else again, p)
+        pieces[p] = send(packed, p)
     for p in range(half - 1, 0, -1):
         pieces[half + p] = send(far, p)
+    early = early_spectra(plan, pieces[: half + 1])
+    column_a, column_b = edges(plan, fields, early[1])
+    sides = (
+        lax.ppermute(column_a, "az", pairs(sectors, 0, True)),
+        lax.ppermute(column_b, "az", pairs(sectors, 1, True)),
+    )
     part, token = outer(plan, coef, fields)
-    early = early_spectra(plan, pieces[: half + 1], token)
-    az_b, ax_a, ax_b = edges(plan, fields, early[1])
-    halos = (
-        pieces[1],
-        lax.ppermute(az_b, "az", pairs(sectors, 1, True)),
-        lax.ppermute(ax_a, "ax", pairs(slabs, 0, False)),
-        lax.ppermute(ax_b, "ax", pairs(slabs, 1, False)),
-    )
-    *parts, message_a, message_b = filtered(plan, pieces[half + 1 :], early)
+    *parts, message_a, message_b = filtered(plan, token, fields, pieces[half + 1 :], early)
     messages = (
         lax.ppermute(message_a, "ax", pairs(slabs, 0, False)),
         lax.ppermute(message_b, "ax", pairs(slabs, 1, False)),
     )
-    partial = seams(plan, coef, fields, (wide, az_b), halos, part)
-    return inner(plan, coef, parts, messages, fields, halos, partial)
+    partial, part = seams(plan, coef, fields, (column_a, column_b), sides, part)
+    near = inner(plan, coef, parts, fields, sides)
+    return finish(plan, near, part, (message_a, message_b), messages, partial)
 
 
 def on_device(fields):

time: 36.5 us -> 32.6 us (0.89)
  the two profiles are of different devices: /device:TPU:1 before, /device:TPU:0 now
where the time goes in v4:
time: 32.6 us; the launch traced here: 32.4 us
  starting transfers between devices  19.8 us (61%)
  Pallas kernels  9.57 us (29%)
  waiting for transfers between devices  2.88 us (9%)
    ppermute x7, starting transfers between devices, send(): return lax.ppermute(x, 'az', [(i, i ^ distance) for i in range(sectors)])  11.1 us
    ppermute x1, starting transfers between devices, fast_on_device(): lax.ppermute(column_b, 'az', pairs(sectors, 1, True))  3.46 us
    ppermute x1, starting transfers between devices, fast_on_device(): lax.ppermute(message_a, 'ax', pairs(slabs, 0, False))  2.94 us
    ppermute x7, waiting for transfers between devices, send(): return lax.ppermute(x, 'az', [(i, i ^ distance) for i in range(sectors)])  2.8 us
    pallas_call x1, Pallas kernels, outer(): pl.pallas_call(functools.partial(outer_kernel, plan), in_specs=[inside] *...  2.25 us
    pallas_call x1, Pallas kernels, pack(): pl.pallas_call(functools.partial(pack_kernel, plan), in_specs=[pl.BlockSp...  2.18 us
    ppermute x1, starting transfers between devices, fast_on_device(): lax.ppermute(column_a, 'az', pairs(sectors, 0, True))  1.6 us
    pallas_call x1, Pallas kernels, seams(): pl.pallas_call(functools.partial(seams_kernel, plan), in_specs=[inside] *...  1.54 us
  transfers between devices with their start and end apart: 11, of which 2 were waited for; matrix products, arithmetic and copies ran while one was open for 0% of the time, Pallas kernels for 20%

profile of v4, /device:TPU:0, one launch (start us, length us, event | category | flops | bytes accessed | tf_op | source)
XLA Modules:
  0.0 32.4 jit_solution(9171443055089028184)
XLA Ops:
  0.0 0.0 copy-start.5
  0.0 0.0 copy-start
  0.0 0.0 copy-start.1
  0.0 2.2 %pack.1.refs_0_ = f32[15,16,128]{2,1,0:T(8,128)} custom-call(f32[5,16,16,512]{3,2,1,0:T(8,128)} %x_ref.9), custom_call_target="tpu_custom_call" | custom-call | flops 1000000 | bytes 800000 | tf_op jit(solution)/shard_map/pack/pallas_call | solution.py:283
  2.2 0.0 copy-start.3
  2.2 0.0 copy-start.2
  2.2 0.0 copy-start.4
  2.2 0.0 copy-start.6
  2.2 4.1 %collective-permute-start.3 = (f32[15,16,128]{2,1,0:T(8,128)}, f32[15,16,128]{2,1,0:T(8,128)S(1)}, u32[]{:S(2)}, u32[]{:S(2)}) collective-permute-start(f32[15,16,128]{2,1,0:T(8,128)} %pack.1.refs_0_), channel_id=1, source_target_pairs={{0,16},{4,20},{8,24},{12,28},{16,0},{20,4},{24,8},{28,12},{1,17},{... | collective-permute-start | bytes 368648 | tf_op jit(solution)/shard_map/ppermute | solution.py:786
  6.3 1.5 %collective-permute-start = (f32[15,16,128]{2,1,0:T(8,128)}, f32[15,16,128]{2,1,0:T(8,128)S(1)}, u32[]{:S(2)}, u32[]{:S(2)}) collective-permute-start(f32[15,16,128]{2,1,0:T(8,128)} %pack.1.refs_0_), channel_id=1, source_target_pairs={{0,4},{4,0},{8,12},{12,8},{16,20},{20,16},{24,28},{28,24},{1,5},{5... | collective-permute-start | bytes 368648 | tf_op jit(solution)/shard_map/ppermute | solution.py:786
  7.8 1.6 %collective-permute-start.1 = (f32[15,16,128]{2,1,0:T(8,128)}, f32[15,16,128]{2,1,0:T(8,128)S(1)}, u32[]{:S(2)}, u32[]{:S(2)}) collective-permute-start(f32[15,16,128]{2,1,0:T(8,128)} %pack.1.refs_0_), channel_id=1, source_target_pairs={{0,8},{4,12},{8,0},{12,4},{16,24},{20,28},{24,16},{28,20},{1,9},{5... | collective-permute-start | bytes 368648 | tf_op jit(solution)/shard_map/ppermute | solution.py:786
  9.4 0.4 %collective-permute-start.2 = (f32[15,16,128]{2,1,0:T(8,128)}, f32[15,16,128]{2,1,0:T(8,128)S(1)}, u32[]{:S(2)}, u32[]{:S(2)}) collective-permute-start(f32[15,16,128]{2,1,0:T(8,128)} %pack.1.refs_0_), channel_id=1, source_target_pairs={{0,12},{4,8},{8,4},{12,0},{16,28},{20,24},{24,20},{28,16},{1,13},{... | collective-permute-start | bytes 368648 | tf_op jit(solution)/shard_map/ppermute | solution.py:786
  9.8 2.8 %collective-permute-done.3.refs_4_ = f32[15,16,128]{2,1,0:T(8,128)S(1)} collective-permute-done((f32[15,16,128]{2,1,0:T(8,128)}, f32[15,16,128]{2,1,0:T(8,128)S(1)}, u32[]{:S(2)}, u32[]{:S(2)}) %collective-permute-start.3) | collective-permute-done | bytes 122912 | tf_op jit(solution)/shard_map/ppermute | solution.py:786
  12.6 1.5 %collective-permute-start.4 = (f32[15,16,128]{2,1,0:T(8,128)S(1)}, f32[15,16,128]{2,1,0:T(8,128)S(1)}, u32[]{:S(2)}, u32[]{:S(2)}) collective-permute-start(f32[15,16,128]{2,1,0:T(8,128)S(1)} %collective-permute-done.3.refs_4_), channel_id=1, source_target_pairs={{0,4},{4,0},{8,12},{12,8},{16,20},{20,16},{24,28},{28,24},{1,5},{5... | collective-permute-start | bytes 368648 | tf_op jit(solution)/shard_map/ppermute | solution.py:786
  14.2 0.7 %collective-permute-start.5 = (f32[15,16,128]{2,1,0:T(8,128)S(1)}, f32[15,16,128]{2,1,0:T(8,128)S(1)}, u32[]{:S(2)}, u32[]{:S(2)}) collective-permute-start(f32[15,16,128]{2,1,0:T(8,128)S(1)} %collective-permute-done.3.refs_4_), channel_id=1, source_target_pairs={{0,8},{4,12},{8,0},{12,4},{16,24},{20,28},{24,16},{28,20},{1,9},{5... | collective-permute-start | bytes 368648 | tf_op jit(solution)/shard_map/ppermute | solution.py:786
  14.9 0.0 collective-permute-done.refs_1_
  14.9 1.2 %collective-permute-start.6 = (f32[15,16,128]{2,1,0:T(8,128)S(1)}, f32[15,16,128]{2,1,0:T(8,128)S(1)}, u32[]{:S(2)}, u32[]{:S(2)}) collective-permute-start(f32[15,16,128]{2,1,0:T(8,128)S(1)} %collective-permute-done.3.refs_4_), channel_id=1, source_target_pairs={{0,12},{4,8},{8,4},{12,0},{16,28},{20,24},{24,20},{28,16},{1,13},{... | collective-permute-start | bytes 368648 | tf_op jit(solution)/shard_map/ppermute | solution.py:786
  16.1 0.0 copy-done.5
  16.1 0.0 copy-done
  16.1 2.3 %outer.1 = (f32[16,5,16,384]{3,2,1,0:T(8,128)S(1)}, f32[8,128]{1,0:T(8,128)S(1)}) custom-call(f32[8,512]{1,0:T(8,128)S(1)} %copy-done.5, f32[5,16,16,512]{3,2,1,0:T(8,128)S(1)} %copy-done), custom_call_target="tpu_custom_call" | custom-call | flops 16000000 | bytes 5000000 | tf_op jit(solution)/shard_map/outer/pallas_call | solution.py:434
  18.4 0.0 collective-permute-done.1.refs_2_
  18.4 0.0 collective-permute-done.2.refs_3_
  18.4 0.0 copy-done.1
  18.4 0.0 copy-done.3
  18.4 0.3 early.1
  18.7 0.3 %edges.1 = (f32[20,16,128]{2,1,0:T(8,128)S(1)}, f32[20,16,128]{2,1,0:T(8,128)S(1)}) custom-call(f32[5,16,16,512]{3,2,1,0:T(8,128)S(1)} %copy-done, f32[16,128]{1,0:T(8,128)S(1)} %get-tuple-element.21.early_total.after_ref), custom_call_target="tpu_custom_call" | custom-call | bytes 1000000 | tf_op jit(solution)/shard_map/edges/pallas_call | solution.py:320
  19.1 1.6 %collective-permute-start.7 = (f32[20,16,128]{2,1,0:T(8,128)S(1)}, f32[20,16,128]{2,1,0:T(8,128)S(1)}, u32[]{:S(2)}, u32[]{:S(2)}) collective-permute-start(f32[20,16,128]{2,1,0:T(8,128)S(1)} %get-tuple-element.26.own_a), channel_id=1, source_target_pairs={{0,4},{4,0},{8,12},{12,8},{16,20},{20,16},{24,28},{28,24},{1,5},{5... | collective-permute-start | bytes 491528 | tf_op jit(solution)/shard_map/ppermute | solution.py:801
  20.7 3.5 %collective-permute-start.8 = (f32[20,16,128]{2,1,0:T(8,128)S(1)}, f32[20,16,128]{2,1,0:T(8,128)S(1)}, u32[]{:S(2)}, u32[]{:S(2)}) collective-permute-start(f32[20,16,128]{2,1,0:T(8,128)S(1)} %get-tuple-element.27.own_b), channel_id=1, source_target_pairs={{4,8},{8,4},{12,16},{16,12},{20,24},{24,20},{28,0},{0,28},{5,9},{9... | collective-permute-start | bytes 491528 | tf_op jit(solution)/shard_map/ppermute | solution.py:802
  24.1 0.0 collective-permute-done.4.refs_0_
  24.1 0.0 collective-permute-done.5.refs_1_
  24.1 0.0 collective-permute-done.6.refs_2_
  24.2 0.0 copy-done.2
  24.2 0.0 copy-done.4
  24.2 0.0 copy-done.6
  24.2 0.9 %filter.1 = (f32[14,16,128]{2,1,0:T(8,128)S(1)}, f32[14,16,128]{2,1,0:T(8,128)S(1)}, f32[14,8,128]{2,1,0:T(8,128)S(1)}, f32[5,16,128]{2,1,0:T(8,128)S(1)}, f32[5...) custom-call(f32[8,128]{1,0:T(8,128)S(1)} %get-tuple-element.19.token_ref, f32[5,16,16,512]{3,2,1,0:T(8,128)S(1)} %copy-done, ...), custom_call_target="tpu_custom_call" | custom-call | flops 200000000 | bytes 1500000 | tf_op jit(solution)/shard_map/filter/pallas_call | solution.py:615
  25.1 0.7 %collective-permute-start.10 = (f32[5,16,512]{2,1,0:T(8,128)S(1)}, f32[5,16,512]{2,1,0:T(8,128)S(1)}, u32[]{:S(2)}, u32[]{:S(2)}) collective-permute-start(f32[5,16,512]{2,1,0:T(8,128)S(1)} %get-tuple-element.31.own_b), channel_id=1, source_target_pairs={{1,2},{2,1},{5,6},{6,5},{9,10},{10,9},{13,14},{14,13},{17,18},{18,... | collective-permute-start | bytes 491528 | tf_op jit(solution)/shard_map/ppermute | solution.py:808
  25.8 2.9 %collective-permute-start.9 = (f32[5,16,512]{2,1,0:T(8,128)S(1)}, f32[5,16,512]{2,1,0:T(8,128)S(1)}, u32[]{:S(2)}, u32[]{:S(2)}) collective-permute-start(f32[5,16,512]{2,1,0:T(8,128)S(1)} %get-tuple-element.30.own_a), channel_id=1, source_target_pairs={{0,1},{1,0},{2,3},{3,2},{4,5},{5,4},{6,7},{7,6},{8,9},{9,8},{10,11... | collective-permute-start | bytes 491528 | tf_op jit(solution)/shard_map/ppermute | solution.py:807
  28.7 0.0 collective-permute-done.7.az_a
  28.7 0.1 collective-permute-done.8.az_b
  28.8 1.5 %seams.1 = (f32[5,16,16,512]{3,2,1,0:T(8,128)}, f32[16,5,16,384]{3,2,1,0:T(8,128)S(1)}) custom-call(f32[8,512]{1,0:T(8,128)S(1)} %copy-done.5, f32[20,16,128]{2,1,0:T(8,128)S(1)} %get-tuple-element.26.own_a, f32[20,16,128]{2,1,0:T(8,128)S(1)} %get-tuple-element.27.own_b, ...), custom_call_target="tpu_custom_call", output_to_operand_aliasing={{1}: (5, {})} | custom-call | flops 1000000 | bytes 4000000 | tf_op jit(solution)/shard_map/seams/pallas_call | solution.py:498
  30.3 1.0 %inner.1.near_ref = f32[16,5,16,128]{3,2,1,0:T(8,128)S(1)} custom-call(f32[8,512]{1,0:T(8,128)S(1)} %copy-done.5, f32[14,16,128]{2,1,0:T(8,128)S(1)} %get-tuple-element.22.own_ref, f32[14,16,128]{2,1,0:T(8,128)S(1)} %get-tuple-element.23.across_ref, f32[14,8,128]{2,1,0:T(8,128)S(1)} %get-tuple-element.24.edge_ref, ...), custom_call_target="tpu_custom_call" | custom-call | flops 6000000 | bytes 2500000 | tf_op jit(solution)/shard_map/inner/pallas_call | solution.py:701
  31.3 0.0 collective-permute-done.10.ax_b
  31.3 0.0 collective-permute-done.9.ax_a
  31.4 1.1 %finish.1 = f32[5,16,16,512]{3,2,1,0:T(8,128)} custom-call(f32[16,5,16,128]{3,2,1,0:T(8,128)S(1)} %inner.1.near_ref, f32[16,5,16,384]{3,2,1,0:T(8,128)S(1)} %get-tuple-element.29.part_ref, f32[5,16,512]{2,1,0:T(8,128)S(1)} %get-tuple-element.30.own_a, f32[5,16,512]{2,1,0:T(8,128)S(1)} %get-tuple-element.31.own_b, ...), custom_call_target="tpu_custom_call", output_to_operand_aliasing={{}: (6, {})} | custom-call | flops 100000 | bytes 1500000 | tf_op jit(solution)/shard_map/finish/pallas_call | solution.py:753
Async XLA Ops:
  0.0 16.1 %copy-start.5 = (f32[8,512]{1,0:T(8,128)S(1)}, f32[8,512]{1,0:T(8,128)}, u32[]{:S(2)}) copy-start(f32[8,512]{1,0:T(8,128)} %constant.10.clone.coef_ref) | copy-start | bytes 49156
  0.0 16.1 %copy-start = (f32[5,16,16,512]{3,2,1,0:T(8,128)S(1)}, f32[5,16,16,512]{3,2,1,0:T(8,128)}, u32[]{:S(2)}) copy-start(f32[5,16,16,512]{3,2,1,0:T(8,128)} %x_ref.9) | copy-start | bytes 7864324
  0.0 18.4 %copy-start.1 = (bf16[8,128,256]{2,1,0:T(8,128)(2,1)S(1)}, bf16[8,128,256]{2,1,0:T(8,128)(2,1)}, u32[]{:S(2)}) copy-start(bf16[8,128,256]{2,1,0:T(8,128)(2,1)} %constant.11.clone.forward_ref) | copy-start | bytes 1572868
  2.2 16.2 %copy-start.3 = (f32[15,16,128]{2,1,0:T(8,128)S(1)}, f32[15,16,128]{2,1,0:T(8,128)}, u32[]{:S(2)}) copy-start(f32[15,16,128]{2,1,0:T(8,128)} %pack.1.refs_0_) | copy-start | bytes 368644
  2.2 21.9 %copy-start.2 = (bf16[8,128,256]{2,1,0:T(8,128)(2,1)S(1)}, bf16[8,128,256]{2,1,0:T(8,128)(2,1)}, u32[]{:S(2)}) copy-start(bf16[8,128,256]{2,1,0:T(8,128)(2,1)} %constant.12.clone.forward_ref) | copy-start | bytes 1572868
  2.2 21.9 %copy-start.4 = (bf16[8,48,384]{2,1,0:T(8,128)(2,1)S(1)}, bf16[8,48,384]{2,1,0:T(8,128)(2,1)}, u32[]{:S(2)}) copy-start(bf16[8,48,384]{2,1,0:T(8,128)(2,1)} %constant.13.clone.inverse_ref) | copy-start | bytes 884740
  2.2 21.9 %copy-start.6 = (f32[128,128]{1,0:T(8,128)S(1)}, f32[128,128]{1,0:T(8,128)}, u32[]{:S(2)}) copy-start(f32[128,128]{1,0:T(8,128)} %constant.14.clone.mask_ref) | copy-start | bytes 196612
  2.2 10.4 %collective-permute-start.3 = (f32[15,16,128]{2,1,0:T(8,128)}, f32[15,16,128]{2,1,0:T(8,128)S(1)}, u32[]{:S(2)}, u32[]{:S(2)}) collective-permute-start(f32[15,16,128]{2,1,0:T(8,128)} %pack.1.refs_0_), channel_id=1, source_target_pairs={{0,16},{4,20},{8,24},{12,28},{16,0},{20,4},{24,8},{28,12},{1,17},{... | collective-permute-start | bytes 368648 | tf_op jit(solution)/shard_map/ppermute | solution.py:786
  6.3 8.5 %collective-permute-start = (f32[15,16,128]{2,1,0:T(8,128)}, f32[15,16,128]{2,1,0:T(8,128)S(1)}, u32[]{:S(2)}, u32[]{:S(2)}) collective-permute-start(f32[15,16,128]{2,1,0:T(8,128)} %pack.1.refs_0_), channel_id=1, source_target_pairs={{0,4},{4,0},{8,12},{12,8},{16,20},{20,16},{24,28},{28,24},{1,5},{5... | collective-permute-start | bytes 368648 | tf_op jit(solution)/shard_map/ppermute | solution.py:786
  7.8 10.5 %collective-permute-start.1 = (f32[15,16,128]{2,1,0:T(8,128)}, f32[15,16,128]{2,1,0:T(8,128)S(1)}, u32[]{:S(2)}, u32[]{:S(2)}) collective-permute-start(f32[15,16,128]{2,1,0:T(8,128)} %pack.1.refs_0_), channel_id=1, source_target_pairs={{0,8},{4,12},{8,0},{12,4},{16,24},{20,28},{24,16},{28,20},{1,9},{5... | collective-permute-start | bytes 368648 | tf_op jit(solution)/shard_map/ppermute | solution.py:786
  9.4 9.0 %collective-permute-start.2 = (f32[15,16,128]{2,1,0:T(8,128)}, f32[15,16,128]{2,1,0:T(8,128)S(1)}, u32[]{:S(2)}, u32[]{:S(2)}) collective-permute-start(f32[15,16,128]{2,1,0:T(8,128)} %pack.1.refs_0_), channel_id=1, source_target_pairs={{0,12},{4,8},{8,4},{12,0},{16,28},{20,24},{24,20},{28,16},{1,13},{... | collective-permute-start | bytes 368648 | tf_op jit(solution)/shard_map/ppermute | solution.py:786
  12.6 11.5 %collective-permute-start.4 = (f32[15,16,128]{2,1,0:T(8,128)S(1)}, f32[15,16,128]{2,1,0:T(8,128)S(1)}, u32[]{:S(2)}, u32[]{:S(2)}) collective-permute-start(f32[15,16,128]{2,1,0:T(8,128)S(1)} %collective-permute-done.3.refs_4_), channel_id=1, source_target_pairs={{0,4},{4,0},{8,12},{12,8},{16,20},{20,16},{24,28},{28,24},{1,5},{5... | collective-permute-start | bytes 368648 | tf_op jit(solution)/shard_map/ppermute | solution.py:786
  14.2 10.0 %collective-permute-start.5 = (f32[15,16,128]{2,1,0:T(8,128)S(1)}, f32[15,16,128]{2,1,0:T(8,128)S(1)}, u32[]{:S(2)}, u32[]{:S(2)}) collective-permute-start(f32[15,16,128]{2,1,0:T(8,128)S(1)} %collective-permute-done.3.refs_4_), channel_id=1, source_target_pairs={{0,8},{4,12},{8,0},{12,4},{16,24},{20,28},{24,16},{28,20},{1,9},{5... | collective-permute-start | bytes 368648 | tf_op jit(solution)/shard_map/ppermute | solution.py:786
  14.9 9.3 %collective-permute-start.6 = (f32[15,16,128]{2,1,0:T(8,128)S(1)}, f32[15,16,128]{2,1,0:T(8,128)S(1)}, u32[]{:S(2)}, u32[]{:S(2)}) collective-permute-start(f32[15,16,128]{2,1,0:T(8,128)S(1)} %collective-permute-done.3.refs_4_), channel_id=1, source_target_pairs={{0,12},{4,8},{8,4},{12,0},{16,28},{20,24},{24,20},{28,16},{1,13},{... | collective-permute-start | bytes 368648 | tf_op jit(solution)/shard_map/ppermute | solution.py:786
  19.1 9.6 %collective-permute-start.7 = (f32[20,16,128]{2,1,0:T(8,128)S(1)}, f32[20,16,128]{2,1,0:T(8,128)S(1)}, u32[]{:S(2)}, u32[]{:S(2)}) collective-permute-start(f32[20,16,128]{2,1,0:T(8,128)S(1)} %get-tuple-element.26.own_a), channel_id=1, source_target_pairs={{0,4},{4,0},{8,12},{12,8},{16,20},{20,16},{24,28},{28,24},{1,5},{5... | collective-permute-start | bytes 491528 | tf_op jit(solution)/shard_map/ppermute | solution.py:801
  20.7 8.1 %collective-permute-start.8 = (f32[20,16,128]{2,1,0:T(8,128)S(1)}, f32[20,16,128]{2,1,0:T(8,128)S(1)}, u32[]{:S(2)}, u32[]{:S(2)}) collective-permute-start(f32[20,16,128]{2,1,0:T(8,128)S(1)} %get-tuple-element.27.own_b), channel_id=1, source_target_pairs={{4,8},{8,4},{12,16},{16,12},{20,24},{24,20},{28,0},{0,28},{5,9},{9... | collective-permute-start | bytes 491528 | tf_op jit(solution)/shard_map/ppermute | solution.py:802
  25.1 6.2 %collective-permute-start.10 = (f32[5,16,512]{2,1,0:T(8,128)S(1)}, f32[5,16,512]{2,1,0:T(8,128)S(1)}, u32[]{:S(2)}, u32[]{:S(2)}) collective-permute-start(f32[5,16,512]{2,1,0:T(8,128)S(1)} %get-tuple-element.31.own_b), channel_id=1, source_target_pairs={{1,2},{2,1},{5,6},{6,5},{9,10},{10,9},{13,14},{14,13},{17,18},{18,... | collective-permute-start | bytes 491528 | tf_op jit(solution)/shard_map/ppermute | solution.py:808
  25.8 5.6 %collective-permute-start.9 = (f32[5,16,512]{2,1,0:T(8,128)S(1)}, f32[5,16,512]{2,1,0:T(8,128)S(1)}, u32[]{:S(2)}, u32[]{:S(2)}) collective-permute-start(f32[5,16,512]{2,1,0:T(8,128)S(1)} %get-tuple-element.30.own_a), channel_id=1, source_target_pairs={{0,1},{1,0},{2,3},{3,2},{4,5},{5,4},{6,7},{7,6},{8,9},{9,8},{10,11... | collective-permute-start | bytes 491528 | tf_op jit(solution)/shard_map/ppermute | solution.py:807

commit v5 on v4

--- a/solution.py
+++ b/solution.py
@@ -16,7 +16,7 @@
 buoyancy = 1.0
 
 LANES = 128
-VMEM_LIMIT = 24 * 1024 * 1024
+VMEM_LIMIT = 16 * 1024 * 1024
 
 
 def swapped(block, axis, distance):
@@ -162,7 +162,7 @@
         return index // self.beside, index % self.beside * self.full
 
     @staticmethod
-    def fits(shape, sectors, total):
+    def fits(shape, sectors, slabs, total):
         if sectors & (sectors - 1) or total // 2 > 128 or total != LANES or shape[2] != 16:
             return False
         plan = Plan(shape, sectors)
@@ -172,6 +172,7 @@
             and plan.planes == plan.theta
             and plan.rest * plan.fields <= LANES
             and plan.groups % 2 == 0
+            and slabs % 2 == 0
             and 3 * len(plan.early) * plan.theta <= plan.depth
             and plan.radial % LANES == 0
             and plan.radial > 2 * LANES
@@ -240,60 +241,6 @@
     return x if lanes % LANES == 0 else pltpu.roll(x, lanes % LANES, 1)
 
 
-def pack_kernel(plan, x_ref, out_ref, buf, sems):
-    shape = (plan.theta, LANES)
-    lane = lax.broadcasted_iota(jnp.int32, shape, 1)
-    row = lax.broadcasted_iota(jnp.int32, shape, 0)
-    sign = (1 - 2 * (row & 1)).astype(jnp.float32)
-    chunk = 4
-    copies = [
-        pltpu.make_async_copy(
-            x_ref.at[:, pl.ds(i * chunk, chunk), :, pl.ds(0, LANES)], buf.at[i], sems.at[i]
-        )
-        for i in range(plan.planes // chunk)
-    ]
-    for copy in copies:
-        copy.start()
-    group = jnp.zeros(shape, jnp.float32)
-    sums = [jnp.zeros(shape, jnp.float32) for _ in range(plan.fields)]
-    for k in range(plan.planes):
-        if k % chunk == 0:
-            copies[k // chunk].wait()
-        for f in range(plan.fields):
-            x = buf[k // chunk, f, k % chunk]
-            number, first = plan.place(f, k)
-            part = moved(x, first)
-            if first:
-                part = jnp.where((lane >= first) & (lane < first + plan.full), part, group)
-            group = part
-            if first // plan.full == plan.beside - 1 or (f, k) == (plan.fields - 1, plan.planes - 1):
-                out_ref[number] = group
-            alternating = jnp.sum(x * sign, axis=0, keepdims=True)
-            sums[f] = jnp.where(row == k, alternating, sums[f])
-    last = sums[0]
-    for f in range(plan.fields):
-        start = f * plan.rest
-        last = jnp.where(lane >= start, moved(sums[f], start - plan.full), last)
-    out_ref[plan.groups] = last
-
-
-def pack(plan, fields):
-    f32 = jnp.float32
-    chunks = plan.planes // 4
-    return pl.pallas_call(
-        functools.partial(pack_kernel, plan),
-        in_specs=[pl.BlockSpec(memory_space=pl.ANY)],
-        out_specs=pl.BlockSpec(memory_space=pltpu.VMEM),
-        out_shape=jax.ShapeDtypeStruct((plan.groups + 1, plan.theta, LANES), f32),
-        scratch_shapes=[
-            pltpu.VMEM((chunks, plan.fields, 4, plan.theta, LANES), f32),
-            pltpu.SemaphoreType.DMA((chunks,)),
-        ],
-        name="pack",
-        cost_estimate=pl.CostEstimate(flops=1000000, bytes_accessed=800000, transcendentals=0),
-    )(fields)
-
-
 def pick_columns(plan, x_ref, keep_high, ref, base):
     last = plan.theta - 1
     tiles = plan.radial // LANES
@@ -306,22 +253,74 @@
                 ref[base + f * tiles + tile, k : k + 1, :] = jnp.where(keep_high, high, low)
 
 
-def edges_kernel(plan, x_ref, after_ref, az_a, az_b):
-    del after_ref
+def pack_kernel(plan, x_ref, out_ref, wide_ref):
+    shape = (plan.theta, LANES)
+    lane = lax.broadcasted_iota(jnp.int32, shape, 1)
+    row = lax.broadcasted_iota(jnp.int32, shape, 0)
+    sign = (1 - 2 * (row & 1)).astype(jnp.float32)
+    group = jnp.zeros(shape, jnp.float32)
+    sums = [jnp.zeros(shape, jnp.float32) for _ in range(plan.fields)]
+    for k in range(plan.planes):
+        for f in range(plan.fields):
+            x = x_ref[f, k, :, :LANES]
+            number, first = plan.place(f, k)
+            part = moved(x, first)
+            if first:
+                part = jnp.where((lane >= first) & (lane < first + plan.full), part, group)
+            group = part
+            if first // plan.full == plan.beside - 1 or (f, k) == (plan.fields - 1, plan.planes - 1):
+                out_ref[number] = group
+                wide_ref[number] = group
+            alternating = jnp.sum(x * sign, axis=0, keepdims=True)
+            sums[f] = jnp.where(row == k, alternating, sums[f])
+    last = sums[0]
+    for f in range(plan.fields):
+        start = f * plan.rest
+        last = jnp.where(lane >= start, moved(sums[f], start - plan.full), last)
+    out_ref[plan.groups] = last
+    wide_ref[plan.groups] = last
     even_theta = lax.axis_index("az") % 2 == 0
-    pick_columns(plan, x_ref, even_theta, az_a, 0)
-    pick_columns(plan, x_ref, jnp.logical_not(even_theta), az_b, 0)
-
-
-def edges(plan, fields, after):
+    pick_columns(plan, x_ref, even_theta, wide_ref, plan.groups + 1)
+
+
+def pack(plan, fields):
     f32 = jnp.float32
     columns = plan.fields * plan.radial // LANES
     inside = pl.BlockSpec(memory_space=pltpu.VMEM)
     return pl.pallas_call(
+        functools.partial(pack_kernel, plan),
+        in_specs=[inside],
+        out_specs=[inside] * 2,
+        out_shape=[
+            jax.ShapeDtypeStruct((plan.groups + 1, plan.theta, LANES), f32),
+            jax.ShapeDtypeStruct((plan.groups + 1 + columns, plan.theta, LANES), f32),
+        ],
+        compiler_params=pltpu.CompilerParams(vmem_limit_bytes=VMEM_LIMIT),
+        name="pack",
+        cost_estimate=pl.CostEstimate(flops=1000000, bytes_accessed=800000, transcendentals=0),
+    )(fields)
+
+
+def edges_kernel(plan, x_ref, after_ref, az_b, ax_a, ax_b):
+    del after_ref
+    odd_plane = lax.axis_index("ax") % 2
+    last = plan.planes - 1
+    ax_a[...] = x_ref[:, (1 - odd_plane) * last, :, LANES:]
+    ax_b[...] = x_ref[:, odd_plane * last, :, LANES:]
+    even_theta = lax.axis_index("az") % 2 == 0
+    pick_columns(plan, x_ref, jnp.logical_not(even_theta), az_b, 0)
+
+
+def edges(plan, fields, after):
+    f32 = jnp.float32
+    columns = plan.fields * plan.radial // LANES
+    plane = jax.ShapeDtypeStruct((plan.fields, plan.theta, plan.radial - LANES), f32)
+    inside = pl.BlockSpec(memory_space=pltpu.VMEM)
+    return pl.pallas_call(
         functools.partial(edges_kernel, plan),
         in_specs=[inside] * 2,
-        out_specs=[inside] * 2,
-        out_shape=[jax.ShapeDtypeStruct((columns, plan.theta, LANES), f32)] * 2,
+        out_specs=[inside] * 3,
+        out_shape=[jax.ShapeDtypeStruct((columns, plan.theta, LANES), f32), plane, plane],
         compiler_params=pltpu.CompilerParams(vmem_limit_bytes=VMEM_LIMIT),
         name="edges",
         cost_estimate=pl.CostEstimate(flops=0, bytes_accessed=1000000, transcendentals=0),
@@ -445,18 +444,22 @@
     )(coef, fields)
 
 
-def seams_kernel(plan, coef_ref, own_a, own_b, az_a, az_b, part_ref, out_ref, done, outs):
-    del part_ref
+def slabs_beside(a, b):
+    slab = lax.axis_index("ax")
+    even_plane = slab % 2 == 0
+    b = jnp.where((slab > 0) & (slab < lax.axis_size("ax") - 1), b, 0.0)
+    return jnp.where(even_plane, b, a), jnp.where(even_plane, a, b)
+
+
+def seams(plan, coef_ref, x_ref, own_a, own_b, az_a, az_b, ax_a, ax_b, part_ref, done):
+    nu_dt = viscosity * time_step
+    half = 0.5 * time_step
     planes = plan.planes
     tiles = plan.radial // LANES
+    base = plan.groups + 1
     even_theta = lax.axis_index("az") % 2 == 0
     last = plan.theta - 1
-
-    def store(k):
-        return pltpu.make_async_copy(
-            done.at[k], out_ref.at[:, k, :, pl.ds(LANES, plan.radial - LANES)], outs.at[k]
-        )
-
+    row = lax.broadcasted_iota(jnp.int32, (plan.theta, LANES), 0)
     for tile in range(1, tiles):
         here = slice(tile * LANES, (tile + 1) * LANES)
         there = slice((tile - 1) * LANES, tile * LANES)
@@ -464,14 +467,14 @@
         angular = coef_ref[3:4, here]
         cross = coef_ref[6:7, here]
         number = tiles + tile
-        mine_a = own_a[number]
+        mine_a = own_a[base + number]
         mine_b = own_b[number]
         turn_low = angular * jnp.where(even_theta, mine_b, mine_a)
         turn_high = angular * jnp.where(even_theta, mine_a, mine_b)
         before = []
         after = []
         for f in range(plan.fields):
-            a = az_a[f * tiles + tile]
+            a = az_a[base + f * tiles + tile]
             b = az_b[f * tiles + tile]
             before.append(jnp.where(even_theta, b, a))
             after.append(jnp.where(even_theta, a, b))
@@ -484,31 +487,33 @@
             if f == 1:
                 low = low - cross * before[0]
                 high = high + cross * after[0]
+            below, above = slabs_beside(ax_a[f, :, there], ax_b[f, :, there])
             for k in range(planes):
-                done[k, f, 0:1, there] += low[k : k + 1]
-                done[k, f, last : last + 1, there] += high[k : k + 1]
-    for k in range(1, planes - 1):
-        store(k).start()
-    for k in range(1, planes - 1):
-        store(k).wait()
-
-
-def seams(plan, coef, fields, own, sides, part):
+                value = part_ref[k, f, :, there]
+                value = value + jnp.where(row == 0, low[k : k + 1], 0.0)
+                value = value + jnp.where(row == last, high[k : k + 1], 0.0)
+                if k == 0:
+                    value = value + (nu_dt + half * x_ref[2, k, :, here]) * below
+                if k == planes - 1:
+                    value = value + (nu_dt - half * x_ref[2, k, :, here]) * above
+                done[k, f, :, there] = value
+
+
+def gate_kernel(x_ref, token_ref, out_ref):
+    del token_ref
+    out_ref[...] = x_ref[...]
+
+
+def gate(x, token):
     inside = pl.BlockSpec(memory_space=pltpu.VMEM)
     return pl.pallas_call(
-        functools.partial(seams_kernel, plan),
-        in_specs=[inside] * 6,
-        out_specs=[pl.BlockSpec(memory_space=pl.ANY), inside],
-        out_shape=[
-            jax.ShapeDtypeStruct(fields.shape, jnp.float32),
-            jax.ShapeDtypeStruct(part.shape, jnp.float32),
-        ],
-        input_output_aliases={5: 1},
-        scratch_shapes=[pltpu.SemaphoreType.DMA((plan.planes,))],
+        gate_kernel,
+        in_specs=[inside] * 2,
+        out_specs=inside,
+        out_shape=jax.ShapeDtypeStruct(x.shape, x.dtype),
         compiler_params=pltpu.CompilerParams(vmem_limit_bytes=VMEM_LIMIT),
-        name="seams",
-        cost_estimate=pl.CostEstimate(flops=1000000, bytes_accessed=4000000, transcendentals=0),
-    )(coef, *own, *sides, part)
+        name="gate",
+    )(x, token)
 
 
 def halves(x, depth=None):
@@ -556,8 +561,7 @@
     )(jnp.asarray(plan.forward(plan.early)), *pieces)
 
 
-def filter_kernel(plan, token_ref, x_ref, forward_ref, inverse_ref, mask_ref, early_ref, early_total, *refs):
-    del token_ref
+def filter_kernel(plan, x_ref, forward_ref, inverse_ref, mask_ref, early_ref, early_total, *refs):
     count = len(plan.late)
     pieces = refs[:count]
     own_ref, across_ref, edge_ref, sums_ref, message_a, message_b = refs[count:]
@@ -596,25 +600,24 @@
         for f in range(plan.fields):
             number, first = plan.place(f, k)
             raw = x_ref[f, k, :, :LANES] - sign * sums_ref[f, k : k + 1]
-            ref[f, :, :LANES] = jnp.where(lane < plan.full, moved(own_ref[number], -first), raw)
-            ref[f, :, LANES:] = x_ref[f, k, :, LANES:]
-
-    def both_messages(ref_low, ref_high):
-        message(ref_low, 0)
-        message(ref_high, plan.planes - 1)
-
-    pl.when(odd_plane == 1)(lambda: both_messages(message_a, message_b))
-    pl.when(odd_plane == 0)(lambda: both_messages(message_b, message_a))
-
-
-def filtered(plan, token, fields, pieces, early):
+            ref[f] = jnp.where(lane < plan.full, moved(own_ref[number], -first), raw)
+
+    def both_messages(a, b):
+        message(message_a, a)
+        message(message_b, b)
+
+    pl.when(odd_plane == 1)(lambda: both_messages(0, plan.planes - 1))
+    pl.when(odd_plane == 0)(lambda: both_messages(plan.planes - 1, 0))
+
+
+def filtered(plan, fields, pieces, early):
     inside = pl.BlockSpec(memory_space=pltpu.VMEM)
     f32 = jnp.float32
     cube = jax.ShapeDtypeStruct((plan.groups, plan.theta, LANES), f32)
-    plane = jax.ShapeDtypeStruct((plan.fields, plan.theta, plan.radial), f32)
+    plane = jax.ShapeDtypeStruct((plan.fields, plan.theta, LANES), f32)
     return pl.pallas_call(
         functools.partial(filter_kernel, plan),
-        in_specs=[inside] * (7 + len(pieces)),
+        in_specs=[inside] * (6 + len(pieces)),
         out_specs=[inside] * 6,
         out_shape=[
             cube,
@@ -628,7 +631,6 @@
         name="filter",
         cost_estimate=pl.CostEstimate(flops=200000000, bytes_accessed=1500000, transcendentals=0),
     )(
-        token,
         fields,
         jnp.asarray(plan.forward(plan.late)),
         jnp.asarray(plan.inverse()),
@@ -639,9 +641,18 @@
 
 
 def inner_kernel(
-    plan, coef_ref, own_ref, across_ref, edge_ref, sums_ref, x_ref, az_a, az_b, done, state
+    plan, coef_ref, own_ref, across_ref, edge_ref, sums_ref, x_ref, own_a, own_b, az_a, az_b,
+    ax_a, ax_b, part_ref, out_ref, done, far_done, state, outs
 ):
     planes = plan.planes
+    seams(plan, coef_ref, x_ref, own_a, own_b, az_a, az_b, ax_a, ax_b, part_ref, far_done)
+    beyond = pl.ds(LANES, plan.radial - LANES)
+    stores = [
+        pltpu.make_async_copy(far_done.at[k], out_ref.at[:, k, :, beyond], outs.at[k])
+        for k in range(planes)
+    ]
+    for copy in stores:
+        copy.start()
     theta = plan.theta
     tiles = plan.radial // LANES
     shape = (theta, LANES)
@@ -666,7 +677,7 @@
     befores = []
     afters = []
     for f in range(plan.fields):
-        a = az_a[f * tiles]
+        a = az_a[plan.groups + 1 + f * tiles]
         b = az_b[f * tiles]
         befores.append(jnp.where(even_theta, b, a) + sums_ref[f])
         afters.append(jnp.where(even_theta, a, b) - sums_ref[f])
@@ -693,28 +704,38 @@
         result = advance(coef, q, jp, jm, tp, tm, kp, km)
         for f in range(plan.fields):
             done[k, f] = result[f]
-
-
-def inner(plan, coef, parts, fields, sides):
+    for copy in stores:
+        copy.wait()
+
+
+def inner(plan, coef, parts, fields, own, sides, rests, part):
     inside = pl.BlockSpec(memory_space=pltpu.VMEM)
     f32 = jnp.float32
     return pl.pallas_call(
         functools.partial(inner_kernel, plan),
-        in_specs=[inside] * 8,
-        out_specs=inside,
-        out_shape=jax.ShapeDtypeStruct((plan.planes, plan.fields, plan.theta, LANES), f32),
-        scratch_shapes=[pltpu.VMEM((plan.planes, plan.fields, plan.theta, LANES), f32)],
+        in_specs=[inside] * 13,
+        out_specs=[pl.BlockSpec(memory_space=pl.ANY), inside],
+        out_shape=[
+            jax.ShapeDtypeStruct(fields.shape, f32),
+            jax.ShapeDtypeStruct((plan.planes, plan.fields, plan.theta, LANES), f32),
+        ],
+        scratch_shapes=[
+            pltpu.VMEM(part.shape, f32),
+            pltpu.VMEM((plan.planes, plan.fields, plan.theta, LANES), f32),
+            pltpu.SemaphoreType.DMA((plan.planes,)),
+        ],
         compiler_params=pltpu.CompilerParams(vmem_limit_bytes=VMEM_LIMIT),
         name="inner",
         cost_estimate=pl.CostEstimate(flops=6000000, bytes_accessed=2500000, transcendentals=0),
-    )(coef, *parts, fields, *sides)
-
-
-def finish_kernel(plan, near_ref, part_ref, own_a, own_b, ax_a, ax_b, other_ref, out_ref, ends, sems):
+    )(coef, *parts, fields, *own, *sides, *rests, part)
+
+
+def finish_kernel(plan, near_ref, own_a, own_b, ax_a, ax_b, other_ref, out_ref, ends, sems):
     del other_ref
     planes = plan.planes
+    first = pl.ds(0, LANES)
     copies = [
-        pltpu.make_async_copy(near_ref.at[k], out_ref.at[:, k, :, pl.ds(0, LANES)], sems.at[k])
+        pltpu.make_async_copy(near_ref.at[k], out_ref.at[:, k, :, first], sems.at[k])
         for k in range(1, planes - 1)
     ]
     for copy in copies:
@@ -722,57 +743,45 @@
     even_plane = lax.axis_index("ax") % 2 == 0
     nu_dt = viscosity * time_step
     half = 0.5 * time_step
-    tiles = plan.radial // LANES
+    sent_a = own_a[2]
+    sent_b = own_b[2]
+    factor_low = nu_dt + half * jnp.where(even_plane, sent_b, sent_a)
+    factor_high = nu_dt - half * jnp.where(even_plane, sent_a, sent_b)
+    for f in range(plan.fields):
+        below, above = slabs_beside(ax_a[f], ax_b[f])
+        ends[0, f] = near_ref[0, f] + factor_low * below
+        ends[1, f] = near_ref[planes - 1, f] + factor_high * above
     for end, k in ((0, 0), (1, planes - 1)):
-        for tile in range(tiles):
-            here = slice(tile * LANES, (tile + 1) * LANES)
-            sent_a = own_a[2, :, here]
-            sent_b = own_b[2, :, here]
-            if end == 0:
-                factor = nu_dt + half * jnp.where(even_plane, sent_b, sent_a)
-            else:
-                factor = nu_dt - half * jnp.where(even_plane, sent_a, sent_b)
-            for f in range(plan.fields):
-                a = ax_a[f, :, here]
-                b = ax_b[f, :, here]
-                value = jnp.where(even_plane, b, a) if end == 0 else jnp.where(even_plane, a, b)
-                if tile == 0:
-                    start = near_ref[k, f]
-                else:
-                    start = part_ref[k, f, :, (tile - 1) * LANES : tile * LANES]
-                ends[end, f, :, here] = start + factor * value
-        copies.append(pltpu.make_async_copy(ends.at[end], out_ref.at[:, k], sems.at[k]))
+        copies.append(pltpu.make_async_copy(ends.at[end], out_ref.at[:, k, :, first], sems.at[k]))
         copies[-1].start()
     for copy in copies:
         copy.wait()
 
 
-def finish(plan, near, part, sent, messages, partial):
+def finish(plan, near, sent, messages, partial):
     anywhere = pl.BlockSpec(memory_space=pl.ANY)
     inside = pl.BlockSpec(memory_space=pltpu.VMEM)
     return pl.pallas_call(
         functools.partial(finish_kernel, plan),
-        in_specs=[inside] * 6 + [anywhere],
+        in_specs=[inside] * 5 + [anywhere],
         out_specs=anywhere,
         out_shape=jax.ShapeDtypeStruct(partial.shape, jnp.float32),
-        input_output_aliases={6: 0},
+        input_output_aliases={5: 0},
         scratch_shapes=[
-            pltpu.VMEM((2, plan.fields, plan.theta, plan.radial), jnp.float32),
+            pltpu.VMEM((2, plan.fields, plan.theta, LANES), jnp.float32),
             pltpu.SemaphoreType.DMA((plan.planes,)),
         ],
         compiler_params=pltpu.CompilerParams(vmem_limit_bytes=VMEM_LIMIT),
         name="finish",
         cost_estimate=pl.CostEstimate(flops=100000, bytes_accessed=1500000, transcendentals=0),
-    )(near, part, *sent, *messages, partial)
-
-
-def pairs(count, start, periodic):
+    )(near, *sent, *messages, partial)
+
+
+def pairs(count, start):
     route = []
     for low in range(start, count, 2):
-        high = low + 1
-        if high == count and not periodic:
-            continue
-        route += [(low, high % count), (high % count, low)]
+        high = (low + 1) % count
+        route += [(low, high), (high, low)]
     return route
 
 
@@ -785,36 +794,38 @@
     def send(x, distance):
         return lax.ppermute(x, "az", [(i, i ^ distance) for i in range(sectors)])
 
-    packed = pack(plan, fields)
+    packed, wide = pack(plan, fields)
     half = sectors // 2
     pieces = [None] * sectors
     pieces[0] = packed
     far = send(packed, half)
     pieces[half] = far
     for p in range(half - 1, 0, -1):
-        pieces[p] = send(packed, p)
+        pieces[p] = send(wide if p == 1 else packed, p)
+    part, token = outer(plan, coef, fields)
+    onward = gate(far, token)
     for p in range(half - 1, 0, -1):
-        pieces[half + p] = send(far, p)
+        pieces[half + p] = send(onward, p)
+    pieces[half] = onward
     early = early_spectra(plan, pieces[: half + 1])
-    column_a, column_b = edges(plan, fields, early[1])
-    sides = (
-        lax.ppermute(column_a, "az", pairs(sectors, 0, True)),
-        lax.ppermute(column_b, "az", pairs(sectors, 1, True)),
-    )
-    part, token = outer(plan, coef, fields)
-    *parts, message_a, message_b = filtered(plan, token, fields, pieces[half + 1 :], early)
+    column, rest_a, rest_b = edges(plan, fields, early[1])
+    sides = (pieces[1], lax.ppermute(column, "az", pairs(sectors, 1)))
+    rests = (
+        lax.ppermute(rest_a, "ax", pairs(slabs, 0)),
+        lax.ppermute(rest_b, "ax", pairs(slabs, 1)),
+    )
+    *parts, message_a, message_b = filtered(plan, fields, pieces[half + 1 :], early)
     messages = (
-        lax.ppermute(message_a, "ax", pairs(slabs, 0, False)),
-        lax.ppermute(message_b, "ax", pairs(slabs, 1, False)),
-    )
-    partial, part = seams(plan, coef, fields, (column_a, column_b), sides, part)
-    near = inner(plan, coef, parts, fields, sides)
-    return finish(plan, near, part, (message_a, message_b), messages, partial)
+        lax.ppermute(message_a, "ax", pairs(slabs, 0)),
+        lax.ppermute(message_b, "ax", pairs(slabs, 1)),
+    )
+    partial, near = inner(plan, coef, parts, fields, (wide, column), sides, rests, part)
+    return finish(plan, near, (message_a, message_b), messages, partial)
 
 
 def on_device(fields):
     total_theta = fields.shape[2] * lax.axis_size("az")
-    if Plan.fits(fields.shape, lax.axis_size("az"), total_theta):
+    if Plan.fits(fields.shape, lax.axis_size("az"), lax.axis_size("ax"), total_theta):
         return fast_on_device(fields)
     return general_on_device(fields)
 

time: 32.6 us -> 30.6 us (0.939)
  Pallas kernels: 9.57 us -> 6.67 us
  starting transfers between devices: 19.8 us -> 17 us
  waiting for transfers between devices: 2.88 us -> 4.84 us
  local copies, waits for them, and re-layouts: 0.04 us -> 1.77 us
    pallas_call x2, Pallas kernels: 3.71 us -> 0.38 us  [the longest x1 0.37 us: pack(): pl.pallas_call(functools.partial(pack_kernel, plan), in_specs=[inside], o...]
    ppermute x4 -> x5, waiting for transfers between devices: 0.08 us -> 3.4 us  [the longest x1 1.81 us: fast_on_device(): lax.ppermute(rest_b, 'ax', pairs(slabs, 1))]
    ppermute x4 -> x5, starting transfers between devices: 8.67 us -> 5.85 us  [the longest x1 3.52 us: fast_on_device(): sides = (pieces[1], lax.ppermute(column, 'az', pairs(sectors, 1)))]
    unnamed x14, local copies, waits for them, and re-layouts: 0.04 us -> 1.77 us
    ppermute x7, waiting for transfers between devices: 2.8 us -> 1.44 us  [send(): return lax.ppermute(x, 'az', [(i, i ^ distance) for i in range(sectors)])]
    pallas_call x1, Pallas kernels: 0.99 us -> 1.66 us  [inner(): pl.pallas_call(functools.partial(inner_kernel, plan), in_specs=[inside] *...]
  transfers between devices with their start and end apart: 11 -> 12, of which waited for: 2 -> 3; matrix products, arithmetic and copies ran while one was open for 0% -> 0% of each run, Pallas kernels for 20% -> 18%
where the time goes in v5:
time: 30.6 us; the launch traced here: 30.4 us
  starting transfers between devices  17 us (56%)
  Pallas kernels  6.67 us (22%)
  waiting for transfers between devices  4.84 us (16%)
  local copies, waits for them, and re-layouts  1.77 us (6%)
    ppermute x7, starting transfers between devices, send(): return lax.ppermute(x, 'az', [(i, i ^ distance) for i in range(sectors)])  11.1 us
    ppermute x1, starting transfers between devices, fast_on_device(): sides = (pieces[1], lax.ppermute(column, 'az', pairs(sectors, 1)))  3.52 us
    pallas_call x1, Pallas kernels, outer(): pl.pallas_call(functools.partial(outer_kernel, plan), in_specs=[inside] *...  2.25 us
    ppermute x1, waiting for transfers between devices, fast_on_device(): lax.ppermute(rest_b, 'ax', pairs(slabs, 1))  1.81 us
    unnamed x14, local copies, waits for them, and re-layouts  1.77 us
    pallas_call x1, Pallas kernels, inner(): pl.pallas_call(functools.partial(inner_kernel, plan), in_specs=[inside] *...  1.66 us
    ppermute x1, starting transfers between devices, fast_on_device(): lax.ppermute(rest_b, 'ax', pairs(slabs, 1))  1.63 us
    ppermute x1, waiting for transfers between devices, fast_on_device(): sides = (pieces[1], lax.ppermute(column, 'az', pairs(sectors, 1)))  1.57 us
  transfers between devices with their start and end apart: 12, of which 3 were waited for; matrix products, arithmetic and copies ran while one was open for 0% of the time, Pallas kernels for 18%

profile of v5, /device:TPU:0, one launch (start us, length us, event | category | flops | bytes accessed | tf_op | source)
XLA Modules:
  0.0 30.4 jit_solution(16415370598586516211)
XLA Ops:
  0.0 0.0 copy-start
  0.0 1.7 %copy-done = f32[5,16,16,512]{3,2,1,0:T(8,128)S(1)} copy-done((f32[5,16,16,512]{3,2,1,0:T(8,128)S(1)}, f32[5,16,16,512]{3,2,1,0:T(8,128)}, u32[]{:S(2)}) %copy-start) | copy-done | bytes 2621464
  1.7 0.0 copy-start.6
  1.7 0.0 copy-start.3
  1.7 0.4 %pack.1 = (f32[15,16,128]{2,1,0:T(8,128)S(1)}, f32[35,16,128]{2,1,0:T(8,128)S(1)}) custom-call(f32[5,16,16,512]{3,2,1,0:T(8,128)S(1)} %copy-done), custom_call_target="tpu_custom_call" | custom-call | flops 1000000 | bytes 800000 | tf_op jit(solution)/shard_map/pack/pallas_call | solution.py:290
  2.1 0.0 copy-start.1
  2.1 3.0 %collective-permute-start = (f32[35,16,128]{2,1,0:T(8,128)S(1)}, f32[35,16,128]{2,1,0:T(8,128)S(1)}, u32[]{:S(2)}, u32[]{:S(2)}) collective-permute-start(f32[35,16,128]{2,1,0:T(8,128)S(1)} %get-tuple-element.23.own_a), channel_id=1, source_target_pairs={{0,4},{4,0},{8,12},{12,8},{16,20},{20,16},{24,28},{28,24},{1,5},{5... | collective-permute-start | bytes 860168 | tf_op jit(solution)/shard_map/ppermute | solution.py:795
  5.1 2.6 %collective-permute-start.3 = (f32[15,16,128]{2,1,0:T(8,128)S(1)}, f32[15,16,128]{2,1,0:T(8,128)S(1)}, u32[]{:S(2)}, u32[]{:S(2)}) collective-permute-start(f32[15,16,128]{2,1,0:T(8,128)S(1)} %get-tuple-element.22.refs_0_), channel_id=1, source_target_pairs={{0,16},{4,20},{8,24},{12,28},{16,0},{20,4},{24,8},{28,12},{1,17},{... | collective-permute-start | bytes 368648 | tf_op jit(solution)/shard_map/ppermute | solution.py:795
  7.7 1.6 %collective-permute-start.1 = (f32[15,16,128]{2,1,0:T(8,128)S(1)}, f32[15,16,128]{2,1,0:T(8,128)S(1)}, u32[]{:S(2)}, u32[]{:S(2)}) collective-permute-start(f32[15,16,128]{2,1,0:T(8,128)S(1)} %get-tuple-element.22.refs_0_), channel_id=1, source_target_pairs={{0,8},{4,12},{8,0},{12,4},{16,24},{20,28},{24,16},{28,20},{1,9},{5... | collective-permute-start | bytes 368648 | tf_op jit(solution)/shard_map/ppermute | solution.py:795
  9.3 0.4 %collective-permute-start.2 = (f32[15,16,128]{2,1,0:T(8,128)S(1)}, f32[15,16,128]{2,1,0:T(8,128)S(1)}, u32[]{:S(2)}, u32[]{:S(2)}) collective-permute-start(f32[15,16,128]{2,1,0:T(8,128)S(1)} %get-tuple-element.22.refs_0_), channel_id=1, source_target_pairs={{0,12},{4,8},{8,4},{12,0},{16,28},{20,24},{24,20},{28,16},{1,13},{... | collective-permute-start | bytes 368648 | tf_op jit(solution)/shard_map/ppermute | solution.py:795
  9.7 0.0 copy-done.6
  9.7 2.3 %outer.1 = (f32[16,5,16,384]{3,2,1,0:T(8,128)S(1)}, f32[8,128]{1,0:T(8,128)S(1)}) custom-call(f32[8,512]{1,0:T(8,128)S(1)} %copy-done.6, f32[5,16,16,512]{3,2,1,0:T(8,128)S(1)} %copy-done), custom_call_target="tpu_custom_call" | custom-call | flops 16000000 | bytes 5000000 | tf_op jit(solution)/shard_map/outer/pallas_call | solution.py:433
  12.0 0.0 copy-start.2
  12.0 0.0 copy-start.4
  12.0 0.0 copy-start.5
  12.0 1.4 %collective-permute-done.3.x_ref = f32[15,16,128]{2,1,0:T(8,128)S(1)} collective-permute-done((f32[15,16,128]{2,1,0:T(8,128)S(1)}, f32[15,16,128]{2,1,0:T(8,128)S(1)}, u32[]{:S(2)}, u32[]{:S(2)}) %collective-permute-start.3) | collective-permute-done | bytes 122912 | tf_op jit(solution)/shard_map/ppermute | solution.py:795
  13.5 0.6 %collective-permute-start.4 = (f32[15,16,128]{2,1,0:T(8,128)S(1)}, f32[15,16,128]{2,1,0:T(8,128)S(1)}, u32[]{:S(2)}, u32[]{:S(2)}) collective-permute-start(f32[15,16,128]{2,1,0:T(8,128)S(1)} %gate.1.refs_4_), channel_id=1, source_target_pairs={{0,4},{4,0},{8,12},{12,8},{16,20},{20,16},{24,28},{28,24},{1,5},{5... | collective-permute-start | bytes 368648 | tf_op jit(solution)/shard_map/ppermute | solution.py:795
  14.0 1.2 %collective-permute-start.5 = (f32[15,16,128]{2,1,0:T(8,128)S(1)}, f32[15,16,128]{2,1,0:T(8,128)S(1)}, u32[]{:S(2)}, u32[]{:S(2)}) collective-permute-start(f32[15,16,128]{2,1,0:T(8,128)S(1)} %gate.1.refs_4_), channel_id=1, source_target_pairs={{0,8},{4,12},{8,0},{12,4},{16,24},{20,28},{24,16},{28,20},{1,9},{5... | collective-permute-start | bytes 368648 | tf_op jit(solution)/shard_map/ppermute | solution.py:795
  15.2 0.0 collective-permute-done.1.refs_2_
  15.2 1.8 %collective-permute-start.6 = (f32[15,16,128]{2,1,0:T(8,128)S(1)}, f32[15,16,128]{2,1,0:T(8,128)S(1)}, u32[]{:S(2)}, u32[]{:S(2)}) collective-permute-start(f32[15,16,128]{2,1,0:T(8,128)S(1)} %gate.1.refs_4_), channel_id=1, source_target_pairs={{0,12},{4,8},{8,4},{12,0},{16,28},{20,24},{24,20},{28,16},{1,13},{... | collective-permute-start | bytes 368648 | tf_op jit(solution)/shard_map/ppermute | solution.py:795
  17.0 0.0 collective-permute-done.2.refs_3_
  17.0 0.0 collective-permute-done.refs_1_.az_a
  17.0 0.0 copy-done.3
  17.0 0.3 %early.1 = (f32[7,128,256]{2,1,0:T(8,128)S(1)}, f32[16,128]{1,0:T(8,128)S(1)}) custom-call(bf16[8,128,256]{2,1,0:T(8,128)(2,1)S(1)} %copy-done.3, f32[15,16,128]{2,1,0:T(8,128)S(1)} %get-tuple-element.22.refs_0_, f32[35,16,128]{2,1,0:T(8,128)S(1)} %collective-permute-done.refs_1_.az_a, f32[15,16,128]{2,1,0:T(8,128)S(1)} %collective-permute-done.1.refs_2_, ...), custom_call_target="tpu_custom_call" | custom-call | flops 200000000 | bytes 1500000 | tf_op jit(solution)/shard_map/early/pallas_call | solution.py:550
  17.3 0.0 copy-done.1
  17.4 0.2 edges.1
  17.6 3.5 %collective-permute-start.7 = (f32[20,16,128]{2,1,0:T(8,128)S(1)}, f32[20,16,128]{2,1,0:T(8,128)S(1)}, u32[]{:S(2)}, u32[]{:S(2)}) collective-permute-start(f32[20,16,128]{2,1,0:T(8,128)S(1)} %get-tuple-element.31.own_b), channel_id=1, source_target_pairs={{4,8},{8,4},{12,16},{16,12},{20,24},{24,20},{28,0},{0,28},{5,9},{9... | collective-permute-start | bytes 491528 | tf_op jit(solution)/shard_map/ppermute | solution.py:812
  21.1 0.0 collective-permute-start.8
  21.1 0.0 collective-permute-done.4.refs_0_
  21.1 1.6 %collective-permute-start.9 = (f32[5,16,384]{2,1,0:T(8,128)S(1)}, f32[5,16,384]{2,1,0:T(8,128)S(1)}, u32[]{:S(2)}, u32[]{:S(2)}) collective-permute-start(f32[5,16,384]{2,1,0:T(8,128)S(1)} %get-tuple-element.33), channel_id=1, source_target_pairs={{1,2},{2,1},{3,0},{0,3},{5,6},{6,5},{7,4},{4,7},{9,10},{10,9},{11,... | collective-permute-start | bytes 368648 | tf_op jit(solution)/shard_map/ppermute | solution.py:815
  22.7 0.0 collective-permute-done.5.refs_1_
  22.7 0.0 collective-permute-done.6.refs_2_
  22.7 0.0 copy-done.2
  22.7 0.0 copy-done.4
  22.7 0.0 copy-done.5
  22.8 0.9 %filter.1 = (f32[14,16,128]{2,1,0:T(8,128)S(1)}, f32[14,16,128]{2,1,0:T(8,128)S(1)}, f32[14,8,128]{2,1,0:T(8,128)S(1)}, f32[5,16,128]{2,1,0:T(8,128)S(1)}, f32[5...) custom-call(f32[5,16,16,512]{3,2,1,0:T(8,128)S(1)} %copy-done.1, bf16[8,128,256]{2,1,0:T(8,128)(2,1)S(1)} %copy-done.2, ...), custom_call_target="tpu_custom_call" | custom-call | flops 200000000 | bytes 1500000 | tf_op jit(solution)/shard_map/filter/pallas_call | solution.py:618
  23.7 0.1 collective-permute-start.10
  23.7 0.6 %collective-permute-start.11 = (f32[5,16,128]{2,1,0:T(8,128)S(1)}, f32[5,16,128]{2,1,0:T(8,128)S(1)}, u32[]{:S(2)}, u32[]{:S(2)}) collective-permute-start(f32[5,16,128]{2,1,0:T(8,128)S(1)} %get-tuple-element.37.own_b), channel_id=1, source_target_pairs={{1,2},{2,1},{3,0},{0,3},{5,6},{6,5},{7,4},{4,7},{9,10},{10,9},{11,... | collective-permute-start | bytes 122888 | tf_op jit(solution)/shard_map/ppermute | solution.py:820
  24.4 0.0 collective-permute-done.8.ax_a
  24.4 1.8 %collective-permute-done.9.ax_b = f32[5,16,384]{2,1,0:T(8,128)S(1)} collective-permute-done((f32[5,16,384]{2,1,0:T(8,128)S(1)}, f32[5,16,384]{2,1,0:T(8,128)S(1)}, u32[]{:S(2)}, u32[]{:S(2)}) %collective-permute-start.9) | collective-permute-done | bytes 122912 | tf_op jit(solution)/shard_map/ppermute | solution.py:815
  26.2 1.6 %collective-permute-done.7.az_b = f32[20,16,128]{2,1,0:T(8,128)S(1)} collective-permute-done((f32[20,16,128]{2,1,0:T(8,128)S(1)}, f32[20,16,128]{2,1,0:T(8,128)S(1)}, u32[]{:S(2)}, u32[]{:S(2)}) %collective-permute-start.7) | collective-permute-done | bytes 163872 | tf_op jit(solution)/shard_map/ppermute | solution.py:812
  27.8 1.7 %inner.1 = (f32[5,16,16,512]{3,2,1,0:T(8,128)}, f32[16,5,16,128]{3,2,1,0:T(8,128)S(1)}) custom-call(f32[8,512]{1,0:T(8,128)S(1)} %copy-done.6, f32[14,16,128]{2,1,0:T(8,128)S(1)} %get-tuple-element.27.own_ref, f32[14,16,128]{2,1,0:T(8,128)S(1)} %get-tuple-element.28.across_ref, f32[14,8,128]{2,1,0:T(8,128)S(1)} %get-tuple-element.29.edge_ref, ...), custom_call_target="tpu_custom_call" | custom-call | flops 6000000 | bytes 2500000 | tf_op jit(solution)/shard_map/inner/pallas_call | solution.py:714
  29.4 0.0 collective-permute-done.10.ax_a
  29.4 0.0 collective-permute-done.11.ax_b
  29.5 1.0 %finish.1 = f32[5,16,16,512]{3,2,1,0:T(8,128)} custom-call(f32[16,5,16,128]{3,2,1,0:T(8,128)S(1)} %get-tuple-element.35.near_ref, f32[5,16,128]{2,1,0:T(8,128)S(1)} %get-tuple-element.36.own_a, f32[5,16,128]{2,1,0:T(8,128)S(1)} %get-tuple-element.37.own_b, f32[5,16,128]{2,1,0:T(8,128)S(1)} %collective-permute-done.10.ax_a, ...), custom_call_target="tpu_custom_call", output_to_operand_aliasing={{}: (5, {})} | custom-call | flops 100000 | bytes 1500000 | tf_op jit(solution)/shard_map/finish/pallas_call | solution.py:764
  (1 shorter events, 0.0 us)
Async XLA Ops:
  0.0 1.7 %copy-start = (f32[5,16,16,512]{3,2,1,0:T(8,128)S(1)}, f32[5,16,16,512]{3,2,1,0:T(8,128)}, u32[]{:S(2)}) copy-start(f32[5,16,16,512]{3,2,1,0:T(8,128)} %x_ref.9) | copy-start | bytes 7864324
  1.7 8.0 %copy-start.6 = (f32[8,512]{1,0:T(8,128)S(1)}, f32[8,512]{1,0:T(8,128)}, u32[]{:S(2)}) copy-start(f32[8,512]{1,0:T(8,128)} %constant.10.clone.coef_ref) | copy-start | bytes 49156
  1.7 15.3 %copy-start.3 = (bf16[8,128,256]{2,1,0:T(8,128)(2,1)S(1)}, bf16[8,128,256]{2,1,0:T(8,128)(2,1)}, u32[]{:S(2)}) copy-start(bf16[8,128,256]{2,1,0:T(8,128)(2,1)} %constant.11.clone.forward_ref) | copy-start | bytes 1572868
  2.1 15.2 %copy-start.1 = (f32[5,16,16,512]{3,2,1,0:T(8,128)S(1)}, f32[5,16,16,512]{3,2,1,0:T(8,128)}, u32[]{:S(2)}) copy-start(f32[5,16,16,512]{3,2,1,0:T(8,128)} %x_ref.9) | copy-start | bytes 7864324
  2.1 14.9 %collective-permute-start = (f32[35,16,128]{2,1,0:T(8,128)S(1)}, f32[35,16,128]{2,1,0:T(8,128)S(1)}, u32[]{:S(2)}, u32[]{:S(2)}) collective-permute-start(f32[35,16,128]{2,1,0:T(8,128)S(1)} %get-tuple-element.23.own_a), channel_id=1, source_target_pairs={{0,4},{4,0},{8,12},{12,8},{16,20},{20,16},{24,28},{28,24},{1,5},{5... | collective-permute-start | bytes 860168 | tf_op jit(solution)/shard_map/ppermute | solution.py:795
  5.1 8.3 %collective-permute-start.3 = (f32[15,16,128]{2,1,0:T(8,128)S(1)}, f32[15,16,128]{2,1,0:T(8,128)S(1)}, u32[]{:S(2)}, u32[]{:S(2)}) collective-permute-start(f32[15,16,128]{2,1,0:T(8,128)S(1)} %get-tuple-element.22.refs_0_), channel_id=1, source_target_pairs={{0,16},{4,20},{8,24},{12,28},{16,0},{20,4},{24,8},{28,12},{1,17},{... | collective-permute-start | bytes 368648 | tf_op jit(solution)/shard_map/ppermute | solution.py:795
  7.7 7.5 %collective-permute-start.1 = (f32[15,16,128]{2,1,0:T(8,128)S(1)}, f32[15,16,128]{2,1,0:T(8,128)S(1)}, u32[]{:S(2)}, u32[]{:S(2)}) collective-permute-start(f32[15,16,128]{2,1,0:T(8,128)S(1)} %get-tuple-element.22.refs_0_), channel_id=1, source_target_pairs={{0,8},{4,12},{8,0},{12,4},{16,24},{20,28},{24,16},{28,20},{1,9},{5... | collective-permute-start | bytes 368648 | tf_op jit(solution)/shard_map/ppermute | solution.py:795
  9.3 7.7 %collective-permute-start.2 = (f32[15,16,128]{2,1,0:T(8,128)S(1)}, f32[15,16,128]{2,1,0:T(8,128)S(1)}, u32[]{:S(2)}, u32[]{:S(2)}) collective-permute-start(f32[15,16,128]{2,1,0:T(8,128)S(1)} %get-tuple-element.22.refs_0_), channel_id=1, source_target_pairs={{0,12},{4,8},{8,4},{12,0},{16,28},{20,24},{24,20},{28,16},{1,13},{... | collective-permute-start | bytes 368648 | tf_op jit(solution)/shard_map/ppermute | solution.py:795
  12.0 10.7 %copy-start.2 = (bf16[8,128,256]{2,1,0:T(8,128)(2,1)S(1)}, bf16[8,128,256]{2,1,0:T(8,128)(2,1)}, u32[]{:S(2)}) copy-start(bf16[8,128,256]{2,1,0:T(8,128)(2,1)} %constant.12.clone.forward_ref) | copy-start | bytes 1572868
  12.0 10.7 %copy-start.4 = (bf16[8,48,384]{2,1,0:T(8,128)(2,1)S(1)}, bf16[8,48,384]{2,1,0:T(8,128)(2,1)}, u32[]{:S(2)}) copy-start(bf16[8,48,384]{2,1,0:T(8,128)(2,1)} %constant.13.clone.inverse_ref) | copy-start | bytes 884740
  12.0 10.7 %copy-start.5 = (f32[128,128]{1,0:T(8,128)S(1)}, f32[128,128]{1,0:T(8,128)}, u32[]{:S(2)}) copy-start(f32[128,128]{1,0:T(8,128)} %constant.14.clone.mask_ref) | copy-start | bytes 196612
  13.5 7.6 %collective-permute-start.4 = (f32[15,16,128]{2,1,0:T(8,128)S(1)}, f32[15,16,128]{2,1,0:T(8,128)S(1)}, u32[]{:S(2)}, u32[]{:S(2)}) collective-permute-start(f32[15,16,128]{2,1,0:T(8,128)S(1)} %gate.1.refs_4_), channel_id=1, source_target_pairs={{0,4},{4,0},{8,12},{12,8},{16,20},{20,16},{24,28},{28,24},{1,5},{5... | collective-permute-start | bytes 368648 | tf_op jit(solution)/shard_map/ppermute | solution.py:795
  14.0 8.7 %collective-permute-start.5 = (f32[15,16,128]{2,1,0:T(8,128)S(1)}, f32[15,16,128]{2,1,0:T(8,128)S(1)}, u32[]{:S(2)}, u32[]{:S(2)}) collective-permute-start(f32[15,16,128]{2,1,0:T(8,128)S(1)} %gate.1.refs_4_), channel_id=1, source_target_pairs={{0,8},{4,12},{8,0},{12,4},{16,24},{20,28},{24,16},{28,20},{1,9},{5... | collective-permute-start | bytes 368648 | tf_op jit(solution)/shard_map/ppermute | solution.py:795
  15.2 7.5 %collective-permute-start.6 = (f32[15,16,128]{2,1,0:T(8,128)S(1)}, f32[15,16,128]{2,1,0:T(8,128)S(1)}, u32[]{:S(2)}, u32[]{:S(2)}) collective-permute-start(f32[15,16,128]{2,1,0:T(8,128)S(1)} %gate.1.refs_4_), channel_id=1, source_target_pairs={{0,12},{4,8},{8,4},{12,0},{16,28},{20,24},{24,20},{28,16},{1,13},{... | collective-permute-start | bytes 368648 | tf_op jit(solution)/shard_map/ppermute | solution.py:795
  17.6 10.2 %collective-permute-start.7 = (f32[20,16,128]{2,1,0:T(8,128)S(1)}, f32[20,16,128]{2,1,0:T(8,128)S(1)}, u32[]{:S(2)}, u32[]{:S(2)}) collective-permute-start(f32[20,16,128]{2,1,0:T(8,128)S(1)} %get-tuple-element.31.own_b), channel_id=1, source_target_pairs={{4,8},{8,4},{12,16},{16,12},{20,24},{24,20},{28,0},{0,28},{5,9},{9... | collective-permute-start | bytes 491528 | tf_op jit(solution)/shard_map/ppermute | solution.py:812
  21.1 3.3 %collective-permute-start.8 = (f32[5,16,384]{2,1,0:T(8,128)S(1)}, f32[5,16,384]{2,1,0:T(8,128)S(1)}, u32[]{:S(2)}, u32[]{:S(2)}) collective-permute-start(f32[5,16,384]{2,1,0:T(8,128)S(1)} %get-tuple-element.32), channel_id=1, source_target_pairs={{0,1},{1,0},{2,3},{3,2},{4,5},{5,4},{6,7},{7,6},{8,9},{9,8},{10,11... | collective-permute-start | bytes 368648 | tf_op jit(solution)/shard_map/ppermute | solution.py:814
  21.1 5.1 %collective-permute-start.9 = (f32[5,16,384]{2,1,0:T(8,128)S(1)}, f32[5,16,384]{2,1,0:T(8,128)S(1)}, u32[]{:S(2)}, u32[]{:S(2)}) collective-permute-start(f32[5,16,384]{2,1,0:T(8,128)S(1)} %get-tuple-element.33), channel_id=1, source_target_pairs={{1,2},{2,1},{3,0},{0,3},{5,6},{6,5},{7,4},{4,7},{9,10},{10,9},{11,... | collective-permute-start | bytes 368648 | tf_op jit(solution)/shard_map/ppermute | solution.py:815
  23.7 5.8 %collective-permute-start.10 = (f32[5,16,128]{2,1,0:T(8,128)S(1)}, f32[5,16,128]{2,1,0:T(8,128)S(1)}, u32[]{:S(2)}, u32[]{:S(2)}) collective-permute-start(f32[5,16,128]{2,1,0:T(8,128)S(1)} %get-tuple-element.36.own_a), channel_id=1, source_target_pairs={{0,1},{1,0},{2,3},{3,2},{4,5},{5,4},{6,7},{7,6},{8,9},{9,8},{10,11... | collective-permute-start | bytes 122888 | tf_op jit(solution)/shard_map/ppermute | solution.py:819
  23.7 5.7 %collective-permute-start.11 = (f32[5,16,128]{2,1,0:T(8,128)S(1)}, f32[5,16,128]{2,1,0:T(8,128)S(1)}, u32[]{:S(2)}, u32[]{:S(2)}) collective-permute-start(f32[5,16,128]{2,1,0:T(8,128)S(1)} %get-tuple-element.37.own_b), channel_id=1, source_target_pairs={{1,2},{2,1},{3,0},{0,3},{5,6},{6,5},{7,4},{4,7},{9,10},{10,9},{11,... | collective-permute-start | bytes 122888 | tf_op jit(solution)/shard_map/ppermute | solution.py:820

commit v6 on v5

--- a/solution.py
+++ b/solution.py
@@ -153,6 +153,8 @@
         self.rest = NEAR - self.full
         self.beside = LANES // max(self.full, 1)
         self.groups = -(-self.fields * self.planes // self.beside)
+        self.spare = LANES - self.beside * self.full
+        self.chunks = -(-self.fields * self.rest // max(self.spare, 1))
         self.early = tuple(range(sectors // 2 + 1))
         self.late = tuple(range(sectors // 2 + 1, sectors))
         self.depth = 256
@@ -172,6 +174,8 @@
             and plan.planes == plan.theta
             and plan.rest * plan.fields <= LANES
             and plan.groups % 2 == 0
+            and plan.spare > 0
+            and plan.chunks <= plan.groups
             and slabs % 2 == 0
             and 3 * len(plan.early) * plan.theta <= plan.depth
             and plan.radial % LANES == 0
@@ -253,7 +257,9 @@
                 ref[base + f * tiles + tile, k : k + 1, :] = jnp.where(keep_high, high, low)
 
 
-def pack_kernel(plan, x_ref, out_ref, wide_ref):
+def pack_kernel(plan, x_ref, out_ref, wide_ref, rest_ref):
+    odd_plane = lax.axis_index("ax") % 2
+    rest_ref[...] = x_ref[:, odd_plane * (plan.planes - 1), :, LANES:]
     shape = (plan.theta, LANES)
     lane = lax.broadcasted_iota(jnp.int32, shape, 1)
     row = lax.broadcasted_iota(jnp.int32, shape, 0)
@@ -270,17 +276,21 @@
             group = part
             if first // plan.full == plan.beside - 1 or (f, k) == (plan.fields - 1, plan.planes - 1):
                 out_ref[number] = group
-                wide_ref[number] = group
+                if number >= plan.chunks:
+                    wide_ref[number] = group
             alternating = jnp.sum(x * sign, axis=0, keepdims=True)
             sums[f] = jnp.where(row == k, alternating, sums[f])
     last = sums[0]
     for f in range(plan.fields):
         start = f * plan.rest
         last = jnp.where(lane >= start, moved(sums[f], start - plan.full), last)
-    out_ref[plan.groups] = last
-    wide_ref[plan.groups] = last
+    for c in range(plan.chunks):
+        start = LANES - plan.spare
+        group = jnp.where(lane >= start, moved(last, start - plan.spare * c), out_ref[c])
+        out_ref[c] = group
+        wide_ref[c] = group
     even_theta = lax.axis_index("az") % 2 == 0
-    pick_columns(plan, x_ref, even_theta, wide_ref, plan.groups + 1)
+    pick_columns(plan, x_ref, even_theta, wide_ref, plan.groups)
 
 
 def pack(plan, fields):
@@ -290,10 +300,11 @@
     return pl.pallas_call(
         functools.partial(pack_kernel, plan),
         in_specs=[inside],
-        out_specs=[inside] * 2,
+        out_specs=[inside] * 3,
         out_shape=[
-            jax.ShapeDtypeStruct((plan.groups + 1, plan.theta, LANES), f32),
-            jax.ShapeDtypeStruct((plan.groups + 1 + columns, plan.theta, LANES), f32),
+            jax.ShapeDtypeStruct((plan.groups, plan.theta, LANES), f32),
+            jax.ShapeDtypeStruct((plan.groups + columns, plan.theta, LANES), f32),
+            jax.ShapeDtypeStruct((plan.fields, plan.theta, plan.radial - LANES), f32),
         ],
         compiler_params=pltpu.CompilerParams(vmem_limit_bytes=VMEM_LIMIT),
         name="pack",
@@ -301,12 +312,8 @@
     )(fields)
 
 
-def edges_kernel(plan, x_ref, after_ref, az_b, ax_a, ax_b):
+def edges_kernel(plan, x_ref, after_ref, az_b):
     del after_ref
-    odd_plane = lax.axis_index("ax") % 2
-    last = plan.planes - 1
-    ax_a[...] = x_ref[:, (1 - odd_plane) * last, :, LANES:]
-    ax_b[...] = x_ref[:, odd_plane * last, :, LANES:]
     even_theta = lax.axis_index("az") % 2 == 0
     pick_columns(plan, x_ref, jnp.logical_not(even_theta), az_b, 0)
 
@@ -314,13 +321,12 @@
 def edges(plan, fields, after):
     f32 = jnp.float32
     columns = plan.fields * plan.radial // LANES
-    plane = jax.ShapeDtypeStruct((plan.fields, plan.theta, plan.radial - LANES), f32)
     inside = pl.BlockSpec(memory_space=pltpu.VMEM)
     return pl.pallas_call(
         functools.partial(edges_kernel, plan),
         in_specs=[inside] * 2,
-        out_specs=[inside] * 3,
-        out_shape=[jax.ShapeDtypeStruct((columns, plan.theta, LANES), f32), plane, plane],
+        out_specs=inside,
+        out_shape=jax.ShapeDtypeStruct((columns, plan.theta, LANES), f32),
         compiler_params=pltpu.CompilerParams(vmem_limit_bytes=VMEM_LIMIT),
         name="edges",
         cost_estimate=pl.CostEstimate(flops=0, bytes_accessed=1000000, transcendentals=0),
@@ -358,24 +364,6 @@
     up = jnp.where(row == last, after, pltpu.roll(x, last, 0))
     down = jnp.where(row == 0, before, pltpu.roll(x, 1, 0))
     return up, down
-
-
-def choose_halos(plan, tiles, az_a, az_b, ax_a, ax_b, side, ends):
-    even_theta = lax.axis_index("az") % 2 == 0
-    even_plane = lax.axis_index("ax") % 2 == 0
-    all_tiles = plan.radial // LANES
-    for f in range(plan.fields):
-        for tile in tiles:
-            here = slice(tile * LANES, (tile + 1) * LANES)
-            number = f * all_tiles + tile
-            a = az_a[plan.groups + 1 + number]
-            b = az_b[number]
-            side[0, number] = jnp.where(even_theta, b, a)
-            side[1, number] = jnp.where(even_theta, a, b)
-            a = ax_a[f, :, here]
-            b = ax_b[f, :, here]
-            ends[0, f, :, here] = jnp.where(even_plane, b, a)
-            ends[1, f, :, here] = jnp.where(even_plane, a, b)
 
 
 def outer_kernel(plan, coef_ref, x_ref, done, token):
@@ -451,12 +439,12 @@
     return jnp.where(even_plane, b, a), jnp.where(even_plane, a, b)
 
 
-def seams(plan, coef_ref, x_ref, own_a, own_b, az_a, az_b, ax_a, ax_b, part_ref, done):
+def seams(plan, coef_ref, x_ref, own_a, own_b, az_a, az_b, ax_b, part_ref, done):
     nu_dt = viscosity * time_step
     half = 0.5 * time_step
     planes = plan.planes
     tiles = plan.radial // LANES
-    base = plan.groups + 1
+    base = plan.groups
     even_theta = lax.axis_index("az") % 2 == 0
     last = plan.theta - 1
     row = lax.broadcasted_iota(jnp.int32, (plan.theta, LANES), 0)
@@ -487,7 +475,7 @@
             if f == 1:
                 low = low - cross * before[0]
                 high = high + cross * after[0]
-            below, above = slabs_beside(ax_a[f, :, there], ax_b[f, :, there])
+            below, above = slabs_beside(0.0, ax_b[f, :, there])
             for k in range(planes):
                 value = part_ref[k, f, :, there]
                 value = value + jnp.where(row == 0, low[k : k + 1], 0.0)
@@ -531,25 +519,36 @@
     )
 
 
-def early_kernel(plan, forward_ref, *refs):
+def alternating_sums(plan, pieces):
+    lane = lax.broadcasted_iota(jnp.int32, (plan.theta, LANES), 1)
+    total = jnp.zeros((plan.theta, LANES), jnp.float32)
+    for c in range(plan.chunks):
+        value = pieces[0][c]
+        for piece in pieces[1:]:
+            value = value + piece[c]
+        start = plan.spare * c
+        here = (lane >= start) & (lane < start + plan.spare)
+        total = jnp.where(here, moved(value, start + plan.spare - LANES), total)
+    return total
+
+
+def early_kernel(plan, forward_ref, after_ref, *refs):
+    del after_ref
     pieces = refs[: len(plan.early)]
     spectra_ref, total_ref = refs[len(plan.early) :]
     table = forward_ref[lax.axis_index("az")]
     for g in range(0, plan.groups, 2):
         both = halves(two_groups(pieces, g), plan.depth)
         spectra_ref[g // 2] = jnp.dot(table, both, preferred_element_type=jnp.float32)
-    total = pieces[0][plan.groups]
-    for piece in pieces[1:]:
-        total = total + piece[plan.groups]
-    total_ref[...] = total
-
-
-def early_spectra(plan, pieces):
+    total_ref[...] = alternating_sums(plan, pieces)
+
+
+def early_spectra(plan, pieces, after):
     inside = pl.BlockSpec(memory_space=pltpu.VMEM)
     f32 = jnp.float32
     return pl.pallas_call(
         functools.partial(early_kernel, plan),
-        in_specs=[inside] * (1 + len(pieces)),
+        in_specs=[inside] * (2 + len(pieces)),
         out_specs=[inside] * 2,
         out_shape=[
             jax.ShapeDtypeStruct((plan.groups // 2, 2 * plan.modes, 2 * LANES), f32),
@@ -558,7 +557,7 @@
         compiler_params=pltpu.CompilerParams(vmem_limit_bytes=VMEM_LIMIT),
         name="early",
         cost_estimate=pl.CostEstimate(flops=200000000, bytes_accessed=1500000, transcendentals=0),
-    )(jnp.asarray(plan.forward(plan.early)), *pieces)
+    )(jnp.asarray(plan.forward(plan.early)), after, *pieces)
 
 
 def filter_kernel(plan, x_ref, forward_ref, inverse_ref, mask_ref, early_ref, early_total, *refs):
@@ -584,9 +583,7 @@
             across_ref[g + i] = state[theta : 2 * theta, lanes]
             edge_ref[g + i] = state[2 * theta : 2 * theta + 8, lanes]
 
-    total = early_total[...]
-    for piece in pieces:
-        total = total + piece[plan.groups]
+    total = early_total[...] + alternating_sums(plan, pieces)
     total = total * (1.0 / plan.total)
     lane = lax.broadcasted_iota(jnp.int32, (plan.planes, LANES), 1)
     for f in range(plan.fields):
@@ -600,10 +597,11 @@
         for f in range(plan.fields):
             number, first = plan.place(f, k)
             raw = x_ref[f, k, :, :LANES] - sign * sums_ref[f, k : k + 1]
-            ref[f] = jnp.where(lane < plan.full, moved(own_ref[number], -first), raw)
+            ref[f, :, :LANES] = jnp.where(lane < plan.full, moved(own_ref[number], -first), raw)
 
     def both_messages(a, b):
         message(message_a, a)
+        message_a[:, :, LANES:] = x_ref[:, a, :, LANES:]
         message(message_b, b)
 
     pl.when(odd_plane == 1)(lambda: both_messages(0, plan.planes - 1))
@@ -624,7 +622,7 @@
             cube,
             jax.ShapeDtypeStruct((plan.groups, 8, LANES), f32),
             jax.ShapeDtypeStruct((plan.fields, plan.planes, LANES), f32),
-            plane,
+            jax.ShapeDtypeStruct((plan.fields, plan.theta, plan.radial), f32),
             plane,
         ],
         compiler_params=pltpu.CompilerParams(vmem_limit_bytes=VMEM_LIMIT),
@@ -642,17 +640,19 @@
 
 def inner_kernel(
     plan, coef_ref, own_ref, across_ref, edge_ref, sums_ref, x_ref, own_a, own_b, az_a, az_b,
-    ax_a, ax_b, part_ref, out_ref, done, far_done, state, outs
+    ax_b, part_ref, out_ref, done, ends, far_done, state, outs
 ):
     planes = plan.planes
-    seams(plan, coef_ref, x_ref, own_a, own_b, az_a, az_b, ax_a, ax_b, part_ref, far_done)
+    seams(plan, coef_ref, x_ref, own_a, own_b, az_a, az_b, ax_b, part_ref, far_done)
     beyond = pl.ds(LANES, plan.radial - LANES)
     stores = [
         pltpu.make_async_copy(far_done.at[k], out_ref.at[:, k, :, beyond], outs.at[k])
-        for k in range(planes)
+        for k in range(1, planes - 1)
     ]
     for copy in stores:
         copy.start()
+    ends[0] = far_done[0]
+    ends[1] = far_done[planes - 1]
     theta = plan.theta
     tiles = plan.radial // LANES
     shape = (theta, LANES)
@@ -677,7 +677,7 @@
     befores = []
     afters = []
     for f in range(plan.fields):
-        a = az_a[plan.groups + 1 + f * tiles]
+        a = az_a[plan.groups + f * tiles]
         b = az_b[f * tiles]
         befores.append(jnp.where(even_theta, b, a) + sums_ref[f])
         afters.append(jnp.where(even_theta, a, b) - sums_ref[f])
@@ -708,16 +708,17 @@
         copy.wait()
 
 
-def inner(plan, coef, parts, fields, own, sides, rests, part):
+def inner(plan, coef, parts, fields, own, sides, rest, part):
     inside = pl.BlockSpec(memory_space=pltpu.VMEM)
     f32 = jnp.float32
     return pl.pallas_call(
         functools.partial(inner_kernel, plan),
-        in_specs=[inside] * 13,
-        out_specs=[pl.BlockSpec(memory_space=pl.ANY), inside],
+        in_specs=[inside] * 12,
+        out_specs=[pl.BlockSpec(memory_space=pl.ANY), inside, inside],
         out_shape=[
             jax.ShapeDtypeStruct(fields.shape, f32),
             jax.ShapeDtypeStruct((plan.planes, plan.fields, plan.theta, LANES), f32),
+            jax.ShapeDtypeStruct((2, *part.shape[1:]), f32),
         ],
         scratch_shapes=[
             pltpu.VMEM(part.shape, f32),
@@ -727,15 +728,14 @@
         compiler_params=pltpu.CompilerParams(vmem_limit_bytes=VMEM_LIMIT),
         name="inner",
         cost_estimate=pl.CostEstimate(flops=6000000, bytes_accessed=2500000, transcendentals=0),
-    )(coef, *parts, fields, *own, *sides, *rests, part)
-
-
-def finish_kernel(plan, near_ref, own_a, own_b, ax_a, ax_b, other_ref, out_ref, ends, sems):
+    )(coef, *parts, fields, *own, *sides, rest, part)
+
+
+def finish_kernel(plan, near_ref, far_ref, own_a, own_b, ax_a, ax_b, other_ref, out_ref, ends, sems):
     del other_ref
     planes = plan.planes
-    first = pl.ds(0, LANES)
     copies = [
-        pltpu.make_async_copy(near_ref.at[k], out_ref.at[:, k, :, first], sems.at[k])
+        pltpu.make_async_copy(near_ref.at[k], out_ref.at[:, k, :, pl.ds(0, LANES)], sems.at[k])
         for k in range(1, planes - 1)
     ]
     for copy in copies:
@@ -743,38 +743,48 @@
     even_plane = lax.axis_index("ax") % 2 == 0
     nu_dt = viscosity * time_step
     half = 0.5 * time_step
-    sent_a = own_a[2]
-    sent_b = own_b[2]
-    factor_low = nu_dt + half * jnp.where(even_plane, sent_b, sent_a)
-    factor_high = nu_dt - half * jnp.where(even_plane, sent_a, sent_b)
-    for f in range(plan.fields):
-        below, above = slabs_beside(ax_a[f], ax_b[f])
-        ends[0, f] = near_ref[0, f] + factor_low * below
-        ends[1, f] = near_ref[planes - 1, f] + factor_high * above
+    for tile in range(plan.radial // LANES):
+        here = slice(tile * LANES, (tile + 1) * LANES)
+        there = slice((tile - 1) * LANES, tile * LANES)
+        sent_a = own_a[2, :, here]
+        if tile == 0:
+            sent_b = own_b[2]
+            factor_low = nu_dt + half * jnp.where(even_plane, sent_b, sent_a)
+            factor_high = nu_dt - half * jnp.where(even_plane, sent_a, sent_b)
+        else:
+            factor_low = nu_dt + half * sent_a
+            factor_high = nu_dt - half * sent_a
+        for f in range(plan.fields):
+            b = ax_b[f] if tile == 0 else 0.0
+            below, above = slabs_beside(ax_a[f, :, here], b)
+            low = near_ref[0, f] if tile == 0 else far_ref[0, f, :, there]
+            high = near_ref[planes - 1, f] if tile == 0 else far_ref[1, f, :, there]
+            ends[0, f, :, here] = low + factor_low * below
+            ends[1, f, :, here] = high + factor_high * above
     for end, k in ((0, 0), (1, planes - 1)):
-        copies.append(pltpu.make_async_copy(ends.at[end], out_ref.at[:, k, :, first], sems.at[k]))
+        copies.append(pltpu.make_async_copy(ends.at[end], out_ref.at[:, k], sems.at[k]))
         copies[-1].start()
     for copy in copies:
         copy.wait()
 
 
-def finish(plan, near, sent, messages, partial):
+def finish(plan, near, far, sent, messages, partial):
     anywhere = pl.BlockSpec(memory_space=pl.ANY)
     inside = pl.BlockSpec(memory_space=pltpu.VMEM)
     return pl.pallas_call(
         functools.partial(finish_kernel, plan),
-        in_specs=[inside] * 5 + [anywhere],
+        in_specs=[inside] * 6 + [anywhere],
         out_specs=anywhere,
         out_shape=jax.ShapeDtypeStruct(partial.shape, jnp.float32),
-        input_output_aliases={5: 0},
+        input_output_aliases={6: 0},
         scratch_shapes=[
-            pltpu.VMEM((2, plan.fields, plan.theta, LANES), jnp.float32),
+            pltpu.VMEM((2, plan.fields, plan.theta, plan.radial), jnp.float32),
             pltpu.SemaphoreType.DMA((plan.planes,)),
         ],
         compiler_params=pltpu.CompilerParams(vmem_limit_bytes=VMEM_LIMIT),
         name="finish",
         cost_estimate=pl.CostEstimate(flops=100000, bytes_accessed=1500000, transcendentals=0),
-    )(near, *sent, *messages, partial)
+    )(near, far, *sent, *messages, partial)
 
 
 def pairs(count, start):
@@ -794,7 +804,8 @@
     def send(x, distance):
         return lax.ppermute(x, "az", [(i, i ^ distance) for i in range(sectors)])
 
-    packed, wide = pack(plan, fields)
+    packed, wide, rest = pack(plan, fields)
+    rest_message = lax.ppermute(rest, "ax", pairs(slabs, 1))
     half = sectors // 2
     pieces = [None] * sectors
     pieces[0] = packed
@@ -807,20 +818,17 @@
     for p in range(half - 1, 0, -1):
         pieces[half + p] = send(onward, p)
     pieces[half] = onward
-    early = early_spectra(plan, pieces[: half + 1])
-    column, rest_a, rest_b = edges(plan, fields, early[1])
+    early = early_spectra(plan, pieces[: half + 1], rest_message)
+    column = edges(plan, fields, early[1])
     sides = (pieces[1], lax.ppermute(column, "az", pairs(sectors, 1)))
-    rests = (
-        lax.ppermute(rest_a, "ax", pairs(slabs, 0)),
-        lax.ppermute(rest_b, "ax", pairs(slabs, 1)),
-    )
     *parts, message_a, message_b = filtered(plan, fields, pieces[half + 1 :], early)
     messages = (
         lax.ppermute(message_a, "ax", pairs(slabs, 0)),
         lax.ppermute(message_b, "ax", pairs(slabs, 1)),
     )
-    partial, near = inner(plan, coef, parts, fields, (wide, column), sides, rests, part)
-    return finish(plan, near, (message_a, message_b), messages, partial)
+    own = (wide, column)
+    partial, near, ends = inner(plan, coef, parts, fields, own, sides, rest_message, part)
+    return finish(plan, near, ends, (message_a, message_b), messages, partial)
 
 
 def on_device(fields):

time: 30.6 us -> 29.8 us (0.974)
  starting transfers between devices: 17 us -> 14.7 us
  waiting for transfers between devices: 4.84 us -> 6.37 us
    ppermute x7, waiting for transfers between devices: 1.44 us -> 3.86 us  [send(): return lax.ppermute(x, 'az', [(i, i ^ distance) for i in range(sectors)])]
    ppermute x2 -> x1, waiting for transfers between devices: 1.82 us -> 0.01 us  [fast_on_device(): rest_message = lax.ppermute(rest, 'ax', pairs(slabs, 1))]
    ppermute x2 -> x1, starting transfers between devices: 1.64 us -> 0.01 us  [fast_on_device(): rest_message = lax.ppermute(rest, 'ax', pairs(slabs, 1))]
    ppermute x1, starting transfers between devices: 3.52 us -> 1.98 us  [fast_on_device(): sides = (pieces[1], lax.ppermute(column, 'az', pairs(sectors, 1)))]
    ppermute x1, waiting for transfers between devices: 1.57 us -> 2.49 us  [fast_on_device(): sides = (pieces[1], lax.ppermute(column, 'az', pairs(sectors, 1)))]
    ppermute x7, starting transfers between devices: 11.1 us -> 11.7 us  [send(): return lax.ppermute(x, 'az', [(i, i ^ distance) for i in range(sectors)])]
    ppermute x1, starting transfers between devices: 0.62 us -> 0.97 us  [fast_on_device(): lax.ppermute(message_b, 'ax', pairs(slabs, 1))]
  transfers between devices with their start and end apart: 12 -> 11, of which waited for: 3 -> 4; matrix products, arithmetic and copies ran while one was open for 0% -> 0% of each run, Pallas kernels for 18% -> 18%
where the time goes in v6:
time: 29.8 us; the launch traced here: 29.6 us
  starting transfers between devices  14.7 us (49%)
  Pallas kernels  6.65 us (22%)
  waiting for transfers between devices  6.37 us (21%)
  local copies, waits for them, and re-layouts  1.77 us (6%)
    ppermute x7, starting transfers between devices, send(): return lax.ppermute(x, 'az', [(i, i ^ distance) for i in range(sectors)])  11.7 us
    ppermute x7, waiting for transfers between devices, send(): return lax.ppermute(x, 'az', [(i, i ^ distance) for i in range(sectors)])  3.86 us
    ppermute x1, waiting for transfers between devices, fast_on_device(): sides = (pieces[1], lax.ppermute(column, 'az', pairs(sectors, 1)))  2.49 us
    pallas_call x1, Pallas kernels, outer(): pl.pallas_call(functools.partial(outer_kernel, plan), in_specs=[inside] *...  2.26 us
    ppermute x1, starting transfers between devices, fast_on_device(): sides = (pieces[1], lax.ppermute(column, 'az', pairs(sectors, 1)))  1.98 us
    unnamed x14, local copies, waits for them, and re-layouts  1.77 us
    pallas_call x1, Pallas kernels, inner(): pl.pallas_call(functools.partial(inner_kernel, plan), in_specs=[inside] *...  1.59 us
    pallas_call x1, Pallas kernels, finish(): pl.pallas_call(functools.partial(finish_kernel, plan), in_specs=[inside]...  1.06 us
  transfers between devices with their start and end apart: 11, of which 4 were waited for; matrix products, arithmetic and copies ran while one was open for 0% of the time, Pallas kernels for 18%

profile of v6, /device:TPU:0, one launch (start us, length us, event | category | flops | bytes accessed | tf_op | source)
XLA Modules:
  0.0 29.6 jit_solution(5587459056530231825)
XLA Ops:
  0.0 0.0 copy-start
  0.0 1.7 %copy-done = f32[5,16,16,512]{3,2,1,0:T(8,128)S(1)} copy-done((f32[5,16,16,512]{3,2,1,0:T(8,128)S(1)}, f32[5,16,16,512]{3,2,1,0:T(8,128)}, u32[]{:S(2)}) %copy-start) | copy-done | bytes 2621464
  1.7 0.0 copy-start.6
  1.7 0.0 copy-start.3
  1.7 0.3 %pack.1 = (f32[14,16,128]{2,1,0:T(8,128)S(1)}, f32[34,16,128]{2,1,0:T(8,128)S(1)}, f32[5,16,384]{2,1,0:T(8,128)S(1)}) custom-call(f32[5,16,16,512]{3,2,1,0:T(8,128)S(1)} %copy-done), custom_call_target="tpu_custom_call" | custom-call | flops 1000000 | bytes 800000 | tf_op jit(solution)/shard_map/pack/pallas_call | solution.py:300
  2.1 0.0 copy-start.1
  2.1 3.0 %collective-permute-start.1 = (f32[34,16,128]{2,1,0:T(8,128)S(1)}, f32[34,16,128]{2,1,0:T(8,128)S(1)}, u32[]{:S(2)}, u32[]{:S(2)}) collective-permute-start(f32[34,16,128]{2,1,0:T(8,128)S(1)} %get-tuple-element.23.own_a), channel_id=1, source_target_pairs={{0,4},{4,0},{8,12},{12,8},{16,20},{20,16},{24,28},{28,24},{1,5},{5... | collective-permute-start | bytes 835592 | tf_op jit(solution)/shard_map/ppermute | solution.py:805
  5.1 2.6 %collective-permute-start.4 = (f32[14,16,128]{2,1,0:T(8,128)S(1)}, f32[14,16,128]{2,1,0:T(8,128)S(1)}, u32[]{:S(2)}, u32[]{:S(2)}) collective-permute-start(f32[14,16,128]{2,1,0:T(8,128)S(1)} %get-tuple-element.22.refs_0_), channel_id=1, source_target_pairs={{0,16},{4,20},{8,24},{12,28},{16,0},{20,4},{24,8},{28,12},{1,17},{... | collective-permute-start | bytes 344072 | tf_op jit(solution)/shard_map/ppermute | solution.py:805
  7.7 1.6 %collective-permute-start.2 = (f32[14,16,128]{2,1,0:T(8,128)S(1)}, f32[14,16,128]{2,1,0:T(8,128)S(1)}, u32[]{:S(2)}, u32[]{:S(2)}) collective-permute-start(f32[14,16,128]{2,1,0:T(8,128)S(1)} %get-tuple-element.22.refs_0_), channel_id=1, source_target_pairs={{0,8},{4,12},{8,0},{12,4},{16,24},{20,28},{24,16},{28,20},{1,9},{5... | collective-permute-start | bytes 344072 | tf_op jit(solution)/shard_map/ppermute | solution.py:805
  9.3 0.4 %collective-permute-start.3 = (f32[14,16,128]{2,1,0:T(8,128)S(1)}, f32[14,16,128]{2,1,0:T(8,128)S(1)}, u32[]{:S(2)}, u32[]{:S(2)}) collective-permute-start(f32[14,16,128]{2,1,0:T(8,128)S(1)} %get-tuple-element.22.refs_0_), channel_id=1, source_target_pairs={{0,12},{4,8},{8,4},{12,0},{16,28},{20,24},{24,20},{28,16},{1,13},{... | collective-permute-start | bytes 344072 | tf_op jit(solution)/shard_map/ppermute | solution.py:805
  9.7 0.0 collective-permute-start
  9.7 0.0 copy-done.6
  9.7 2.3 %outer.1 = (f32[16,5,16,384]{3,2,1,0:T(8,128)S(1)}, f32[8,128]{1,0:T(8,128)S(1)}) custom-call(f32[8,512]{1,0:T(8,128)S(1)} %copy-done.6, f32[5,16,16,512]{3,2,1,0:T(8,128)S(1)} %copy-done), custom_call_target="tpu_custom_call" | custom-call | flops 16000000 | bytes 5000000 | tf_op jit(solution)/shard_map/outer/pallas_call | solution.py:421
  12.0 0.0 copy-start.2
  12.0 0.0 copy-start.4
  12.0 0.0 copy-start.5
  12.0 1.0 %collective-permute-done.4.x_ref = f32[14,16,128]{2,1,0:T(8,128)S(1)} collective-permute-done((f32[14,16,128]{2,1,0:T(8,128)S(1)}, f32[14,16,128]{2,1,0:T(8,128)S(1)}, u32[]{:S(2)}, u32[]{:S(2)}) %collective-permute-start.4) | collective-permute-done | bytes 114720 | tf_op jit(solution)/shard_map/ppermute | solution.py:805
  13.1 0.5 %collective-permute-start.5 = (f32[14,16,128]{2,1,0:T(8,128)S(1)}, f32[14,16,128]{2,1,0:T(8,128)S(1)}, u32[]{:S(2)}, u32[]{:S(2)}) collective-permute-start(f32[14,16,128]{2,1,0:T(8,128)S(1)} %gate.1.refs_4_), channel_id=1, source_target_pairs={{0,4},{4,0},{8,12},{12,8},{16,20},{20,16},{24,28},{28,24},{1,5},{5... | collective-permute-start | bytes 344072 | tf_op jit(solution)/shard_map/ppermute | solution.py:805
  13.6 1.0 %collective-permute-done.2.refs_2_ = f32[14,16,128]{2,1,0:T(8,128)S(1)} collective-permute-done((f32[14,16,128]{2,1,0:T(8,128)S(1)}, f32[14,16,128]{2,1,0:T(8,128)S(1)}, u32[]{:S(2)}, u32[]{:S(2)}) %collective-permute-start.2) | collective-permute-done | bytes 114720 | tf_op jit(solution)/shard_map/ppermute | solution.py:805
  14.6 1.5 %collective-permute-start.6 = (f32[14,16,128]{2,1,0:T(8,128)S(1)}, f32[14,16,128]{2,1,0:T(8,128)S(1)}, u32[]{:S(2)}, u32[]{:S(2)}) collective-permute-start(f32[14,16,128]{2,1,0:T(8,128)S(1)} %gate.1.refs_4_), channel_id=1, source_target_pairs={{0,8},{4,12},{8,0},{12,4},{16,24},{20,28},{24,16},{28,20},{1,9},{5... | collective-permute-start | bytes 344072 | tf_op jit(solution)/shard_map/ppermute | solution.py:805
  16.1 0.0 collective-permute-done.3.refs_3_
  16.1 2.1 %collective-permute-start.7 = (f32[14,16,128]{2,1,0:T(8,128)S(1)}, f32[14,16,128]{2,1,0:T(8,128)S(1)}, u32[]{:S(2)}, u32[]{:S(2)}) collective-permute-start(f32[14,16,128]{2,1,0:T(8,128)S(1)} %gate.1.refs_4_), channel_id=1, source_target_pairs={{0,12},{4,8},{8,4},{12,0},{16,28},{20,24},{24,20},{28,16},{1,13},{... | collective-permute-start | bytes 344072 | tf_op jit(solution)/shard_map/ppermute | solution.py:805
  18.2 0.0 collective-permute-done.after_ref.ax_b
  18.2 0.0 collective-permute-done.1.refs_1_.az_a
  18.2 0.0 copy-done.3
  18.2 0.3 %early.1 = (f32[7,128,256]{2,1,0:T(8,128)S(1)}, f32[16,128]{1,0:T(8,128)S(1)}) custom-call(bf16[8,128,256]{2,1,0:T(8,128)(2,1)S(1)} %copy-done.3, f32[5,16,384]{2,1,0:T(8,128)S(1)} %collective-permute-done.after_ref.ax_b, f32[14,16,128]{2,1,0:T(8,128)S(1)} %get-tuple-element.22.refs_0_, f32[34,16,128]{2,1,0:T(8,128)S(1)} %collective-permute-done.1.refs_1_.az_a, ...), custom_call_target="tpu_custom_call" | custom-call | flops 200000000 | bytes 1500000 | tf_op jit(solution)/shard_map/early/pallas_call | solution.py:549
  18.5 0.0 copy-done.1
  18.5 0.2 edges.1.own_b
  18.7 2.0 %collective-permute-start.8 = (f32[20,16,128]{2,1,0:T(8,128)S(1)}, f32[20,16,128]{2,1,0:T(8,128)S(1)}, u32[]{:S(2)}, u32[]{:S(2)}) collective-permute-start(f32[20,16,128]{2,1,0:T(8,128)S(1)} %edges.1.own_b), channel_id=1, source_target_pairs={{4,8},{8,4},{12,16},{16,12},{20,24},{24,20},{28,0},{0,28},{5,9},{9... | collective-permute-start | bytes 491528 | tf_op jit(solution)/shard_map/ppermute | solution.py:823
  20.7 0.0 collective-permute-done.5.refs_0_
  20.7 0.0 collective-permute-done.6.refs_1_
  20.7 1.8 %collective-permute-done.7.refs_2_ = f32[14,16,128]{2,1,0:T(8,128)S(1)} collective-permute-done((f32[14,16,128]{2,1,0:T(8,128)S(1)}, f32[14,16,128]{2,1,0:T(8,128)S(1)}, u32[]{:S(2)}, u32[]{:S(2)}) %collective-permute-start.7) | collective-permute-done | bytes 114720 | tf_op jit(solution)/shard_map/ppermute | solution.py:805
  22.5 0.0 copy-done.2
  22.5 0.0 copy-done.4
  22.5 0.0 copy-done.5
  22.5 0.9 %filter.1 = (f32[14,16,128]{2,1,0:T(8,128)S(1)}, f32[14,16,128]{2,1,0:T(8,128)S(1)}, f32[14,8,128]{2,1,0:T(8,128)S(1)}, f32[5,16,128]{2,1,0:T(8,128)S(1)}, f32[5...) custom-call(f32[5,16,16,512]{3,2,1,0:T(8,128)S(1)} %copy-done.1, bf16[8,128,256]{2,1,0:T(8,128)(2,1)S(1)} %copy-done.2, ...), custom_call_target="tpu_custom_call" | custom-call | flops 200000000 | bytes 1500000 | tf_op jit(solution)/shard_map/filter/pallas_call | solution.py:616
  23.4 0.1 collective-permute-start.9
  23.5 1.0 %collective-permute-start.10 = (f32[5,16,128]{2,1,0:T(8,128)S(1)}, f32[5,16,128]{2,1,0:T(8,128)S(1)}, u32[]{:S(2)}, u32[]{:S(2)}) collective-permute-start(f32[5,16,128]{2,1,0:T(8,128)S(1)} %get-tuple-element.35.own_b), channel_id=1, source_target_pairs={{1,2},{2,1},{3,0},{0,3},{5,6},{6,5},{7,4},{4,7},{9,10},{10,9},{11,... | collective-permute-start | bytes 122888 | tf_op jit(solution)/shard_map/ppermute | solution.py:827
  24.5 2.5 %collective-permute-done.8.az_b = f32[20,16,128]{2,1,0:T(8,128)S(1)} collective-permute-done((f32[20,16,128]{2,1,0:T(8,128)S(1)}, f32[20,16,128]{2,1,0:T(8,128)S(1)}, u32[]{:S(2)}, u32[]{:S(2)}) %collective-permute-start.8) | collective-permute-done | bytes 163872 | tf_op jit(solution)/shard_map/ppermute | solution.py:823
  27.0 1.6 %inner.1 = (f32[5,16,16,512]{3,2,1,0:T(8,128)}, f32[16,5,16,128]{3,2,1,0:T(8,128)S(1)}, f32[2,5,16,384]{3,2,1,0:T(8,128)S(1)}) custom-call(f32[8,512]{1,0:T(8,128)S(1)} %copy-done.6, f32[14,16,128]{2,1,0:T(8,128)S(1)} %get-tuple-element.27.own_ref, f32[14,16,128]{2,1,0:T(8,128)S(1)} %get-tuple-element.28.across_ref, ...), custom_call_target="tpu_custom_call" | custom-call | flops 6000000 | bytes 2500000 | tf_op jit(solution)/shard_map/inner/pallas_call | solution.py:714
  28.6 0.0 collective-permute-done.10.ax_b
  28.6 0.0 collective-permute-done.9.ax_a
  28.6 1.1 %finish.1 = f32[5,16,16,512]{3,2,1,0:T(8,128)} custom-call(f32[16,5,16,128]{3,2,1,0:T(8,128)S(1)} %get-tuple-element.32.near_ref, f32[2,5,16,384]{3,2,1,0:T(8,128)S(1)} %get-tuple-element.33.far_ref, f32[5,16,512]{2,1,0:T(8,128)S(1)} %get-tuple-element.34.own_a, f32[5,16,128]{2,1,0:T(8,128)S(1)} %get-tuple-element.35.own_b, ...), custom_call_target="tpu_custom_call", output_to_operand_aliasing={{}: (6, {})} | custom-call | flops 100000 | bytes 1500000 | tf_op jit(solution)/shard_map/finish/pallas_call | solution.py:774
  (1 shorter events, 0.0 us)
Async XLA Ops:
  0.0 1.7 %copy-start = (f32[5,16,16,512]{3,2,1,0:T(8,128)S(1)}, f32[5,16,16,512]{3,2,1,0:T(8,128)}, u32[]{:S(2)}) copy-start(f32[5,16,16,512]{3,2,1,0:T(8,128)} %x_ref.9) | copy-start | bytes 7864324
  1.7 8.0 %copy-start.6 = (f32[8,512]{1,0:T(8,128)S(1)}, f32[8,512]{1,0:T(8,128)}, u32[]{:S(2)}) copy-start(f32[8,512]{1,0:T(8,128)} %constant.10.clone.coef_ref) | copy-start | bytes 49156
  1.7 16.5 %copy-start.3 = (bf16[8,128,256]{2,1,0:T(8,128)(2,1)S(1)}, bf16[8,128,256]{2,1,0:T(8,128)(2,1)}, u32[]{:S(2)}) copy-start(bf16[8,128,256]{2,1,0:T(8,128)(2,1)} %constant.11.clone.forward_ref) | copy-start | bytes 1572868
  2.1 16.4 %copy-start.1 = (f32[5,16,16,512]{3,2,1,0:T(8,128)S(1)}, f32[5,16,16,512]{3,2,1,0:T(8,128)}, u32[]{:S(2)}) copy-start(f32[5,16,16,512]{3,2,1,0:T(8,128)} %x_ref.9) | copy-start | bytes 7864324
  2.1 16.1 %collective-permute-start.1 = (f32[34,16,128]{2,1,0:T(8,128)S(1)}, f32[34,16,128]{2,1,0:T(8,128)S(1)}, u32[]{:S(2)}, u32[]{:S(2)}) collective-permute-start(f32[34,16,128]{2,1,0:T(8,128)S(1)} %get-tuple-element.23.own_a), channel_id=1, source_target_pairs={{0,4},{4,0},{8,12},{12,8},{16,20},{20,16},{24,28},{28,24},{1,5},{5... | collective-permute-start | bytes 835592 | tf_op jit(solution)/shard_map/ppermute | solution.py:805
  5.1 7.9 %collective-permute-start.4 = (f32[14,16,128]{2,1,0:T(8,128)S(1)}, f32[14,16,128]{2,1,0:T(8,128)S(1)}, u32[]{:S(2)}, u32[]{:S(2)}) collective-permute-start(f32[14,16,128]{2,1,0:T(8,128)S(1)} %get-tuple-element.22.refs_0_), channel_id=1, source_target_pairs={{0,16},{4,20},{8,24},{12,28},{16,0},{20,4},{24,8},{28,12},{1,17},{... | collective-permute-start | bytes 344072 | tf_op jit(solution)/shard_map/ppermute | solution.py:805
  7.7 6.9 %collective-permute-start.2 = (f32[14,16,128]{2,1,0:T(8,128)S(1)}, f32[14,16,128]{2,1,0:T(8,128)S(1)}, u32[]{:S(2)}, u32[]{:S(2)}) collective-permute-start(f32[14,16,128]{2,1,0:T(8,128)S(1)} %get-tuple-element.22.refs_0_), channel_id=1, source_target_pairs={{0,8},{4,12},{8,0},{12,4},{16,24},{20,28},{24,16},{28,20},{1,9},{5... | collective-permute-start | bytes 344072 | tf_op jit(solution)/shard_map/ppermute | solution.py:805
  9.3 6.8 %collective-permute-start.3 = (f32[14,16,128]{2,1,0:T(8,128)S(1)}, f32[14,16,128]{2,1,0:T(8,128)S(1)}, u32[]{:S(2)}, u32[]{:S(2)}) collective-permute-start(f32[14,16,128]{2,1,0:T(8,128)S(1)} %get-tuple-element.22.refs_0_), channel_id=1, source_target_pairs={{0,12},{4,8},{8,4},{12,0},{16,28},{20,24},{24,20},{28,16},{1,13},{... | collective-permute-start | bytes 344072 | tf_op jit(solution)/shard_map/ppermute | solution.py:805
  9.7 8.5 %collective-permute-start = (f32[5,16,384]{2,1,0:T(8,128)S(1)}, f32[5,16,384]{2,1,0:T(8,128)S(1)}, u32[]{:S(2)}, u32[]{:S(2)}) collective-permute-start(f32[5,16,384]{2,1,0:T(8,128)S(1)} %get-tuple-element.21), channel_id=1, source_target_pairs={{1,2},{2,1},{3,0},{0,3},{5,6},{6,5},{7,4},{4,7},{9,10},{10,9},{11,... | collective-permute-start | bytes 368648 | tf_op jit(solution)/shard_map/ppermute | solution.py:808
  12.0 10.5 %copy-start.2 = (bf16[8,128,256]{2,1,0:T(8,128)(2,1)S(1)}, bf16[8,128,256]{2,1,0:T(8,128)(2,1)}, u32[]{:S(2)}) copy-start(bf16[8,128,256]{2,1,0:T(8,128)(2,1)} %constant.12.clone.forward_ref) | copy-start | bytes 1572868
  12.0 10.5 %copy-start.4 = (bf16[8,48,384]{2,1,0:T(8,128)(2,1)S(1)}, bf16[8,48,384]{2,1,0:T(8,128)(2,1)}, u32[]{:S(2)}) copy-start(bf16[8,48,384]{2,1,0:T(8,128)(2,1)} %constant.13.clone.inverse_ref) | copy-start | bytes 884740
  12.0 10.5 %copy-start.5 = (f32[128,128]{1,0:T(8,128)S(1)}, f32[128,128]{1,0:T(8,128)}, u32[]{:S(2)}) copy-start(f32[128,128]{1,0:T(8,128)} %constant.14.clone.mask_ref) | copy-start | bytes 196612
  13.1 7.6 %collective-permute-start.5 = (f32[14,16,128]{2,1,0:T(8,128)S(1)}, f32[14,16,128]{2,1,0:T(8,128)S(1)}, u32[]{:S(2)}, u32[]{:S(2)}) collective-permute-start(f32[14,16,128]{2,1,0:T(8,128)S(1)} %gate.1.refs_4_), channel_id=1, source_target_pairs={{0,4},{4,0},{8,12},{12,8},{16,20},{20,16},{24,28},{28,24},{1,5},{5... | collective-permute-start | bytes 344072 | tf_op jit(solution)/shard_map/ppermute | solution.py:805
  14.6 6.1 %collective-permute-start.6 = (f32[14,16,128]{2,1,0:T(8,128)S(1)}, f32[14,16,128]{2,1,0:T(8,128)S(1)}, u32[]{:S(2)}, u32[]{:S(2)}) collective-permute-start(f32[14,16,128]{2,1,0:T(8,128)S(1)} %gate.1.refs_4_), channel_id=1, source_target_pairs={{0,8},{4,12},{8,0},{12,4},{16,24},{20,28},{24,16},{28,20},{1,9},{5... | collective-permute-start | bytes 344072 | tf_op jit(solution)/shard_map/ppermute | solution.py:805
  16.1 6.4 %collective-permute-start.7 = (f32[14,16,128]{2,1,0:T(8,128)S(1)}, f32[14,16,128]{2,1,0:T(8,128)S(1)}, u32[]{:S(2)}, u32[]{:S(2)}) collective-permute-start(f32[14,16,128]{2,1,0:T(8,128)S(1)} %gate.1.refs_4_), channel_id=1, source_target_pairs={{0,12},{4,8},{8,4},{12,0},{16,28},{20,24},{24,20},{28,16},{1,13},{... | collective-permute-start | bytes 344072 | tf_op jit(solution)/shard_map/ppermute | solution.py:805
  18.7 8.3 %collective-permute-start.8 = (f32[20,16,128]{2,1,0:T(8,128)S(1)}, f32[20,16,128]{2,1,0:T(8,128)S(1)}, u32[]{:S(2)}, u32[]{:S(2)}) collective-permute-start(f32[20,16,128]{2,1,0:T(8,128)S(1)} %edges.1.own_b), channel_id=1, source_target_pairs={{4,8},{8,4},{12,16},{16,12},{20,24},{24,20},{28,0},{0,28},{5,9},{9... | collective-permute-start | bytes 491528 | tf_op jit(solution)/shard_map/ppermute | solution.py:823
  23.4 5.2 %collective-permute-start.9 = (f32[5,16,512]{2,1,0:T(8,128)S(1)}, f32[5,16,512]{2,1,0:T(8,128)S(1)}, u32[]{:S(2)}, u32[]{:S(2)}) collective-permute-start(f32[5,16,512]{2,1,0:T(8,128)S(1)} %get-tuple-element.34.own_a), channel_id=1, source_target_pairs={{0,1},{1,0},{2,3},{3,2},{4,5},{5,4},{6,7},{7,6},{8,9},{9,8},{10,11... | collective-permute-start | bytes 491528 | tf_op jit(solution)/shard_map/ppermute | solution.py:826
  23.5 5.1 %collective-permute-start.10 = (f32[5,16,128]{2,1,0:T(8,128)S(1)}, f32[5,16,128]{2,1,0:T(8,128)S(1)}, u32[]{:S(2)}, u32[]{:S(2)}) collective-permute-start(f32[5,16,128]{2,1,0:T(8,128)S(1)} %get-tuple-element.35.own_b), channel_id=1, source_target_pairs={{1,2},{2,1},{3,0},{0,3},{5,6},{6,5},{7,4},{4,7},{9,10},{10,9},{11,... | collective-permute-start | bytes 122888 | tf_op jit(solution)/shard_map/ppermute | solution.py:827

commit v7 on v6

--- a/solution.py
+++ b/solution.py
@@ -257,9 +257,9 @@
                 ref[base + f * tiles + tile, k : k + 1, :] = jnp.where(keep_high, high, low)
 
 
-def pack_kernel(plan, x_ref, out_ref, wide_ref, rest_ref):
+def pack_kernel(plan, x_ref, out_ref, wide_ref, rest_b):
     odd_plane = lax.axis_index("ax") % 2
-    rest_ref[...] = x_ref[:, odd_plane * (plan.planes - 1), :, LANES:]
+    rest_b[...] = x_ref[:, odd_plane * (plan.planes - 1), :, LANES:]
     shape = (plan.theta, LANES)
     lane = lax.broadcasted_iota(jnp.int32, shape, 1)
     row = lax.broadcasted_iota(jnp.int32, shape, 0)
@@ -296,6 +296,7 @@
 def pack(plan, fields):
     f32 = jnp.float32
     columns = plan.fields * plan.radial // LANES
+    plane = jax.ShapeDtypeStruct((plan.fields, plan.theta, plan.radial - LANES), f32)
     inside = pl.BlockSpec(memory_space=pltpu.VMEM)
     return pl.pallas_call(
         functools.partial(pack_kernel, plan),
@@ -304,7 +305,7 @@
         out_shape=[
             jax.ShapeDtypeStruct((plan.groups, plan.theta, LANES), f32),
             jax.ShapeDtypeStruct((plan.groups + columns, plan.theta, LANES), f32),
-            jax.ShapeDtypeStruct((plan.fields, plan.theta, plan.radial - LANES), f32),
+            plane,
         ],
         compiler_params=pltpu.CompilerParams(vmem_limit_bytes=VMEM_LIMIT),
         name="pack",
@@ -312,8 +313,10 @@
     )(fields)
 
 
-def edges_kernel(plan, x_ref, after_ref, az_b):
+def edges_kernel(plan, x_ref, after_ref, az_b, rest_a):
     del after_ref
+    even_plane = 1 - lax.axis_index("ax") % 2
+    rest_a[...] = x_ref[:, even_plane * (plan.planes - 1), :, LANES:]
     even_theta = lax.axis_index("az") % 2 == 0
     pick_columns(plan, x_ref, jnp.logical_not(even_theta), az_b, 0)
 
@@ -325,8 +328,11 @@
     return pl.pallas_call(
         functools.partial(edges_kernel, plan),
         in_specs=[inside] * 2,
-        out_specs=inside,
-        out_shape=jax.ShapeDtypeStruct((columns, plan.theta, LANES), f32),
+        out_specs=[inside] * 2,
+        out_shape=[
+            jax.ShapeDtypeStruct((columns, plan.theta, LANES), f32),
+            jax.ShapeDtypeStruct((plan.fields, plan.theta, plan.radial - LANES), f32),
+        ],
         compiler_params=pltpu.CompilerParams(vmem_limit_bytes=VMEM_LIMIT),
         name="edges",
         cost_estimate=pl.CostEstimate(flops=0, bytes_accessed=1000000, transcendentals=0),
@@ -439,7 +445,7 @@
     return jnp.where(even_plane, b, a), jnp.where(even_plane, a, b)
 
 
-def seams(plan, coef_ref, x_ref, own_a, own_b, az_a, az_b, ax_b, part_ref, done):
+def seams(plan, coef_ref, x_ref, own_a, own_b, az_a, az_b, ax_a, ax_b, part_ref, done, terms, store):
     nu_dt = viscosity * time_step
     half = 0.5 * time_step
     planes = plan.planes
@@ -450,7 +456,6 @@
     row = lax.broadcasted_iota(jnp.int32, (plan.theta, LANES), 0)
     for tile in range(1, tiles):
         here = slice(tile * LANES, (tile + 1) * LANES)
-        there = slice((tile - 1) * LANES, tile * LANES)
         c2 = coef_ref[1:2, here]
         angular = coef_ref[3:4, here]
         cross = coef_ref[6:7, here]
@@ -475,16 +480,24 @@
             if f == 1:
                 low = low - cross * before[0]
                 high = high + cross * after[0]
-            below, above = slabs_beside(0.0, ax_b[f, :, there])
-            for k in range(planes):
+            terms[0, f * tiles + tile] = low
+            terms[1, f * tiles + tile] = high
+    for k in range(planes):
+        for f in range(plan.fields):
+            for tile in range(1, tiles):
+                here = slice(tile * LANES, (tile + 1) * LANES)
+                there = slice((tile - 1) * LANES, tile * LANES)
                 value = part_ref[k, f, :, there]
-                value = value + jnp.where(row == 0, low[k : k + 1], 0.0)
-                value = value + jnp.where(row == last, high[k : k + 1], 0.0)
-                if k == 0:
-                    value = value + (nu_dt + half * x_ref[2, k, :, here]) * below
-                if k == planes - 1:
-                    value = value + (nu_dt - half * x_ref[2, k, :, here]) * above
+                value = value + jnp.where(row == 0, terms[0, f * tiles + tile, k : k + 1], 0.0)
+                value = value + jnp.where(row == last, terms[1, f * tiles + tile, k : k + 1], 0.0)
+                if k in (0, planes - 1):
+                    below, above = slabs_beside(ax_a[f, :, there], ax_b[f, :, there])
+                    if k == 0:
+                        value = value + (nu_dt + half * x_ref[2, k, :, here]) * below
+                    else:
+                        value = value + (nu_dt - half * x_ref[2, k, :, here]) * above
                 done[k, f, :, there] = value
+        store(k).start()
 
 
 def gate_kernel(x_ref, token_ref, out_ref):
@@ -597,12 +610,12 @@
         for f in range(plan.fields):
             number, first = plan.place(f, k)
             raw = x_ref[f, k, :, :LANES] - sign * sums_ref[f, k : k + 1]
-            ref[f, :, :LANES] = jnp.where(lane < plan.full, moved(own_ref[number], -first), raw)
+            ref[f, :theta] = jnp.where(lane < plan.full, moved(own_ref[number], -first), raw)
 
     def both_messages(a, b):
         message(message_a, a)
-        message_a[:, :, LANES:] = x_ref[:, a, :, LANES:]
         message(message_b, b)
+        message_b[:, theta:] = jnp.zeros((plan.fields, 8, LANES), jnp.float32)
 
     pl.when(odd_plane == 1)(lambda: both_messages(0, plan.planes - 1))
     pl.when(odd_plane == 0)(lambda: both_messages(plan.planes - 1, 0))
@@ -622,8 +635,8 @@
             cube,
             jax.ShapeDtypeStruct((plan.groups, 8, LANES), f32),
             jax.ShapeDtypeStruct((plan.fields, plan.planes, LANES), f32),
-            jax.ShapeDtypeStruct((plan.fields, plan.theta, plan.radial), f32),
             plane,
+            jax.ShapeDtypeStruct((plan.fields, plan.theta + 8, LANES), f32),
         ],
         compiler_params=pltpu.CompilerParams(vmem_limit_bytes=VMEM_LIMIT),
         name="filter",
@@ -640,19 +653,17 @@
 
 def inner_kernel(
     plan, coef_ref, own_ref, across_ref, edge_ref, sums_ref, x_ref, own_a, own_b, az_a, az_b,
-    ax_b, part_ref, out_ref, done, ends, far_done, state, outs
+    ax_a, ax_b, part_ref, out_ref, done, far_done, terms, state, outs
 ):
     planes = plan.planes
-    seams(plan, coef_ref, x_ref, own_a, own_b, az_a, az_b, ax_b, part_ref, far_done)
     beyond = pl.ds(LANES, plan.radial - LANES)
-    stores = [
-        pltpu.make_async_copy(far_done.at[k], out_ref.at[:, k, :, beyond], outs.at[k])
-        for k in range(1, planes - 1)
-    ]
-    for copy in stores:
-        copy.start()
-    ends[0] = far_done[0]
-    ends[1] = far_done[planes - 1]
+
+    def store(k):
+        return pltpu.make_async_copy(far_done.at[k], out_ref.at[:, k, :, beyond], outs.at[k])
+
+    seams(
+        plan, coef_ref, x_ref, own_a, own_b, az_a, az_b, ax_a, ax_b, part_ref, far_done, terms, store
+    )
     theta = plan.theta
     tiles = plan.radial // LANES
     shape = (theta, LANES)
@@ -704,38 +715,39 @@
         result = advance(coef, q, jp, jm, tp, tm, kp, km)
         for f in range(plan.fields):
             done[k, f] = result[f]
-    for copy in stores:
-        copy.wait()
-
-
-def inner(plan, coef, parts, fields, own, sides, rest, part):
+    for k in range(planes):
+        store(k).wait()
+
+
+def inner(plan, coef, parts, fields, own, sides, rests, part):
     inside = pl.BlockSpec(memory_space=pltpu.VMEM)
     f32 = jnp.float32
     return pl.pallas_call(
         functools.partial(inner_kernel, plan),
-        in_specs=[inside] * 12,
-        out_specs=[pl.BlockSpec(memory_space=pl.ANY), inside, inside],
+        in_specs=[inside] * 13,
+        out_specs=[pl.BlockSpec(memory_space=pl.ANY), inside],
         out_shape=[
             jax.ShapeDtypeStruct(fields.shape, f32),
             jax.ShapeDtypeStruct((plan.planes, plan.fields, plan.theta, LANES), f32),
-            jax.ShapeDtypeStruct((2, *part.shape[1:]), f32),
         ],
         scratch_shapes=[
             pltpu.VMEM(part.shape, f32),
+            pltpu.VMEM((2, plan.fields * plan.radial // LANES, plan.planes, LANES), f32),
             pltpu.VMEM((plan.planes, plan.fields, plan.theta, LANES), f32),
             pltpu.SemaphoreType.DMA((plan.planes,)),
         ],
         compiler_params=pltpu.CompilerParams(vmem_limit_bytes=VMEM_LIMIT),
         name="inner",
         cost_estimate=pl.CostEstimate(flops=6000000, bytes_accessed=2500000, transcendentals=0),
-    )(coef, *parts, fields, *own, *sides, rest, part)
-
-
-def finish_kernel(plan, near_ref, far_ref, own_a, own_b, ax_a, ax_b, other_ref, out_ref, ends, sems):
+    )(coef, *parts, fields, *own, *sides, *rests, part)
+
+
+def finish_kernel(plan, near_ref, own_a, own_b, ax_a, ax_b, other_ref, out_ref, ends, sems):
     del other_ref
     planes = plan.planes
+    first = pl.ds(0, LANES)
     copies = [
-        pltpu.make_async_copy(near_ref.at[k], out_ref.at[:, k, :, pl.ds(0, LANES)], sems.at[k])
+        pltpu.make_async_copy(near_ref.at[k], out_ref.at[:, k, :, first], sems.at[k])
         for k in range(1, planes - 1)
     ]
     for copy in copies:
@@ -743,48 +755,38 @@
     even_plane = lax.axis_index("ax") % 2 == 0
     nu_dt = viscosity * time_step
     half = 0.5 * time_step
-    for tile in range(plan.radial // LANES):
-        here = slice(tile * LANES, (tile + 1) * LANES)
-        there = slice((tile - 1) * LANES, tile * LANES)
-        sent_a = own_a[2, :, here]
-        if tile == 0:
-            sent_b = own_b[2]
-            factor_low = nu_dt + half * jnp.where(even_plane, sent_b, sent_a)
-            factor_high = nu_dt - half * jnp.where(even_plane, sent_a, sent_b)
-        else:
-            factor_low = nu_dt + half * sent_a
-            factor_high = nu_dt - half * sent_a
-        for f in range(plan.fields):
-            b = ax_b[f] if tile == 0 else 0.0
-            below, above = slabs_beside(ax_a[f, :, here], b)
-            low = near_ref[0, f] if tile == 0 else far_ref[0, f, :, there]
-            high = near_ref[planes - 1, f] if tile == 0 else far_ref[1, f, :, there]
-            ends[0, f, :, here] = low + factor_low * below
-            ends[1, f, :, here] = high + factor_high * above
+    sent_a = own_a[2]
+    sent_b = own_b[2, : plan.theta]
+    factor_low = nu_dt + half * jnp.where(even_plane, sent_b, sent_a)
+    factor_high = nu_dt - half * jnp.where(even_plane, sent_a, sent_b)
+    for f in range(plan.fields):
+        below, above = slabs_beside(ax_a[f], ax_b[f, : plan.theta])
+        ends[0, f] = near_ref[0, f] + factor_low * below
+        ends[1, f] = near_ref[planes - 1, f] + factor_high * above
     for end, k in ((0, 0), (1, planes - 1)):
-        copies.append(pltpu.make_async_copy(ends.at[end], out_ref.at[:, k], sems.at[k]))
+        copies.append(pltpu.make_async_copy(ends.at[end], out_ref.at[:, k, :, first], sems.at[k]))
         copies[-1].start()
     for copy in copies:
         copy.wait()
 
 
-def finish(plan, near, far, sent, messages, partial):
+def finish(plan, near, sent, messages, partial):
     anywhere = pl.BlockSpec(memory_space=pl.ANY)
     inside = pl.BlockSpec(memory_space=pltpu.VMEM)
     return pl.pallas_call(
         functools.partial(finish_kernel, plan),
-        in_specs=[inside] * 6 + [anywhere],
+        in_specs=[inside] * 5 + [anywhere],
         out_specs=anywhere,
         out_shape=jax.ShapeDtypeStruct(partial.shape, jnp.float32),
-        input_output_aliases={6: 0},
+        input_output_aliases={5: 0},
         scratch_shapes=[
-            pltpu.VMEM((2, plan.fields, plan.theta, plan.radial), jnp.float32),
+            pltpu.VMEM((2, plan.fields, plan.theta, LANES), jnp.float32),
             pltpu.SemaphoreType.DMA((plan.planes,)),
         ],
         compiler_params=pltpu.CompilerParams(vmem_limit_bytes=VMEM_LIMIT),
         name="finish",
         cost_estimate=pl.CostEstimate(flops=100000, bytes_accessed=1500000, transcendentals=0),
-    )(near, far, *sent, *messages, partial)
+    )(near, *sent, *messages, partial)
 
 
 def pairs(count, start):
@@ -804,8 +806,8 @@
     def send(x, distance):
         return lax.ppermute(x, "az", [(i, i ^ distance) for i in range(sectors)])
 
-    packed, wide, rest = pack(plan, fields)
-    rest_message = lax.ppermute(rest, "ax", pairs(slabs, 1))
+    packed, wide, rest_b = pack(plan, fields)
+    rest_b = lax.ppermute(rest_b, "ax", pairs(slabs, 1))
     half = sectors // 2
     pieces = [None] * sectors
     pieces[0] = packed
@@ -818,17 +820,17 @@
     for p in range(half - 1, 0, -1):
         pieces[half + p] = send(onward, p)
     pieces[half] = onward
-    early = early_spectra(plan, pieces[: half + 1], rest_message)
-    column = edges(plan, fields, early[1])
+    early = early_spectra(plan, pieces[: half + 1], rest_b)
+    column, rest_a = edges(plan, fields, early[1])
+    rests = (lax.ppermute(rest_a, "ax", pairs(slabs, 0)), rest_b)
     sides = (pieces[1], lax.ppermute(column, "az", pairs(sectors, 1)))
     *parts, message_a, message_b = filtered(plan, fields, pieces[half + 1 :], early)
     messages = (
         lax.ppermute(message_a, "ax", pairs(slabs, 0)),
         lax.ppermute(message_b, "ax", pairs(slabs, 1)),
     )
-    own = (wide, column)
-    partial, near, ends = inner(plan, coef, parts, fields, own, sides, rest_message, part)
-    return finish(plan, near, ends, (message_a, message_b), messages, partial)
+    partial, near = inner(plan, coef, parts, fields, (wide, column), sides, rests, part)
+    return finish(plan, near, (message_a, message_b), messages, partial)
 
 
 def on_device(fields):

time: 29.8 us -> 29.6 us (level)
    ppermute x1, starting transfers between devices: 0.97 us -> 0.07 us  [fast_on_device(): lax.ppermute(message_b, 'ax', pairs(slabs, 1))]
    ppermute x1, starting transfers between devices: 0.07 us -> 0.96 us  [fast_on_device(): lax.ppermute(message_a, 'ax', pairs(slabs, 0))]
  transfers between devices with their start and end apart: 11 -> 12, of which waited for: 4 -> 4; matrix products, arithmetic and copies ran while one was open for 0% -> 0% of each run, Pallas kernels for 18% -> 18%
where the time goes in v7:
time: 29.6 us; the launch traced here: 29.5 us
  starting transfers between devices  14.7 us (50%)
  Pallas kernels  6.48 us (22%)
  waiting for transfers between devices  6.38 us (22%)
  local copies, waits for them, and re-layouts  1.77 us (6%)
    ppermute x7, starting transfers between devices, send(): return lax.ppermute(x, 'az', [(i, i ^ distance) for i in range(sectors)])  11.7 us
    ppermute x7, waiting for transfers between devices, send(): return lax.ppermute(x, 'az', [(i, i ^ distance) for i in range(sectors)])  3.88 us
    ppermute x1, waiting for transfers between devices, fast_on_device(): sides = (pieces[1], lax.ppermute(column, 'az', pairs(sectors, 1)))  2.5 us
    pallas_call x1, Pallas kernels, outer(): pl.pallas_call(functools.partial(outer_kernel, plan), in_specs=[inside] *...  2.25 us
    ppermute x1, starting transfers between devices, fast_on_device(): sides = (pieces[1], lax.ppermute(column, 'az', pairs(sectors, 1)))  1.99 us
    unnamed x14, local copies, waits for them, and re-layouts  1.77 us
    pallas_call x1, Pallas kernels, inner(): pl.pallas_call(functools.partial(inner_kernel, plan), in_specs=[inside] *...  1.52 us
    pallas_call x1, Pallas kernels, finish(): pl.pallas_call(functools.partial(finish_kernel, plan), in_specs=[inside]...  0.97 us
  transfers between devices with their start and end apart: 12, of which 4 were waited for; matrix products, arithmetic and copies ran while one was open for 0% of the time, Pallas kernels for 18%

profile of v7, /device:TPU:0, one launch (start us, length us, event | category | flops | bytes accessed | tf_op | source)
XLA Modules:
  0.0 29.5 jit_solution(76992320342254522)
XLA Ops:
  0.0 0.0 copy-start
  0.0 1.7 %copy-done = f32[5,16,16,512]{3,2,1,0:T(8,128)S(1)} copy-done((f32[5,16,16,512]{3,2,1,0:T(8,128)S(1)}, f32[5,16,16,512]{3,2,1,0:T(8,128)}, u32[]{:S(2)}) %copy-start) | copy-done | bytes 2621464
  1.7 0.0 copy-start.6
  1.7 0.0 copy-start.3
  1.7 0.3 %pack.1 = (f32[14,16,128]{2,1,0:T(8,128)S(1)}, f32[34,16,128]{2,1,0:T(8,128)S(1)}, f32[5,16,384]{2,1,0:T(8,128)S(1)}) custom-call(f32[5,16,16,512]{3,2,1,0:T(8,128)S(1)} %copy-done), custom_call_target="tpu_custom_call" | custom-call | flops 1000000 | bytes 800000 | tf_op jit(solution)/shard_map/pack/pallas_call | solution.py:301
  2.1 0.0 copy-start.1
  2.1 3.0 %collective-permute-start.1 = (f32[34,16,128]{2,1,0:T(8,128)S(1)}, f32[34,16,128]{2,1,0:T(8,128)S(1)}, u32[]{:S(2)}, u32[]{:S(2)}) collective-permute-start(f32[34,16,128]{2,1,0:T(8,128)S(1)} %get-tuple-element.24.own_a), channel_id=1, source_target_pairs={{0,4},{4,0},{8,12},{12,8},{16,20},{20,16},{24,28},{28,24},{1,5},{5... | collective-permute-start | bytes 835592 | tf_op jit(solution)/shard_map/ppermute | solution.py:807
  5.1 2.6 %collective-permute-start.4 = (f32[14,16,128]{2,1,0:T(8,128)S(1)}, f32[14,16,128]{2,1,0:T(8,128)S(1)}, u32[]{:S(2)}, u32[]{:S(2)}) collective-permute-start(f32[14,16,128]{2,1,0:T(8,128)S(1)} %get-tuple-element.23.refs_0_), channel_id=1, source_target_pairs={{0,16},{4,20},{8,24},{12,28},{16,0},{20,4},{24,8},{28,12},{1,17},{... | collective-permute-start | bytes 344072 | tf_op jit(solution)/shard_map/ppermute | solution.py:807
  7.7 1.6 %collective-permute-start.2 = (f32[14,16,128]{2,1,0:T(8,128)S(1)}, f32[14,16,128]{2,1,0:T(8,128)S(1)}, u32[]{:S(2)}, u32[]{:S(2)}) collective-permute-start(f32[14,16,128]{2,1,0:T(8,128)S(1)} %get-tuple-element.23.refs_0_), channel_id=1, source_target_pairs={{0,8},{4,12},{8,0},{12,4},{16,24},{20,28},{24,16},{28,20},{1,9},{5... | collective-permute-start | bytes 344072 | tf_op jit(solution)/shard_map/ppermute | solution.py:807
  9.3 0.4 %collective-permute-start.3 = (f32[14,16,128]{2,1,0:T(8,128)S(1)}, f32[14,16,128]{2,1,0:T(8,128)S(1)}, u32[]{:S(2)}, u32[]{:S(2)}) collective-permute-start(f32[14,16,128]{2,1,0:T(8,128)S(1)} %get-tuple-element.23.refs_0_), channel_id=1, source_target_pairs={{0,12},{4,8},{8,4},{12,0},{16,28},{20,24},{24,20},{28,16},{1,13},{... | collective-permute-start | bytes 344072 | tf_op jit(solution)/shard_map/ppermute | solution.py:807
  9.7 0.0 collective-permute-start
  9.7 0.0 copy-done.6
  9.7 2.3 %outer.1 = (f32[16,5,16,384]{3,2,1,0:T(8,128)S(1)}, f32[8,128]{1,0:T(8,128)S(1)}) custom-call(f32[8,512]{1,0:T(8,128)S(1)} %copy-done.6, f32[5,16,16,512]{3,2,1,0:T(8,128)S(1)} %copy-done), custom_call_target="tpu_custom_call" | custom-call | flops 16000000 | bytes 5000000 | tf_op jit(solution)/shard_map/outer/pallas_call | solution.py:427
  12.0 0.0 copy-start.2
  12.0 0.0 copy-start.4
  12.0 0.0 copy-start.5
  12.0 1.0 %collective-permute-done.4.x_ref = f32[14,16,128]{2,1,0:T(8,128)S(1)} collective-permute-done((f32[14,16,128]{2,1,0:T(8,128)S(1)}, f32[14,16,128]{2,1,0:T(8,128)S(1)}, u32[]{:S(2)}, u32[]{:S(2)}) %collective-permute-start.4) | collective-permute-done | bytes 114720 | tf_op jit(solution)/shard_map/ppermute | solution.py:807
  13.1 0.5 %collective-permute-start.5 = (f32[14,16,128]{2,1,0:T(8,128)S(1)}, f32[14,16,128]{2,1,0:T(8,128)S(1)}, u32[]{:S(2)}, u32[]{:S(2)}) collective-permute-start(f32[14,16,128]{2,1,0:T(8,128)S(1)} %gate.1.refs_4_), channel_id=1, source_target_pairs={{0,4},{4,0},{8,12},{12,8},{16,20},{20,16},{24,28},{28,24},{1,5},{5... | collective-permute-start | bytes 344072 | tf_op jit(solution)/shard_map/ppermute | solution.py:807
  13.6 1.0 %collective-permute-done.2.refs_2_ = f32[14,16,128]{2,1,0:T(8,128)S(1)} collective-permute-done((f32[14,16,128]{2,1,0:T(8,128)S(1)}, f32[14,16,128]{2,1,0:T(8,128)S(1)}, u32[]{:S(2)}, u32[]{:S(2)}) %collective-permute-start.2) | collective-permute-done | bytes 114720 | tf_op jit(solution)/shard_map/ppermute | solution.py:807
  14.6 1.5 %collective-permute-start.6 = (f32[14,16,128]{2,1,0:T(8,128)S(1)}, f32[14,16,128]{2,1,0:T(8,128)S(1)}, u32[]{:S(2)}, u32[]{:S(2)}) collective-permute-start(f32[14,16,128]{2,1,0:T(8,128)S(1)} %gate.1.refs_4_), channel_id=1, source_target_pairs={{0,8},{4,12},{8,0},{12,4},{16,24},{20,28},{24,16},{28,20},{1,9},{5... | collective-permute-start | bytes 344072 | tf_op jit(solution)/shard_map/ppermute | solution.py:807
  16.1 0.0 collective-permute-done.3.refs_3_
  16.1 2.1 %collective-permute-start.7 = (f32[14,16,128]{2,1,0:T(8,128)S(1)}, f32[14,16,128]{2,1,0:T(8,128)S(1)}, u32[]{:S(2)}, u32[]{:S(2)}) collective-permute-start(f32[14,16,128]{2,1,0:T(8,128)S(1)} %gate.1.refs_4_), channel_id=1, source_target_pairs={{0,12},{4,8},{8,4},{12,0},{16,28},{20,24},{24,20},{28,16},{1,13},{... | collective-permute-start | bytes 344072 | tf_op jit(solution)/shard_map/ppermute | solution.py:807
  18.2 0.0 collective-permute-done.after_ref.ax_b
  18.2 0.0 collective-permute-done.1.refs_1_.az_a
  18.2 0.0 copy-done.3
  18.2 0.3 early.1
  18.5 0.0 copy-done.1
  18.5 0.2 edges.1
  18.7 2.0 %collective-permute-start.8 = (f32[20,16,128]{2,1,0:T(8,128)S(1)}, f32[20,16,128]{2,1,0:T(8,128)S(1)}, u32[]{:S(2)}, u32[]{:S(2)}) collective-permute-start(f32[20,16,128]{2,1,0:T(8,128)S(1)} %get-tuple-element.32.own_b), channel_id=1, source_target_pairs={{4,8},{8,4},{12,16},{16,12},{20,24},{24,20},{28,0},{0,28},{5,9},{9... | collective-permute-start | bytes 491528 | tf_op jit(solution)/shard_map/ppermute | solution.py:826
  20.7 0.0 collective-permute-start.9
  20.7 0.0 collective-permute-done.5.refs_0_
  20.7 0.0 collective-permute-done.6.refs_1_
  20.7 1.8 %collective-permute-done.7.refs_2_ = f32[14,16,128]{2,1,0:T(8,128)S(1)} collective-permute-done((f32[14,16,128]{2,1,0:T(8,128)S(1)}, f32[14,16,128]{2,1,0:T(8,128)S(1)}, u32[]{:S(2)}, u32[]{:S(2)}) %collective-permute-start.7) | collective-permute-done | bytes 114720 | tf_op jit(solution)/shard_map/ppermute | solution.py:807
  22.5 0.0 copy-done.2
  22.5 0.0 copy-done.4
  22.5 0.0 copy-done.5
  22.5 0.9 %filter.1 = (f32[14,16,128]{2,1,0:T(8,128)S(1)}, f32[14,16,128]{2,1,0:T(8,128)S(1)}, f32[14,8,128]{2,1,0:T(8,128)S(1)}, f32[5,16,128]{2,1,0:T(8,128)S(1)}, f32[5...) custom-call(f32[5,16,16,512]{3,2,1,0:T(8,128)S(1)} %copy-done.1, bf16[8,128,256]{2,1,0:T(8,128)(2,1)S(1)} %copy-done.2, ...), custom_call_target="tpu_custom_call" | custom-call | flops 200000000 | bytes 1500000 | tf_op jit(solution)/shard_map/filter/pallas_call | solution.py:629
  23.4 0.1 collective-permute-start.11
  23.5 1.0 %collective-permute-start.10 = (f32[5,16,128]{2,1,0:T(8,128)S(1)}, f32[5,16,128]{2,1,0:T(8,128)S(1)}, u32[]{:S(2)}, u32[]{:S(2)}) collective-permute-start(f32[5,16,128]{2,1,0:T(8,128)S(1)} %get-tuple-element.36.own_a), channel_id=1, source_target_pairs={{0,1},{1,0},{2,3},{3,2},{4,5},{5,4},{6,7},{7,6},{8,9},{9,8},{10,11... | collective-permute-start | bytes 122888 | tf_op jit(solution)/shard_map/ppermute | solution.py:829
  24.5 0.0 collective-permute-done.9.ax_a
  24.5 2.5 %collective-permute-done.8.az_b = f32[20,16,128]{2,1,0:T(8,128)S(1)} collective-permute-done((f32[20,16,128]{2,1,0:T(8,128)S(1)}, f32[20,16,128]{2,1,0:T(8,128)S(1)}, u32[]{:S(2)}, u32[]{:S(2)}) %collective-permute-start.8) | collective-permute-done | bytes 163872 | tf_op jit(solution)/shard_map/ppermute | solution.py:826
  27.0 1.5 %inner.1 = (f32[5,16,16,512]{3,2,1,0:T(8,128)}, f32[16,5,16,128]{3,2,1,0:T(8,128)S(1)}) custom-call(f32[8,512]{1,0:T(8,128)S(1)} %copy-done.6, f32[14,16,128]{2,1,0:T(8,128)S(1)} %get-tuple-element.28.own_ref, f32[14,16,128]{2,1,0:T(8,128)S(1)} %get-tuple-element.29.across_ref, f32[14,8,128]{2,1,0:T(8,128)S(1)} %get-tuple-element.30.edge_ref, ...), custom_call_target="tpu_custom_call" | custom-call | flops 6000000 | bytes 2500000 | tf_op jit(solution)/shard_map/inner/pallas_call | solution.py:725
  28.5 0.0 collective-permute-done.10.ax_a
  28.5 0.0 collective-permute-done.11.ax_b
  28.5 1.0 %finish.1 = f32[5,16,16,512]{3,2,1,0:T(8,128)} custom-call(f32[16,5,16,128]{3,2,1,0:T(8,128)S(1)} %get-tuple-element.35.near_ref, f32[5,16,128]{2,1,0:T(8,128)S(1)} %get-tuple-element.36.own_a, f32[5,24,128]{2,1,0:T(8,128)S(1)} %get-tuple-element.37.own_b, f32[5,16,128]{2,1,0:T(8,128)S(1)} %collective-permute-done.10.ax_a, ...), custom_call_target="tpu_custom_call", output_to_operand_aliasing={{}: (5, {})} | custom-call | flops 100000 | bytes 1500000 | tf_op jit(solution)/shard_map/finish/pallas_call | solution.py:776
  (1 shorter events, 0.0 us)
Async XLA Ops:
  0.0 1.7 %copy-start = (f32[5,16,16,512]{3,2,1,0:T(8,128)S(1)}, f32[5,16,16,512]{3,2,1,0:T(8,128)}, u32[]{:S(2)}) copy-start(f32[5,16,16,512]{3,2,1,0:T(8,128)} %x_ref.9) | copy-start | bytes 7864324
  1.7 8.0 %copy-start.6 = (f32[8,512]{1,0:T(8,128)S(1)}, f32[8,512]{1,0:T(8,128)}, u32[]{:S(2)}) copy-start(f32[8,512]{1,0:T(8,128)} %constant.10.clone.coef_ref) | copy-start | bytes 49156
  1.7 16.5 %copy-start.3 = (bf16[8,128,256]{2,1,0:T(8,128)(2,1)S(1)}, bf16[8,128,256]{2,1,0:T(8,128)(2,1)}, u32[]{:S(2)}) copy-start(bf16[8,128,256]{2,1,0:T(8,128)(2,1)} %constant.11.clone.forward_ref) | copy-start | bytes 1572868
  2.1 16.4 %copy-start.1 = (f32[5,16,16,512]{3,2,1,0:T(8,128)S(1)}, f32[5,16,16,512]{3,2,1,0:T(8,128)}, u32[]{:S(2)}) copy-start(f32[5,16,16,512]{3,2,1,0:T(8,128)} %x_ref.9) | copy-start | bytes 7864324
  2.1 16.1 %collective-permute-start.1 = (f32[34,16,128]{2,1,0:T(8,128)S(1)}, f32[34,16,128]{2,1,0:T(8,128)S(1)}, u32[]{:S(2)}, u32[]{:S(2)}) collective-permute-start(f32[34,16,128]{2,1,0:T(8,128)S(1)} %get-tuple-element.24.own_a), channel_id=1, source_target_pairs={{0,4},{4,0},{8,12},{12,8},{16,20},{20,16},{24,28},{28,24},{1,5},{5... | collective-permute-start | bytes 835592 | tf_op jit(solution)/shard_map/ppermute | solution.py:807
  5.1 7.9 %collective-permute-start.4 = (f32[14,16,128]{2,1,0:T(8,128)S(1)}, f32[14,16,128]{2,1,0:T(8,128)S(1)}, u32[]{:S(2)}, u32[]{:S(2)}) collective-permute-start(f32[14,16,128]{2,1,0:T(8,128)S(1)} %get-tuple-element.23.refs_0_), channel_id=1, source_target_pairs={{0,16},{4,20},{8,24},{12,28},{16,0},{20,4},{24,8},{28,12},{1,17},{... | collective-permute-start | bytes 344072 | tf_op jit(solution)/shard_map/ppermute | solution.py:807
  7.7 6.9 %collective-permute-start.2 = (f32[14,16,128]{2,1,0:T(8,128)S(1)}, f32[14,16,128]{2,1,0:T(8,128)S(1)}, u32[]{:S(2)}, u32[]{:S(2)}) collective-permute-start(f32[14,16,128]{2,1,0:T(8,128)S(1)} %get-tuple-element.23.refs_0_), channel_id=1, source_target_pairs={{0,8},{4,12},{8,0},{12,4},{16,24},{20,28},{24,16},{28,20},{1,9},{5... | collective-permute-start | bytes 344072 | tf_op jit(solution)/shard_map/ppermute | solution.py:807
  9.3 6.8 %collective-permute-start.3 = (f32[14,16,128]{2,1,0:T(8,128)S(1)}, f32[14,16,128]{2,1,0:T(8,128)S(1)}, u32[]{:S(2)}, u32[]{:S(2)}) collective-permute-start(f32[14,16,128]{2,1,0:T(8,128)S(1)} %get-tuple-element.23.refs_0_), channel_id=1, source_target_pairs={{0,12},{4,8},{8,4},{12,0},{16,28},{20,24},{24,20},{28,16},{1,13},{... | collective-permute-start | bytes 344072 | tf_op jit(solution)/shard_map/ppermute | solution.py:807
  9.7 8.5 %collective-permute-start = (f32[5,16,384]{2,1,0:T(8,128)S(1)}, f32[5,16,384]{2,1,0:T(8,128)S(1)}, u32[]{:S(2)}, u32[]{:S(2)}) collective-permute-start(f32[5,16,384]{2,1,0:T(8,128)S(1)} %get-tuple-element.22), channel_id=1, source_target_pairs={{1,2},{2,1},{3,0},{0,3},{5,6},{6,5},{7,4},{4,7},{9,10},{10,9},{11,... | collective-permute-start | bytes 368648 | tf_op jit(solution)/shard_map/ppermute | solution.py:810
  12.0 10.5 %copy-start.2 = (bf16[8,128,256]{2,1,0:T(8,128)(2,1)S(1)}, bf16[8,128,256]{2,1,0:T(8,128)(2,1)}, u32[]{:S(2)}) copy-start(bf16[8,128,256]{2,1,0:T(8,128)(2,1)} %constant.12.clone.forward_ref) | copy-start | bytes 1572868
  12.0 10.5 %copy-start.4 = (bf16[8,48,384]{2,1,0:T(8,128)(2,1)S(1)}, bf16[8,48,384]{2,1,0:T(8,128)(2,1)}, u32[]{:S(2)}) copy-start(bf16[8,48,384]{2,1,0:T(8,128)(2,1)} %constant.13.clone.inverse_ref) | copy-start | bytes 884740
  12.0 10.5 %copy-start.5 = (f32[128,128]{1,0:T(8,128)S(1)}, f32[128,128]{1,0:T(8,128)}, u32[]{:S(2)}) copy-start(f32[128,128]{1,0:T(8,128)} %constant.14.clone.mask_ref) | copy-start | bytes 196612
  13.1 7.6 %collective-permute-start.5 = (f32[14,16,128]{2,1,0:T(8,128)S(1)}, f32[14,16,128]{2,1,0:T(8,128)S(1)}, u32[]{:S(2)}, u32[]{:S(2)}) collective-permute-start(f32[14,16,128]{2,1,0:T(8,128)S(1)} %gate.1.refs_4_), channel_id=1, source_target_pairs={{0,4},{4,0},{8,12},{12,8},{16,20},{20,16},{24,28},{28,24},{1,5},{5... | collective-permute-start | bytes 344072 | tf_op jit(solution)/shard_map/ppermute | solution.py:807
  14.6 6.1 %collective-permute-start.6 = (f32[14,16,128]{2,1,0:T(8,128)S(1)}, f32[14,16,128]{2,1,0:T(8,128)S(1)}, u32[]{:S(2)}, u32[]{:S(2)}) collective-permute-start(f32[14,16,128]{2,1,0:T(8,128)S(1)} %gate.1.refs_4_), channel_id=1, source_target_pairs={{0,8},{4,12},{8,0},{12,4},{16,24},{20,28},{24,16},{28,20},{1,9},{5... | collective-permute-start | bytes 344072 | tf_op jit(solution)/shard_map/ppermute | solution.py:807
  16.1 6.4 %collective-permute-start.7 = (f32[14,16,128]{2,1,0:T(8,128)S(1)}, f32[14,16,128]{2,1,0:T(8,128)S(1)}, u32[]{:S(2)}, u32[]{:S(2)}) collective-permute-start(f32[14,16,128]{2,1,0:T(8,128)S(1)} %gate.1.refs_4_), channel_id=1, source_target_pairs={{0,12},{4,8},{8,4},{12,0},{16,28},{20,24},{24,20},{28,16},{1,13},{... | collective-permute-start | bytes 344072 | tf_op jit(solution)/shard_map/ppermute | solution.py:807
  18.7 8.3 %collective-permute-start.8 = (f32[20,16,128]{2,1,0:T(8,128)S(1)}, f32[20,16,128]{2,1,0:T(8,128)S(1)}, u32[]{:S(2)}, u32[]{:S(2)}) collective-permute-start(f32[20,16,128]{2,1,0:T(8,128)S(1)} %get-tuple-element.32.own_b), channel_id=1, source_target_pairs={{4,8},{8,4},{12,16},{16,12},{20,24},{24,20},{28,0},{0,28},{5,9},{9... | collective-permute-start | bytes 491528 | tf_op jit(solution)/shard_map/ppermute | solution.py:826
  20.7 3.8 %collective-permute-start.9 = (f32[5,16,384]{2,1,0:T(8,128)S(1)}, f32[5,16,384]{2,1,0:T(8,128)S(1)}, u32[]{:S(2)}, u32[]{:S(2)}) collective-permute-start(f32[5,16,384]{2,1,0:T(8,128)S(1)} %get-tuple-element.33), channel_id=1, source_target_pairs={{0,1},{1,0},{2,3},{3,2},{4,5},{5,4},{6,7},{7,6},{8,9},{9,8},{10,11... | collective-permute-start | bytes 368648 | tf_op jit(solution)/shard_map/ppermute | solution.py:825
  23.4 5.1 %collective-permute-start.11 = (f32[5,24,128]{2,1,0:T(8,128)S(1)}, f32[5,24,128]{2,1,0:T(8,128)S(1)}, u32[]{:S(2)}, u32[]{:S(2)}) collective-permute-start(f32[5,24,128]{2,1,0:T(8,128)S(1)} %get-tuple-element.37.own_b), channel_id=1, source_target_pairs={{1,2},{2,1},{3,0},{0,3},{5,6},{6,5},{7,4},{4,7},{9,10},{10,9},{11,... | collective-permute-start | bytes 184328 | tf_op jit(solution)/shard_map/ppermute | solution.py:830
  23.5 5.0 %collective-permute-start.10 = (f32[5,16,128]{2,1,0:T(8,128)S(1)}, f32[5,16,128]{2,1,0:T(8,128)S(1)}, u32[]{:S(2)}, u32[]{:S(2)}) collective-permute-start(f32[5,16,128]{2,1,0:T(8,128)S(1)} %get-tuple-element.36.own_a), channel_id=1, source_target_pairs={{0,1},{1,0},{2,3},{3,2},{4,5},{5,4},{6,7},{7,6},{8,9},{9,8},{10,11... | collective-permute-start | bytes 122888 | tf_op jit(solution)/shard_map/ppermute | solution.py:829

commit v8 on v7

--- a/solution.py
+++ b/solution.py
@@ -445,7 +445,7 @@
     return jnp.where(even_plane, b, a), jnp.where(even_plane, a, b)
 
 
-def seams(plan, coef_ref, x_ref, own_a, own_b, az_a, az_b, ax_a, ax_b, part_ref, done, terms, store):
+def seams(plan, coef_ref, x_ref, own_a, own_b, az_a, ax_a, ax_b, part_ref, done, terms):
     nu_dt = viscosity * time_step
     half = 0.5 * time_step
     planes = plan.planes
@@ -468,9 +468,8 @@
         after = []
         for f in range(plan.fields):
             a = az_a[base + f * tiles + tile]
-            b = az_b[f * tiles + tile]
-            before.append(jnp.where(even_theta, b, a))
-            after.append(jnp.where(even_theta, a, b))
+            before.append(jnp.where(even_theta, 0.0, a))
+            after.append(jnp.where(even_theta, a, 0.0))
         for f in range(plan.fields):
             low = (c2 + turn_low) * before[f]
             high = (c2 - turn_high) * after[f]
@@ -497,7 +496,6 @@
                     else:
                         value = value + (nu_dt - half * x_ref[2, k, :, here]) * above
                 done[k, f, :, there] = value
-        store(k).start()
 
 
 def gate_kernel(x_ref, token_ref, out_ref):
@@ -652,18 +650,11 @@
 
 
 def inner_kernel(
-    plan, coef_ref, own_ref, across_ref, edge_ref, sums_ref, x_ref, own_a, own_b, az_a, az_b,
-    ax_a, ax_b, part_ref, out_ref, done, far_done, terms, state, outs
+    plan, coef_ref, own_ref, across_ref, edge_ref, sums_ref, x_ref, own_a, own_b, az_a,
+    ax_a, ax_b, part_ref, done, far_done, swirl_ref, terms, state
 ):
     planes = plan.planes
-    beyond = pl.ds(LANES, plan.radial - LANES)
-
-    def store(k):
-        return pltpu.make_async_copy(far_done.at[k], out_ref.at[:, k, :, beyond], outs.at[k])
-
-    seams(
-        plan, coef_ref, x_ref, own_a, own_b, az_a, az_b, ax_a, ax_b, part_ref, far_done, terms, store
-    )
+    seams(plan, coef_ref, x_ref, own_a, own_b, az_a, ax_a, ax_b, part_ref, far_done, terms)
     theta = plan.theta
     tiles = plan.radial // LANES
     shape = (theta, LANES)
@@ -689,9 +680,8 @@
     afters = []
     for f in range(plan.fields):
         a = az_a[plan.groups + f * tiles]
-        b = az_b[f * tiles]
-        befores.append(jnp.where(even_theta, b, a) + sums_ref[f])
-        afters.append(jnp.where(even_theta, a, b) - sums_ref[f])
+        befores.append(jnp.where(even_theta, 0.0, a) + sums_ref[f])
+        afters.append(jnp.where(even_theta, a, 0.0) - sums_ref[f])
 
     zero = jnp.zeros(shape, jnp.float32)
     for k in range(planes):
@@ -716,30 +706,98 @@
         for f in range(plan.fields):
             done[k, f] = result[f]
     for k in range(planes):
-        store(k).wait()
-
-
-def inner(plan, coef, parts, fields, own, sides, rests, part):
+        x = state[k, 1]
+        swirl_ref[k : k + 1] = jnp.where(even_theta, x[:1], x[theta - 1 :])
+
+
+def inner(plan, coef, parts, fields, own, side, rests, part):
     inside = pl.BlockSpec(memory_space=pltpu.VMEM)
     f32 = jnp.float32
     return pl.pallas_call(
         functools.partial(inner_kernel, plan),
-        in_specs=[inside] * 13,
-        out_specs=[pl.BlockSpec(memory_space=pl.ANY), inside],
+        in_specs=[inside] * 12,
+        out_specs=[inside, inside, inside],
         out_shape=[
-            jax.ShapeDtypeStruct(fields.shape, f32),
             jax.ShapeDtypeStruct((plan.planes, plan.fields, plan.theta, LANES), f32),
+            jax.ShapeDtypeStruct(part.shape, f32),
+            jax.ShapeDtypeStruct((plan.planes, LANES), f32),
         ],
         scratch_shapes=[
-            pltpu.VMEM(part.shape, f32),
             pltpu.VMEM((2, plan.fields * plan.radial // LANES, plan.planes, LANES), f32),
             pltpu.VMEM((plan.planes, plan.fields, plan.theta, LANES), f32),
-            pltpu.SemaphoreType.DMA((plan.planes,)),
         ],
         compiler_params=pltpu.CompilerParams(vmem_limit_bytes=VMEM_LIMIT),
         name="inner",
         cost_estimate=pl.CostEstimate(flops=6000000, bytes_accessed=2500000, transcendentals=0),
-    )(coef, *parts, fields, *own, *sides, *rests, part)
+    )(coef, *parts, fields, *own, side, *rests, part)
+
+
+def column_kernel(
+    plan, coef_ref, own_b, az_b, near_ref, far_ref, swirl_ref, out_ref, near, far, terms, outs
+):
+    planes = plan.planes
+    tiles = plan.radial // LANES
+    even_theta = lax.axis_index("az") % 2 == 0
+    sign = jnp.where(even_theta, 1.0, -1.0)
+    beyond = pl.ds(LANES, plan.radial - LANES)
+    lane = lax.broadcasted_iota(jnp.int32, (planes, LANES), 1)
+    for tile in range(tiles):
+        here = slice(tile * LANES, (tile + 1) * LANES)
+        c2 = coef_ref[1:2, here]
+        cross = sign * coef_ref[6:7, here]
+        swirl = swirl_ref[...] if tile == 0 else own_b[tiles + tile]
+        turn = c2 + sign * coef_ref[3:4, here] * swirl
+        column = [az_b[f * tiles + tile] for f in range(plan.fields)]
+        if tile == 0:
+            column = [jnp.where(lane < plan.full, 0.0, x) for x in column]
+        for f in range(plan.fields):
+            value = turn * column[f]
+            if f == 0:
+                value = value + cross * column[1]
+            if f == 1:
+                value = value - cross * column[0]
+            terms[f * tiles + tile] = value
+    row = lax.broadcasted_iota(jnp.int32, (plan.theta, LANES), 0)
+    edge = jnp.where(even_theta, 0, plan.theta - 1)
+    copies = []
+    for k in range(planes):
+        for f in range(plan.fields):
+            for tile in range(1, tiles):
+                there = slice((tile - 1) * LANES, tile * LANES)
+                term = terms[f * tiles + tile, k : k + 1]
+                far[k, f, :, there] = far_ref[k, f, :, there] + jnp.where(row == edge, term, 0.0)
+        copies.append(pltpu.make_async_copy(far.at[k], out_ref.at[:, k, :, beyond], outs.at[k]))
+        copies[-1].start()
+    for k in range(planes):
+        for f in range(plan.fields):
+            near[k, f] = near_ref[k, f] + jnp.where(
+                row == edge, terms[f * tiles, k : k + 1], 0.0
+            )
+    for copy in copies:
+        copy.wait()
+
+
+def last_column(plan, coef, own, side, near, far, swirl, fields):
+    anywhere = pl.BlockSpec(memory_space=pl.ANY)
+    inside = pl.BlockSpec(memory_space=pltpu.VMEM)
+    f32 = jnp.float32
+    return pl.pallas_call(
+        functools.partial(column_kernel, plan),
+        in_specs=[inside] * 6,
+        out_specs=[anywhere, inside],
+        out_shape=[
+            jax.ShapeDtypeStruct(fields.shape, f32),
+            jax.ShapeDtypeStruct(near.shape, f32),
+        ],
+        scratch_shapes=[
+            pltpu.VMEM((plan.planes, plan.fields, plan.theta, plan.radial - LANES), f32),
+            pltpu.VMEM((plan.fields * plan.radial // LANES, plan.planes, LANES), f32),
+            pltpu.SemaphoreType.DMA((plan.planes,)),
+        ],
+        compiler_params=pltpu.CompilerParams(vmem_limit_bytes=VMEM_LIMIT),
+        name="last_column",
+        cost_estimate=pl.CostEstimate(flops=1000000, bytes_accessed=2500000, transcendentals=0),
+    )(coef, own, side, near, far, swirl)
 
 
 def finish_kernel(plan, near_ref, own_a, own_b, ax_a, ax_b, other_ref, out_ref, ends, sems):
@@ -829,7 +887,9 @@
         lax.ppermute(message_a, "ax", pairs(slabs, 0)),
         lax.ppermute(message_b, "ax", pairs(slabs, 1)),
     )
-    partial, near = inner(plan, coef, parts, fields, (wide, column), sides, rests, part)
+    own = (wide, column)
+    near, far, swirl = inner(plan, coef, parts, fields, own, sides[0], rests, part)
+    partial, near = last_column(plan, coef, column, sides[1], near, far, swirl, fields)
     return finish(plan, near, (message_a, message_b), messages, partial)
 
 

time: 29.6 us -> 29.5 us (level)
  waiting for transfers between devices: 6.38 us -> 4.98 us
  Pallas kernels: 6.48 us -> 7.77 us
    pallas_call x0 -> x1, Pallas kernels: none -> 1.43 us  [last_column(): pl.pallas_call(functools.partial(column_kernel, plan), in_specs=[inside]...]
    ppermute x1, waiting for transfers between devices: 2.5 us -> 1.14 us  [fast_on_device(): sides = (pieces[1], lax.ppermute(column, 'az', pairs(sectors, 1)))]
  transfers between devices with their start and end apart: 12 -> 12, of which waited for: 4 -> 4; matrix products, arithmetic and copies ran while one was open for 0% -> 0% of each run, Pallas kernels for 18% -> 22%
where the time goes in v8:
time: 29.5 us; the launch traced here: 29.4 us
  starting transfers between devices  14.7 us (50%)
  Pallas kernels  7.77 us (26%)
  waiting for transfers between devices  4.98 us (17%)
  local copies, waits for them, and re-layouts  1.77 us (6%)
    ppermute x7, starting transfers between devices, send(): return lax.ppermute(x, 'az', [(i, i ^ distance) for i in range(sectors)])  11.7 us
    ppermute x7, waiting for transfers between devices, send(): return lax.ppermute(x, 'az', [(i, i ^ distance) for i in range(sectors)])  3.83 us
    pallas_call x1, Pallas kernels, outer(): pl.pallas_call(functools.partial(outer_kernel, plan), in_specs=[inside] *...  2.26 us
    ppermute x1, starting transfers between devices, fast_on_device(): sides = (pieces[1], lax.ppermute(column, 'az', pairs(sectors, 1)))  1.99 us
    unnamed x14, local copies, waits for them, and re-layouts  1.77 us
    pallas_call x1, Pallas kernels, last_column(): pl.pallas_call(functools.partial(column_kernel, plan), in_specs=[inside]...  1.43 us
    pallas_call x1, Pallas kernels, inner(): pl.pallas_call(functools.partial(inner_kernel, plan), in_specs=[inside] *...  1.36 us
    ppermute x1, waiting for transfers between devices, fast_on_device(): sides = (pieces[1], lax.ppermute(column, 'az', pairs(sectors, 1)))  1.14 us
  transfers between devices with their start and end apart: 12, of which 4 were waited for; matrix products, arithmetic and copies ran while one was open for 0% of the time, Pallas kernels for 22%

profile of v8, /device:TPU:0, one launch (start us, length us, event | category | flops | bytes accessed | tf_op | source)
XLA Modules:
  0.0 29.4 jit_solution(5810500959594564752)
XLA Ops:
  0.0 0.0 copy-start
  0.0 1.7 %copy-done = f32[5,16,16,512]{3,2,1,0:T(8,128)S(1)} copy-done((f32[5,16,16,512]{3,2,1,0:T(8,128)S(1)}, f32[5,16,16,512]{3,2,1,0:T(8,128)}, u32[]{:S(2)}) %copy-start) | copy-done | bytes 2621464
  1.7 0.0 copy-start.5
  1.7 0.0 copy-start.3
  1.7 0.3 %pack.1 = (f32[14,16,128]{2,1,0:T(8,128)S(1)}, f32[34,16,128]{2,1,0:T(8,128)S(1)}, f32[5,16,384]{2,1,0:T(8,128)S(1)}) custom-call(f32[5,16,16,512]{3,2,1,0:T(8,128)S(1)} %copy-done), custom_call_target="tpu_custom_call" | custom-call | flops 1000000 | bytes 800000 | tf_op jit(solution)/shard_map/pack/pallas_call | solution.py:301
  2.1 0.0 copy-start.1
  2.1 3.0 %collective-permute-start.1 = (f32[34,16,128]{2,1,0:T(8,128)S(1)}, f32[34,16,128]{2,1,0:T(8,128)S(1)}, u32[]{:S(2)}, u32[]{:S(2)}) collective-permute-start(f32[34,16,128]{2,1,0:T(8,128)S(1)} %get-tuple-element.27.own_a), channel_id=1, source_target_pairs={{0,4},{4,0},{8,12},{12,8},{16,20},{20,16},{24,28},{28,24},{1,5},{5... | collective-permute-start | bytes 835592 | tf_op jit(solution)/shard_map/ppermute | solution.py:865
  5.1 2.6 %collective-permute-start.4 = (f32[14,16,128]{2,1,0:T(8,128)S(1)}, f32[14,16,128]{2,1,0:T(8,128)S(1)}, u32[]{:S(2)}, u32[]{:S(2)}) collective-permute-start(f32[14,16,128]{2,1,0:T(8,128)S(1)} %get-tuple-element.26.refs_0_), channel_id=1, source_target_pairs={{0,16},{4,20},{8,24},{12,28},{16,0},{20,4},{24,8},{28,12},{1,17},{... | collective-permute-start | bytes 344072 | tf_op jit(solution)/shard_map/ppermute | solution.py:865
  7.7 1.6 %collective-permute-start.2 = (f32[14,16,128]{2,1,0:T(8,128)S(1)}, f32[14,16,128]{2,1,0:T(8,128)S(1)}, u32[]{:S(2)}, u32[]{:S(2)}) collective-permute-start(f32[14,16,128]{2,1,0:T(8,128)S(1)} %get-tuple-element.26.refs_0_), channel_id=1, source_target_pairs={{0,8},{4,12},{8,0},{12,4},{16,24},{20,28},{24,16},{28,20},{1,9},{5... | collective-permute-start | bytes 344072 | tf_op jit(solution)/shard_map/ppermute | solution.py:865
  9.3 0.4 %collective-permute-start.3 = (f32[14,16,128]{2,1,0:T(8,128)S(1)}, f32[14,16,128]{2,1,0:T(8,128)S(1)}, u32[]{:S(2)}, u32[]{:S(2)}) collective-permute-start(f32[14,16,128]{2,1,0:T(8,128)S(1)} %get-tuple-element.26.refs_0_), channel_id=1, source_target_pairs={{0,12},{4,8},{8,4},{12,0},{16,28},{20,24},{24,20},{28,16},{1,13},{... | collective-permute-start | bytes 344072 | tf_op jit(solution)/shard_map/ppermute | solution.py:865
  9.7 0.0 collective-permute-start
  9.7 0.0 copy-done.5
  9.7 2.3 %outer.1 = (f32[16,5,16,384]{3,2,1,0:T(8,128)S(1)}, f32[8,128]{1,0:T(8,128)S(1)}) custom-call(f32[8,512]{1,0:T(8,128)S(1)} %copy-done.5, f32[5,16,16,512]{3,2,1,0:T(8,128)S(1)} %copy-done), custom_call_target="tpu_custom_call" | custom-call | flops 16000000 | bytes 5000000 | tf_op jit(solution)/shard_map/outer/pallas_call | solution.py:427
  12.0 0.0 copy-start.2
  12.0 0.0 copy-start.4
  12.0 0.0 copy-start.6
  12.0 1.0 %collective-permute-done.4.x_ref = f32[14,16,128]{2,1,0:T(8,128)S(1)} collective-permute-done((f32[14,16,128]{2,1,0:T(8,128)S(1)}, f32[14,16,128]{2,1,0:T(8,128)S(1)}, u32[]{:S(2)}, u32[]{:S(2)}) %collective-permute-start.4) | collective-permute-done | bytes 114720 | tf_op jit(solution)/shard_map/ppermute | solution.py:865
  13.1 0.5 %collective-permute-start.6 = (f32[14,16,128]{2,1,0:T(8,128)S(1)}, f32[14,16,128]{2,1,0:T(8,128)S(1)}, u32[]{:S(2)}, u32[]{:S(2)}) collective-permute-start(f32[14,16,128]{2,1,0:T(8,128)S(1)} %gate.1.refs_4_), channel_id=1, source_target_pairs={{0,4},{4,0},{8,12},{12,8},{16,20},{20,16},{24,28},{28,24},{1,5},{5... | collective-permute-start | bytes 344072 | tf_op jit(solution)/shard_map/ppermute | solution.py:865
  13.6 1.0 %collective-permute-done.2.refs_2_ = f32[14,16,128]{2,1,0:T(8,128)S(1)} collective-permute-done((f32[14,16,128]{2,1,0:T(8,128)S(1)}, f32[14,16,128]{2,1,0:T(8,128)S(1)}, u32[]{:S(2)}, u32[]{:S(2)}) %collective-permute-start.2) | collective-permute-done | bytes 114720 | tf_op jit(solution)/shard_map/ppermute | solution.py:865
  14.6 1.5 %collective-permute-start.7 = (f32[14,16,128]{2,1,0:T(8,128)S(1)}, f32[14,16,128]{2,1,0:T(8,128)S(1)}, u32[]{:S(2)}, u32[]{:S(2)}) collective-permute-start(f32[14,16,128]{2,1,0:T(8,128)S(1)} %gate.1.refs_4_), channel_id=1, source_target_pairs={{0,8},{4,12},{8,0},{12,4},{16,24},{20,28},{24,16},{28,20},{1,9},{5... | collective-permute-start | bytes 344072 | tf_op jit(solution)/shard_map/ppermute | solution.py:865
  16.1 0.0 collective-permute-done.3.refs_3_
  16.1 2.1 %collective-permute-start.8 = (f32[14,16,128]{2,1,0:T(8,128)S(1)}, f32[14,16,128]{2,1,0:T(8,128)S(1)}, u32[]{:S(2)}, u32[]{:S(2)}) collective-permute-start(f32[14,16,128]{2,1,0:T(8,128)S(1)} %gate.1.refs_4_), channel_id=1, source_target_pairs={{0,12},{4,8},{8,4},{12,0},{16,28},{20,24},{24,20},{28,16},{1,13},{... | collective-permute-start | bytes 344072 | tf_op jit(solution)/shard_map/ppermute | solution.py:865
  18.2 0.0 collective-permute-done.after_ref.ax_b
  18.2 0.0 collective-permute-done.1.refs_1_.az_a
  18.2 0.0 copy-done.3
  18.2 0.3 %early.1 = (f32[7,128,256]{2,1,0:T(8,128)S(1)}, f32[16,128]{1,0:T(8,128)S(1)}) custom-call(bf16[8,128,256]{2,1,0:T(8,128)(2,1)S(1)} %copy-done.3, f32[5,16,384]{2,1,0:T(8,128)S(1)} %collective-permute-done.after_ref.ax_b, f32[14,16,128]{2,1,0:T(8,128)S(1)} %get-tuple-element.26.refs_0_, f32[34,16,128]{2,1,0:T(8,128)S(1)} %collective-permute-done.1.refs_1_.az_a, ...), custom_call_target="tpu_custom_call" | custom-call | flops 200000000 | bytes 1500000 | tf_op jit(solution)/shard_map/early/pallas_call | solution.py:560
  18.5 0.0 copy-done.1
  18.5 0.2 edges.1
  18.7 2.0 %collective-permute-start.5 = (f32[20,16,128]{2,1,0:T(8,128)S(1)}, f32[20,16,128]{2,1,0:T(8,128)S(1)}, u32[]{:S(2)}, u32[]{:S(2)}) collective-permute-start(f32[20,16,128]{2,1,0:T(8,128)S(1)} %get-tuple-element.30.own_b), channel_id=1, source_target_pairs={{4,8},{8,4},{12,16},{16,12},{20,24},{24,20},{28,0},{0,28},{5,9},{9... | collective-permute-start | bytes 491528 | tf_op jit(solution)/shard_map/ppermute | solution.py:884
  20.7 0.0 collective-permute-start.9
  20.7 0.0 collective-permute-done.6.refs_0_
  20.7 0.0 collective-permute-done.7.refs_1_
  20.7 1.8 %collective-permute-done.8.refs_2_ = f32[14,16,128]{2,1,0:T(8,128)S(1)} collective-permute-done((f32[14,16,128]{2,1,0:T(8,128)S(1)}, f32[14,16,128]{2,1,0:T(8,128)S(1)}, u32[]{:S(2)}, u32[]{:S(2)}) %collective-permute-start.8) | collective-permute-done | bytes 114720 | tf_op jit(solution)/shard_map/ppermute | solution.py:865
  22.5 0.0 copy-done.2
  22.5 0.0 copy-done.4
  22.5 0.0 copy-done.6
  22.5 0.9 %filter.1 = (f32[14,16,128]{2,1,0:T(8,128)S(1)}, f32[14,16,128]{2,1,0:T(8,128)S(1)}, f32[14,8,128]{2,1,0:T(8,128)S(1)}, f32[5,16,128]{2,1,0:T(8,128)S(1)}, f32[5...) custom-call(f32[5,16,16,512]{3,2,1,0:T(8,128)S(1)} %copy-done.1, bf16[8,128,256]{2,1,0:T(8,128)(2,1)S(1)} %copy-done.2, ...), custom_call_target="tpu_custom_call" | custom-call | flops 200000000 | bytes 1500000 | tf_op jit(solution)/shard_map/filter/pallas_call | solution.py:627
  23.4 0.1 collective-permute-start.11
  23.5 1.0 %collective-permute-start.10 = (f32[5,16,128]{2,1,0:T(8,128)S(1)}, f32[5,16,128]{2,1,0:T(8,128)S(1)}, u32[]{:S(2)}, u32[]{:S(2)}) collective-permute-start(f32[5,16,128]{2,1,0:T(8,128)S(1)} %get-tuple-element.42.own_a), channel_id=1, source_target_pairs={{0,1},{1,0},{2,3},{3,2},{4,5},{5,4},{6,7},{7,6},{8,9},{9,8},{10,11... | collective-permute-start | bytes 122888 | tf_op jit(solution)/shard_map/ppermute | solution.py:887
  24.5 0.0 collective-permute-done.9.ax_a
  24.5 1.4 %inner.1 = (f32[16,5,16,128]{3,2,1,0:T(8,128)S(1)}, f32[16,5,16,384]{3,2,1,0:T(8,128)S(1)}, f32[16,128]{1,0:T(8,128)S(1)}) custom-call(f32[8,512]{1,0:T(8,128)S(1)} %copy-done.5, f32[14,16,128]{2,1,0:T(8,128)S(1)} %get-tuple-element.32.own_ref, f32[14,16,128]{2,1,0:T(8,128)S(1)} %get-tuple-element.33.across_ref, ...), custom_call_target="tpu_custom_call" | custom-call | flops 6000000 | bytes 2500000 | tf_op jit(solution)/shard_map/inner/pallas_call | solution.py:716
  25.8 1.1 %collective-permute-done.5.az_b = f32[20,16,128]{2,1,0:T(8,128)S(1)} collective-permute-done((f32[20,16,128]{2,1,0:T(8,128)S(1)}, f32[20,16,128]{2,1,0:T(8,128)S(1)}, u32[]{:S(2)}, u32[]{:S(2)}) %collective-permute-start.5) | collective-permute-done | bytes 163872 | tf_op jit(solution)/shard_map/ppermute | solution.py:884
  27.0 1.4 %last_column.1 = (f32[5,16,16,512]{3,2,1,0:T(8,128)}, f32[16,5,16,128]{3,2,1,0:T(8,128)S(1)}) custom-call(f32[8,512]{1,0:T(8,128)S(1)} %copy-done.5, f32[20,16,128]{2,1,0:T(8,128)S(1)} %get-tuple-element.30.own_b, f32[20,16,128]{2,1,0:T(8,128)S(1)} %collective-permute-done.5.az_b, f32[16,5,16,128]{3,2,1,0:T(8,128)S(1)} %get-tuple-element.38.near_ref, ...), custom_call_target="tpu_custom_call" | custom-call | flops 1000000 | bytes 2500000 | tf_op jit(solution)/shard_map/last_column/pallas_call | solution.py:784
  28.4 0.0 collective-permute-done.10.ax_a
  28.4 0.0 collective-permute-done.11.ax_b
  28.4 1.0 %finish.1 = f32[5,16,16,512]{3,2,1,0:T(8,128)} custom-call(f32[16,5,16,128]{3,2,1,0:T(8,128)S(1)} %get-tuple-element.41.near_ref, f32[5,16,128]{2,1,0:T(8,128)S(1)} %get-tuple-element.42.own_a, f32[5,24,128]{2,1,0:T(8,128)S(1)} %get-tuple-element.43.own_b, f32[5,16,128]{2,1,0:T(8,128)S(1)} %collective-permute-done.10.ax_a, ...), custom_call_target="tpu_custom_call", output_to_operand_aliasing={{}: (5, {})} | custom-call | flops 100000 | bytes 1500000 | tf_op jit(solution)/shard_map/finish/pallas_call | solution.py:834
  (1 shorter events, 0.0 us)
Async XLA Ops:
  0.0 1.7 %copy-start = (f32[5,16,16,512]{3,2,1,0:T(8,128)S(1)}, f32[5,16,16,512]{3,2,1,0:T(8,128)}, u32[]{:S(2)}) copy-start(f32[5,16,16,512]{3,2,1,0:T(8,128)} %x_ref.9) | copy-start | bytes 7864324
  1.7 8.0 %copy-start.5 = (f32[8,512]{1,0:T(8,128)S(1)}, f32[8,512]{1,0:T(8,128)}, u32[]{:S(2)}) copy-start(f32[8,512]{1,0:T(8,128)} %constant.10.clone.coef_ref) | copy-start | bytes 49156
  1.7 16.5 %copy-start.3 = (bf16[8,128,256]{2,1,0:T(8,128)(2,1)S(1)}, bf16[8,128,256]{2,1,0:T(8,128)(2,1)}, u32[]{:S(2)}) copy-start(bf16[8,128,256]{2,1,0:T(8,128)(2,1)} %constant.11.clone.forward_ref) | copy-start | bytes 1572868
  2.1 16.4 %copy-start.1 = (f32[5,16,16,512]{3,2,1,0:T(8,128)S(1)}, f32[5,16,16,512]{3,2,1,0:T(8,128)}, u32[]{:S(2)}) copy-start(f32[5,16,16,512]{3,2,1,0:T(8,128)} %x_ref.9) | copy-start | bytes 7864324
  2.1 16.1 %collective-permute-start.1 = (f32[34,16,128]{2,1,0:T(8,128)S(1)}, f32[34,16,128]{2,1,0:T(8,128)S(1)}, u32[]{:S(2)}, u32[]{:S(2)}) collective-permute-start(f32[34,16,128]{2,1,0:T(8,128)S(1)} %get-tuple-element.27.own_a), channel_id=1, source_target_pairs={{0,4},{4,0},{8,12},{12,8},{16,20},{20,16},{24,28},{28,24},{1,5},{5... | collective-permute-start | bytes 835592 | tf_op jit(solution)/shard_map/ppermute | solution.py:865
  5.1 7.9 %collective-permute-start.4 = (f32[14,16,128]{2,1,0:T(8,128)S(1)}, f32[14,16,128]{2,1,0:T(8,128)S(1)}, u32[]{:S(2)}, u32[]{:S(2)}) collective-permute-start(f32[14,16,128]{2,1,0:T(8,128)S(1)} %get-tuple-element.26.refs_0_), channel_id=1, source_target_pairs={{0,16},{4,20},{8,24},{12,28},{16,0},{20,4},{24,8},{28,12},{1,17},{... | collective-permute-start | bytes 344072 | tf_op jit(solution)/shard_map/ppermute | solution.py:865
  7.7 6.9 %collective-permute-start.2 = (f32[14,16,128]{2,1,0:T(8,128)S(1)}, f32[14,16,128]{2,1,0:T(8,128)S(1)}, u32[]{:S(2)}, u32[]{:S(2)}) collective-permute-start(f32[14,16,128]{2,1,0:T(8,128)S(1)} %get-tuple-element.26.refs_0_), channel_id=1, source_target_pairs={{0,8},{4,12},{8,0},{12,4},{16,24},{20,28},{24,16},{28,20},{1,9},{5... | collective-permute-start | bytes 344072 | tf_op jit(solution)/shard_map/ppermute | solution.py:865
  9.3 6.8 %collective-permute-start.3 = (f32[14,16,128]{2,1,0:T(8,128)S(1)}, f32[14,16,128]{2,1,0:T(8,128)S(1)}, u32[]{:S(2)}, u32[]{:S(2)}) collective-permute-start(f32[14,16,128]{2,1,0:T(8,128)S(1)} %get-tuple-element.26.refs_0_), channel_id=1, source_target_pairs={{0,12},{4,8},{8,4},{12,0},{16,28},{20,24},{24,20},{28,16},{1,13},{... | collective-permute-start | bytes 344072 | tf_op jit(solution)/shard_map/ppermute | solution.py:865
  9.7 8.5 %collective-permute-start = (f32[5,16,384]{2,1,0:T(8,128)S(1)}, f32[5,16,384]{2,1,0:T(8,128)S(1)}, u32[]{:S(2)}, u32[]{:S(2)}) collective-permute-start(f32[5,16,384]{2,1,0:T(8,128)S(1)} %get-tuple-element.25), channel_id=1, source_target_pairs={{1,2},{2,1},{3,0},{0,3},{5,6},{6,5},{7,4},{4,7},{9,10},{10,9},{11,... | collective-permute-start | bytes 368648 | tf_op jit(solution)/shard_map/ppermute | solution.py:868
  12.0 10.5 %copy-start.2 = (bf16[8,128,256]{2,1,0:T(8,128)(2,1)S(1)}, bf16[8,128,256]{2,1,0:T(8,128)(2,1)}, u32[]{:S(2)}) copy-start(bf16[8,128,256]{2,1,0:T(8,128)(2,1)} %constant.12.clone.forward_ref) | copy-start | bytes 1572868
  12.0 10.5 %copy-start.4 = (bf16[8,48,384]{2,1,0:T(8,128)(2,1)S(1)}, bf16[8,48,384]{2,1,0:T(8,128)(2,1)}, u32[]{:S(2)}) copy-start(bf16[8,48,384]{2,1,0:T(8,128)(2,1)} %constant.13.clone.inverse_ref) | copy-start | bytes 884740
  12.0 10.5 %copy-start.6 = (f32[128,128]{1,0:T(8,128)S(1)}, f32[128,128]{1,0:T(8,128)}, u32[]{:S(2)}) copy-start(f32[128,128]{1,0:T(8,128)} %constant.14.clone.mask_ref) | copy-start | bytes 196612
  13.1 7.6 %collective-permute-start.6 = (f32[14,16,128]{2,1,0:T(8,128)S(1)}, f32[14,16,128]{2,1,0:T(8,128)S(1)}, u32[]{:S(2)}, u32[]{:S(2)}) collective-permute-start(f32[14,16,128]{2,1,0:T(8,128)S(1)} %gate.1.refs_4_), channel_id=1, source_target_pairs={{0,4},{4,0},{8,12},{12,8},{16,20},{20,16},{24,28},{28,24},{1,5},{5... | collective-permute-start | bytes 344072 | tf_op jit(solution)/shard_map/ppermute | solution.py:865
  14.6 6.1 %collective-permute-start.7 = (f32[14,16,128]{2,1,0:T(8,128)S(1)}, f32[14,16,128]{2,1,0:T(8,128)S(1)}, u32[]{:S(2)}, u32[]{:S(2)}) collective-permute-start(f32[14,16,128]{2,1,0:T(8,128)S(1)} %gate.1.refs_4_), channel_id=1, source_target_pairs={{0,8},{4,12},{8,0},{12,4},{16,24},{20,28},{24,16},{28,20},{1,9},{5... | collective-permute-start | bytes 344072 | tf_op jit(solution)/shard_map/ppermute | solution.py:865
  16.1 6.4 %collective-permute-start.8 = (f32[14,16,128]{2,1,0:T(8,128)S(1)}, f32[14,16,128]{2,1,0:T(8,128)S(1)}, u32[]{:S(2)}, u32[]{:S(2)}) collective-permute-start(f32[14,16,128]{2,1,0:T(8,128)S(1)} %gate.1.refs_4_), channel_id=1, source_target_pairs={{0,12},{4,8},{8,4},{12,0},{16,28},{20,24},{24,20},{28,16},{1,13},{... | collective-permute-start | bytes 344072 | tf_op jit(solution)/shard_map/ppermute | solution.py:865
  18.7 8.3 %collective-permute-start.5 = (f32[20,16,128]{2,1,0:T(8,128)S(1)}, f32[20,16,128]{2,1,0:T(8,128)S(1)}, u32[]{:S(2)}, u32[]{:S(2)}) collective-permute-start(f32[20,16,128]{2,1,0:T(8,128)S(1)} %get-tuple-element.30.own_b), channel_id=1, source_target_pairs={{4,8},{8,4},{12,16},{16,12},{20,24},{24,20},{28,0},{0,28},{5,9},{9... | collective-permute-start | bytes 491528 | tf_op jit(solution)/shard_map/ppermute | solution.py:884
  20.7 3.8 %collective-permute-start.9 = (f32[5,16,384]{2,1,0:T(8,128)S(1)}, f32[5,16,384]{2,1,0:T(8,128)S(1)}, u32[]{:S(2)}, u32[]{:S(2)}) collective-permute-start(f32[5,16,384]{2,1,0:T(8,128)S(1)} %get-tuple-element.36), channel_id=1, source_target_pairs={{0,1},{1,0},{2,3},{3,2},{4,5},{5,4},{6,7},{7,6},{8,9},{9,8},{10,11... | collective-permute-start | bytes 368648 | tf_op jit(solution)/shard_map/ppermute | solution.py:883
  23.4 5.0 %collective-permute-start.11 = (f32[5,24,128]{2,1,0:T(8,128)S(1)}, f32[5,24,128]{2,1,0:T(8,128)S(1)}, u32[]{:S(2)}, u32[]{:S(2)}) collective-permute-start(f32[5,24,128]{2,1,0:T(8,128)S(1)} %get-tuple-element.43.own_b), channel_id=1, source_target_pairs={{1,2},{2,1},{3,0},{0,3},{5,6},{6,5},{7,4},{4,7},{9,10},{10,9},{11,... | collective-permute-start | bytes 184328 | tf_op jit(solution)/shard_map/ppermute | solution.py:888
  23.5 4.9 %collective-permute-start.10 = (f32[5,16,128]{2,1,0:T(8,128)S(1)}, f32[5,16,128]{2,1,0:T(8,128)S(1)}, u32[]{:S(2)}, u32[]{:S(2)}) collective-permute-start(f32[5,16,128]{2,1,0:T(8,128)S(1)} %get-tuple-element.42.own_a), channel_id=1, source_target_pairs={{0,1},{1,0},{2,3},{3,2},{4,5},{5,4},{6,7},{7,6},{8,9},{9,8},{10,11... | collective-permute-start | bytes 122888 | tf_op jit(solution)/shard_map/ppermute | solution.py:887

commit v9 on v8

--- a/solution.py
+++ b/solution.py
@@ -311,32 +311,6 @@
         name="pack",
         cost_estimate=pl.CostEstimate(flops=1000000, bytes_accessed=800000, transcendentals=0),
     )(fields)
-
-
-def edges_kernel(plan, x_ref, after_ref, az_b, rest_a):
-    del after_ref
-    even_plane = 1 - lax.axis_index("ax") % 2
-    rest_a[...] = x_ref[:, even_plane * (plan.planes - 1), :, LANES:]
-    even_theta = lax.axis_index("az") % 2 == 0
-    pick_columns(plan, x_ref, jnp.logical_not(even_theta), az_b, 0)
-
-
-def edges(plan, fields, after):
-    f32 = jnp.float32
-    columns = plan.fields * plan.radial // LANES
-    inside = pl.BlockSpec(memory_space=pltpu.VMEM)
-    return pl.pallas_call(
-        functools.partial(edges_kernel, plan),
-        in_specs=[inside] * 2,
-        out_specs=[inside] * 2,
-        out_shape=[
-            jax.ShapeDtypeStruct((columns, plan.theta, LANES), f32),
-            jax.ShapeDtypeStruct((plan.fields, plan.theta, plan.radial - LANES), f32),
-        ],
-        compiler_params=pltpu.CompilerParams(vmem_limit_bytes=VMEM_LIMIT),
-        name="edges",
-        cost_estimate=pl.CostEstimate(flops=0, bytes_accessed=1000000, transcendentals=0),
-    )(fields, after)
 
 
 def advance(coef, q, jp, jm, tp, tm, kp, km):
@@ -543,10 +517,14 @@
     return total
 
 
-def early_kernel(plan, forward_ref, after_ref, *refs):
+def early_kernel(plan, x_ref, forward_ref, after_ref, *refs):
     del after_ref
     pieces = refs[: len(plan.early)]
-    spectra_ref, total_ref = refs[len(plan.early) :]
+    spectra_ref, total_ref, az_b, rest_a = refs[len(plan.early) :]
+    odd_theta = lax.axis_index("az") % 2 == 1
+    pick_columns(plan, x_ref, odd_theta, az_b, 0)
+    even_plane = 1 - lax.axis_index("ax") % 2
+    rest_a[...] = x_ref[:, even_plane * (plan.planes - 1), :, LANES:]
     table = forward_ref[lax.axis_index("az")]
     for g in range(0, plan.groups, 2):
         both = halves(two_groups(pieces, g), plan.depth)
@@ -554,21 +532,24 @@
     total_ref[...] = alternating_sums(plan, pieces)
 
 
-def early_spectra(plan, pieces, after):
+def early_spectra(plan, fields, pieces, after):
+    columns = plan.fields * plan.radial // LANES
     inside = pl.BlockSpec(memory_space=pltpu.VMEM)
     f32 = jnp.float32
     return pl.pallas_call(
         functools.partial(early_kernel, plan),
-        in_specs=[inside] * (2 + len(pieces)),
-        out_specs=[inside] * 2,
+        in_specs=[inside] * (3 + len(pieces)),
+        out_specs=[inside] * 4,
         out_shape=[
             jax.ShapeDtypeStruct((plan.groups // 2, 2 * plan.modes, 2 * LANES), f32),
             jax.ShapeDtypeStruct((plan.theta, LANES), f32),
+            jax.ShapeDtypeStruct((columns, plan.theta, LANES), f32),
+            jax.ShapeDtypeStruct((plan.fields, plan.theta, plan.radial - LANES), f32),
         ],
         compiler_params=pltpu.CompilerParams(vmem_limit_bytes=VMEM_LIMIT),
         name="early",
         cost_estimate=pl.CostEstimate(flops=200000000, bytes_accessed=1500000, transcendentals=0),
-    )(jnp.asarray(plan.forward(plan.early)), after, *pieces)
+    )(fields, jnp.asarray(plan.forward(plan.early)), after, *pieces)
 
 
 def filter_kernel(plan, x_ref, forward_ref, inverse_ref, mask_ref, early_ref, early_total, *refs):
@@ -878,8 +859,7 @@
     for p in range(half - 1, 0, -1):
         pieces[half + p] = send(onward, p)
     pieces[half] = onward
-    early = early_spectra(plan, pieces[: half + 1], rest_b)
-    column, rest_a = edges(plan, fields, early[1])
+    *early, column, rest_a = early_spectra(plan, fields, pieces[: half + 1], rest_b)
     rests = (lax.ppermute(rest_a, "ax", pairs(slabs, 0)), rest_b)
     sides = (pieces[1], lax.ppermute(column, "az", pairs(sectors, 1)))
     *parts, message_a, message_b = filtered(plan, fields, pieces[half + 1 :], early)

time: 29.5 us -> 29.7 us (level)
  waiting for transfers between devices: 4.98 us -> 3.85 us
  local copies, waits for them, and re-layouts: 1.77 us -> 2.49 us
  starting transfers between devices: 14.7 us -> 15.3 us
    ppermute x7, waiting for transfers between devices: 3.83 us -> 2.92 us  [send(): return lax.ppermute(x, 'az', [(i, i ^ distance) for i in range(sectors)])]
    unnamed x14 -> x16, local copies, waits for them, and re-layouts: 1.77 us -> 2.49 us
    ppermute x7, starting transfers between devices: 11.7 us -> 12.4 us  [send(): return lax.ppermute(x, 'az', [(i, i ^ distance) for i in range(sectors)])]
where the time goes in v9:
time: 29.7 us; the launch traced here: 29.5 us
  starting transfers between devices  15.3 us (52%)
  Pallas kernels  7.74 us (26%)
  waiting for transfers between devices  3.85 us (13%)
  local copies, waits for them, and re-layouts  2.49 us (8%)
    ppermute x7, starting transfers between devices, send(): return lax.ppermute(x, 'az', [(i, i ^ distance) for i in range(sectors)])  12.4 us
    ppermute x7, waiting for transfers between devices, send(): return lax.ppermute(x, 'az', [(i, i ^ distance) for i in range(sectors)])  2.92 us
    unnamed x16, local copies, waits for them, and re-layouts  2.49 us
    pallas_call x1, Pallas kernels, outer(): pl.pallas_call(functools.partial(outer_kernel, plan), in_specs=[inside] *...  2.26 us
    ppermute x1, starting transfers between devices, fast_on_device(): sides = (pieces[1], lax.ppermute(column, 'az', pairs(sectors, 1)))  1.98 us
    pallas_call x1, Pallas kernels, last_column(): pl.pallas_call(functools.partial(column_kernel, plan), in_specs=[inside]...  1.43 us
    pallas_call x1, Pallas kernels, inner(): pl.pallas_call(functools.partial(inner_kernel, plan), in_specs=[inside] *...  1.36 us
    pallas_call x1, Pallas kernels, finish(): pl.pallas_call(functools.partial(finish_kernel, plan), in_specs=[inside]...  0.97 us
  transfers between devices with their start and end apart: 12, of which 4 were waited for; matrix products, arithmetic and copies ran while one was open for 0% of the time, Pallas kernels for 22%

profile of v9, /device:TPU:0, one launch (start us, length us, event | category | flops | bytes accessed | tf_op | source)
XLA Modules:
  0.0 29.5 jit_solution(14239263564824208343)
XLA Ops:
  0.0 0.0 copy-start
  0.0 1.7 %copy-done = f32[5,16,16,512]{3,2,1,0:T(8,128)S(1)} copy-done((f32[5,16,16,512]{3,2,1,0:T(8,128)S(1)}, f32[5,16,16,512]{3,2,1,0:T(8,128)}, u32[]{:S(2)}) %copy-start) | copy-done | bytes 2621464
  1.7 0.0 copy-start.1
  1.7 0.0 copy-start.3
  1.7 0.3 %pack.1 = (f32[14,16,128]{2,1,0:T(8,128)S(1)}, f32[34,16,128]{2,1,0:T(8,128)S(1)}, f32[5,16,384]{2,1,0:T(8,128)S(1)}) custom-call(f32[5,16,16,512]{3,2,1,0:T(8,128)S(1)} %copy-done), custom_call_target="tpu_custom_call" | custom-call | flops 1000000 | bytes 800000 | tf_op jit(solution)/shard_map/pack/pallas_call | solution.py:301
  2.1 3.0 %collective-permute-start.1 = (f32[34,16,128]{2,1,0:T(8,128)S(1)}, f32[34,16,128]{2,1,0:T(8,128)S(1)}, u32[]{:S(2)}, u32[]{:S(2)}) collective-permute-start(f32[34,16,128]{2,1,0:T(8,128)S(1)} %get-tuple-element.27.own_a), channel_id=1, source_target_pairs={{0,4},{4,0},{8,12},{12,8},{16,20},{20,16},{24,28},{28,24},{1,5},{5... | collective-permute-start | bytes 835592 | tf_op jit(solution)/shard_map/ppermute | solution.py:846
  5.1 2.6 %collective-permute-start.4 = (f32[14,16,128]{2,1,0:T(8,128)S(1)}, f32[14,16,128]{2,1,0:T(8,128)S(1)}, u32[]{:S(2)}, u32[]{:S(2)}) collective-permute-start(f32[14,16,128]{2,1,0:T(8,128)S(1)} %get-tuple-element.26.refs_0_), channel_id=1, source_target_pairs={{0,16},{4,20},{8,24},{12,28},{16,0},{20,4},{24,8},{28,12},{1,17},{... | collective-permute-start | bytes 344072 | tf_op jit(solution)/shard_map/ppermute | solution.py:846
  7.7 1.6 %collective-permute-start.2 = (f32[14,16,128]{2,1,0:T(8,128)S(1)}, f32[14,16,128]{2,1,0:T(8,128)S(1)}, u32[]{:S(2)}, u32[]{:S(2)}) collective-permute-start(f32[14,16,128]{2,1,0:T(8,128)S(1)} %get-tuple-element.26.refs_0_), channel_id=1, source_target_pairs={{0,8},{4,12},{8,0},{12,4},{16,24},{20,28},{24,16},{28,20},{1,9},{5... | collective-permute-start | bytes 344072 | tf_op jit(solution)/shard_map/ppermute | solution.py:846
  9.3 0.4 %collective-permute-start.3 = (f32[14,16,128]{2,1,0:T(8,128)S(1)}, f32[14,16,128]{2,1,0:T(8,128)S(1)}, u32[]{:S(2)}, u32[]{:S(2)}) collective-permute-start(f32[14,16,128]{2,1,0:T(8,128)S(1)} %get-tuple-element.26.refs_0_), channel_id=1, source_target_pairs={{0,12},{4,8},{8,4},{12,0},{16,28},{20,24},{24,20},{28,16},{1,13},{... | collective-permute-start | bytes 344072 | tf_op jit(solution)/shard_map/ppermute | solution.py:846
  9.7 0.0 collective-permute-start
  9.7 0.0 copy-start.5
  9.7 0.7 %copy-done.5 = f32[8,512]{1,0:T(8,128)S(1)} copy-done((f32[8,512]{1,0:T(8,128)S(1)}, f32[8,512]{1,0:T(8,128)}, u32[]{:S(2)}) %copy-start.5) | copy-done | bytes 16408
  10.4 2.3 %outer.1 = (f32[16,5,16,384]{3,2,1,0:T(8,128)S(1)}, f32[8,128]{1,0:T(8,128)S(1)}) custom-call(f32[8,512]{1,0:T(8,128)S(1)} %copy-done.5, f32[5,16,16,512]{3,2,1,0:T(8,128)S(1)} %copy-done), custom_call_target="tpu_custom_call" | custom-call | flops 16000000 | bytes 5000000 | tf_op jit(solution)/shard_map/outer/pallas_call | solution.py:401
  12.7 0.0 copy-start.2
  12.7 0.0 copy-start.4
  12.7 0.0 copy-start.7
  12.7 0.3 %collective-permute-done.4.x_ref = f32[14,16,128]{2,1,0:T(8,128)S(1)} collective-permute-done((f32[14,16,128]{2,1,0:T(8,128)S(1)}, f32[14,16,128]{2,1,0:T(8,128)S(1)}, u32[]{:S(2)}, u32[]{:S(2)}) %collective-permute-start.4) | collective-permute-done | bytes 114720 | tf_op jit(solution)/shard_map/ppermute | solution.py:846
  13.1 1.3 %collective-permute-start.6 = (f32[14,16,128]{2,1,0:T(8,128)S(1)}, f32[14,16,128]{2,1,0:T(8,128)S(1)}, u32[]{:S(2)}, u32[]{:S(2)}) collective-permute-start(f32[14,16,128]{2,1,0:T(8,128)S(1)} %gate.1.refs_4_), channel_id=1, source_target_pairs={{0,4},{4,0},{8,12},{12,8},{16,20},{20,16},{24,28},{28,24},{1,5},{5... | collective-permute-start | bytes 344072 | tf_op jit(solution)/shard_map/ppermute | solution.py:846
  14.3 0.3 collective-permute-done.2.refs_2_
  14.6 1.5 %collective-permute-start.7 = (f32[14,16,128]{2,1,0:T(8,128)S(1)}, f32[14,16,128]{2,1,0:T(8,128)S(1)}, u32[]{:S(2)}, u32[]{:S(2)}) collective-permute-start(f32[14,16,128]{2,1,0:T(8,128)S(1)} %gate.1.refs_4_), channel_id=1, source_target_pairs={{0,8},{4,12},{8,0},{12,4},{16,24},{20,28},{24,16},{28,20},{1,9},{5... | collective-permute-start | bytes 344072 | tf_op jit(solution)/shard_map/ppermute | solution.py:846
  16.1 0.0 collective-permute-done.3.refs_3_
  16.1 2.1 %collective-permute-start.8 = (f32[14,16,128]{2,1,0:T(8,128)S(1)}, f32[14,16,128]{2,1,0:T(8,128)S(1)}, u32[]{:S(2)}, u32[]{:S(2)}) collective-permute-start(f32[14,16,128]{2,1,0:T(8,128)S(1)} %gate.1.refs_4_), channel_id=1, source_target_pairs={{0,12},{4,8},{8,4},{12,0},{16,28},{20,24},{24,20},{28,16},{1,13},{... | collective-permute-start | bytes 344072 | tf_op jit(solution)/shard_map/ppermute | solution.py:846
  18.2 0.0 collective-permute-done.after_ref.ax_b
  18.2 0.0 collective-permute-done.1.refs_1_.az_a
  18.2 0.0 copy-done.1
  18.2 0.0 copy-done.3
  18.2 0.5 %early.1 = (f32[7,128,256]{2,1,0:T(8,128)S(1)}, f32[16,128]{1,0:T(8,128)S(1)}, f32[20,16,128]{2,1,0:T(8,128)S(1)}, f32[5,16,384]{2,1,0:T(8,128)S(1)}) custom-call(f32[5,16,16,512]{3,2,1,0:T(8,128)S(1)} %copy-done.1, bf16[8,128,256]{2,1,0:T(8,128)(2,1)S(1)} %copy-done.3, f32[5,16,384]{2,1,0:T(8,128)S(1)} %collective-permute-done.after_ref.ax_b, ...), custom_call_target="tpu_custom_call" | custom-call | flops 200000000 | bytes 1500000 | tf_op jit(solution)/shard_map/early/pallas_call | solution.py:539
  18.7 0.0 copy-start.6
  18.7 2.0 %collective-permute-start.5 = (f32[20,16,128]{2,1,0:T(8,128)S(1)}, f32[20,16,128]{2,1,0:T(8,128)S(1)}, u32[]{:S(2)}, u32[]{:S(2)}) collective-permute-start(f32[20,16,128]{2,1,0:T(8,128)S(1)} %get-tuple-element.29.own_b), channel_id=1, source_target_pairs={{4,8},{8,4},{12,16},{16,12},{20,24},{24,20},{28,0},{0,28},{5,9},{9... | collective-permute-start | bytes 491528 | tf_op jit(solution)/shard_map/ppermute | solution.py:864
  20.7 0.0 collective-permute-start.9
  20.7 0.0 collective-permute-done.6.refs_0_
  20.7 0.0 collective-permute-done.7.refs_1_
  20.7 2.3 %collective-permute-done.8.refs_2_ = f32[14,16,128]{2,1,0:T(8,128)S(1)} collective-permute-done((f32[14,16,128]{2,1,0:T(8,128)S(1)}, f32[14,16,128]{2,1,0:T(8,128)S(1)}, u32[]{:S(2)}, u32[]{:S(2)}) %collective-permute-start.8) | collective-permute-done | bytes 114720 | tf_op jit(solution)/shard_map/ppermute | solution.py:846
  23.0 0.0 copy-done.2
  23.0 0.0 copy-done.4
  23.0 0.0 copy-done.7
  23.0 0.9 %filter.1 = (f32[14,16,128]{2,1,0:T(8,128)S(1)}, f32[14,16,128]{2,1,0:T(8,128)S(1)}, f32[14,8,128]{2,1,0:T(8,128)S(1)}, f32[5,16,128]{2,1,0:T(8,128)S(1)}, f32[5...) custom-call(f32[5,16,16,512]{3,2,1,0:T(8,128)S(1)} %copy-done.1, bf16[8,128,256]{2,1,0:T(8,128)(2,1)S(1)} %copy-done.2, ...), custom_call_target="tpu_custom_call" | custom-call | flops 200000000 | bytes 1500000 | tf_op jit(solution)/shard_map/filter/pallas_call | solution.py:608
  23.9 0.1 collective-permute-start.11
  24.0 0.8 %collective-permute-start.10 = (f32[5,16,128]{2,1,0:T(8,128)S(1)}, f32[5,16,128]{2,1,0:T(8,128)S(1)}, u32[]{:S(2)}, u32[]{:S(2)}) collective-permute-start(f32[5,16,128]{2,1,0:T(8,128)S(1)} %get-tuple-element.42.own_a), channel_id=1, source_target_pairs={{0,1},{1,0},{2,3},{3,2},{4,5},{5,4},{6,7},{7,6},{8,9},{9,8},{10,11... | collective-permute-start | bytes 122888 | tf_op jit(solution)/shard_map/ppermute | solution.py:867
  24.7 0.0 collective-permute-done.9.ax_a
  24.7 0.0 copy-done.6
  24.7 1.4 %inner.1 = (f32[16,5,16,128]{3,2,1,0:T(8,128)S(1)}, f32[16,5,16,384]{3,2,1,0:T(8,128)S(1)}, f32[16,128]{1,0:T(8,128)S(1)}) custom-call(f32[8,512]{1,0:T(8,128)S(1)} %copy-done.6, f32[14,16,128]{2,1,0:T(8,128)S(1)} %get-tuple-element.32.own_ref, f32[14,16,128]{2,1,0:T(8,128)S(1)} %get-tuple-element.33.across_ref, ...), custom_call_target="tpu_custom_call" | custom-call | flops 6000000 | bytes 2500000 | tf_op jit(solution)/shard_map/inner/pallas_call | solution.py:697
  26.1 0.9 %collective-permute-done.5.az_b = f32[20,16,128]{2,1,0:T(8,128)S(1)} collective-permute-done((f32[20,16,128]{2,1,0:T(8,128)S(1)}, f32[20,16,128]{2,1,0:T(8,128)S(1)}, u32[]{:S(2)}, u32[]{:S(2)}) %collective-permute-start.5) | collective-permute-done | bytes 163872 | tf_op jit(solution)/shard_map/ppermute | solution.py:864
  27.0 1.4 %last_column.1 = (f32[5,16,16,512]{3,2,1,0:T(8,128)}, f32[16,5,16,128]{3,2,1,0:T(8,128)S(1)}) custom-call(f32[8,512]{1,0:T(8,128)S(1)} %copy-done.6, f32[20,16,128]{2,1,0:T(8,128)S(1)} %get-tuple-element.29.own_b, f32[20,16,128]{2,1,0:T(8,128)S(1)} %collective-permute-done.5.az_b, f32[16,5,16,128]{3,2,1,0:T(8,128)S(1)} %get-tuple-element.38.near_ref, ...), custom_call_target="tpu_custom_call" | custom-call | flops 1000000 | bytes 2500000 | tf_op jit(solution)/shard_map/last_column/pallas_call | solution.py:765
  28.5 0.0 collective-permute-done.10.ax_a
  28.5 0.0 collective-permute-done.11.ax_b
  28.5 1.0 %finish.1 = f32[5,16,16,512]{3,2,1,0:T(8,128)} custom-call(f32[16,5,16,128]{3,2,1,0:T(8,128)S(1)} %get-tuple-element.41.near_ref, f32[5,16,128]{2,1,0:T(8,128)S(1)} %get-tuple-element.42.own_a, f32[5,24,128]{2,1,0:T(8,128)S(1)} %get-tuple-element.43.own_b, f32[5,16,128]{2,1,0:T(8,128)S(1)} %collective-permute-done.10.ax_a, ...), custom_call_target="tpu_custom_call", output_to_operand_aliasing={{}: (5, {})} | custom-call | flops 100000 | bytes 1500000 | tf_op jit(solution)/shard_map/finish/pallas_call | solution.py:815
  (1 shorter events, 0.0 us)
Async XLA Ops:
  0.0 1.7 %copy-start = (f32[5,16,16,512]{3,2,1,0:T(8,128)S(1)}, f32[5,16,16,512]{3,2,1,0:T(8,128)}, u32[]{:S(2)}) copy-start(f32[5,16,16,512]{3,2,1,0:T(8,128)} %x_ref.9) | copy-start | bytes 7864324
  1.7 16.4 %copy-start.1 = (f32[5,16,16,512]{3,2,1,0:T(8,128)S(1)}, f32[5,16,16,512]{3,2,1,0:T(8,128)}, u32[]{:S(2)}) copy-start(f32[5,16,16,512]{3,2,1,0:T(8,128)} %x_ref.9) | copy-start | bytes 7864324
  1.7 16.5 %copy-start.3 = (bf16[8,128,256]{2,1,0:T(8,128)(2,1)S(1)}, bf16[8,128,256]{2,1,0:T(8,128)(2,1)}, u32[]{:S(2)}) copy-start(bf16[8,128,256]{2,1,0:T(8,128)(2,1)} %constant.11.clone.forward_ref) | copy-start | bytes 1572868
  2.1 16.1 %collective-permute-start.1 = (f32[34,16,128]{2,1,0:T(8,128)S(1)}, f32[34,16,128]{2,1,0:T(8,128)S(1)}, u32[]{:S(2)}, u32[]{:S(2)}) collective-permute-start(f32[34,16,128]{2,1,0:T(8,128)S(1)} %get-tuple-element.27.own_a), channel_id=1, source_target_pairs={{0,4},{4,0},{8,12},{12,8},{16,20},{20,16},{24,28},{28,24},{1,5},{5... | collective-permute-start | bytes 835592 | tf_op jit(solution)/shard_map/ppermute | solution.py:846
  5.1 7.9 %collective-permute-start.4 = (f32[14,16,128]{2,1,0:T(8,128)S(1)}, f32[14,16,128]{2,1,0:T(8,128)S(1)}, u32[]{:S(2)}, u32[]{:S(2)}) collective-permute-start(f32[14,16,128]{2,1,0:T(8,128)S(1)} %get-tuple-element.26.refs_0_), channel_id=1, source_target_pairs={{0,16},{4,20},{8,24},{12,28},{16,0},{20,4},{24,8},{28,12},{1,17},{... | collective-permute-start | bytes 344072 | tf_op jit(solution)/shard_map/ppermute | solution.py:846
  7.7 6.9 %collective-permute-start.2 = (f32[14,16,128]{2,1,0:T(8,128)S(1)}, f32[14,16,128]{2,1,0:T(8,128)S(1)}, u32[]{:S(2)}, u32[]{:S(2)}) collective-permute-start(f32[14,16,128]{2,1,0:T(8,128)S(1)} %get-tuple-element.26.refs_0_), channel_id=1, source_target_pairs={{0,8},{4,12},{8,0},{12,4},{16,24},{20,28},{24,16},{28,20},{1,9},{5... | collective-permute-start | bytes 344072 | tf_op jit(solution)/shard_map/ppermute | solution.py:846
  9.3 6.8 %collective-permute-start.3 = (f32[14,16,128]{2,1,0:T(8,128)S(1)}, f32[14,16,128]{2,1,0:T(8,128)S(1)}, u32[]{:S(2)}, u32[]{:S(2)}) collective-permute-start(f32[14,16,128]{2,1,0:T(8,128)S(1)} %get-tuple-element.26.refs_0_), channel_id=1, source_target_pairs={{0,12},{4,8},{8,4},{12,0},{16,28},{20,24},{24,20},{28,16},{1,13},{... | collective-permute-start | bytes 344072 | tf_op jit(solution)/shard_map/ppermute | solution.py:846
  9.7 8.5 %collective-permute-start = (f32[5,16,384]{2,1,0:T(8,128)S(1)}, f32[5,16,384]{2,1,0:T(8,128)S(1)}, u32[]{:S(2)}, u32[]{:S(2)}) collective-permute-start(f32[5,16,384]{2,1,0:T(8,128)S(1)} %get-tuple-element.25), channel_id=1, source_target_pairs={{1,2},{2,1},{3,0},{0,3},{5,6},{6,5},{7,4},{4,7},{9,10},{10,9},{11,... | collective-permute-start | bytes 368648 | tf_op jit(solution)/shard_map/ppermute | solution.py:849
  9.7 0.7 %copy-start.5 = (f32[8,512]{1,0:T(8,128)S(1)}, f32[8,512]{1,0:T(8,128)}, u32[]{:S(2)}) copy-start(f32[8,512]{1,0:T(8,128)} %constant.10.clone.coef_ref) | copy-start | bytes 49156
  12.7 10.3 %copy-start.2 = (bf16[8,128,256]{2,1,0:T(8,128)(2,1)S(1)}, bf16[8,128,256]{2,1,0:T(8,128)(2,1)}, u32[]{:S(2)}) copy-start(bf16[8,128,256]{2,1,0:T(8,128)(2,1)} %constant.12.clone.forward_ref) | copy-start | bytes 1572868
  12.7 10.3 %copy-start.4 = (bf16[8,48,384]{2,1,0:T(8,128)(2,1)S(1)}, bf16[8,48,384]{2,1,0:T(8,128)(2,1)}, u32[]{:S(2)}) copy-start(bf16[8,48,384]{2,1,0:T(8,128)(2,1)} %constant.13.clone.inverse_ref) | copy-start | bytes 884740
  12.7 10.3 %copy-start.7 = (f32[128,128]{1,0:T(8,128)S(1)}, f32[128,128]{1,0:T(8,128)}, u32[]{:S(2)}) copy-start(f32[128,128]{1,0:T(8,128)} %constant.14.clone.mask_ref) | copy-start | bytes 196612
  13.1 7.6 %collective-permute-start.6 = (f32[14,16,128]{2,1,0:T(8,128)S(1)}, f32[14,16,128]{2,1,0:T(8,128)S(1)}, u32[]{:S(2)}, u32[]{:S(2)}) collective-permute-start(f32[14,16,128]{2,1,0:T(8,128)S(1)} %gate.1.refs_4_), channel_id=1, source_target_pairs={{0,4},{4,0},{8,12},{12,8},{16,20},{20,16},{24,28},{28,24},{1,5},{5... | collective-permute-start | bytes 344072 | tf_op jit(solution)/shard_map/ppermute | solution.py:846
  14.6 6.1 %collective-permute-start.7 = (f32[14,16,128]{2,1,0:T(8,128)S(1)}, f32[14,16,128]{2,1,0:T(8,128)S(1)}, u32[]{:S(2)}, u32[]{:S(2)}) collective-permute-start(f32[14,16,128]{2,1,0:T(8,128)S(1)} %gate.1.refs_4_), channel_id=1, source_target_pairs={{0,8},{4,12},{8,0},{12,4},{16,24},{20,28},{24,16},{28,20},{1,9},{5... | collective-permute-start | bytes 344072 | tf_op jit(solution)/shard_map/ppermute | solution.py:846
  16.1 6.9 %collective-permute-start.8 = (f32[14,16,128]{2,1,0:T(8,128)S(1)}, f32[14,16,128]{2,1,0:T(8,128)S(1)}, u32[]{:S(2)}, u32[]{:S(2)}) collective-permute-start(f32[14,16,128]{2,1,0:T(8,128)S(1)} %gate.1.refs_4_), channel_id=1, source_target_pairs={{0,12},{4,8},{8,4},{12,0},{16,28},{20,24},{24,20},{28,16},{1,13},{... | collective-permute-start | bytes 344072 | tf_op jit(solution)/shard_map/ppermute | solution.py:846
  18.7 6.1 %copy-start.6 = (f32[8,512]{1,0:T(8,128)S(1)}, f32[8,512]{1,0:T(8,128)}, u32[]{:S(2)}) copy-start(f32[8,512]{1,0:T(8,128)} %constant.10.clone.coef_ref) | copy-start | bytes 49156
  18.7 8.4 %collective-permute-start.5 = (f32[20,16,128]{2,1,0:T(8,128)S(1)}, f32[20,16,128]{2,1,0:T(8,128)S(1)}, u32[]{:S(2)}, u32[]{:S(2)}) collective-permute-start(f32[20,16,128]{2,1,0:T(8,128)S(1)} %get-tuple-element.29.own_b), channel_id=1, source_target_pairs={{4,8},{8,4},{12,16},{16,12},{20,24},{24,20},{28,0},{0,28},{5,9},{9... | collective-permute-start | bytes 491528 | tf_op jit(solution)/shard_map/ppermute | solution.py:864
  20.7 4.1 %collective-permute-start.9 = (f32[5,16,384]{2,1,0:T(8,128)S(1)}, f32[5,16,384]{2,1,0:T(8,128)S(1)}, u32[]{:S(2)}, u32[]{:S(2)}) collective-permute-start(f32[5,16,384]{2,1,0:T(8,128)S(1)} %get-tuple-element.36), channel_id=1, source_target_pairs={{0,1},{1,0},{2,3},{3,2},{4,5},{5,4},{6,7},{7,6},{8,9},{9,8},{10,11... | collective-permute-start | bytes 368648 | tf_op jit(solution)/shard_map/ppermute | solution.py:863
  23.9 4.6 %collective-permute-start.11 = (f32[5,24,128]{2,1,0:T(8,128)S(1)}, f32[5,24,128]{2,1,0:T(8,128)S(1)}, u32[]{:S(2)}, u32[]{:S(2)}) collective-permute-start(f32[5,24,128]{2,1,0:T(8,128)S(1)} %get-tuple-element.43.own_b), channel_id=1, source_target_pairs={{1,2},{2,1},{3,0},{0,3},{5,6},{6,5},{7,4},{4,7},{9,10},{10,9},{11,... | collective-permute-start | bytes 184328 | tf_op jit(solution)/shard_map/ppermute | solution.py:868
  24.0 4.5 %collective-permute-start.10 = (f32[5,16,128]{2,1,0:T(8,128)S(1)}, f32[5,16,128]{2,1,0:T(8,128)S(1)}, u32[]{:S(2)}, u32[]{:S(2)}) collective-permute-start(f32[5,16,128]{2,1,0:T(8,128)S(1)} %get-tuple-element.42.own_a), channel_id=1, source_target_pairs={{0,1},{1,0},{2,3},{3,2},{4,5},{5,4},{6,7},{7,6},{8,9},{9,8},{10,11... | collective-permute-start | bytes 122888 | tf_op jit(solution)/shard_map/ppermute | solution.py:867
